TPU v7x, 128 devices: a whole 4x4x4 slice. The times are simulated.
128 devices in a mesh: prompt: 8 (over y, core), sample: 16 (over z, x).
Axes of the slice: x: 4, y: 4, z: 4, core: 2. Of those that a mesh axis runs over, the one named last changes fastest.
Arguments:
- prompt_states: bfloat16 [8, 4096, 8192], P('prompt', None, 'sample'), may hold values from -6 to 6
- kv_weight: bfloat16 [8192, 2048], P('sample', 'prompt'), may hold values from -0.0625 to 0.0625
- queries: bfloat16 [8, 16, 8192], P('prompt', 'sample'), may hold values from -10 to 10
- new_kv: bfloat16 [8, 16, 2048], P('prompt', 'sample'), may hold values from -8 to 8
- local_pages: bfloat16 [8, 16, 16, 128, 2048], P('prompt', 'sample'), may hold values from -6 to 6
- pool_pages: bfloat16 [8, 16, 16, 128, 2048], P('prompt', 'sample'), may hold values from -6 to 6
- prompt_pages: int32 [8], P('prompt'), may hold values from 1 to 32, as said below
- comp_pages: int32 [8, 16], P('prompt', 'sample'), may hold values from 8 to 16, as said below
- preempted: int32 [8, 16], P('prompt', 'sample'), may hold values from 0 to 1, as said below
- page_where: int32 [8, 16, 16], P('prompt', 'sample'), may hold values from 0 to 255, as said below
Outputs:
- prefix_cache: bfloat16 [8, 4096, 2048], P('prompt', 'sample')
- attended: bfloat16 [8, 16, 8192], P('prompt', 'sample')
Inputs may be any that keep to these rules, and one draw needn't show every extreme that they name: `prompt_pages`: some prompt has 32 pages. `comp_pages`: every prompt has a sample of 16 pages. A preempted sample's pages c < comp_pages are read from the pool, the others' from local_pages; every prompt has a preempted sample of 16 pages. `page_where`: within one prompt every pool device and slot is named by exactly one page of one sample, and no pool device holds two pages of the same sample; entries of pages that are not read name slots of unrelated content.
All inputs are finite; a program needn't handle non-finite values.
Results may differ from a plain program's by a relative error of at most 0.039.
Values may be sent and summed in bfloat16 or wider, within the bound.
No kernel may reach another device: no remote copies, remote signals or barrier semaphores. Data moves between devices by JAX's collectives and lax.ppermute only.
A program may use at most 192 MiB of HBM per device.

v0:
```python
import functools
import math

import jax
import jax.numpy as jnp
from jax import lax
from jax.experimental import pallas as pl
from jax.experimental.pallas import tpu as pltpu
from jax.sharding import PartitionSpec as P

QUERY_HEADS = 64
GROUPS = 8
HEADS = 8
HEAD_SIZE = 128
PAGE = 128
SAMPLES = 16
CMAX = 16
ROWS = 256
SLICE = 512
COLUMNS = 256
KVW = 2048
KEYS = GROUPS * HEAD_SIZE
PACK = QUERY_HEADS + HEADS
LOW = -1e30
SCALE = 1.0 / math.sqrt(HEAD_SIZE)
MIB = 1 << 20
F32 = jnp.float32
BF16 = jnp.bfloat16

X_RIGHT = [(z * 4 + x, z * 4 + (x + 1) % 4) for z in range(4) for x in range(4)]
X_LEFT = [(z * 4 + x, z * 4 + (x + 3) % 4) for z in range(4) for x in range(4)]
X_FAR = [(z * 4 + x, z * 4 + (x + 2) % 4) for z in range(4) for x in range(4)]
Z_UP = [(z * 4 + x, (z + 1) % 4 * 4 + x) for z in range(4) for x in range(4)]
Z_DOWN = [(z * 4 + x, (z + 3) % 4 * 4 + x) for z in range(4) for x in range(4)]
Z_FAR = [(z * 4 + x, (z + 2) % 4 * 4 + x) for z in range(4) for x in range(4)]
SWAP = [(y * 2 + c, y * 2 + 1 - c) for y in range(4) for c in range(2)]
Y_SPLIT = [(y * 2 + c, (y + (1 if c == 0 else 3)) % 4 * 2 + c) for y in range(4) for c in range(2)]


def params(mib):
    return pltpu.CompilerParams(vmem_limit_bytes=mib * MIB)


def cost(flops, bytes_accessed):
    return pl.CostEstimate(flops=flops, bytes_accessed=bytes_accessed, transcendentals=0)


def nt_dot(a, b):
    return lax.dot_general(a, b, (((1,), (1,)), ((), ())), preferred_element_type=F32)


def put_lane(running, lane, column):
    at = lax.broadcasted_iota(jnp.int32, running.shape, len(running.shape) - 1)
    return jnp.where(at == lane, column, running)


def pick_kernel(states, *refs):
    outs, sems = refs[:6], refs[6]
    me = lax.axis_index("sample")
    z, x = me // 4, lax.rem(me, 4)
    copies = []
    for i, step in enumerate((1, 3, 2)):
        column = lax.rem(x + step, 4)
        for k, up in enumerate((2, 1, 3)):
            copies.append((states.at[lax.rem(z + up, 4), column], outs[2 * i].at[k]))
        copies.append((states.at[z, column], outs[2 * i + 1]))
    copies = [pltpu.make_async_copy(src, dst, sems.at[n]) for n, (src, dst) in enumerate(copies)]
    for copy in copies:
        copy.start()
    for copy in copies:
        copy.wait()


def pick(states):
    far = jax.ShapeDtypeStruct((3, ROWS, SLICE), BF16)
    near = jax.ShapeDtypeStruct((ROWS, SLICE), BF16)
    hbm = pl.BlockSpec(memory_space=pl.ANY)
    return pl.pallas_call(
        pick_kernel,
        out_shape=[far, near] * 3,
        in_specs=[hbm],
        out_specs=[hbm] * 6,
        scratch_shapes=[pltpu.SemaphoreType.DMA((12,))],
        compiler_params=params(16),
        cost_estimate=cost(0, 6 * MIB),
        name="pick_rows",
    )(states)


def product_kernel(blocks, *refs):
    states, pieces, outs = refs[:4], refs[4:12], refs[12:]
    for j in range(8):
        for k, block in enumerate(blocks):
            total = jnp.zeros((ROWS, COLUMNS), F32)
            for d in range(4):
                left = states[d][...] if block is None else states[d][block]
                total += jnp.dot(left, pieces[j][d], preferred_element_type=F32)
            out = outs[2 * k + j // 4]
            out[:, (j % 4) * COLUMNS : (j % 4 + 1) * COLUMNS] = total.astype(out.dtype)


def product(states, pieces, blocks, kind, name):
    vmem = pl.BlockSpec(memory_space=pltpu.VMEM)
    outs = [jax.ShapeDtypeStruct((ROWS, KVW // 2), kind)] * (2 * len(blocks))
    return pl.pallas_call(
        functools.partial(product_kernel, blocks),
        out_shape=outs,
        in_specs=[vmem] * 12,
        out_specs=[vmem] * len(outs),
        compiler_params=params(40),
        cost_estimate=cost(2 * len(blocks) * ROWS * KVW * KVW, 2 * MIB),
        name=name,
    )(*states, *pieces)


def log_rows(logs):
    out = jnp.full((HEADS, HEAD_SIZE), LOW, F32)
    for g in range(GROUPS):
        out = put_lane(out, g, logs[g * HEADS : (g + 1) * HEADS])
    return out


POOL_PAGES = 4


def page_kernel(slots, alive, query, *refs):
    pages, out = refs[:POOL_PAGES], refs[POOL_PAGES]
    step = pl.program_id(0)
    scores = []
    for k in range(POOL_PAGES):
        for g in range(GROUPS):
            keys = pages[k][0, :, g * HEAD_SIZE : (g + 1) * HEAD_SIZE]
            scores.append(nt_dot(query[k, g * HEADS : (g + 1) * HEADS], keys))
    scores = jnp.concatenate(scores) * SCALE
    top = jnp.max(scores, axis=-1, keepdims=True)
    exponent = jnp.exp(scores - top)
    total = jnp.sum(exponent, axis=-1, keepdims=True)
    logs, share = top + jnp.log(total), 1.0 / total
    for k in range(POOL_PAGES):
        live = alive[step * POOL_PAGES + k] != 0
        for g in range(GROUPS):
            rows = slice(k * QUERY_HEADS + g * HEADS, k * QUERY_HEADS + (g + 1) * HEADS)
            values = pages[k][0, :, KEYS + g * HEAD_SIZE : KEYS + (g + 1) * HEAD_SIZE]
            mixture = jnp.dot(exponent[rows].astype(BF16), values, preferred_element_type=F32)
            out[k, g * HEADS : (g + 1) * HEADS] = jnp.where(live, mixture * share[rows], 0.0)
        mine = log_rows(logs[k * QUERY_HEADS : (k + 1) * QUERY_HEADS])
        out[k, QUERY_HEADS:] = jnp.where(live, mine, LOW)


def pool_attention(slots, alive, queries_all, pool):
    def page_of(k):
        return lambda s, slots, alive: (slots[s * POOL_PAGES + k], 0, 0)

    return pl.pallas_call(
        page_kernel,
        out_shape=jax.ShapeDtypeStruct((SAMPLES, PACK, HEAD_SIZE), F32),
        grid_spec=pltpu.PrefetchScalarGridSpec(
            num_scalar_prefetch=2,
            grid=(SAMPLES // POOL_PAGES,),
            in_specs=[
                pl.BlockSpec(
                    (POOL_PAGES, QUERY_HEADS, HEAD_SIZE), lambda s, slots, alive: (s, 0, 0)
                )
            ]
            + [pl.BlockSpec((1, PAGE, KVW), page_of(k)) for k in range(POOL_PAGES)],
            out_specs=pl.BlockSpec(
                (POOL_PAGES, PACK, HEAD_SIZE), lambda s, slots, alive: (s, 0, 0)
            ),
        ),
        compiler_params=params(32),
        cost_estimate=cost(10_000_000_000, 8 * MIB),
        name="pool_attention",
    )(slots, alive, queries_all, *[pool] * POOL_PAGES)


LOCAL_PAGES = 4


def local_kernel(pages_alive, query, new, pages, out, top_ref, sum_ref, mix_ref):
    step = pl.program_id(0)
    width = LOCAL_PAGES * PAGE

    @pl.when(step == 0)
    def _():
        for g in range(GROUPS):
            rows = slice(g * HEADS, (g + 1) * HEADS)
            lanes = slice(g * HEAD_SIZE, (g + 1) * HEAD_SIZE)
            value_lanes = slice(KEYS + g * HEAD_SIZE, KEYS + (g + 1) * HEAD_SIZE)
            products = query[rows].astype(F32) * new[0:1, lanes].astype(F32)
            top_ref[rows] = jnp.sum(products, axis=-1, keepdims=True) * SCALE
            sum_ref[rows] = jnp.ones((HEADS, 1), F32)
            mix_ref[rows] = jnp.broadcast_to(new[0:1, value_lanes].astype(F32), (HEADS, HEAD_SIZE))

    @pl.when(step * LOCAL_PAGES < pages_alive[0])
    def _():
        block = pages.reshape(width, KVW)
        at = step * width + lax.broadcasted_iota(jnp.int32, (QUERY_HEADS, width), 1)
        live = at < pages_alive[0] * PAGE
        scores = jnp.concatenate(
            [
                nt_dot(
                    query[g * HEADS : (g + 1) * HEADS],
                    block[:, g * HEAD_SIZE : (g + 1) * HEAD_SIZE],
                )
                for g in range(GROUPS)
            ]
        )
        scores = jnp.where(live, scores * SCALE, LOW)
        old = top_ref[...]
        top = jnp.maximum(old, jnp.max(scores, axis=-1, keepdims=True))
        shrink = jnp.exp(old - top)
        exponent = jnp.where(live, jnp.exp(scores - top), 0.0)
        top_ref[...] = top
        sum_ref[...] = sum_ref[...] * shrink + jnp.sum(exponent, axis=-1, keepdims=True)
        for g in range(GROUPS):
            rows = slice(g * HEADS, (g + 1) * HEADS)
            values = block[:, KEYS + g * HEAD_SIZE : KEYS + (g + 1) * HEAD_SIZE]
            mix_ref[rows] = mix_ref[rows] * shrink[rows] + jnp.dot(
                exponent[rows].astype(BF16), values, preferred_element_type=F32
            )

    @pl.when(step == CMAX // LOCAL_PAGES - 1)
    def _():
        out[:QUERY_HEADS] = mix_ref[...] / sum_ref[...]
        out[QUERY_HEADS:] = log_rows(top_ref[...] + jnp.log(sum_ref[...]))


def local_attention(pages_alive, query, new, pages):
    def block_of(step, alive):
        last = jnp.maximum(alive[0] - 1, 0) // LOCAL_PAGES
        return (jnp.minimum(step, last), 0, 0)

    return pl.pallas_call(
        local_kernel,
        out_shape=jax.ShapeDtypeStruct((PACK, HEAD_SIZE), F32),
        grid_spec=pltpu.PrefetchScalarGridSpec(
            num_scalar_prefetch=1,
            grid=(CMAX // LOCAL_PAGES,),
            in_specs=[
                pl.BlockSpec((QUERY_HEADS, HEAD_SIZE), lambda step, alive: (0, 0)),
                pl.BlockSpec((1, KVW), lambda step, alive: (0, 0)),
                pl.BlockSpec((LOCAL_PAGES, PAGE, KVW), block_of),
            ],
            out_specs=pl.BlockSpec((PACK, HEAD_SIZE), lambda step, alive: (0, 0)),
            scratch_shapes=[
                pltpu.VMEM((QUERY_HEADS, 1), F32),
                pltpu.VMEM((QUERY_HEADS, 1), F32),
                pltpu.VMEM((QUERY_HEADS, HEAD_SIZE), F32),
            ],
        ),
        compiler_params=params(32),
        cost_estimate=cost(10_000_000_000, 8 * MIB),
        name="local_attention",
    )(pages_alive, query, new, pages)


def prefix_kernel(
    prompt_pages, own_l, own_r, up_l, up_r, down_l, down_r, queries, pool, cache, packed
):
    me, prompt = lax.axis_index("sample"), lax.axis_index("prompt")
    z, x = me // 4, lax.rem(me, 4)
    y, core = prompt // 2, lax.rem(prompt, 2)
    near = lax.rem(y + 3 - 2 * core, 4)
    other = lax.rem(y + 1 + 2 * core, 4)
    far = lax.rem(y + 2, 4)
    columns = (
        2 * y + core, 2 * y + 1 - core, 2 * near + core, 2 * near + 1 - core,
        2 * other + 1 - core, 2 * other + core, 2 * far + core, 2 * far + 1 - core,
    )
    for j in range(8):
        lanes = slice((j % 4) * COLUMNS, (j % 4 + 1) * COLUMNS)
        own, up, down = (own_l, up_l, down_l) if j < 4 else (own_r, up_r, down_r)
        total = own[:, lanes] + up[:, lanes].astype(F32) + down[:, lanes].astype(F32)
        target = pl.ds(pl.multiple_of(columns[j] * COLUMNS, COLUMNS), COLUMNS)
        cache[0, :, target] = total.astype(BF16)
    sources = [
        lax.rem(z + 4 - dz, 4) * 4 + lax.rem(x + 4 - dx, 4) for dz in (0, 1, 3, 2) for dx in (0, 1, 3, 2)
    ]
    live = lax.broadcasted_iota(jnp.int32, (SAMPLES * HEADS, ROWS), 1) < prompt_pages[0] * PAGE - me * ROWS
    logs = jnp.full((SAMPLES * HEADS, HEAD_SIZE), LOW, F32)
    for g in range(GROUPS):
        keys = cache[0, :, g * HEAD_SIZE : (g + 1) * HEAD_SIZE]
        values = cache[0, :, KEYS + g * HEAD_SIZE : KEYS + (g + 1) * HEAD_SIZE]
        scores = jnp.where(live, nt_dot(queries[g], keys) * SCALE, LOW)
        top = jnp.max(scores, axis=-1, keepdims=True)
        exponent = jnp.where(live, jnp.exp(scores - top), 0.0)
        total = jnp.sum(exponent, axis=-1, keepdims=True)
        mixture = jnp.dot(exponent.astype(BF16), values, preferred_element_type=F32)
        some = total > 0.0
        total = jnp.where(some, total, 1.0)
        log = jnp.where(some, top + jnp.log(total), LOW)
        rows = slice(g * HEADS, (g + 1) * HEADS)
        pool_log = pool[:, QUERY_HEADS:, g : g + 1].reshape(SAMPLES * HEADS, 1)
        pool_mixture = pool[:, rows].reshape(SAMPLES * HEADS, HEAD_SIZE)
        high = jnp.maximum(log, pool_log)
        here, there = jnp.exp(log - high), jnp.exp(pool_log - high)
        both = here + there
        merged = mixture * (here / (total * both)) + pool_mixture * (there / both)
        for r, source in enumerate(sources):
            packed[source, rows] = merged[r * HEADS : (r + 1) * HEADS]
        logs = put_lane(logs, g, high + jnp.log(both))
    for r, source in enumerate(sources):
        packed[source, QUERY_HEADS:] = logs[r * HEADS : (r + 1) * HEADS]


def prefix_attention(prompt_pages, parts, queries, pool):
    smem, vmem = pl.BlockSpec(memory_space=pltpu.SMEM), pl.BlockSpec(memory_space=pltpu.VMEM)
    return pl.pallas_call(
        prefix_kernel,
        out_shape=[
            jax.ShapeDtypeStruct((1, ROWS, KVW), BF16),
            jax.ShapeDtypeStruct((SAMPLES, PACK, HEAD_SIZE), F32),
        ],
        in_specs=[smem] + [vmem] * 8,
        out_specs=[vmem, vmem],
        compiler_params=params(32),
        cost_estimate=cost(300_000_000, 6 * MIB),
        name="prefix_attention",
    )(prompt_pages, *parts, queries, pool)


def combine_kernel(arrived, local, out):
    for g in range(GROUPS):
        rows = slice(g * HEADS, (g + 1) * HEADS)
        logs = arrived[:, QUERY_HEADS:, g : g + 1]
        local_log = local[QUERY_HEADS:, g : g + 1]
        high = jnp.maximum(jnp.max(logs, axis=0), local_log)
        shares = jnp.exp(logs - high[None])
        local_share = jnp.exp(local_log - high)
        total = jnp.sum(shares, axis=0) + local_share
        mixture = jnp.sum(arrived[:, rows] * shares, axis=0) + local[rows] * local_share
        out[rows] = (mixture / total).astype(BF16)


def combine(arrived, local):
    vmem = pl.BlockSpec(memory_space=pltpu.VMEM)
    return pl.pallas_call(
        combine_kernel,
        out_shape=jax.ShapeDtypeStruct((QUERY_HEADS, HEAD_SIZE), BF16),
        in_specs=[vmem, vmem],
        out_specs=vmem,
        compiler_params=params(32),
        cost_estimate=cost(1_000_000, MIB),
        name="combine",
    )(arrived, local)


def per_device(
    prompt_states,
    kv_weight,
    queries,
    new_kv,
    local_pages,
    pool_pages,
    prompt_pages,
    comp_pages,
    preempted,
    page_where,
):
    own_index = lax.axis_index("sample")
    tie = lax.optimization_barrier

    plan = jnp.concatenate([page_where[0, 0], comp_pages[0], preempted[0]]).astype(BF16)
    plan = jnp.pad(plan.reshape(1, -1), ((0, 7), (0, COLUMNS - CMAX - 2)))
    query = queries.reshape(QUERY_HEADS, HEAD_SIZE)
    sent = jnp.concatenate([kv_weight, queries.reshape(-1, COLUMNS), plan])
    along_x = [sent] + [lax.ppermute(sent, "sample", to) for to in (X_RIGHT, X_LEFT, X_FAR)]

    states = prompt_states.reshape(4, 4, ROWS, SLICE)
    to_right, last_right, to_left, last_left, to_far, last_far = pick(states)
    rows_right = lax.ppermute(to_right, "sample", X_RIGHT)
    rows_left = lax.ppermute(to_left, "sample", X_LEFT)
    rows_far = lax.ppermute(to_far, "sample", X_FAR)
    last_right, last_left, last_far, rows_right = tie((last_right, last_left, last_far, rows_right))
    own_states = [
        lax.ppermute(last_right, "sample", X_RIGHT),
        lax.ppermute(last_left, "sample", X_LEFT),
        lax.ppermute(last_far, "sample", X_FAR),
    ]

    here = jnp.stack([a[:SLICE] for a in along_x])
    here_other = lax.ppermute(here, "prompt", SWAP)
    near = lax.ppermute(here, "prompt", Y_SPLIT)
    near_other = lax.ppermute(here_other, "prompt", Y_SPLIT)
    far = lax.ppermute(near, "prompt", Y_SPLIT)
    near_swapped = lax.ppermute(near, "prompt", SWAP)
    near_other_swapped = lax.ppermute(near_other, "prompt", SWAP)
    far_other = lax.ppermute(far, "prompt", SWAP)
    pieces = [
        here, here_other, near, near_other,
        near_swapped, near_other_swapped, far, far_other,
    ]

    of_row = jnp.stack([a[SLICE:] for a in along_x])
    everyone = jnp.concatenate(
        [of_row] + [lax.ppermute(of_row, "sample", to) for to in (Z_UP, Z_DOWN, Z_FAR)]
    )
    queries_all = everyone[:, : QUERY_HEADS // 2].reshape(SAMPLES, QUERY_HEADS, HEAD_SIZE)
    queries_all, rows_right = tie((queries_all, rows_right))
    plans = everyone[:, QUERY_HEADS // 2, : CMAX + 2].astype(jnp.int32)
    where_all, lens_all, flags_all = plans[:, :CMAX], plans[:, CMAX], plans[:, CMAX + 1]
    page_ids = jnp.arange(CMAX, dtype=jnp.int32)
    here_page = where_all // CMAX == own_index
    slots = jnp.sum(jnp.where(here_page, where_all % CMAX, 0), axis=1)
    live_all = (page_ids[None, :] < lens_all[:, None]) & (flags_all[:, None] > 0)
    alive = jnp.any(here_page & live_all, axis=1).astype(jnp.int32)
    pool = pool_attention(slots, alive, queries_all, pool_pages[0, 0])
    local_alive = jnp.where(preempted[0] > 0, 0, comp_pages[0])
    query, here_other = tie((query, here_other))
    local = local_attention(local_alive, query, new_kv[0], local_pages[0, 0])
    by_group = queries_all.reshape(SAMPLES, GROUPS, HEADS, HEAD_SIZE)
    by_group = by_group.transpose(1, 0, 2, 3).reshape(GROUPS, SAMPLES * HEADS, HEAD_SIZE)

    z, x = own_index // 4, own_index % 4
    mine = lax.dynamic_index_in_dim(states, x, 1, keepdims=False)
    mine_rows = jnp.stack(
        [lax.dynamic_index_in_dim(mine, (z + up) % 4, 0, keepdims=False) for up in (2, 1, 3)]
    )
    mine_last = lax.dynamic_index_in_dim(mine, z, 0, keepdims=False)
    mine_rows, pool, local = tie((mine_rows, pool, local))
    rows = [mine_rows, rows_right, rows_left, rows_far]
    far_l, far_r = product(rows, pieces, (0,), BF16, "product_far")
    up_l, up_r, down_l, down_r = product(rows, pieces, (1, 2), BF16, "product_near")
    own_l, own_r = product([mine_last] + own_states, pieces, (None,), F32, "product_own")
    from_down = lax.ppermute(far_l, "sample", Z_UP)
    from_up = lax.ppermute(far_r, "sample", Z_DOWN)
    up_l = (up_l.astype(F32) + from_down.astype(F32)).astype(BF16)
    down_r = (down_r.astype(F32) + from_up.astype(F32)).astype(BF16)
    sums = [
        own_l,
        own_r,
        lax.ppermute(up_l, "sample", Z_UP),
        lax.ppermute(up_r, "sample", Z_UP),
        lax.ppermute(down_l, "sample", Z_DOWN),
        lax.ppermute(down_r, "sample", Z_DOWN),
    ]

    cache, packed = prefix_attention(prompt_pages, sums, by_group, pool)
    arrived = lax.all_to_all(packed, "sample", split_axis=0, concat_axis=0, tiled=True)
    attended = combine(arrived, local)
    return (cache, attended.reshape(1, 1, -1))


def solution(mesh):
    return jax.shard_map(
        per_device,
        mesh=mesh,
        in_specs=(
            P("prompt", None, "sample"),
            P("sample", "prompt"),
            P("prompt", "sample", None),
            P("prompt", "sample", None),
            P("prompt", "sample", None, None, None),
            P("prompt", "sample", None, None, None),
            P("prompt"),
            P("prompt", "sample"),
            P("prompt", "sample"),
            P("prompt", "sample", None),
        ),
        out_specs=(P("prompt", "sample", None), P("prompt", "sample", None)),
        check_vma=False,
    )
```

profile of v0, /device:TPU:0, one launch (start us, length us, event | category | flops | bytes accessed | tf_op | source)
XLA Modules:
  0.0 143.0 jit_solution(13604612818127371797)
XLA Ops:
  2.0 0.7 convert_bitcast_fusion
  2.6 0.8 reduce
  3.6 1.0 pad_maximum_fusion.2
  4.6 3.2 %collective-permute-start.6 = (bf16[552,256]{1,0:T(8,128)(2,1)S(1)}, bf16[552,256]{1,0:T(8,128)(2,1)S(1)}, u32[]{:S(2)}, u32[]{:S(2)}) collective-permute-start(bf16[552,256]{1,0:T(8,128)(2,1)S(1)} %pad_maximum_fusion.2), channel_id=1, source_target_pairs={{0,2},{1,3},{2,0},{3,1},{4,6},{5,7},{6,4},{7,5},{8,10},{9,11},{10,... | collective-permute-start | bytes 847880 | tf_op jit(solution)/shard_map/ppermute | solution.py:367
  7.8 1.1 collective-permute-start.5
  8.9 0.9 collective-permute-start.4
  9.8 2.2 %copy-done = bf16[1,4096,512]{2,1,0:T(8,128)(2,1)S(1)} copy-done((bf16[1,4096,512]{2,1,0:T(8,128)(2,1)S(1)}, bf16[1,4096,512]{2,1,0:T(8,128)(2,1)}, u32[]{:S(2)}) %copy-start) | copy-done | bytes 4194328
  12.0 1.2 pick_rows.1
  13.2 0.9 copy-done.5
  14.1 0.7 copy-done.6
  14.8 0.7 copy-done.8
  15.5 0.7 copy-done.10
  16.2 0.6 collective-permute-start
  16.8 2.6 %collective-permute-start.17 = (bf16[3,256,512]{2,1,0:T(8,128)(2,1)}, bf16[3,256,512]{2,1,0:T(8,128)(2,1)}, u32[]{:S(2)}, u32[]{:S(2)}) collective-permute-start(bf16[3,256,512]{2,1,0:T(8,128)(2,1)} %get-tuple-element.42), channel_id=1, source_target_pairs={{0,3},{1,0},{2,1},{3,2},{4,7},{5,4},{6,5},{7,6},{8,11},{9,8},{10,9... | collective-permute-start | bytes 2359304 | tf_op jit(solution)/shard_map/ppermute | solution.py:372
  19.5 1.9 %dynamic-slice_bitcast_fusion.2 = (bf16[1,256,512]{2,1,0:T(8,128)(2,1)S(1)}, bf16[1,256,512]{2,1,0:T(8,128)(2,1)S(1)}, bf16[1,256,512]{2,1,0:T(8,128)(2,1)S(1)}, bf16[256,512]{1,0:T(8,128)(2,1)}) fusion(bf16[4,4,256,512]{3,2,1,0:T(8,128)(2,1)} %bitcast.47, s32[]{:T(128)S(6)} %select_n.79, s32[]{:T(128)S(6)} %select_n.76, s32[]{:T(128)S(6)} %select_n.85, ...), kind=kLoop, calls=%fused_computation.11 | loop fusion | bytes 2097172 | tf_op jit(solution)/shard_map/jit(dynamic_index_in_dim)/dynamic_slice | solution.py:417
  21.4 1.0 pad_maximum_fusion.1.refs_0_
  22.5 0.6 copy-done.14
  23.5 1.6 %collective-permute-start.8 = (bf16[4,512,256]{2,1,0:T(8,128)(2,1)S(1)}, bf16[4,512,256]{2,1,0:T(8,128)(2,1)S(1)}, u32[]{:S(2)}, u32[]{:S(2)}) collective-permute-start(bf16[4,512,256]{2,1,0:T(8,128)(2,1)S(1)} %pad_maximum_fusion.refs_4_), channel_id=1, source_target_pairs={{0,32},{16,112},{32,64},{48,16},{64,96},{80,48},{96,0},{112,80},{1... | collective-permute-start | bytes 3145736 | tf_op jit(solution)/shard_map/ppermute | solution.py:383
  25.1 0.7 slice_bitcast_fusion.4
  25.9 0.7 slice_bitcast_fusion.5
  26.6 2.0 %collective-permute-start.14 = (bf16[4,40,256]{2,1,0:T(8,128)(2,1)S(1)}, bf16[4,40,256]{2,1,0:T(8,128)(2,1)S(1)}, u32[]{:S(2)}, u32[]{:S(2)}) collective-permute-start(bf16[4,40,256]{2,1,0:T(8,128)(2,1)S(1)} %pad_maximum_fusion.3), channel_id=1, source_target_pairs={{0,4},{1,5},{2,6},{3,7},{4,8},{5,9},{6,10},{7,11},{8,12},{9,13},{1... | collective-permute-start | bytes 245768 | tf_op jit(solution)/shard_map/ppermute | solution.py:396
  28.6 0.7 constant_dynamic-update-slice_fusion.5
  29.3 0.7 constant_dynamic-update-slice_fusion.4
  30.1 3.1 %collective-permute-done.14 = bf16[4,40,256]{2,1,0:T(8,128)(2,1)S(1)} collective-permute-done((bf16[4,40,256]{2,1,0:T(8,128)(2,1)S(1)}, bf16[4,40,256]{2,1,0:T(8,128)(2,1)S(1)}, u32[]{:S(2)}, u32[]{:S(2)}) %collective-permute-start.14) | collective-permute-done | bytes 81952 | tf_op jit(solution)/shard_map/ppermute | solution.py:396
  33.1 2.3 %collective-permute-start.15 = (bf16[4,40,256]{2,1,0:T(8,128)(2,1)S(1)}, bf16[4,40,256]{2,1,0:T(8,128)(2,1)S(1)}, u32[]{:S(2)}, u32[]{:S(2)}) collective-permute-start(bf16[4,40,256]{2,1,0:T(8,128)(2,1)S(1)} %pad_maximum_fusion.3), channel_id=1, source_target_pairs={{0,12},{1,13},{2,14},{3,15},{4,0},{5,1},{6,2},{7,3},{8,4},{9,5},{1... | collective-permute-start | bytes 245768 | tf_op jit(solution)/shard_map/ppermute | solution.py:396
  35.5 1.3 collective-permute-start.9
  36.8 2.8 %collective-permute-done.8.refs_6_ = bf16[4,512,256]{2,1,0:T(8,128)(2,1)S(1)} collective-permute-done((bf16[4,512,256]{2,1,0:T(8,128)(2,1)S(1)}, bf16[4,512,256]{2,1,0:T(8,128)(2,1)S(1)}, u32[]{:S(2)}, u32[]{:S(2)}) %collective-permute-start.8) | collective-permute-done | bytes 1048608 | tf_op jit(solution)/shard_map/ppermute | solution.py:383
  39.6 0.4 collective-permute-start.12
  40.0 4.0 %collective-permute-start.16 = (bf16[4,40,256]{2,1,0:T(8,128)(2,1)S(1)}, bf16[4,40,256]{2,1,0:T(8,128)(2,1)S(1)}, u32[]{:S(2)}, u32[]{:S(2)}) collective-permute-start(bf16[4,40,256]{2,1,0:T(8,128)(2,1)S(1)} %pad_maximum_fusion.3), channel_id=1, source_target_pairs={{0,8},{1,9},{2,10},{3,11},{4,12},{5,13},{6,14},{7,15},{8,0},{9,1},... | collective-permute-start | bytes 245768 | tf_op jit(solution)/shard_map/ppermute | solution.py:396
  43.9 2.4 %collective-permute-done.16 = bf16[4,40,256]{2,1,0:T(8,128)(2,1)S(1)} collective-permute-done((bf16[4,40,256]{2,1,0:T(8,128)(2,1)S(1)}, bf16[4,40,256]{2,1,0:T(8,128)(2,1)S(1)}, u32[]{:S(2)}, u32[]{:S(2)}) %collective-permute-start.16) | collective-permute-done | bytes 81952 | tf_op jit(solution)/shard_map/ppermute | solution.py:396
  46.3 1.6 %collective-permute-start.18 = (bf16[3,256,512]{2,1,0:T(8,128)(2,1)}, bf16[3,256,512]{2,1,0:T(8,128)(2,1)}, u32[]{:S(2)}, u32[]{:S(2)}) collective-permute-start(bf16[3,256,512]{2,1,0:T(8,128)(2,1)} %copy-done.5), channel_id=1, source_target_pairs={{0,2},{1,3},{2,0},{3,1},{4,6},{5,7},{6,4},{7,5},{8,10},{9,11},{10,... | collective-permute-start | bytes 2359304 | tf_op jit(solution)/shard_map/ppermute | solution.py:373
  48.0 0.7 slice.56
  48.7 0.2 slice_reduce_fusion
  48.9 0.2 fusion.10
  49.1 0.2 fusion.11
  49.3 1.0 reshape.79.query
  50.5 0.6 collective-permute-start.10
  51.0 0.6 collective-permute-done.9.refs_7_
  51.6 11.2 %collective-permute-done.12.refs_10_ = bf16[4,512,256]{2,1,0:T(8,128)(2,1)} collective-permute-done((bf16[4,512,256]{2,1,0:T(8,128)(2,1)S(1)}, bf16[4,512,256]{2,1,0:T(8,128)(2,1)}, u32[]{:S(2)}, u32[]{:S(2)}) %collective-permute-start.12) | collective-permute-done | bytes 1048608 | tf_op jit(solution)/shard_map/ppermute | solution.py:385
  62.8 3.4 %copy-done.3 = bf16[1,1,16,128,2048]{4,3,2,1,0:T(8,128)(2,1)S(1)} copy-done((bf16[1,1,16,128,2048]{4,3,2,1,0:T(8,128)(2,1)S(1)}, bf16[1,1,16,128,2048]{4,3,2,1,0:T(8,128)(2,1)}, u32[]{:S(2)}) %copy-start.3) | copy-done | bytes 8388632
  66.2 4.3 %pool_attention.1.pool = f32[16,72,128]{2,1,0:T(8,128)S(1)} custom-call(s32[16]{0:T(128)S(1)} %fusion.2.slots, s32[16]{0:T(128)S(1)} %convert_element_type.39.alive, bf16[16,64,128]{2,1,0:T(8,128)(2,1)S(1)} %reshape.79.query, bf16[16,128,2048]{2,1,0:T(8,128)(2,1)S(1)} %bitcast.50, bf16[16,128,2048]{2,1,0:T(8,128)(2,1)S(1)} %bitcast.51, ...), custom_call_target="tpu_custom_call" | custom-call | flops 10000000000 | bytes 8388608 | tf_op jit(solution)/shard_map/pool_attention/pallas_call | solution.py:154
  70.5 3.4 %copy-done.4 = bf16[1,1,16,128,2048]{4,3,2,1,0:T(8,128)(2,1)S(1)} copy-done((bf16[1,1,16,128,2048]{4,3,2,1,0:T(8,128)(2,1)S(1)}, bf16[1,1,16,128,2048]{4,3,2,1,0:T(8,128)(2,1)}, u32[]{:S(2)}) %copy-start.4) | copy-done | bytes 8388632
  73.9 0.2 local_attention.1.local
  74.2 0.8 copy-done.1
  75.0 4.6 %product_far.1 = (bf16[256,1024]{1,0:T(8,128)(2,1)S(1)}, bf16[256,1024]{1,0:T(8,128)(2,1)S(1)}) custom-call(bf16[3,256,512]{2,1,0:T(8,128)(2,1)S(1)} %copy-done.1, bf16[3,256,512]{2,1,0:T(8,128)(2,1)} %collective-permute-done.refs_1_, bf16[3,256,512]{2,1,0:T(8,128)(2,1)} %collective-permute-done.17.refs_2_, ...), custom_call_target="tpu_custom_call" | custom-call | flops 2147483648 | bytes 2097152 | tf_op jit(solution)/shard_map/product_far/pallas_call | solution.py:105
  79.6 3.4 %collective-permute-start.23 = (bf16[256,1024]{1,0:T(8,128)(2,1)S(1)}, bf16[256,1024]{1,0:T(8,128)(2,1)S(1)}, u32[]{:S(2)}, u32[]{:S(2)}) collective-permute-start(bf16[256,1024]{1,0:T(8,128)(2,1)S(1)} %get-tuple-element.49), channel_id=1, source_target_pairs={{0,12},{1,13},{2,14},{3,15},{4,0},{5,1},{6,2},{7,3},{8,4},{9,5},{1... | collective-permute-start | bytes 1572872 | tf_op jit(solution)/shard_map/ppermute | solution.py:426
  83.1 0.9 collective-permute-start.1
  84.0 2.3 %collective-permute-start.2 = (bf16[256,512]{1,0:T(8,128)(2,1)S(1)}, bf16[256,512]{1,0:T(8,128)(2,1)S(1)}, u32[]{:S(2)}, u32[]{:S(2)}) collective-permute-start(bf16[256,512]{1,0:T(8,128)(2,1)S(1)} %copy-done.9), channel_id=1, source_target_pairs={{0,3},{1,0},{2,1},{3,2},{4,7},{5,4},{6,5},{7,6},{8,11},{9,8},{10,9... | collective-permute-start | bytes 786440 | tf_op jit(solution)/shard_map/ppermute | solution.py:377
  86.3 6.8 %product_near.1 = (bf16[256,1024]{1,0:T(8,128)(2,1)S(1)}, bf16[256,1024]{1,0:T(8,128)(2,1)S(1)}, bf16[256,1024]{1,0:T(8,128)(2,1)S(1)}, bf16[256,1024]{1,0:T(8,128)(2,1)S(1)}) custom-call(bf16[3,256,512]{2,1,0:T(8,128)(2,1)S(1)} %copy-done.1, bf16[3,256,512]{2,1,0:T(8,128)(2,1)} %collective-permute-done.refs_1_, ...), custom_call_target="tpu_custom_call" | custom-call | flops 4294967296 | bytes 2097152 | tf_op jit(solution)/shard_map/product_near/pallas_call | solution.py:105
  93.2 1.7 %collective-permute-done.23 = bf16[256,1024]{1,0:T(8,128)(2,1)S(1)} collective-permute-done((bf16[256,1024]{1,0:T(8,128)(2,1)S(1)}, bf16[256,1024]{1,0:T(8,128)(2,1)S(1)}, u32[]{:S(2)}, u32[]{:S(2)}) %collective-permute-start.23) | collective-permute-done | bytes 524320 | tf_op jit(solution)/shard_map/ppermute | solution.py:426
  94.9 3.7 %collective-permute-start.22 = (bf16[256,1024]{1,0:T(8,128)(2,1)S(1)}, bf16[256,1024]{1,0:T(8,128)(2,1)S(1)}, u32[]{:S(2)}, u32[]{:S(2)}) collective-permute-start(bf16[256,1024]{1,0:T(8,128)(2,1)S(1)} %get-tuple-element.47), channel_id=1, source_target_pairs={{0,12},{1,13},{2,14},{3,15},{4,0},{5,1},{6,2},{7,3},{8,4},{9,5},{1... | collective-permute-start | bytes 1572872 | tf_op jit(solution)/shard_map/ppermute | solution.py:434
  98.6 0.2 add_convert_fusion
  98.8 3.5 %collective-permute-done.19 = bf16[256,1024]{1,0:T(8,128)(2,1)S(1)} collective-permute-done((bf16[256,1024]{1,0:T(8,128)(2,1)S(1)}, bf16[256,1024]{1,0:T(8,128)(2,1)S(1)}, u32[]{:S(2)}, u32[]{:S(2)}) %collective-permute-start.19) | collective-permute-done | bytes 524320 | tf_op jit(solution)/shard_map/ppermute | solution.py:425
  102.3 0.2 add_convert_fusion.1
  102.6 2.1 %collective-permute-start.20 = (bf16[256,1024]{1,0:T(8,128)(2,1)S(1)}, bf16[256,1024]{1,0:T(8,128)(2,1)S(1)}, u32[]{:S(2)}, u32[]{:S(2)}) collective-permute-start(bf16[256,1024]{1,0:T(8,128)(2,1)S(1)} %add_convert_fusion.1), channel_id=1, source_target_pairs={{0,4},{1,5},{2,6},{3,7},{4,8},{5,9},{6,10},{7,11},{8,12},{9,13},{1... | collective-permute-start | bytes 1572872 | tf_op jit(solution)/shard_map/ppermute | solution.py:432
  104.7 1.5 %collective-permute-start.3 = (bf16[256,512]{1,0:T(8,128)(2,1)S(1)}, bf16[256,512]{1,0:T(8,128)(2,1)S(1)}, u32[]{:S(2)}, u32[]{:S(2)}) collective-permute-start(bf16[256,512]{1,0:T(8,128)(2,1)S(1)} %copy-done.7), channel_id=1, source_target_pairs={{0,2},{1,3},{2,0},{3,1},{4,6},{5,7},{6,4},{7,5},{8,10},{9,11},{10,... | collective-permute-start | bytes 786440 | tf_op jit(solution)/shard_map/ppermute | solution.py:378
  106.8 5.7 %collective-permute-done.3.refs_3_ = bf16[256,512]{1,0:T(8,128)(2,1)S(1)} collective-permute-done((bf16[256,512]{1,0:T(8,128)(2,1)S(1)}, bf16[256,512]{1,0:T(8,128)(2,1)S(1)}, u32[]{:S(2)}, u32[]{:S(2)}) %collective-permute-start.3) | collective-permute-done | bytes 262176 | tf_op jit(solution)/shard_map/ppermute | solution.py:378
  112.5 3.9 %product_own.1 = (f32[256,1024]{1,0:T(8,128)S(1)}, f32[256,1024]{1,0:T(8,128)S(1)}) custom-call(bf16[256,512]{1,0:T(8,128)(2,1)S(1)} %copy-done.2, bf16[256,512]{1,0:T(8,128)(2,1)S(1)} %collective-permute-done.1.refs_1_, bf16[256,512]{1,0:T(8,128)(2,1)S(1)} %collective-permute-done.2.refs_2_, bf16[256,512]{1,0:T(8,128)(2,1)S(1)} %collective-permute-done.3.refs_3_, ...), custom_call_target="tpu_custom_call" | custom-call | flops 2147483648 | bytes 2097152 | tf_op jit(solution)/shard_map/product_own/pallas_call | solution.py:105
  116.4 4.5 %collective-permute-done.24.down_r = bf16[256,1024]{1,0:T(8,128)(2,1)S(1)} collective-permute-done((bf16[256,1024]{1,0:T(8,128)(2,1)S(1)}, bf16[256,1024]{1,0:T(8,128)(2,1)S(1)}, u32[]{:S(2)}, u32[]{:S(2)}) %collective-permute-start.24) | collective-permute-done | bytes 524320 | tf_op jit(solution)/shard_map/ppermute | solution.py:435
  120.9 2.6 %collective-permute-done.20.up_l = bf16[256,1024]{1,0:T(8,128)(2,1)S(1)} collective-permute-done((bf16[256,1024]{1,0:T(8,128)(2,1)S(1)}, bf16[256,1024]{1,0:T(8,128)(2,1)S(1)}, u32[]{:S(2)}, u32[]{:S(2)}) %collective-permute-start.20) | collective-permute-done | bytes 524320 | tf_op jit(solution)/shard_map/ppermute | solution.py:432
  123.5 2.8 %prefix_attention.1 = (bf16[1,256,2048]{2,1,0:T(8,128)(2,1)}, f32[16,72,128]{2,1,0:T(8,128)S(1)}) custom-call(s32[1]{0:T(128)S(6)} %copy.21.prompt_pages, f32[256,1024]{1,0:T(8,128)S(1)} %get-tuple-element.35.own_l, f32[256,1024]{1,0:T(8,128)S(1)} %get-tuple-element.36.own_r, bf16[256,1024]{1,0:T(8,128)(2,1)S(1)} %collective-permute-done.20.up_l, ...), custom_call_target="tpu_custom_call" | custom-call | flops 300000000 | bytes 6291456 | tf_op jit(solution)/shard_map/prefix_attention/pallas_call | solution.py:308
  126.3 15.8 %all_to_all.5.arrived = f32[16,72,128]{2,1,0:T(8,128)S(1)} all-to-all(f32[16,72,128]{2,1,0:T(8,128)S(1)} %get-tuple-element.52), channel_id=1, replica_groups=mesh['prompt'=8,'sample'=16] {'sample'}, dimensions={0} | all-to-all | bytes 1179648 | tf_op jit(solution)/shard_map/all_to_all | solution.py:439
  142.1 0.3 combine.1
  142.4 0.6 reshape.83
  (62 shorter events, 0.9 us)
Async XLA Ops:
  0.6 22.6 %copy-start.13 = (bf16[512,256]{1,0:T(8,128)(2,1)S(1)}, bf16[512,256]{1,0:T(8,128)(2,1)}, u32[]{:S(2)}) copy-start(bf16[512,256]{1,0:T(8,128)(2,1)} %param.11) | copy-start | bytes 786436
  4.6 17.8 %collective-permute-start.6 = (bf16[552,256]{1,0:T(8,128)(2,1)S(1)}, bf16[552,256]{1,0:T(8,128)(2,1)S(1)}, u32[]{:S(2)}, u32[]{:S(2)}) collective-permute-start(bf16[552,256]{1,0:T(8,128)(2,1)S(1)} %pad_maximum_fusion.2), channel_id=1, source_target_pairs={{0,2},{1,3},{2,0},{3,1},{4,6},{5,7},{6,4},{7,5},{8,10},{9,11},{10,... | collective-permute-start | bytes 847880 | tf_op jit(solution)/shard_map/ppermute | solution.py:367
  7.8 14.7 %collective-permute-start.5 = (bf16[552,256]{1,0:T(8,128)(2,1)S(1)}, bf16[552,256]{1,0:T(8,128)(2,1)S(1)}, u32[]{:S(2)}, u32[]{:S(2)}) collective-permute-start(bf16[552,256]{1,0:T(8,128)(2,1)S(1)} %pad_maximum_fusion.2), channel_id=1, source_target_pairs={{0,3},{1,0},{2,1},{3,2},{4,7},{5,4},{6,5},{7,6},{8,11},{9,8},{10,9... | collective-permute-start | bytes 847880 | tf_op jit(solution)/shard_map/ppermute | solution.py:367
  8.9 13.6 %collective-permute-start.4 = (bf16[552,256]{1,0:T(8,128)(2,1)S(1)}, bf16[552,256]{1,0:T(8,128)(2,1)S(1)}, u32[]{:S(2)}, u32[]{:S(2)}) collective-permute-start(bf16[552,256]{1,0:T(8,128)(2,1)S(1)} %pad_maximum_fusion.2), channel_id=1, source_target_pairs={{0,1},{1,2},{2,3},{3,0},{4,5},{5,6},{6,7},{7,4},{8,9},{9,10},{10,1... | collective-permute-start | bytes 847880 | tf_op jit(solution)/shard_map/ppermute | solution.py:367
  9.8 2.2 %copy-start = (bf16[1,4096,512]{2,1,0:T(8,128)(2,1)S(1)}, bf16[1,4096,512]{2,1,0:T(8,128)(2,1)}, u32[]{:S(2)}) copy-start(bf16[1,4096,512]{2,1,0:T(8,128)(2,1)} %param.10) | copy-start | bytes 12582916
  13.2 0.9 copy-start.5
  14.1 0.7 copy-start.6
  14.8 0.7 copy-start.8
  15.5 0.7 copy-start.10
  16.2 34.2 %collective-permute-start = (bf16[3,256,512]{2,1,0:T(8,128)(2,1)}, bf16[3,256,512]{2,1,0:T(8,128)(2,1)}, u32[]{:S(2)}, u32[]{:S(2)}) collective-permute-start(bf16[3,256,512]{2,1,0:T(8,128)(2,1)} %get-tuple-element.31), channel_id=1, source_target_pairs={{0,1},{1,2},{2,3},{3,0},{4,5},{5,6},{6,7},{7,4},{8,9},{9,10},{10,1... | collective-permute-start | bytes 2359304 | tf_op jit(solution)/shard_map/ppermute | solution.py:371
  16.8 57.4 %collective-permute-start.17 = (bf16[3,256,512]{2,1,0:T(8,128)(2,1)}, bf16[3,256,512]{2,1,0:T(8,128)(2,1)}, u32[]{:S(2)}, u32[]{:S(2)}) collective-permute-start(bf16[3,256,512]{2,1,0:T(8,128)(2,1)} %get-tuple-element.42), channel_id=1, source_target_pairs={{0,3},{1,0},{2,1},{3,2},{4,7},{5,4},{6,5},{7,6},{8,11},{9,8},{10,9... | collective-permute-start | bytes 2359304 | tf_op jit(solution)/shard_map/ppermute | solution.py:372
  22.4 0.7 copy-start.14
  22.5 0.8 copy-start.15
  23.4 12.1 %collective-permute-start.7 = (bf16[4,512,256]{2,1,0:T(8,128)(2,1)S(1)}, bf16[4,512,256]{2,1,0:T(8,128)(2,1)S(1)}, u32[]{:S(2)}, u32[]{:S(2)}) collective-permute-start(bf16[4,512,256]{2,1,0:T(8,128)(2,1)S(1)} %pad_maximum_fusion.refs_4_), channel_id=1, source_target_pairs={{0,16},{16,0},{32,48},{48,32},{64,80},{80,64},{96,112},{112,96},{1... | collective-permute-start | bytes 3145736 | tf_op jit(solution)/shard_map/ppermute | solution.py:382
  23.5 16.1 %collective-permute-start.8 = (bf16[4,512,256]{2,1,0:T(8,128)(2,1)S(1)}, bf16[4,512,256]{2,1,0:T(8,128)(2,1)S(1)}, u32[]{:S(2)}, u32[]{:S(2)}) collective-permute-start(bf16[4,512,256]{2,1,0:T(8,128)(2,1)S(1)} %pad_maximum_fusion.refs_4_), channel_id=1, source_target_pairs={{0,32},{16,112},{32,64},{48,16},{64,96},{80,48},{96,0},{112,80},{1... | collective-permute-start | bytes 3145736 | tf_op jit(solution)/shard_map/ppermute | solution.py:383
  26.6 6.5 %collective-permute-start.14 = (bf16[4,40,256]{2,1,0:T(8,128)(2,1)S(1)}, bf16[4,40,256]{2,1,0:T(8,128)(2,1)S(1)}, u32[]{:S(2)}, u32[]{:S(2)}) collective-permute-start(bf16[4,40,256]{2,1,0:T(8,128)(2,1)S(1)} %pad_maximum_fusion.3), channel_id=1, source_target_pairs={{0,4},{1,5},{2,6},{3,7},{4,8},{5,9},{6,10},{7,11},{8,12},{9,13},{1... | collective-permute-start | bytes 245768 | tf_op jit(solution)/shard_map/ppermute | solution.py:396
  33.1 6.8 %collective-permute-start.15 = (bf16[4,40,256]{2,1,0:T(8,128)(2,1)S(1)}, bf16[4,40,256]{2,1,0:T(8,128)(2,1)S(1)}, u32[]{:S(2)}, u32[]{:S(2)}) collective-permute-start(bf16[4,40,256]{2,1,0:T(8,128)(2,1)S(1)} %pad_maximum_fusion.3), channel_id=1, source_target_pairs={{0,12},{1,13},{2,14},{3,15},{4,0},{5,1},{6,2},{7,3},{8,4},{9,5},{1... | collective-permute-start | bytes 245768 | tf_op jit(solution)/shard_map/ppermute | solution.py:396
  35.5 16.1 %collective-permute-start.9 = (bf16[4,512,256]{2,1,0:T(8,128)(2,1)S(1)}, bf16[4,512,256]{2,1,0:T(8,128)(2,1)}, u32[]{:S(2)}, u32[]{:S(2)}) collective-permute-start(bf16[4,512,256]{2,1,0:T(8,128)(2,1)S(1)} %collective-permute-done.7.refs_5_), channel_id=1, source_target_pairs={{0,32},{16,112},{32,64},{48,16},{64,96},{80,48},{96,0},{112,80},{1... | collective-permute-start | bytes 3145736 | tf_op jit(solution)/shard_map/ppermute | solution.py:384
  39.6 23.3 %collective-permute-start.12 = (bf16[4,512,256]{2,1,0:T(8,128)(2,1)S(1)}, bf16[4,512,256]{2,1,0:T(8,128)(2,1)}, u32[]{:S(2)}, u32[]{:S(2)}) collective-permute-start(bf16[4,512,256]{2,1,0:T(8,128)(2,1)S(1)} %collective-permute-done.8.refs_6_), channel_id=1, source_target_pairs={{0,32},{16,112},{32,64},{48,16},{64,96},{80,48},{96,0},{112,80},{1... | collective-permute-start | bytes 3145736 | tf_op jit(solution)/shard_map/ppermute | solution.py:385
  40.0 6.4 %collective-permute-start.16 = (bf16[4,40,256]{2,1,0:T(8,128)(2,1)S(1)}, bf16[4,40,256]{2,1,0:T(8,128)(2,1)S(1)}, u32[]{:S(2)}, u32[]{:S(2)}) collective-permute-start(bf16[4,40,256]{2,1,0:T(8,128)(2,1)S(1)} %pad_maximum_fusion.3), channel_id=1, source_target_pairs={{0,8},{1,9},{2,10},{3,11},{4,12},{5,13},{6,14},{7,15},{8,0},{9,1},... | collective-permute-start | bytes 245768 | tf_op jit(solution)/shard_map/ppermute | solution.py:396
  46.3 27.9 %collective-permute-start.18 = (bf16[3,256,512]{2,1,0:T(8,128)(2,1)}, bf16[3,256,512]{2,1,0:T(8,128)(2,1)}, u32[]{:S(2)}, u32[]{:S(2)}) collective-permute-start(bf16[3,256,512]{2,1,0:T(8,128)(2,1)} %copy-done.5), channel_id=1, source_target_pairs={{0,2},{1,3},{2,0},{3,1},{4,6},{5,7},{6,4},{7,5},{8,10},{9,11},{10,... | collective-permute-start | bytes 2359304 | tf_op jit(solution)/shard_map/ppermute | solution.py:373
  50.5 23.8 %collective-permute-start.10 = (bf16[4,512,256]{2,1,0:T(8,128)(2,1)S(1)}, bf16[4,512,256]{2,1,0:T(8,128)(2,1)S(1)}, u32[]{:S(2)}, u32[]{:S(2)}) collective-permute-start(bf16[4,512,256]{2,1,0:T(8,128)(2,1)S(1)} %collective-permute-done.8.refs_6_), channel_id=1, source_target_pairs={{0,16},{16,0},{32,48},{48,32},{64,80},{80,64},{96,112},{112,96},{1... | collective-permute-start | bytes 3145736 | tf_op jit(solution)/shard_map/ppermute | solution.py:386
  51.6 22.6 %collective-permute-start.11 = (bf16[4,512,256]{2,1,0:T(8,128)(2,1)}, bf16[4,512,256]{2,1,0:T(8,128)(2,1)S(1)}, u32[]{:S(2)}, u32[]{:S(2)}) collective-permute-start(bf16[4,512,256]{2,1,0:T(8,128)(2,1)} %collective-permute-done.9.refs_7_), channel_id=1, source_target_pairs={{0,16},{16,0},{32,48},{48,32},{64,80},{80,64},{96,112},{112,96},{1... | collective-permute-start | bytes 3145736 | tf_op jit(solution)/shard_map/ppermute | solution.py:387
  62.8 11.4 %collective-permute-start.13 = (bf16[4,512,256]{2,1,0:T(8,128)(2,1)}, bf16[4,512,256]{2,1,0:T(8,128)(2,1)S(1)}, u32[]{:S(2)}, u32[]{:S(2)}) collective-permute-start(bf16[4,512,256]{2,1,0:T(8,128)(2,1)} %collective-permute-done.12.refs_10_), channel_id=1, source_target_pairs={{0,16},{16,0},{32,48},{48,32},{64,80},{80,64},{96,112},{112,96},{1... | collective-permute-start | bytes 3145736 | tf_op jit(solution)/shard_map/ppermute | solution.py:388
  62.8 3.4 %copy-start.3 = (bf16[1,1,16,128,2048]{4,3,2,1,0:T(8,128)(2,1)S(1)}, bf16[1,1,16,128,2048]{4,3,2,1,0:T(8,128)(2,1)}, u32[]{:S(2)}) copy-start(bf16[1,1,16,128,2048]{4,3,2,1,0:T(8,128)(2,1)} %param.15) | copy-start | bytes 25165828
  66.2 4.3 %copy-start.12 = (bf16[1,1,2048]{2,1,0:T(2,128)(2,1)S(1)}, bf16[1,1,2048]{2,1,0:T(2,128)(2,1)}, u32[]{:S(2)}) copy-start(bf16[1,1,2048]{2,1,0:T(2,128)(2,1)} %param.13) | copy-start | bytes 12292
  70.5 3.4 %copy-start.4 = (bf16[1,1,16,128,2048]{4,3,2,1,0:T(8,128)(2,1)S(1)}, bf16[1,1,16,128,2048]{4,3,2,1,0:T(8,128)(2,1)}, u32[]{:S(2)}) copy-start(bf16[1,1,16,128,2048]{4,3,2,1,0:T(8,128)(2,1)} %param.14) | copy-start | bytes 25165828
  73.9 1.1 copy-start.1
  74.2 8.9 %copy-start.11 = (bf16[256,512]{1,0:T(8,128)(2,1)S(1)}, bf16[256,512]{1,0:T(8,128)(2,1)}, u32[]{:S(2)}) copy-start(bf16[256,512]{1,0:T(8,128)(2,1)} %copy-done.10) | copy-start | bytes 786436
  74.2 9.8 %copy-start.9 = (bf16[256,512]{1,0:T(8,128)(2,1)S(1)}, bf16[256,512]{1,0:T(8,128)(2,1)}, u32[]{:S(2)}) copy-start(bf16[256,512]{1,0:T(8,128)(2,1)} %copy-done.8) | copy-start | bytes 786436
  79.6 15.3 %collective-permute-start.23 = (bf16[256,1024]{1,0:T(8,128)(2,1)S(1)}, bf16[256,1024]{1,0:T(8,128)(2,1)S(1)}, u32[]{:S(2)}, u32[]{:S(2)}) collective-permute-start(bf16[256,1024]{1,0:T(8,128)(2,1)S(1)} %get-tuple-element.49), channel_id=1, source_target_pairs={{0,12},{1,13},{2,14},{3,15},{4,0},{5,1},{6,2},{7,3},{8,4},{9,5},{1... | collective-permute-start | bytes 1572872 | tf_op jit(solution)/shard_map/ppermute | solution.py:426
  83.1 19.5 %collective-permute-start.1 = (bf16[256,512]{1,0:T(8,128)(2,1)S(1)}, bf16[256,512]{1,0:T(8,128)(2,1)S(1)}, u32[]{:S(2)}, u32[]{:S(2)}) collective-permute-start(bf16[256,512]{1,0:T(8,128)(2,1)S(1)} %copy-done.11), channel_id=1, source_target_pairs={{0,1},{1,2},{2,3},{3,0},{4,5},{5,6},{6,7},{7,4},{8,9},{9,10},{10,1... | collective-permute-start | bytes 786440 | tf_op jit(solution)/shard_map/ppermute | solution.py:376
  84.0 20.7 %collective-permute-start.2 = (bf16[256,512]{1,0:T(8,128)(2,1)S(1)}, bf16[256,512]{1,0:T(8,128)(2,1)S(1)}, u32[]{:S(2)}, u32[]{:S(2)}) collective-permute-start(bf16[256,512]{1,0:T(8,128)(2,1)S(1)} %copy-done.9), channel_id=1, source_target_pairs={{0,3},{1,0},{2,1},{3,2},{4,7},{5,4},{6,5},{7,6},{8,11},{9,8},{10,9... | collective-permute-start | bytes 786440 | tf_op jit(solution)/shard_map/ppermute | solution.py:377
  86.3 18.4 %copy-start.7 = (bf16[256,512]{1,0:T(8,128)(2,1)S(1)}, bf16[256,512]{1,0:T(8,128)(2,1)}, u32[]{:S(2)}) copy-start(bf16[256,512]{1,0:T(8,128)(2,1)} %copy-done.6) | copy-start | bytes 786436
  86.3 26.2 %copy-start.2 = (bf16[256,512]{1,0:T(8,128)(2,1)S(1)}, bf16[256,512]{1,0:T(8,128)(2,1)}, u32[]{:S(2)}) copy-start(bf16[256,512]{1,0:T(8,128)(2,1)} %get-tuple-element.60.refs_0_) | copy-start | bytes 786436
  86.3 16.0 %collective-permute-start.19 = (bf16[256,1024]{1,0:T(8,128)(2,1)S(1)}, bf16[256,1024]{1,0:T(8,128)(2,1)S(1)}, u32[]{:S(2)}, u32[]{:S(2)}) collective-permute-start(bf16[256,1024]{1,0:T(8,128)(2,1)S(1)} %get-tuple-element.45), channel_id=1, source_target_pairs={{0,4},{1,5},{2,6},{3,7},{4,8},{5,9},{6,10},{7,11},{8,12},{9,13},{1... | collective-permute-start | bytes 1572872 | tf_op jit(solution)/shard_map/ppermute | solution.py:425
  93.1 23.3 %collective-permute-start.21 = (bf16[256,1024]{1,0:T(8,128)(2,1)S(1)}, bf16[256,1024]{1,0:T(8,128)(2,1)S(1)}, u32[]{:S(2)}, u32[]{:S(2)}) collective-permute-start(bf16[256,1024]{1,0:T(8,128)(2,1)S(1)} %get-tuple-element.46), channel_id=1, source_target_pairs={{0,4},{1,5},{2,6},{3,7},{4,8},{5,9},{6,10},{7,11},{8,12},{9,13},{1... | collective-permute-start | bytes 1572872 | tf_op jit(solution)/shard_map/ppermute | solution.py:433
  94.9 21.5 %collective-permute-start.22 = (bf16[256,1024]{1,0:T(8,128)(2,1)S(1)}, bf16[256,1024]{1,0:T(8,128)(2,1)S(1)}, u32[]{:S(2)}, u32[]{:S(2)}) collective-permute-start(bf16[256,1024]{1,0:T(8,128)(2,1)S(1)} %get-tuple-element.47), channel_id=1, source_target_pairs={{0,12},{1,13},{2,14},{3,15},{4,0},{5,1},{6,2},{7,3},{8,4},{9,5},{1... | collective-permute-start | bytes 1572872 | tf_op jit(solution)/shard_map/ppermute | solution.py:434
  102.3 18.6 %collective-permute-start.24 = (bf16[256,1024]{1,0:T(8,128)(2,1)S(1)}, bf16[256,1024]{1,0:T(8,128)(2,1)S(1)}, u32[]{:S(2)}, u32[]{:S(2)}) collective-permute-start(bf16[256,1024]{1,0:T(8,128)(2,1)S(1)} %add_convert_fusion), channel_id=1, source_target_pairs={{0,12},{1,13},{2,14},{3,15},{4,0},{5,1},{6,2},{7,3},{8,4},{9,5},{1... | collective-permute-start | bytes 1572872 | tf_op jit(solution)/shard_map/ppermute | solution.py:435
  102.6 20.9 %collective-permute-start.20 = (bf16[256,1024]{1,0:T(8,128)(2,1)S(1)}, bf16[256,1024]{1,0:T(8,128)(2,1)S(1)}, u32[]{:S(2)}, u32[]{:S(2)}) collective-permute-start(bf16[256,1024]{1,0:T(8,128)(2,1)S(1)} %add_convert_fusion.1), channel_id=1, source_target_pairs={{0,4},{1,5},{2,6},{3,7},{4,8},{5,9},{6,10},{7,11},{8,12},{9,13},{1... | collective-permute-start | bytes 1572872 | tf_op jit(solution)/shard_map/ppermute | solution.py:432
  104.7 7.9 %collective-permute-start.3 = (bf16[256,512]{1,0:T(8,128)(2,1)S(1)}, bf16[256,512]{1,0:T(8,128)(2,1)S(1)}, u32[]{:S(2)}, u32[]{:S(2)}) collective-permute-start(bf16[256,512]{1,0:T(8,128)(2,1)S(1)} %copy-done.7), channel_id=1, source_target_pairs={{0,2},{1,3},{2,0},{3,1},{4,6},{5,7},{6,4},{7,5},{8,10},{9,11},{10,... | collective-permute-start | bytes 786440 | tf_op jit(solution)/shard_map/ppermute | solution.py:378
where the time goes:
time: 143 us
  waiting for transfers between devices  38.2 us (27%)
  starting transfers between devices  36.3 us (25%)
  Pallas kernels  24.1 us (17%)
  local copies, waits for them, and re-layouts  21.1 us (15%)
  blocking collectives  15.8 us (11%)
  other arithmetic  4.58 us (3%)
  between operations  2.94 us (2%)
    all_to_all x1, blocking collectives, per_device(): lax.all_to_all(packed, 'sample', split_axis=0, concat_axis=0, tiled=True)  15.8 us
    pallas_call x3, Pallas kernels, product(): pl.pallas_call(functools.partial(product_kernel, blocks), out_shape=outs,...  15.2 us
    unnamed x37, local copies, waits for them, and re-layouts  15 us
    ppermute x1, waiting for transfers between devices, per_device(): far = lax.ppermute(near, 'prompt', Y_SPLIT)  11.2 us
    ppermute x3, starting transfers between devices, per_device(): lax.ppermute(of_row, 'sample', to)  8.28 us
    ppermute x1, waiting for transfers between devices, per_device(): lax.ppermute(last_far, 'sample', X_FAR)  5.7 us
    ppermute x3, waiting for transfers between devices, per_device(): lax.ppermute(of_row, 'sample', to)  5.49 us
    ppermute x3, starting transfers between devices, per_device(): lax.ppermute(sent, 'sample', to)  5.21 us
  transfers between devices with their start and end apart: 25, of which 10 were waited for; matrix products, arithmetic and copies ran while one was open for 6% of the time, Pallas kernels for 11%

commit v1 on v0

--- a/solution.py
+++ b/solution.py
@@ -54,12 +54,93 @@
     return jnp.where(at == lane, column, running)
 
 
-def pick_kernel(states, *refs):
-    outs, sems = refs[:6], refs[6]
+SENT = SLICE + QUERY_HEADS // 2 + 8
+HALF = QUERY_HEADS // 2
+
+
+def prepare_kernel(where, length, flag, weight, query, sent, own):
+    sent[:SLICE] = weight[...]
+    heads = [query[0, 0:1, h * HEAD_SIZE : (h + 1) * HEAD_SIZE].astype(F32) for h in range(QUERY_HEADS)]
+    low, high = jnp.concatenate(heads[:HALF]), jnp.concatenate(heads[HALF:])
+    own[:HALF] = low.astype(BF16)
+    own[HALF:] = high.astype(BF16)
+    sent[SLICE : SLICE + HALF, :HEAD_SIZE] = low.astype(BF16)
+    sent[SLICE : SLICE + HALF, HEAD_SIZE:] = high.astype(BF16)
+    plan = jnp.zeros((8, COLUMNS), F32)
+    for c in range(CMAX):
+        plan = put_lane(plan, c, where[0, 0, c].astype(F32))
+    plan = put_lane(plan, CMAX, length[0, 0].astype(F32))
+    plan = put_lane(plan, CMAX + 1, flag[0, 0].astype(F32))
+    sent[SLICE + HALF :] = plan.astype(BF16)
+
+
+def prepare(weight, query, where, length, flag):
+    smem, vmem = pl.BlockSpec(memory_space=pltpu.SMEM), pl.BlockSpec(memory_space=pltpu.VMEM)
+    return pl.pallas_call(
+        prepare_kernel,
+        out_shape=[
+            jax.ShapeDtypeStruct((SENT, COLUMNS), BF16),
+            jax.ShapeDtypeStruct((QUERY_HEADS, HEAD_SIZE), BF16),
+        ],
+        in_specs=[smem] * 3 + [vmem] * 2,
+        out_specs=[vmem, vmem],
+        compiler_params=params(16),
+        cost_estimate=cost(1000, 1000),
+        name="prepare",
+    )(where, length, flag, weight, query)
+
+
+def unpack_kernel(*refs):
+    arrived, (queries, by_group, slots, alive) = refs[:4], refs[4:]
+    me = lax.axis_index("sample")
+    plans = []
+    for r in range(SAMPLES):
+        block = arrived[r // 4][r % 4].astype(F32)
+        for half in range(2):
+            lanes = slice(half * HEAD_SIZE, (half + 1) * HEAD_SIZE)
+            queries[r, half * HALF : (half + 1) * HALF] = block[:HALF, lanes].astype(BF16)
+        plans.append(block[HALF : HALF + 1])
+    for g in range(GROUPS):
+        lanes = slice(g // 4 * HEAD_SIZE, (g // 4 + 1) * HEAD_SIZE)
+        rows = slice(g % 4 * HEADS, (g % 4 + 1) * HEADS)
+        parts = [arrived[r // 4][r % 4].astype(F32)[rows, lanes] for r in range(SAMPLES)]
+        by_group[g] = jnp.concatenate(parts).astype(BF16)
+    plan = jnp.concatenate(plans)
+    lane = lax.broadcasted_iota(jnp.int32, plan.shape, 1)
+    first = (me * CMAX).astype(F32)
+    here = (lane < CMAX) & (plan >= first) & (plan < first + CMAX)
+    live = here & (lane.astype(F32) < plan[:, CMAX : CMAX + 1]) & (plan[:, CMAX + 1 : CMAX + 2] > 0.5)
+    slot = jnp.sum(jnp.where(here, plan - first, 0.0), axis=1, keepdims=True).astype(jnp.int32)
+    some = jnp.max(jnp.where(live, 1.0, 0.0), axis=1, keepdims=True).astype(jnp.int32)
+    for r in range(SAMPLES):
+        slots[r] = slot[r, 0]
+        alive[r] = some[r, 0]
+
+
+def unpack(arrived):
+    smem, vmem = pl.BlockSpec(memory_space=pltpu.SMEM), pl.BlockSpec(memory_space=pltpu.VMEM)
+    return pl.pallas_call(
+        unpack_kernel,
+        out_shape=[
+            jax.ShapeDtypeStruct((SAMPLES, QUERY_HEADS, HEAD_SIZE), BF16),
+            jax.ShapeDtypeStruct((GROUPS, SAMPLES * HEADS, HEAD_SIZE), BF16),
+            jax.ShapeDtypeStruct((SAMPLES,), jnp.int32),
+            jax.ShapeDtypeStruct((SAMPLES,), jnp.int32),
+        ],
+        in_specs=[vmem] * 4,
+        out_specs=[vmem, vmem, smem, smem],
+        compiler_params=params(16),
+        cost_estimate=cost(1000, 1000),
+        name="unpack",
+    )(*arrived)
+
+
+def pick_kernel(steps, states, *refs):
+    outs, sems = refs[:-1], refs[-1]
     me = lax.axis_index("sample")
     z, x = me // 4, lax.rem(me, 4)
     copies = []
-    for i, step in enumerate((1, 3, 2)):
+    for i, step in enumerate(steps):
         column = lax.rem(x + step, 4)
         for k, up in enumerate((2, 1, 3)):
             copies.append((states.at[lax.rem(z + up, 4), column], outs[2 * i].at[k]))
@@ -71,19 +152,18 @@
         copy.wait()
 
 
-def pick(states):
-    far = jax.ShapeDtypeStruct((3, ROWS, SLICE), BF16)
-    near = jax.ShapeDtypeStruct((ROWS, SLICE), BF16)
-    hbm = pl.BlockSpec(memory_space=pl.ANY)
-    return pl.pallas_call(
-        pick_kernel,
-        out_shape=[far, near] * 3,
-        in_specs=[hbm],
-        out_specs=[hbm] * 6,
-        scratch_shapes=[pltpu.SemaphoreType.DMA((12,))],
-        compiler_params=params(16),
-        cost_estimate=cost(0, 6 * MIB),
-        name="pick_rows",
+def pick(states, steps, space, mib, name):
+    rest = jax.ShapeDtypeStruct((3, ROWS, SLICE), BF16)
+    own = jax.ShapeDtypeStruct((ROWS, SLICE), BF16)
+    return pl.pallas_call(
+        functools.partial(pick_kernel, steps),
+        out_shape=[rest, own] * len(steps),
+        in_specs=[pl.BlockSpec(memory_space=pl.ANY)],
+        out_specs=[pl.BlockSpec(memory_space=space)] * (2 * len(steps)),
+        scratch_shapes=[pltpu.SemaphoreType.DMA((4 * len(steps),))],
+        compiler_params=params(mib),
+        cost_estimate=cost(1000, 1000),
+        name=name,
     )(states)
 
 
@@ -107,8 +187,8 @@
         out_shape=outs,
         in_specs=[vmem] * 12,
         out_specs=[vmem] * len(outs),
-        compiler_params=params(40),
-        cost_estimate=cost(2 * len(blocks) * ROWS * KVW * KVW, 2 * MIB),
+        compiler_params=params(20),
+        cost_estimate=cost(1000, 1000),
         name=name,
     )(*states, *pieces)
 
@@ -167,8 +247,8 @@
                 (POOL_PAGES, PACK, HEAD_SIZE), lambda s, slots, alive: (s, 0, 0)
             ),
         ),
-        compiler_params=params(32),
-        cost_estimate=cost(10_000_000_000, 8 * MIB),
+        compiler_params=params(16),
+        cost_estimate=cost(1000, 1000),
         name="pool_attention",
     )(slots, alive, queries_all, *[pool] * POOL_PAGES)
 
@@ -248,8 +328,8 @@
                 pltpu.VMEM((QUERY_HEADS, HEAD_SIZE), F32),
             ],
         ),
-        compiler_params=params(32),
-        cost_estimate=cost(10_000_000_000, 8 * MIB),
+        compiler_params=params(16),
+        cost_estimate=cost(1000, 1000),
         name="local_attention",
     )(pages_alive, query, new, pages)
 
@@ -313,7 +393,7 @@
         ],
         in_specs=[smem] + [vmem] * 8,
         out_specs=[vmem, vmem],
-        compiler_params=params(32),
+        compiler_params=params(20),
         cost_estimate=cost(300_000_000, 6 * MIB),
         name="prefix_attention",
     )(prompt_pages, *parts, queries, pool)
@@ -339,7 +419,7 @@
         out_shape=jax.ShapeDtypeStruct((QUERY_HEADS, HEAD_SIZE), BF16),
         in_specs=[vmem, vmem],
         out_specs=vmem,
-        compiler_params=params(32),
+        compiler_params=params(16),
         cost_estimate=cost(1_000_000, MIB),
         name="combine",
     )(arrived, local)
@@ -357,20 +437,20 @@
     preempted,
     page_where,
 ):
-    own_index = lax.axis_index("sample")
     tie = lax.optimization_barrier
 
-    plan = jnp.concatenate([page_where[0, 0], comp_pages[0], preempted[0]]).astype(BF16)
-    plan = jnp.pad(plan.reshape(1, -1), ((0, 7), (0, COLUMNS - CMAX - 2)))
-    query = queries.reshape(QUERY_HEADS, HEAD_SIZE)
-    sent = jnp.concatenate([kv_weight, queries.reshape(-1, COLUMNS), plan])
+    sent, query = prepare(kv_weight, queries, page_where, comp_pages, preempted)
     along_x = [sent] + [lax.ppermute(sent, "sample", to) for to in (X_RIGHT, X_LEFT, X_FAR)]
 
     states = prompt_states.reshape(4, 4, ROWS, SLICE)
-    to_right, last_right, to_left, last_left, to_far, last_far = pick(states)
+    to_right, last_right, to_left, last_left, to_far, last_far = pick(
+        states, (1, 3, 2), pl.ANY, 56, "pick_sent"
+    )
+    to_far, *along_x = tie((to_far, *along_x))
+    rows_far = lax.ppermute(to_far, "sample", X_FAR)
+    to_right, to_left, query, rows_far = tie((to_right, to_left, query, rows_far))
     rows_right = lax.ppermute(to_right, "sample", X_RIGHT)
     rows_left = lax.ppermute(to_left, "sample", X_LEFT)
-    rows_far = lax.ppermute(to_far, "sample", X_FAR)
     last_right, last_left, last_far, rows_right = tie((last_right, last_left, last_far, rows_right))
     own_states = [
         lax.ppermute(last_right, "sample", X_RIGHT),
@@ -378,46 +458,33 @@
         lax.ppermute(last_far, "sample", X_FAR),
     ]
 
+    of_row = jnp.stack([a[SLICE:] for a in along_x])
+    everyone = [of_row] + [lax.ppermute(of_row, "sample", to) for to in (Z_UP, Z_DOWN, Z_FAR)]
+
     here = jnp.stack([a[:SLICE] for a in along_x])
     here_other = lax.ppermute(here, "prompt", SWAP)
     near = lax.ppermute(here, "prompt", Y_SPLIT)
     near_other = lax.ppermute(here_other, "prompt", Y_SPLIT)
+    near, *everyone = tie((near, *everyone))
     far = lax.ppermute(near, "prompt", Y_SPLIT)
     near_swapped = lax.ppermute(near, "prompt", SWAP)
     near_other_swapped = lax.ppermute(near_other, "prompt", SWAP)
+
+    queries_all, by_group, slots, alive = unpack(everyone)
+    queries_all, rows_far = tie((queries_all, rows_far))
+    pool = pool_attention(slots, alive, queries_all, pool_pages[0, 0])
+    local_alive = jnp.where(preempted[0] > 0, 0, comp_pages[0])
+    query, here_other = tie((query, here_other))
+    local = local_attention(local_alive, query, new_kv[0], local_pages[0, 0])
+
+    far, pool, local, rows_right, rows_left = tie((far, pool, local, rows_right, rows_left))
     far_other = lax.ppermute(far, "prompt", SWAP)
     pieces = [
         here, here_other, near, near_other,
         near_swapped, near_other_swapped, far, far_other,
     ]
 
-    of_row = jnp.stack([a[SLICE:] for a in along_x])
-    everyone = jnp.concatenate(
-        [of_row] + [lax.ppermute(of_row, "sample", to) for to in (Z_UP, Z_DOWN, Z_FAR)]
-    )
-    queries_all = everyone[:, : QUERY_HEADS // 2].reshape(SAMPLES, QUERY_HEADS, HEAD_SIZE)
-    queries_all, rows_right = tie((queries_all, rows_right))
-    plans = everyone[:, QUERY_HEADS // 2, : CMAX + 2].astype(jnp.int32)
-    where_all, lens_all, flags_all = plans[:, :CMAX], plans[:, CMAX], plans[:, CMAX + 1]
-    page_ids = jnp.arange(CMAX, dtype=jnp.int32)
-    here_page = where_all // CMAX == own_index
-    slots = jnp.sum(jnp.where(here_page, where_all % CMAX, 0), axis=1)
-    live_all = (page_ids[None, :] < lens_all[:, None]) & (flags_all[:, None] > 0)
-    alive = jnp.any(here_page & live_all, axis=1).astype(jnp.int32)
-    pool = pool_attention(slots, alive, queries_all, pool_pages[0, 0])
-    local_alive = jnp.where(preempted[0] > 0, 0, comp_pages[0])
-    query, here_other = tie((query, here_other))
-    local = local_attention(local_alive, query, new_kv[0], local_pages[0, 0])
-    by_group = queries_all.reshape(SAMPLES, GROUPS, HEADS, HEAD_SIZE)
-    by_group = by_group.transpose(1, 0, 2, 3).reshape(GROUPS, SAMPLES * HEADS, HEAD_SIZE)
-
-    z, x = own_index // 4, own_index % 4
-    mine = lax.dynamic_index_in_dim(states, x, 1, keepdims=False)
-    mine_rows = jnp.stack(
-        [lax.dynamic_index_in_dim(mine, (z + up) % 4, 0, keepdims=False) for up in (2, 1, 3)]
-    )
-    mine_last = lax.dynamic_index_in_dim(mine, z, 0, keepdims=False)
-    mine_rows, pool, local = tie((mine_rows, pool, local))
+    mine_rows, mine_last = pick(states, (0,), pltpu.VMEM, 16, "pick_own")
     rows = [mine_rows, rows_right, rows_left, rows_far]
     far_l, far_r = product(rows, pieces, (0,), BF16, "product_far")
     up_l, up_r, down_l, down_r = product(rows, pieces, (1, 2), BF16, "product_near")

time: 143 us -> 220 us (1.54)
  Pallas kernels: 24.1 us -> 115 us
  local copies, waits for them, and re-layouts: 21.1 us -> 6.47 us
  other arithmetic: 4.58 us -> 0.53 us
  waiting for transfers between devices: 38.2 us -> 41.8 us
    pallas_call x1 -> x4, Pallas kernels: 1.24 us -> 98 us  [the longest x2 96.6 us: pick(): pl.pallas_call(functools.partial(pick_kernel, steps), out_shape=[rest, ow...]
    ppermute x1, waiting for transfers between devices: 11.2 us -> 0.01 us  [per_device(): far = lax.ppermute(near, 'prompt', Y_SPLIT)]
    unnamed x37 -> x22, local copies, waits for them, and re-layouts: 15 us -> 5.76 us
    ppermute x1, waiting for transfers between devices: 0.01 us -> 8.33 us  [per_device(): rows_right = lax.ppermute(to_right, 'sample', X_RIGHT)]
    pallas_call x3, Pallas kernels: 15.2 us -> 9.13 us  [product(): pl.pallas_call(functools.partial(product_kernel, blocks), out_shape=outs,...]
    ppermute x1, waiting for transfers between devices: 0.01 us -> 4.16 us  [per_device(): rows_far = lax.ppermute(to_far, 'sample', X_FAR)]
    ppermute x1, waiting for transfers between devices: 4.48 us -> 8.5 us  [per_device(): lax.ppermute(down_r, 'sample', Z_DOWN)]
    ppermute x1, waiting for transfers between devices: 3.55 us -> 0.65 us  [per_device(): from_down = lax.ppermute(far_l, 'sample', Z_UP)]
  transfers between devices with their start and end apart: 25 -> 25, of which waited for: 10 -> 11; matrix products, arithmetic and copies ran while one was open for 6% -> 0% of each run, Pallas kernels for 11% -> 49%
where the time goes in v1:
time: 220 us
  Pallas kernels  115 us (52%)
  waiting for transfers between devices  41.8 us (19%)
  starting transfers between devices  35.8 us (16%)
  blocking collectives  17.8 us (8%)
  local copies, waits for them, and re-layouts  6.47 us (3%)
  between operations  2.87 us (1%)
    pallas_call x2, Pallas kernels, pick(): pl.pallas_call(functools.partial(pick_kernel, steps), out_shape=[rest, ow...  96.6 us
    all_to_all x1, blocking collectives, per_device(): lax.all_to_all(packed, 'sample', split_axis=0, concat_axis=0, tiled=True)  17.8 us
    pallas_call x3, Pallas kernels, product(): pl.pallas_call(functools.partial(product_kernel, blocks), out_shape=outs,...  9.13 us
    ppermute x1, waiting for transfers between devices, per_device(): lax.ppermute(down_r, 'sample', Z_DOWN)  8.5 us
    ppermute x1, waiting for transfers between devices, per_device(): rows_right = lax.ppermute(to_right, 'sample', X_RIGHT)  8.33 us
    ppermute x3, waiting for transfers between devices, per_device(): lax.ppermute(of_row, 'sample', to)  6.93 us
    ppermute x3, starting transfers between devices, per_device(): lax.ppermute(of_row, 'sample', to)  5.8 us
    ppermute x1, waiting for transfers between devices, per_device(): lax.ppermute(last_far, 'sample', X_FAR)  5.76 us
  transfers between devices with their start and end apart: 25, of which 11 were waited for; matrix products, arithmetic and copies ran while one was open for 0% of the time, Pallas kernels for 49%

profile of v1, /device:TPU:0, one launch (start us, length us, event | category | flops | bytes accessed | tf_op | source)
XLA Modules:
  0.0 220.0 jit_solution(3784765675544592084)
XLA Ops:
  1.9 0.9 copy-done.2
  2.9 0.8 copy-done.3
  3.6 0.7 copy-done.5
  4.3 0.6 prepare.1
  4.9 1.6 collective-permute-start
  6.5 1.7 collective-permute-start.1
  8.2 1.9 collective-permute-start.2
  10.1 96.5 %pick_sent.1 = (bf16[3,256,512]{2,1,0:T(8,128)(2,1)}, bf16[256,512]{1,0:T(8,128)(2,1)}, bf16[3,256,512]{2,1,0:T(8,128)(2,1)}, bf16[256,512]{1,0:T(8,128)(2,1)}, ...) custom-call(bf16[4,4,256,512]{3,2,1,0:T(8,128)(2,1)} %bitcast.25), custom_call_target="tpu_custom_call" | custom-call | flops 1000 | bytes 1000 | tf_op jit(solution)/shard_map/pick_sent/pallas_call | solution.py:158
  106.6 0.0 collective-permute-done
  106.6 0.0 collective-permute-done.1
  106.6 0.0 collective-permute-done.2
  106.7 0.1 pad_maximum_fusion.refs_4_
  106.9 1.6 collective-permute-start.9
  108.5 0.2 collective-permute-start.8
  108.7 1.7 collective-permute-start.3
  110.4 2.0 collective-permute-start.10
  112.4 2.2 %collective-permute-start.11 = (bf16[4,40,256]{2,1,0:T(8,128)(2,1)S(1)}, bf16[4,40,256]{2,1,0:T(8,128)(2,1)S(1)}, u32[]{:S(2)}, u32[]{:S(2)}) collective-permute-start(bf16[4,40,256]{2,1,0:T(8,128)(2,1)S(1)} %pad_maximum_fusion.1.refs_0_), channel_id=1, source_target_pairs={{0,12},{1,13},{2,14},{3,15},{4,0},{5,1},{6,2},{7,3},{8,4},{9,5},{1... | collective-permute-start | bytes 245768 | tf_op jit(solution)/shard_map/ppermute | solution.py:462
  114.6 2.6 %collective-permute-done.10.refs_1_ = bf16[4,40,256]{2,1,0:T(8,128)(2,1)S(1)} collective-permute-done((bf16[4,40,256]{2,1,0:T(8,128)(2,1)S(1)}, bf16[4,40,256]{2,1,0:T(8,128)(2,1)S(1)}, u32[]{:S(2)}, u32[]{:S(2)}) %collective-permute-start.10) | collective-permute-done | bytes 81952 | tf_op jit(solution)/shard_map/ppermute | solution.py:462
  117.2 1.6 collective-permute-start.12
  118.8 0.0 collective-permute-done.11.refs_2_
  118.8 4.3 %collective-permute-done.12.refs_3_ = bf16[4,40,256]{2,1,0:T(8,128)(2,1)S(1)} collective-permute-done((bf16[4,40,256]{2,1,0:T(8,128)(2,1)S(1)}, bf16[4,40,256]{2,1,0:T(8,128)(2,1)S(1)}, u32[]{:S(2)}, u32[]{:S(2)}) %collective-permute-start.12) | collective-permute-done | bytes 81952 | tf_op jit(solution)/shard_map/ppermute | solution.py:462
  123.1 0.0 collective-permute-done.9.refs_6_
  123.1 1.6 collective-permute-start.16
  124.7 0.0 collective-permute-done.8.refs_5_
  124.7 1.3 collective-permute-start.13
  126.0 4.2 %collective-permute-done.3.refs_3_ = bf16[3,256,512]{2,1,0:T(8,128)(2,1)S(1)} collective-permute-done((bf16[3,256,512]{2,1,0:T(8,128)(2,1)}, bf16[3,256,512]{2,1,0:T(8,128)(2,1)S(1)}, u32[]{:S(2)}, u32[]{:S(2)}) %collective-permute-start.3) | collective-permute-done | bytes 786464 | tf_op jit(solution)/shard_map/ppermute | solution.py:450
  130.2 0.6 collective-permute-start.4
  130.8 2.6 %collective-permute-start.17 = (bf16[3,256,512]{2,1,0:T(8,128)(2,1)}, bf16[3,256,512]{2,1,0:T(8,128)(2,1)S(1)}, u32[]{:S(2)}, u32[]{:S(2)}) collective-permute-start(bf16[3,256,512]{2,1,0:T(8,128)(2,1)} %get-tuple-element.85), channel_id=1, source_target_pairs={{0,3},{1,0},{2,1},{3,2},{4,7},{5,4},{6,5},{7,6},{8,11},{9,8},{10,9... | collective-permute-start | bytes 2359304 | tf_op jit(solution)/shard_map/ppermute | solution.py:453
  133.4 0.8 unpack.1
  134.2 0.0 copy-start
  134.2 3.4 %copy-done = bf16[1,1,16,128,2048]{4,3,2,1,0:T(8,128)(2,1)S(1)} copy-done((bf16[1,1,16,128,2048]{4,3,2,1,0:T(8,128)(2,1)S(1)}, bf16[1,1,16,128,2048]{4,3,2,1,0:T(8,128)(2,1)}, u32[]{:S(2)}) %copy-start) | copy-done | bytes 8388632
  137.6 4.3 %pool_attention.1.pool = f32[16,72,128]{2,1,0:T(8,128)S(1)} custom-call(s32[16]{0:T(128)S(1)} %get-tuple-element.78.slots, s32[16]{0:T(128)S(1)} %get-tuple-element.79.alive, bf16[16,64,128]{2,1,0:T(8,128)(2,1)S(1)} %get-tuple-element.82.query, bf16[16,128,2048]{2,1,0:T(8,128)(2,1)S(1)} %bitcast.21, bf16[16,128,2048]{2,1,0:T(8,128)(2,1)S(1)} %bitcast.22, ...), custom_call_target="tpu_custom_call" | custom-call | flops 1000 | bytes 1000 | tf_op jit(solution)/shard_map/pool_attention/pallas_call | solution.py:234
  141.9 0.0 slice-done.1
  142.0 0.3 local_attention.1.local
  142.3 8.3 %collective-permute-done.4.refs_1_ = bf16[3,256,512]{2,1,0:T(8,128)(2,1)S(1)} collective-permute-done((bf16[3,256,512]{2,1,0:T(8,128)(2,1)}, bf16[3,256,512]{2,1,0:T(8,128)(2,1)S(1)}, u32[]{:S(2)}, u32[]{:S(2)}) %collective-permute-start.4) | collective-permute-done | bytes 786464 | tf_op jit(solution)/shard_map/ppermute | solution.py:452
  150.6 0.0 collective-permute-done.13.refs_7_
  150.6 0.5 collective-permute-start.15
  151.1 0.1 pick_own.1
  151.2 2.0 collective-permute-done.18.refs_11_
  153.3 1.5 collective-permute-done.15.refs_9_
  154.8 2.3 %product_far.1 = (bf16[256,1024]{1,0:T(8,128)(2,1)S(1)}, bf16[256,1024]{1,0:T(8,128)(2,1)S(1)}) custom-call(bf16[3,256,512]{2,1,0:T(8,128)(2,1)S(1)} %get-tuple-element.89.refs_0_, bf16[3,256,512]{2,1,0:T(8,128)(2,1)S(1)} %collective-permute-done.4.refs_1_, bf16[3,256,512]{2,1,0:T(8,128)(2,1)S(1)} %collective-permute-done.17.refs_2_, ...), custom_call_target="tpu_custom_call" | custom-call | flops 1000 | bytes 1000 | tf_op jit(solution)/shard_map/product_far/pallas_call | solution.py:185
  157.1 4.1 %collective-permute-start.23 = (bf16[256,1024]{1,0:T(8,128)(2,1)S(1)}, bf16[256,1024]{1,0:T(8,128)(2,1)S(1)}, u32[]{:S(2)}, u32[]{:S(2)}) collective-permute-start(bf16[256,1024]{1,0:T(8,128)(2,1)S(1)} %get-tuple-element.98), channel_id=1, source_target_pairs={{0,12},{1,13},{2,14},{3,15},{4,0},{5,1},{6,2},{7,3},{8,4},{9,5},{1... | collective-permute-start | bytes 1572872 | tf_op jit(solution)/shard_map/ppermute | solution.py:493
  161.2 0.2 collective-permute-start.5
  161.4 3.1 %collective-permute-start.6 = (bf16[256,512]{1,0:T(8,128)(2,1)S(1)}, bf16[256,512]{1,0:T(8,128)(2,1)S(1)}, u32[]{:S(2)}, u32[]{:S(2)}) collective-permute-start(bf16[256,512]{1,0:T(8,128)(2,1)S(1)} %copy-done.7), channel_id=1, source_target_pairs={{0,3},{1,0},{2,1},{3,2},{4,7},{5,4},{6,5},{7,6},{8,11},{9,8},{10,9... | collective-permute-start | bytes 786440 | tf_op jit(solution)/shard_map/ppermute | solution.py:457
  164.4 4.5 %product_near.1 = (bf16[256,1024]{1,0:T(8,128)(2,1)S(1)}, bf16[256,1024]{1,0:T(8,128)(2,1)S(1)}, bf16[256,1024]{1,0:T(8,128)(2,1)S(1)}, bf16[256,1024]{1,0:T(8,128)(2,1)S(1)}) custom-call(bf16[3,256,512]{2,1,0:T(8,128)(2,1)S(1)} %get-tuple-element.89.refs_0_, bf16[3,256,512]{2,1,0:T(8,128)(2,1)S(1)} %collective-permute-done.4.refs_1_, ...), custom_call_target="tpu_custom_call" | custom-call | flops 1000 | bytes 1000 | tf_op jit(solution)/shard_map/product_near/pallas_call | solution.py:185
  168.9 0.1 collective-permute-start.21
  169.0 3.7 %collective-permute-done.23 = bf16[256,1024]{1,0:T(8,128)(2,1)S(1)} collective-permute-done((bf16[256,1024]{1,0:T(8,128)(2,1)S(1)}, bf16[256,1024]{1,0:T(8,128)(2,1)S(1)}, u32[]{:S(2)}, u32[]{:S(2)}) %collective-permute-start.23) | collective-permute-done | bytes 524320 | tf_op jit(solution)/shard_map/ppermute | solution.py:493
  172.7 3.7 %collective-permute-start.22 = (bf16[256,1024]{1,0:T(8,128)(2,1)S(1)}, bf16[256,1024]{1,0:T(8,128)(2,1)S(1)}, u32[]{:S(2)}, u32[]{:S(2)}) collective-permute-start(bf16[256,1024]{1,0:T(8,128)(2,1)S(1)} %get-tuple-element.96), channel_id=1, source_target_pairs={{0,12},{1,13},{2,14},{3,15},{4,0},{5,1},{6,2},{7,3},{8,4},{9,5},{1... | collective-permute-start | bytes 1572872 | tf_op jit(solution)/shard_map/ppermute | solution.py:501
  176.4 0.2 add_convert_fusion
  176.6 0.6 collective-permute-done.19
  177.2 0.0 collective-permute-start.24
  177.2 0.2 add_convert_fusion.1
  177.4 2.1 collective-permute-start.20
  179.5 0.0 collective-permute-done.6.refs_2_
  179.5 1.5 collective-permute-start.7
  181.6 5.8 %collective-permute-done.7.refs_3_ = bf16[256,512]{1,0:T(8,128)(2,1)S(1)} collective-permute-done((bf16[256,512]{1,0:T(8,128)(2,1)S(1)}, bf16[256,512]{1,0:T(8,128)(2,1)S(1)}, u32[]{:S(2)}, u32[]{:S(2)}) %collective-permute-start.7) | collective-permute-done | bytes 262176 | tf_op jit(solution)/shard_map/ppermute | solution.py:458
  187.4 2.3 %product_own.1 = (f32[256,1024]{1,0:T(8,128)S(1)}, f32[256,1024]{1,0:T(8,128)S(1)}) custom-call(bf16[256,512]{1,0:T(8,128)(2,1)S(1)} %get-tuple-element.53.refs_0_, bf16[256,512]{1,0:T(8,128)(2,1)S(1)} %collective-permute-done.5.refs_1_, bf16[256,512]{1,0:T(8,128)(2,1)S(1)} %collective-permute-done.6.refs_2_, ...), custom_call_target="tpu_custom_call" | custom-call | flops 1000 | bytes 1000 | tf_op jit(solution)/shard_map/product_own/pallas_call | solution.py:185
  189.7 0.0 collective-permute-done.21.up_r
  189.8 8.5 %collective-permute-done.24.down_r = bf16[256,1024]{1,0:T(8,128)(2,1)S(1)} collective-permute-done((bf16[256,1024]{1,0:T(8,128)(2,1)S(1)}, bf16[256,1024]{1,0:T(8,128)(2,1)S(1)}, u32[]{:S(2)}, u32[]{:S(2)}) %collective-permute-start.24) | collective-permute-done | bytes 524320 | tf_op jit(solution)/shard_map/ppermute | solution.py:502
  198.3 0.3 collective-permute-done.20.up_l
  198.6 2.8 %prefix_attention.1 = (bf16[1,256,2048]{2,1,0:T(8,128)(2,1)}, f32[16,72,128]{2,1,0:T(8,128)S(1)}) custom-call(s32[1]{0:T(128)S(6)} %copy.12.prompt_pages, f32[256,1024]{1,0:T(8,128)S(1)} %get-tuple-element.87.own_l, f32[256,1024]{1,0:T(8,128)S(1)} %get-tuple-element.88.own_r, bf16[256,1024]{1,0:T(8,128)(2,1)S(1)} %collective-permute-done.20.up_l, ...), custom_call_target="tpu_custom_call" | custom-call | flops 300000000 | bytes 6291456 | tf_op jit(solution)/shard_map/prefix_attention/pallas_call | solution.py:388
  201.4 17.8 %all_to_all.5.arrived = f32[16,72,128]{2,1,0:T(8,128)S(1)} all-to-all(f32[16,72,128]{2,1,0:T(8,128)S(1)} %get-tuple-element.102), channel_id=1, replica_groups=mesh['prompt'=8,'sample'=16] {'sample'}, dimensions={0} | all-to-all | bytes 1179648 | tf_op jit(solution)/shard_map/all_to_all | solution.py:506
  219.2 0.3 combine.1
  219.4 0.6 reshape.15
  (30 shorter events, 0.1 us)
Async XLA Ops:
  1.9 1.0 copy-start.2
  2.9 0.8 copy-start.3
  3.6 0.7 copy-start.5
  4.9 101.7 %collective-permute-start = (bf16[552,256]{1,0:T(8,128)(2,1)S(1)}, bf16[552,256]{1,0:T(8,128)(2,1)S(1)}, u32[]{:S(2)}, u32[]{:S(2)}) collective-permute-start(bf16[552,256]{1,0:T(8,128)(2,1)S(1)} %get-tuple-element.67), channel_id=1, source_target_pairs={{0,1},{1,2},{2,3},{3,0},{4,5},{5,6},{6,7},{7,4},{8,9},{9,10},{10,1... | collective-permute-start | bytes 847880 | tf_op jit(solution)/shard_map/ppermute | solution.py:443
  6.5 100.1 %collective-permute-start.1 = (bf16[552,256]{1,0:T(8,128)(2,1)S(1)}, bf16[552,256]{1,0:T(8,128)(2,1)S(1)}, u32[]{:S(2)}, u32[]{:S(2)}) collective-permute-start(bf16[552,256]{1,0:T(8,128)(2,1)S(1)} %get-tuple-element.67), channel_id=1, source_target_pairs={{0,3},{1,0},{2,1},{3,2},{4,7},{5,4},{6,5},{7,6},{8,11},{9,8},{10,9... | collective-permute-start | bytes 847880 | tf_op jit(solution)/shard_map/ppermute | solution.py:443
  8.2 98.4 %collective-permute-start.2 = (bf16[552,256]{1,0:T(8,128)(2,1)S(1)}, bf16[552,256]{1,0:T(8,128)(2,1)S(1)}, u32[]{:S(2)}, u32[]{:S(2)}) collective-permute-start(bf16[552,256]{1,0:T(8,128)(2,1)S(1)} %get-tuple-element.67), channel_id=1, source_target_pairs={{0,2},{1,3},{2,0},{3,1},{4,6},{5,7},{6,4},{7,5},{8,10},{9,11},{10,... | collective-permute-start | bytes 847880 | tf_op jit(solution)/shard_map/ppermute | solution.py:443
  10.1 131.8 %slice-start = ((s8[8388608]{0:T(1024)(128)(4,1)}), s8[4194304]{0:T(1024)(128)(4,1)S(1)}, s32[]{:S(2)}) async-start(s8[8388608]{0:T(1024)(128)(4,1)} %bitcast.27), calls=%async_computation.1 | async-start | bytes 8388608
  106.9 16.3 %collective-permute-start.9 = (bf16[4,512,256]{2,1,0:T(8,128)(2,1)S(1)}, bf16[4,512,256]{2,1,0:T(8,128)(2,1)S(1)}, u32[]{:S(2)}, u32[]{:S(2)}) collective-permute-start(bf16[4,512,256]{2,1,0:T(8,128)(2,1)S(1)} %pad_maximum_fusion.refs_4_), channel_id=1, source_target_pairs={{0,32},{16,112},{32,64},{48,16},{64,96},{80,48},{96,0},{112,80},{1... | collective-permute-start | bytes 3145736 | tf_op jit(solution)/shard_map/ppermute | solution.py:466
  108.5 16.2 %collective-permute-start.8 = (bf16[4,512,256]{2,1,0:T(8,128)(2,1)S(1)}, bf16[4,512,256]{2,1,0:T(8,128)(2,1)S(1)}, u32[]{:S(2)}, u32[]{:S(2)}) collective-permute-start(bf16[4,512,256]{2,1,0:T(8,128)(2,1)S(1)} %pad_maximum_fusion.refs_4_), channel_id=1, source_target_pairs={{0,16},{16,0},{32,48},{48,32},{64,80},{80,64},{96,112},{112,96},{1... | collective-permute-start | bytes 3145736 | tf_op jit(solution)/shard_map/ppermute | solution.py:465
  108.7 21.5 %collective-permute-start.3 = (bf16[3,256,512]{2,1,0:T(8,128)(2,1)}, bf16[3,256,512]{2,1,0:T(8,128)(2,1)S(1)}, u32[]{:S(2)}, u32[]{:S(2)}) collective-permute-start(bf16[3,256,512]{2,1,0:T(8,128)(2,1)} %get-tuple-element.62), channel_id=1, source_target_pairs={{0,2},{1,3},{2,0},{3,1},{4,6},{5,7},{6,4},{7,5},{8,10},{9,11},{10,... | collective-permute-start | bytes 2359304 | tf_op jit(solution)/shard_map/ppermute | solution.py:450
  110.4 6.8 %collective-permute-start.10 = (bf16[4,40,256]{2,1,0:T(8,128)(2,1)S(1)}, bf16[4,40,256]{2,1,0:T(8,128)(2,1)S(1)}, u32[]{:S(2)}, u32[]{:S(2)}) collective-permute-start(bf16[4,40,256]{2,1,0:T(8,128)(2,1)S(1)} %pad_maximum_fusion.1.refs_0_), channel_id=1, source_target_pairs={{0,4},{1,5},{2,6},{3,7},{4,8},{5,9},{6,10},{7,11},{8,12},{9,13},{1... | collective-permute-start | bytes 245768 | tf_op jit(solution)/shard_map/ppermute | solution.py:462
  112.4 6.4 %collective-permute-start.11 = (bf16[4,40,256]{2,1,0:T(8,128)(2,1)S(1)}, bf16[4,40,256]{2,1,0:T(8,128)(2,1)S(1)}, u32[]{:S(2)}, u32[]{:S(2)}) collective-permute-start(bf16[4,40,256]{2,1,0:T(8,128)(2,1)S(1)} %pad_maximum_fusion.1.refs_0_), channel_id=1, source_target_pairs={{0,12},{1,13},{2,14},{3,15},{4,0},{5,1},{6,2},{7,3},{8,4},{9,5},{1... | collective-permute-start | bytes 245768 | tf_op jit(solution)/shard_map/ppermute | solution.py:462
  117.2 5.9 %collective-permute-start.12 = (bf16[4,40,256]{2,1,0:T(8,128)(2,1)S(1)}, bf16[4,40,256]{2,1,0:T(8,128)(2,1)S(1)}, u32[]{:S(2)}, u32[]{:S(2)}) collective-permute-start(bf16[4,40,256]{2,1,0:T(8,128)(2,1)S(1)} %pad_maximum_fusion.1.refs_0_), channel_id=1, source_target_pairs={{0,8},{1,9},{2,10},{3,11},{4,12},{5,13},{6,14},{7,15},{8,0},{9,1},... | collective-permute-start | bytes 245768 | tf_op jit(solution)/shard_map/ppermute | solution.py:462
  123.1 27.4 %collective-permute-start.16 = (bf16[4,512,256]{2,1,0:T(8,128)(2,1)S(1)}, bf16[4,512,256]{2,1,0:T(8,128)(2,1)S(1)}, u32[]{:S(2)}, u32[]{:S(2)}) collective-permute-start(bf16[4,512,256]{2,1,0:T(8,128)(2,1)S(1)} %collective-permute-done.9.refs_6_), channel_id=1, source_target_pairs={{0,32},{16,112},{32,64},{48,16},{64,96},{80,48},{96,0},{112,80},{1... | collective-permute-start | bytes 3145736 | tf_op jit(solution)/shard_map/ppermute | solution.py:469
  124.7 25.9 %collective-permute-start.13 = (bf16[4,512,256]{2,1,0:T(8,128)(2,1)S(1)}, bf16[4,512,256]{2,1,0:T(8,128)(2,1)S(1)}, u32[]{:S(2)}, u32[]{:S(2)}) collective-permute-start(bf16[4,512,256]{2,1,0:T(8,128)(2,1)S(1)} %collective-permute-done.8.refs_5_), channel_id=1, source_target_pairs={{0,32},{16,112},{32,64},{48,16},{64,96},{80,48},{96,0},{112,80},{1... | collective-permute-start | bytes 3145736 | tf_op jit(solution)/shard_map/ppermute | solution.py:467
  130.2 20.4 %collective-permute-start.4 = (bf16[3,256,512]{2,1,0:T(8,128)(2,1)}, bf16[3,256,512]{2,1,0:T(8,128)(2,1)S(1)}, u32[]{:S(2)}, u32[]{:S(2)}) collective-permute-start(bf16[3,256,512]{2,1,0:T(8,128)(2,1)} %get-tuple-element.63), channel_id=1, source_target_pairs={{0,1},{1,2},{2,3},{3,0},{4,5},{5,6},{6,7},{7,4},{8,9},{9,10},{10,1... | collective-permute-start | bytes 2359304 | tf_op jit(solution)/shard_map/ppermute | solution.py:452
  130.8 19.8 %collective-permute-start.17 = (bf16[3,256,512]{2,1,0:T(8,128)(2,1)}, bf16[3,256,512]{2,1,0:T(8,128)(2,1)S(1)}, u32[]{:S(2)}, u32[]{:S(2)}) collective-permute-start(bf16[3,256,512]{2,1,0:T(8,128)(2,1)} %get-tuple-element.85), channel_id=1, source_target_pairs={{0,3},{1,0},{2,1},{3,2},{4,7},{5,4},{6,5},{7,6},{8,11},{9,8},{10,9... | collective-permute-start | bytes 2359304 | tf_op jit(solution)/shard_map/ppermute | solution.py:453
  133.4 17.8 %collective-permute-start.14 = (bf16[4,512,256]{2,1,0:T(8,128)(2,1)S(1)}, bf16[4,512,256]{2,1,0:T(8,128)(2,1)S(1)}, u32[]{:S(2)}, u32[]{:S(2)}) collective-permute-start(bf16[4,512,256]{2,1,0:T(8,128)(2,1)S(1)} %collective-permute-done.9.refs_6_), channel_id=1, source_target_pairs={{0,16},{16,0},{32,48},{48,32},{64,80},{80,64},{96,112},{112,96},{1... | collective-permute-start | bytes 3145736 | tf_op jit(solution)/shard_map/ppermute | solution.py:470
  134.2 3.4 %copy-start = (bf16[1,1,16,128,2048]{4,3,2,1,0:T(8,128)(2,1)S(1)}, bf16[1,1,16,128,2048]{4,3,2,1,0:T(8,128)(2,1)}, u32[]{:S(2)}) copy-start(bf16[1,1,16,128,2048]{4,3,2,1,0:T(8,128)(2,1)} %param.15) | copy-start | bytes 25165828
  137.6 4.3 %slice-start.1 = ((s8[8388608]{0:T(1024)(128)(4,1)}), s8[4194304]{0:T(1024)(128)(4,1)S(1)}, s32[]{:S(2)}) async-start(s8[8388608]{0:T(1024)(128)(4,1)} %bitcast.27), calls=%async_computation.2 | async-start | bytes 8388608
  137.6 4.3 %copy-start.4 = (bf16[1,1,2048]{2,1,0:T(2,128)(2,1)S(1)}, bf16[1,1,2048]{2,1,0:T(2,128)(2,1)}, u32[]{:S(2)}) copy-start(bf16[1,1,2048]{2,1,0:T(2,128)(2,1)} %param.13) | copy-start | bytes 12292
  141.9 9.2 %copy-start.1 = (bf16[1,4096,512]{2,1,0:T(8,128)(2,1)S(1)}, bf16[1,4096,512]{2,1,0:T(8,128)(2,1)}, u32[]{:S(2)}) copy-start(bf16[1,4096,512]{2,1,0:T(8,128)(2,1)} %param.10) | copy-start | bytes 12582916
  142.2 19.0 %copy-start.8 = (bf16[256,512]{1,0:T(8,128)(2,1)S(1)}, bf16[256,512]{1,0:T(8,128)(2,1)}, u32[]{:S(2)}) copy-start(bf16[256,512]{1,0:T(8,128)(2,1)} %get-tuple-element.64) | copy-start | bytes 786436
  142.2 19.1 %copy-start.7 = (bf16[256,512]{1,0:T(8,128)(2,1)S(1)}, bf16[256,512]{1,0:T(8,128)(2,1)}, u32[]{:S(2)}) copy-start(bf16[256,512]{1,0:T(8,128)(2,1)} %get-tuple-element.65) | copy-start | bytes 786436
  150.6 2.7 %collective-permute-start.18 = (bf16[4,512,256]{2,1,0:T(8,128)(2,1)S(1)}, bf16[4,512,256]{2,1,0:T(8,128)(2,1)S(1)}, u32[]{:S(2)}, u32[]{:S(2)}) collective-permute-start(bf16[4,512,256]{2,1,0:T(8,128)(2,1)S(1)} %collective-permute-done.16.refs_10_), channel_id=1, source_target_pairs={{0,16},{16,0},{32,48},{48,32},{64,80},{80,64},{96,112},{112,96},{1... | collective-permute-start | bytes 3145736 | tf_op jit(solution)/shard_map/ppermute | solution.py:481
  150.6 4.1 %collective-permute-start.15 = (bf16[4,512,256]{2,1,0:T(8,128)(2,1)S(1)}, bf16[4,512,256]{2,1,0:T(8,128)(2,1)S(1)}, u32[]{:S(2)}, u32[]{:S(2)}) collective-permute-start(bf16[4,512,256]{2,1,0:T(8,128)(2,1)S(1)} %collective-permute-done.13.refs_7_), channel_id=1, source_target_pairs={{0,16},{16,0},{32,48},{48,32},{64,80},{80,64},{96,112},{112,96},{1... | collective-permute-start | bytes 3145736 | tf_op jit(solution)/shard_map/ppermute | solution.py:471
  157.1 22.4 %copy-start.6 = (bf16[256,512]{1,0:T(8,128)(2,1)S(1)}, bf16[256,512]{1,0:T(8,128)(2,1)}, u32[]{:S(2)}) copy-start(bf16[256,512]{1,0:T(8,128)(2,1)} %get-tuple-element.66) | copy-start | bytes 786436
  157.1 15.6 %collective-permute-start.23 = (bf16[256,1024]{1,0:T(8,128)(2,1)S(1)}, bf16[256,1024]{1,0:T(8,128)(2,1)S(1)}, u32[]{:S(2)}, u32[]{:S(2)}) collective-permute-start(bf16[256,1024]{1,0:T(8,128)(2,1)S(1)} %get-tuple-element.98), channel_id=1, source_target_pairs={{0,12},{1,13},{2,14},{3,15},{4,0},{5,1},{6,2},{7,3},{8,4},{9,5},{1... | collective-permute-start | bytes 1572872 | tf_op jit(solution)/shard_map/ppermute | solution.py:493
  161.2 16.0 %collective-permute-start.19 = (bf16[256,1024]{1,0:T(8,128)(2,1)S(1)}, bf16[256,1024]{1,0:T(8,128)(2,1)S(1)}, u32[]{:S(2)}, u32[]{:S(2)}) collective-permute-start(bf16[256,1024]{1,0:T(8,128)(2,1)S(1)} %get-tuple-element.94), channel_id=1, source_target_pairs={{0,4},{1,5},{2,6},{3,7},{4,8},{5,9},{6,10},{7,11},{8,12},{9,13},{1... | collective-permute-start | bytes 1572872 | tf_op jit(solution)/shard_map/ppermute | solution.py:492
  161.2 16.2 %collective-permute-start.5 = (bf16[256,512]{1,0:T(8,128)(2,1)S(1)}, bf16[256,512]{1,0:T(8,128)(2,1)S(1)}, u32[]{:S(2)}, u32[]{:S(2)}) collective-permute-start(bf16[256,512]{1,0:T(8,128)(2,1)S(1)} %copy-done.8), channel_id=1, source_target_pairs={{0,1},{1,2},{2,3},{3,0},{4,5},{5,6},{6,7},{7,4},{8,9},{9,10},{10,1... | collective-permute-start | bytes 786440 | tf_op jit(solution)/shard_map/ppermute | solution.py:456
  161.4 18.1 %collective-permute-start.6 = (bf16[256,512]{1,0:T(8,128)(2,1)S(1)}, bf16[256,512]{1,0:T(8,128)(2,1)S(1)}, u32[]{:S(2)}, u32[]{:S(2)}) collective-permute-start(bf16[256,512]{1,0:T(8,128)(2,1)S(1)} %copy-done.7), channel_id=1, source_target_pairs={{0,3},{1,0},{2,1},{3,2},{4,7},{5,4},{6,5},{7,6},{8,11},{9,8},{10,9... | collective-permute-start | bytes 786440 | tf_op jit(solution)/shard_map/ppermute | solution.py:457
  168.9 20.8 %collective-permute-start.21 = (bf16[256,1024]{1,0:T(8,128)(2,1)S(1)}, bf16[256,1024]{1,0:T(8,128)(2,1)S(1)}, u32[]{:S(2)}, u32[]{:S(2)}) collective-permute-start(bf16[256,1024]{1,0:T(8,128)(2,1)S(1)} %get-tuple-element.95), channel_id=1, source_target_pairs={{0,4},{1,5},{2,6},{3,7},{4,8},{5,9},{6,10},{7,11},{8,12},{9,13},{1... | collective-permute-start | bytes 1572872 | tf_op jit(solution)/shard_map/ppermute | solution.py:500
  172.7 17.1 %collective-permute-start.22 = (bf16[256,1024]{1,0:T(8,128)(2,1)S(1)}, bf16[256,1024]{1,0:T(8,128)(2,1)S(1)}, u32[]{:S(2)}, u32[]{:S(2)}) collective-permute-start(bf16[256,1024]{1,0:T(8,128)(2,1)S(1)} %get-tuple-element.96), channel_id=1, source_target_pairs={{0,12},{1,13},{2,14},{3,15},{4,0},{5,1},{6,2},{7,3},{8,4},{9,5},{1... | collective-permute-start | bytes 1572872 | tf_op jit(solution)/shard_map/ppermute | solution.py:501
  177.2 21.0 %collective-permute-start.24 = (bf16[256,1024]{1,0:T(8,128)(2,1)S(1)}, bf16[256,1024]{1,0:T(8,128)(2,1)S(1)}, u32[]{:S(2)}, u32[]{:S(2)}) collective-permute-start(bf16[256,1024]{1,0:T(8,128)(2,1)S(1)} %add_convert_fusion), channel_id=1, source_target_pairs={{0,12},{1,13},{2,14},{3,15},{4,0},{5,1},{6,2},{7,3},{8,4},{9,5},{1... | collective-permute-start | bytes 1572872 | tf_op jit(solution)/shard_map/ppermute | solution.py:502
  177.4 21.1 %collective-permute-start.20 = (bf16[256,1024]{1,0:T(8,128)(2,1)S(1)}, bf16[256,1024]{1,0:T(8,128)(2,1)S(1)}, u32[]{:S(2)}, u32[]{:S(2)}) collective-permute-start(bf16[256,1024]{1,0:T(8,128)(2,1)S(1)} %add_convert_fusion.1), channel_id=1, source_target_pairs={{0,4},{1,5},{2,6},{3,7},{4,8},{5,9},{6,10},{7,11},{8,12},{9,13},{1... | collective-permute-start | bytes 1572872 | tf_op jit(solution)/shard_map/ppermute | solution.py:499
  179.5 7.9 %collective-permute-start.7 = (bf16[256,512]{1,0:T(8,128)(2,1)S(1)}, bf16[256,512]{1,0:T(8,128)(2,1)S(1)}, u32[]{:S(2)}, u32[]{:S(2)}) collective-permute-start(bf16[256,512]{1,0:T(8,128)(2,1)S(1)} %copy-done.6), channel_id=1, source_target_pairs={{0,2},{1,3},{2,0},{3,1},{4,6},{5,7},{6,4},{7,5},{8,10},{9,11},{10,... | collective-permute-start | bytes 786440 | tf_op jit(solution)/shard_map/ppermute | solution.py:458

commit v2 on v1

--- a/solution.py
+++ b/solution.py
@@ -58,8 +58,12 @@
 HALF = QUERY_HEADS // 2
 
 
-def prepare_kernel(where, length, flag, weight, query, sent, own):
-    sent[:SLICE] = weight[...]
+def prepare_kernel(where, length, flag, weight, query_hbm, sent, own, query, sems):
+    weight_copy = pltpu.make_async_copy(weight, sent.at[pl.ds(0, SLICE)], sems.at[0])
+    query_copy = pltpu.make_async_copy(query_hbm, query, sems.at[1])
+    query_copy.start()
+    weight_copy.start()
+    query_copy.wait()
     heads = [query[0, 0:1, h * HEAD_SIZE : (h + 1) * HEAD_SIZE].astype(F32) for h in range(QUERY_HEADS)]
     low, high = jnp.concatenate(heads[:HALF]), jnp.concatenate(heads[HALF:])
     own[:HALF] = low.astype(BF16)
@@ -72,6 +76,7 @@
     plan = put_lane(plan, CMAX, length[0, 0].astype(F32))
     plan = put_lane(plan, CMAX + 1, flag[0, 0].astype(F32))
     sent[SLICE + HALF :] = plan.astype(BF16)
+    weight_copy.wait()
 
 
 def prepare(weight, query, where, length, flag):
@@ -82,9 +87,13 @@
             jax.ShapeDtypeStruct((SENT, COLUMNS), BF16),
             jax.ShapeDtypeStruct((QUERY_HEADS, HEAD_SIZE), BF16),
         ],
-        in_specs=[smem] * 3 + [vmem] * 2,
+        in_specs=[smem] * 3 + [pl.BlockSpec(memory_space=pl.ANY)] * 2,
         out_specs=[vmem, vmem],
-        compiler_params=params(16),
+        scratch_shapes=[
+            pltpu.VMEM((1, 1, QUERY_HEADS * HEAD_SIZE), BF16),
+            pltpu.SemaphoreType.DMA((2,)),
+        ],
+        compiler_params=params(58),
         cost_estimate=cost(1000, 1000),
         name="prepare",
     )(where, length, flag, weight, query)
@@ -142,9 +151,10 @@
     copies = []
     for i, step in enumerate(steps):
         column = lax.rem(x + step, 4)
-        for k, up in enumerate((2, 1, 3)):
-            copies.append((states.at[lax.rem(z + up, 4), column], outs[2 * i].at[k]))
-        copies.append((states.at[z, column], outs[2 * i + 1]))
+        copies.append((states.at[lax.rem(z + 2, 4), column], outs[3 * i]))
+        copies.append((states.at[lax.rem(z + 1, 4), column], outs[3 * i + 1].at[0]))
+        copies.append((states.at[lax.rem(z + 3, 4), column], outs[3 * i + 1].at[1]))
+        copies.append((states.at[z, column], outs[3 * i + 2]))
     copies = [pltpu.make_async_copy(src, dst, sems.at[n]) for n, (src, dst) in enumerate(copies)]
     for copy in copies:
         copy.start()
@@ -152,14 +162,14 @@
         copy.wait()
 
 
-def pick(states, steps, space, mib, name):
-    rest = jax.ShapeDtypeStruct((3, ROWS, SLICE), BF16)
-    own = jax.ShapeDtypeStruct((ROWS, SLICE), BF16)
+def pick(states, steps, mib, name):
+    one = jax.ShapeDtypeStruct((ROWS, SLICE), BF16)
+    two = jax.ShapeDtypeStruct((2, ROWS, SLICE), BF16)
     return pl.pallas_call(
         functools.partial(pick_kernel, steps),
-        out_shape=[rest, own] * len(steps),
+        out_shape=[one, two, one] * len(steps),
         in_specs=[pl.BlockSpec(memory_space=pl.ANY)],
-        out_specs=[pl.BlockSpec(memory_space=space)] * (2 * len(steps)),
+        out_specs=[pl.BlockSpec(memory_space=pltpu.VMEM)] * (3 * len(steps)),
         scratch_shapes=[pltpu.SemaphoreType.DMA((4 * len(steps),))],
         compiler_params=params(mib),
         cost_estimate=cost(1000, 1000),
@@ -167,25 +177,26 @@
     )(states)
 
 
-def product_kernel(blocks, *refs):
-    states, pieces, outs = refs[:4], refs[4:12], refs[12:]
-    for j in range(8):
+def product_kernel(blocks, count, *refs):
+    states, pieces, outs = refs[:4], refs[4 : 4 + count], refs[4 + count :]
+    for j in range(count):
         for k, block in enumerate(blocks):
             total = jnp.zeros((ROWS, COLUMNS), F32)
             for d in range(4):
                 left = states[d][...] if block is None else states[d][block]
                 total += jnp.dot(left, pieces[j][d], preferred_element_type=F32)
-            out = outs[2 * k + j // 4]
+            out = outs[k * count // 4 + j // 4]
             out[:, (j % 4) * COLUMNS : (j % 4 + 1) * COLUMNS] = total.astype(out.dtype)
 
 
 def product(states, pieces, blocks, kind, name):
     vmem = pl.BlockSpec(memory_space=pltpu.VMEM)
-    outs = [jax.ShapeDtypeStruct((ROWS, KVW // 2), kind)] * (2 * len(blocks))
-    return pl.pallas_call(
-        functools.partial(product_kernel, blocks),
+    count = len(pieces)
+    outs = [jax.ShapeDtypeStruct((ROWS, KVW // 2), kind)] * (len(blocks) * count // 4)
+    return pl.pallas_call(
+        functools.partial(product_kernel, blocks, count),
         out_shape=outs,
-        in_specs=[vmem] * 12,
+        in_specs=[vmem] * (4 + count),
         out_specs=[vmem] * len(outs),
         compiler_params=params(20),
         cost_estimate=cost(1000, 1000),
@@ -335,7 +346,7 @@
 
 
 def prefix_kernel(
-    prompt_pages, own_l, own_r, up_l, up_r, down_l, down_r, queries, pool, cache, packed
+    prompt_pages, own_l, own_r, up_l, up_r, down_l, down_r, far_l, far_r, queries, pool, cache, packed
 ):
     me, prompt = lax.axis_index("sample"), lax.axis_index("prompt")
     z, x = me // 4, lax.rem(me, 4)
@@ -349,8 +360,10 @@
     )
     for j in range(8):
         lanes = slice((j % 4) * COLUMNS, (j % 4 + 1) * COLUMNS)
-        own, up, down = (own_l, up_l, down_l) if j < 4 else (own_r, up_r, down_r)
-        total = own[:, lanes] + up[:, lanes].astype(F32) + down[:, lanes].astype(F32)
+        terms = (up_l, down_l, far_l) if j < 4 else (up_r, down_r, far_r)
+        total = (own_l if j < 4 else own_r)[:, lanes]
+        for term in terms:
+            total = total + term[:, lanes].astype(F32)
         target = pl.ds(pl.multiple_of(columns[j] * COLUMNS, COLUMNS), COLUMNS)
         cache[0, :, target] = total.astype(BF16)
     sources = [
@@ -391,7 +404,7 @@
             jax.ShapeDtypeStruct((1, ROWS, KVW), BF16),
             jax.ShapeDtypeStruct((SAMPLES, PACK, HEAD_SIZE), F32),
         ],
-        in_specs=[smem] + [vmem] * 8,
+        in_specs=[smem] + [vmem] * 10,
         out_specs=[vmem, vmem],
         compiler_params=params(20),
         cost_estimate=cost(300_000_000, 6 * MIB),
@@ -443,56 +456,54 @@
     along_x = [sent] + [lax.ppermute(sent, "sample", to) for to in (X_RIGHT, X_LEFT, X_FAR)]
 
     states = prompt_states.reshape(4, 4, ROWS, SLICE)
-    to_right, last_right, to_left, last_left, to_far, last_far = pick(
-        states, (1, 3, 2), pl.ANY, 56, "pick_sent"
+    picked = pick(states, (1, 3, 2), 52, "pick_sent")
+    towards = (X_RIGHT, X_LEFT, X_FAR)
+
+    def across(batch):
+        return [lax.ppermute(a, "sample", to) for a, to in zip(batch, towards)]
+
+    first, second, third = (list(picked[k::3]) for k in range(3))
+    *first, along_x[0], along_x[1], along_x[2], along_x[3] = tie((*first, *along_x))
+    mine = list(pick(states, (0,), 16, "pick_own"))
+    here = jnp.stack([a[:SLICE] for a in along_x])
+    of_row = jnp.stack([a[SLICE:] for a in along_x])
+
+    near = lax.ppermute(here, "prompt", Y_SPLIT)
+    here_other = lax.ppermute(here, "prompt", SWAP)
+    first = across(first)
+
+    near, here_other, second[0], second[1], of_row, *rest = tie(
+        (near, here_other, second[0], second[1], of_row, *first)
     )
-    to_far, *along_x = tie((to_far, *along_x))
-    rows_far = lax.ppermute(to_far, "sample", X_FAR)
-    to_right, to_left, query, rows_far = tie((to_right, to_left, query, rows_far))
-    rows_right = lax.ppermute(to_right, "sample", X_RIGHT)
-    rows_left = lax.ppermute(to_left, "sample", X_LEFT)
-    last_right, last_left, last_far, rows_right = tie((last_right, last_left, last_far, rows_right))
-    own_states = [
-        lax.ppermute(last_right, "sample", X_RIGHT),
-        lax.ppermute(last_left, "sample", X_LEFT),
-        lax.ppermute(last_far, "sample", X_FAR),
-    ]
-
-    of_row = jnp.stack([a[SLICE:] for a in along_x])
+    first = rest
+    near_other = lax.ppermute(here_other, "prompt", Y_SPLIT)
+    near_swapped = lax.ppermute(near, "prompt", SWAP)
+    right_left = across(second[:2])
     everyone = [of_row] + [lax.ppermute(of_row, "sample", to) for to in (Z_UP, Z_DOWN, Z_FAR)]
 
-    here = jnp.stack([a[:SLICE] for a in along_x])
-    here_other = lax.ppermute(here, "prompt", SWAP)
-    near = lax.ppermute(here, "prompt", Y_SPLIT)
-    near_other = lax.ppermute(here_other, "prompt", Y_SPLIT)
-    near, *everyone = tie((near, *everyone))
+    near, near_other, second[2], *rest = tie(
+        (near, near_other, second[2], *right_left, *everyone, *mine)
+    )
+    right_left, everyone, mine = rest[:2], rest[2:6], rest[6:]
     far = lax.ppermute(near, "prompt", Y_SPLIT)
-    near_swapped = lax.ppermute(near, "prompt", SWAP)
     near_other_swapped = lax.ppermute(near_other, "prompt", SWAP)
-
-    queries_all, by_group, slots, alive = unpack(everyone)
-    queries_all, rows_far = tie((queries_all, rows_far))
-    pool = pool_attention(slots, alive, queries_all, pool_pages[0, 0])
-    local_alive = jnp.where(preempted[0] > 0, 0, comp_pages[0])
-    query, here_other = tie((query, here_other))
-    local = local_attention(local_alive, query, new_kv[0], local_pages[0, 0])
-
-    far, pool, local, rows_right, rows_left = tie((far, pool, local, rows_right, rows_left))
+    second = [*right_left, lax.ppermute(second[2], "sample", X_FAR)]
+    left_half = [here, here_other, near, near_other]
+    (far_l,) = product([mine[0], *first], left_half, (None,), BF16, "product_far_l")
+    far_l = lax.ppermute(far_l, "sample", Z_FAR)
+
+    far, far_l, *rest = tie((far, far_l, *second, *third))
+    second, third = rest[:3], rest[3:]
     far_other = lax.ppermute(far, "prompt", SWAP)
-    pieces = [
-        here, here_other, near, near_other,
-        near_swapped, near_other_swapped, far, far_other,
-    ]
-
-    mine_rows, mine_last = pick(states, (0,), pltpu.VMEM, 16, "pick_own")
-    rows = [mine_rows, rows_right, rows_left, rows_far]
-    far_l, far_r = product(rows, pieces, (0,), BF16, "product_far")
-    up_l, up_r, down_l, down_r = product(rows, pieces, (1, 2), BF16, "product_near")
-    own_l, own_r = product([mine_last] + own_states, pieces, (None,), F32, "product_own")
-    from_down = lax.ppermute(far_l, "sample", Z_UP)
-    from_up = lax.ppermute(far_r, "sample", Z_DOWN)
-    up_l = (up_l.astype(F32) + from_down.astype(F32)).astype(BF16)
-    down_r = (down_r.astype(F32) + from_up.astype(F32)).astype(BF16)
+    third = across(third)
+    up_l, down_l = product([mine[1], *second], left_half, (0, 1), BF16, "product_near_l")
+
+    far_other, up_l, down_l = tie((far_other, up_l, down_l))
+    right_half = [near_swapped, near_other_swapped, far, far_other]
+    (far_r,) = product([mine[0], *first], right_half, (None,), BF16, "product_far_r")
+    up_r, down_r = product([mine[1], *second], right_half, (0, 1), BF16, "product_near_r")
+    query, far_r, up_r, down_r, *everyone = tie((query, far_r, up_r, down_r, *everyone))
+    own_l, own_r = product([mine[2], *third], left_half + right_half, (None,), F32, "product_own")
     sums = [
         own_l,
         own_r,
@@ -500,7 +511,14 @@
         lax.ppermute(up_r, "sample", Z_UP),
         lax.ppermute(down_l, "sample", Z_DOWN),
         lax.ppermute(down_r, "sample", Z_DOWN),
+        far_l,
+        lax.ppermute(far_r, "sample", Z_FAR),
     ]
+
+    queries_all, by_group, slots, alive = unpack(everyone)
+    pool = pool_attention(slots, alive, queries_all, pool_pages[0, 0])
+    local_alive = jnp.where(preempted[0] > 0, 0, comp_pages[0])
+    local = local_attention(local_alive, query, new_kv[0], local_pages[0, 0])
 
     cache, packed = prefix_attention(prompt_pages, sums, by_group, pool)
     arrived = lax.all_to_all(packed, "sample", split_axis=0, concat_axis=0, tiled=True)

time: 220 us -> 148 us (0.67)
  Pallas kernels: 115 us -> 24.4 us
  waiting for transfers between devices: 41.8 us -> 70.9 us
  blocking collectives: 17.8 us -> 0 us
  starting transfers between devices: 35.8 us -> 42.9 us
    pallas_call x5 -> x7, Pallas kernels: 106 us -> 12.7 us  [the longest x5 9.47 us: product(): pl.pallas_call(functools.partial(product_kernel, blocks, count), out_shap...]
    all_to_all x1 -> x0, blocking collectives: 17.8 us -> none  [per_device(): lax.all_to_all(packed, 'sample', split_axis=0, concat_axis=0, tiled=True)]
    ppermute x1, waiting for transfers between devices: 0.3 us -> 10.1 us  [per_device(): lax.ppermute(up_l, 'sample', Z_UP)]
    ppermute x1, waiting for transfers between devices: 0.01 us -> 9.06 us  [per_device(): lax.ppermute(up_r, 'sample', Z_UP)]
    ppermute x3, waiting for transfers between devices: 0.01 us -> 8.79 us  [per_device(): lax.ppermute(sent, 'sample', to)]
    ppermute x1, waiting for transfers between devices: 8.5 us -> 0.01 us  [per_device(): lax.ppermute(down_r, 'sample', Z_DOWN)]
    all_to_all x0 -> x1, waiting for transfers between devices: none -> 7.17 us  [per_device(): lax.all_to_all(packed, 'sample', split_axis=0, concat_axis=0, tiled=True)]
    all_to_all x0 -> x1, starting transfers between devices: none -> 7.02 us  [per_device(): lax.all_to_all(packed, 'sample', split_axis=0, concat_axis=0, tiled=True)]
  transfers between devices with their start and end apart: 25 -> 29, of which waited for: 11 -> 15; matrix products, arithmetic and copies ran while one was open for 0% -> 1% of each run, Pallas kernels for 49% -> 12%
where the time goes in v2:
time: 148 us; the launch traced here: 147 us
  waiting for transfers between devices  70.9 us (48%)
  starting transfers between devices  42.9 us (29%)
  Pallas kernels  24.4 us (16%)
  local copies, waits for them, and re-layouts  5.79 us (4%)
  between operations  3.14 us (2%)
    ppermute x8, waiting for transfers between devices, across(): return [lax.ppermute(a, 'sample', to) for a, to in zip(batch, towards)]  15.6 us
    ppermute x1, waiting for transfers between devices, per_device(): far_l = lax.ppermute(far_l, 'sample', Z_FAR)  10.7 us
    ppermute x1, waiting for transfers between devices, per_device(): lax.ppermute(up_l, 'sample', Z_UP)  10.1 us
    pallas_call x5, Pallas kernels, product(): pl.pallas_call(functools.partial(product_kernel, blocks, count), out_shap...  9.47 us
    ppermute x8, starting transfers between devices, across(): return [lax.ppermute(a, 'sample', to) for a, to in zip(batch, towards)]  9.39 us
    ppermute x1, waiting for transfers between devices, per_device(): lax.ppermute(up_r, 'sample', Z_UP)  9.06 us
    ppermute x3, waiting for transfers between devices, per_device(): lax.ppermute(sent, 'sample', to)  8.79 us
    all_to_all x1, waiting for transfers between devices, per_device(): lax.all_to_all(packed, 'sample', split_axis=0, concat_axis=0, tiled=True)  7.17 us
  transfers between devices with their start and end apart: 29, of which 15 were waited for; matrix products, arithmetic and copies ran while one was open for 1% of the time, Pallas kernels for 12%

profile of v2, /device:TPU:0, one launch (start us, length us, event | category | flops | bytes accessed | tf_op | source)
XLA Modules:
  0.0 147.3 jit_solution(8345788591124002616)
XLA Ops:
  0.6 0.0 copy-start
  2.2 2.4 %prepare.1 = (bf16[552,256]{1,0:T(8,128)(2,1)}, bf16[64,128]{1,0:T(8,128)(2,1)}) custom-call(s32[1,1,16]{2,1,0:T(1,128)} %where.1, s32[1,1]{1,0:T(1,128)S(6)} %copy.13.length, s32[1,1]{1,0:T(1,128)S(6)} %copy.14.flag, bf16[512,256]{1,0:T(8,128)(2,1)} %weight.1, bf16[1,1,8192]{2,1,0:T(2,128)(2,1)} %query_hbm.1), custom_call_target="tpu_custom_call" | custom-call | flops 1000 | bytes 1000 | tf_op jit(solution)/shard_map/prepare/pallas_call | solution.py:84
  4.6 1.6 %collective-permute-start = (bf16[552,256]{1,0:T(8,128)(2,1)}, bf16[552,256]{1,0:T(8,128)(2,1)S(1)}, u32[]{:S(2)}, u32[]{:S(2)}) collective-permute-start(bf16[552,256]{1,0:T(8,128)(2,1)} %get-tuple-element.78), channel_id=1, source_target_pairs={{0,1},{1,2},{2,3},{3,0},{4,5},{5,6},{6,7},{7,4},{8,9},{9,10},{10,1... | collective-permute-start | bytes 847880 | tf_op jit(solution)/shard_map/ppermute | solution.py:456
  6.3 1.7 %collective-permute-start.1 = (bf16[552,256]{1,0:T(8,128)(2,1)}, bf16[552,256]{1,0:T(8,128)(2,1)S(1)}, u32[]{:S(2)}, u32[]{:S(2)}) collective-permute-start(bf16[552,256]{1,0:T(8,128)(2,1)} %get-tuple-element.78), channel_id=1, source_target_pairs={{0,3},{1,0},{2,1},{3,2},{4,7},{5,4},{6,5},{7,6},{8,11},{9,8},{10,9... | collective-permute-start | bytes 847880 | tf_op jit(solution)/shard_map/ppermute | solution.py:456
  7.9 1.9 %collective-permute-start.2 = (bf16[552,256]{1,0:T(8,128)(2,1)}, bf16[552,256]{1,0:T(8,128)(2,1)S(1)}, u32[]{:S(2)}, u32[]{:S(2)}) collective-permute-start(bf16[552,256]{1,0:T(8,128)(2,1)} %get-tuple-element.78), channel_id=1, source_target_pairs={{0,2},{1,3},{2,0},{3,1},{4,6},{5,7},{6,4},{7,5},{8,10},{9,11},{10,... | collective-permute-start | bytes 847880 | tf_op jit(solution)/shard_map/ppermute | solution.py:456
  9.8 3.1 %pick_sent.1 = (bf16[256,512]{1,0:T(8,128)(2,1)S(1)}, bf16[2,256,512]{2,1,0:T(8,128)(2,1)}, bf16[256,512]{1,0:T(8,128)(2,1)S(1)}, bf16[256,512]{1,0:T(8,128)(2,1...) custom-call(bf16[4,4,256,512]{3,2,1,0:T(8,128)(2,1)} %bitcast.27), custom_call_target="tpu_custom_call" | custom-call | flops 1000 | bytes 1000 | tf_op jit(solution)/shard_map/pick_sent/pallas_call | solution.py:168
  12.9 1.6 %collective-permute-done = bf16[552,256]{1,0:T(8,128)(2,1)S(1)} collective-permute-done((bf16[552,256]{1,0:T(8,128)(2,1)}, bf16[552,256]{1,0:T(8,128)(2,1)S(1)}, u32[]{:S(2)}, u32[]{:S(2)}) %collective-permute-start) | collective-permute-done | bytes 282656 | tf_op jit(solution)/shard_map/ppermute | solution.py:456
  14.5 1.7 %collective-permute-done.1 = bf16[552,256]{1,0:T(8,128)(2,1)S(1)} collective-permute-done((bf16[552,256]{1,0:T(8,128)(2,1)}, bf16[552,256]{1,0:T(8,128)(2,1)S(1)}, u32[]{:S(2)}, u32[]{:S(2)}) %collective-permute-start.1) | collective-permute-done | bytes 282656 | tf_op jit(solution)/shard_map/ppermute | solution.py:456
  16.1 5.6 %collective-permute-done.2 = bf16[552,256]{1,0:T(8,128)(2,1)S(1)} collective-permute-done((bf16[552,256]{1,0:T(8,128)(2,1)}, bf16[552,256]{1,0:T(8,128)(2,1)S(1)}, u32[]{:S(2)}, u32[]{:S(2)}) %collective-permute-start.2) | collective-permute-done | bytes 282656 | tf_op jit(solution)/shard_map/ppermute | solution.py:456
  21.7 1.0 slice_bitcast_fusion.2
  22.7 0.1 pad_maximum_fusion.refs_4_
  22.9 1.6 %collective-permute-start.3 = (bf16[4,512,256]{2,1,0:T(8,128)(2,1)S(1)}, bf16[4,512,256]{2,1,0:T(8,128)(2,1)S(1)}, u32[]{:S(2)}, u32[]{:S(2)}) collective-permute-start(bf16[4,512,256]{2,1,0:T(8,128)(2,1)S(1)} %pad_maximum_fusion.refs_4_), channel_id=1, source_target_pairs={{0,32},{16,112},{32,64},{48,16},{64,96},{80,48},{96,0},{112,80},{1... | collective-permute-start | bytes 3145736 | tf_op jit(solution)/shard_map/ppermute | solution.py:471
  24.5 0.1 collective-permute-start.4
  24.7 1.0 collective-permute-start.5
  25.7 2.2 %collective-permute-start.6 = (bf16[256,512]{1,0:T(8,128)(2,1)S(1)}, bf16[256,512]{1,0:T(8,128)(2,1)S(1)}, u32[]{:S(2)}, u32[]{:S(2)}) collective-permute-start(bf16[256,512]{1,0:T(8,128)(2,1)S(1)} %get-tuple-element.85), channel_id=1, source_target_pairs={{0,3},{1,0},{2,1},{3,2},{4,7},{5,4},{6,5},{7,6},{8,11},{9,8},{10,9... | collective-permute-start | bytes 786440 | tf_op jit(solution)/shard_map/ppermute | solution.py:463
  27.9 0.1 collective-permute-start.7
  28.0 0.7 slice_bitcast_fusion.6
  28.7 5.9 %collective-permute-done.5.refs_1_ = bf16[256,512]{1,0:T(8,128)(2,1)S(1)} collective-permute-done((bf16[256,512]{1,0:T(8,128)(2,1)S(1)}, bf16[256,512]{1,0:T(8,128)(2,1)S(1)}, u32[]{:S(2)}, u32[]{:S(2)}) %collective-permute-start.5) | collective-permute-done | bytes 262176 | tf_op jit(solution)/shard_map/ppermute | solution.py:463
  34.6 4.7 %collective-permute-done.6.refs_2_ = bf16[256,512]{1,0:T(8,128)(2,1)S(1)} collective-permute-done((bf16[256,512]{1,0:T(8,128)(2,1)S(1)}, bf16[256,512]{1,0:T(8,128)(2,1)S(1)}, u32[]{:S(2)}, u32[]{:S(2)}) %collective-permute-start.6) | collective-permute-done | bytes 262176 | tf_op jit(solution)/shard_map/ppermute | solution.py:463
  39.4 0.9 collective-permute-done.7.refs_3_
  40.3 1.6 %collective-permute-start.8 = (bf16[4,512,256]{2,1,0:T(8,128)(2,1)S(1)}, bf16[4,512,256]{2,1,0:T(8,128)(2,1)S(1)}, u32[]{:S(2)}, u32[]{:S(2)}) collective-permute-start(bf16[4,512,256]{2,1,0:T(8,128)(2,1)S(1)} %collective-permute-done.4.refs_5_), channel_id=1, source_target_pairs={{0,32},{16,112},{32,64},{48,16},{64,96},{80,48},{96,0},{112,80},{1... | collective-permute-start | bytes 3145736 | tf_op jit(solution)/shard_map/ppermute | solution.py:479
  41.9 2.8 %collective-permute-start.10 = (bf16[2,256,512]{2,1,0:T(8,128)(2,1)}, bf16[2,256,512]{2,1,0:T(8,128)(2,1)S(1)}, u32[]{:S(2)}, u32[]{:S(2)}) collective-permute-start(bf16[2,256,512]{2,1,0:T(8,128)(2,1)} %get-tuple-element.91), channel_id=1, source_target_pairs={{0,3},{1,0},{2,1},{3,2},{4,7},{5,4},{6,5},{7,6},{8,11},{9,8},{10,9... | collective-permute-start | bytes 1572872 | tf_op jit(solution)/shard_map/ppermute | solution.py:463
  44.7 1.9 %collective-permute-start.11 = (bf16[4,40,256]{2,1,0:T(8,128)(2,1)S(1)}, bf16[4,40,256]{2,1,0:T(8,128)(2,1)S(1)}, u32[]{:S(2)}, u32[]{:S(2)}) collective-permute-start(bf16[4,40,256]{2,1,0:T(8,128)(2,1)S(1)} %pad_maximum_fusion.1.refs_0_), channel_id=1, source_target_pairs={{0,4},{1,5},{2,6},{3,7},{4,8},{5,9},{6,10},{7,11},{8,12},{9,13},{1... | collective-permute-start | bytes 245768 | tf_op jit(solution)/shard_map/ppermute | solution.py:482
  46.6 2.1 %collective-permute-start.12 = (bf16[4,40,256]{2,1,0:T(8,128)(2,1)S(1)}, bf16[4,40,256]{2,1,0:T(8,128)(2,1)S(1)}, u32[]{:S(2)}, u32[]{:S(2)}) collective-permute-start(bf16[4,40,256]{2,1,0:T(8,128)(2,1)S(1)} %pad_maximum_fusion.1.refs_0_), channel_id=1, source_target_pairs={{0,12},{1,13},{2,14},{3,15},{4,0},{5,1},{6,2},{7,3},{8,4},{9,5},{1... | collective-permute-start | bytes 245768 | tf_op jit(solution)/shard_map/ppermute | solution.py:482
  48.7 2.4 %collective-permute-done.11.refs_1_ = bf16[4,40,256]{2,1,0:T(8,128)(2,1)S(1)} collective-permute-done((bf16[4,40,256]{2,1,0:T(8,128)(2,1)S(1)}, bf16[4,40,256]{2,1,0:T(8,128)(2,1)S(1)}, u32[]{:S(2)}, u32[]{:S(2)}) %collective-permute-start.11) | collective-permute-done | bytes 81952 | tf_op jit(solution)/shard_map/ppermute | solution.py:482
  51.2 1.9 %collective-permute-start.13 = (bf16[4,40,256]{2,1,0:T(8,128)(2,1)S(1)}, bf16[4,40,256]{2,1,0:T(8,128)(2,1)S(1)}, u32[]{:S(2)}, u32[]{:S(2)}) collective-permute-start(bf16[4,40,256]{2,1,0:T(8,128)(2,1)S(1)} %pad_maximum_fusion.1.refs_0_), channel_id=1, source_target_pairs={{0,8},{1,9},{2,10},{3,11},{4,12},{5,13},{6,14},{7,15},{8,0},{9,1},... | collective-permute-start | bytes 245768 | tf_op jit(solution)/shard_map/ppermute | solution.py:482
  53.0 0.1 pick_own.1
  53.2 3.9 %collective-permute-done.13.refs_3_ = bf16[4,40,256]{2,1,0:T(8,128)(2,1)S(1)} collective-permute-done((bf16[4,40,256]{2,1,0:T(8,128)(2,1)S(1)}, bf16[4,40,256]{2,1,0:T(8,128)(2,1)S(1)}, u32[]{:S(2)}, u32[]{:S(2)}) %collective-permute-start.13) | collective-permute-done | bytes 81952 | tf_op jit(solution)/shard_map/ppermute | solution.py:482
  57.1 0.0 collective-permute-done.10.refs_2_
  57.1 1.1 collective-permute-done.9.refs_1_
  58.2 0.4 collective-permute-start.14
  58.6 1.2 product_far_l.1
  59.8 4.0 %collective-permute-start.15 = (bf16[256,1024]{1,0:T(8,128)(2,1)S(1)}, bf16[256,1024]{1,0:T(8,128)(2,1)S(1)}, u32[]{:S(2)}, u32[]{:S(2)}) collective-permute-start(bf16[256,1024]{1,0:T(8,128)(2,1)S(1)} %product_far_l.1), channel_id=1, source_target_pairs={{0,8},{1,9},{2,10},{3,11},{4,12},{5,13},{6,14},{7,15},{8,0},{9,1},... | collective-permute-start | bytes 1572872 | tf_op jit(solution)/shard_map/ppermute | solution.py:493
  63.8 0.0 collective-permute-start.16
  63.8 10.7 %collective-permute-done.15.far_l = bf16[256,1024]{1,0:T(8,128)(2,1)S(1)} collective-permute-done((bf16[256,1024]{1,0:T(8,128)(2,1)S(1)}, bf16[256,1024]{1,0:T(8,128)(2,1)S(1)}, u32[]{:S(2)}, u32[]{:S(2)}) %collective-permute-start.15) | collective-permute-done | bytes 524320 | tf_op jit(solution)/shard_map/ppermute | solution.py:493
  74.5 3.0 %collective-permute-done.16.refs_3_ = bf16[2,256,512]{2,1,0:T(8,128)(2,1)S(1)} collective-permute-done((bf16[2,256,512]{2,1,0:T(8,128)(2,1)S(1)}, bf16[2,256,512]{2,1,0:T(8,128)(2,1)S(1)}, u32[]{:S(2)}, u32[]{:S(2)}) %collective-permute-start.16) | collective-permute-done | bytes 524320 | tf_op jit(solution)/shard_map/ppermute | solution.py:490
  77.5 0.0 collective-permute-done.14.refs_10_.refs_6_
  77.5 0.5 collective-permute-start.20
  78.0 0.1 collective-permute-start.21
  78.1 3.2 %collective-permute-start.18 = (bf16[256,512]{1,0:T(8,128)(2,1)S(1)}, bf16[256,512]{1,0:T(8,128)(2,1)S(1)}, u32[]{:S(2)}, u32[]{:S(2)}) collective-permute-start(bf16[256,512]{1,0:T(8,128)(2,1)S(1)} %get-tuple-element.110), channel_id=1, source_target_pairs={{0,3},{1,0},{2,1},{3,2},{4,7},{5,4},{6,5},{7,6},{8,11},{9,8},{10,9... | collective-permute-start | bytes 786440 | tf_op jit(solution)/shard_map/ppermute | solution.py:463
  81.3 0.0 collective-permute-start.19
  81.3 2.3 %product_near_l.1 = (bf16[256,1024]{1,0:T(8,128)(2,1)S(1)}, bf16[256,1024]{1,0:T(8,128)(2,1)S(1)}) custom-call(bf16[2,256,512]{2,1,0:T(8,128)(2,1)S(1)} %get-tuple-element.113.refs_0_, bf16[2,256,512]{2,1,0:T(8,128)(2,1)S(1)} %collective-permute-done.9.refs_1_, bf16[2,256,512]{2,1,0:T(8,128)(2,1)S(1)} %collective-permute-done.10.refs_2_, ...), custom_call_target="tpu_custom_call" | custom-call | flops 1000 | bytes 1000 | tf_op jit(solution)/shard_map/product_near_l/pallas_call | solution.py:196
  83.7 0.0 slice-start.1
  83.7 2.3 %product_near_r.1 = (bf16[256,1024]{1,0:T(8,128)(2,1)S(1)}, bf16[256,1024]{1,0:T(8,128)(2,1)S(1)}) custom-call(bf16[2,256,512]{2,1,0:T(8,128)(2,1)S(1)} %get-tuple-element.113.refs_0_, bf16[2,256,512]{2,1,0:T(8,128)(2,1)S(1)} %collective-permute-done.9.refs_1_, bf16[2,256,512]{2,1,0:T(8,128)(2,1)S(1)} %collective-permute-done.10.refs_2_, ...), custom_call_target="tpu_custom_call" | custom-call | flops 1000 | bytes 1000 | tf_op jit(solution)/shard_map/product_near_r/pallas_call | solution.py:196
  86.0 1.2 product_far_r.1
  87.3 1.1 collective-permute-start.24
  88.4 2.2 %collective-permute-start.26 = (bf16[256,1024]{1,0:T(8,128)(2,1)S(1)}, bf16[256,1024]{1,0:T(8,128)(2,1)S(1)}, u32[]{:S(2)}, u32[]{:S(2)}) collective-permute-start(bf16[256,1024]{1,0:T(8,128)(2,1)S(1)} %get-tuple-element.132), channel_id=1, source_target_pairs={{0,12},{1,13},{2,14},{3,15},{4,0},{5,1},{6,2},{7,3},{8,4},{9,5},{1... | collective-permute-start | bytes 1572872 | tf_op jit(solution)/shard_map/ppermute | solution.py:513
  90.6 3.0 %collective-permute-done.17.refs_1_ = bf16[256,512]{1,0:T(8,128)(2,1)S(1)} collective-permute-done((bf16[256,512]{1,0:T(8,128)(2,1)S(1)}, bf16[256,512]{1,0:T(8,128)(2,1)S(1)}, u32[]{:S(2)}, u32[]{:S(2)}) %collective-permute-start.17) | collective-permute-done | bytes 262176 | tf_op jit(solution)/shard_map/ppermute | solution.py:463
  93.6 0.6 collective-permute-start.27
  94.2 1.0 collective-permute-start.23
  95.2 2.2 %collective-permute-start.25 = (bf16[256,1024]{1,0:T(8,128)(2,1)S(1)}, bf16[256,1024]{1,0:T(8,128)(2,1)S(1)}, u32[]{:S(2)}, u32[]{:S(2)}) collective-permute-start(bf16[256,1024]{1,0:T(8,128)(2,1)S(1)} %get-tuple-element.131), channel_id=1, source_target_pairs={{0,12},{1,13},{2,14},{3,15},{4,0},{5,1},{6,2},{7,3},{8,4},{9,5},{1... | collective-permute-start | bytes 1572872 | tf_op jit(solution)/shard_map/ppermute | solution.py:512
  98.1 0.8 unpack.1
  98.9 4.3 %pool_attention.1.pool = f32[16,72,128]{2,1,0:T(8,128)S(1)} custom-call(s32[16]{0:T(128)S(1)} %get-tuple-element.140.slots, s32[16]{0:T(128)S(1)} %get-tuple-element.141.alive, bf16[16,64,128]{2,1,0:T(8,128)(2,1)S(1)} %get-tuple-element.142.query, bf16[16,128,2048]{2,1,0:T(8,128)(2,1)S(1)} %bitcast.23, bf16[16,128,2048]{2,1,0:T(8,128)(2,1)S(1)} %bitcast.24, ...), custom_call_target="tpu_custom_call" | custom-call | flops 1000 | bytes 1000 | tf_op jit(solution)/shard_map/pool_attention/pallas_call | solution.py:245
  103.2 2.3 %product_own.1 = (f32[256,1024]{1,0:T(8,128)S(1)}, f32[256,1024]{1,0:T(8,128)S(1)}) custom-call(bf16[256,512]{1,0:T(8,128)(2,1)S(1)} %get-tuple-element.96.refs_0_, bf16[256,512]{1,0:T(8,128)(2,1)S(1)} %collective-permute-done.17.refs_1_, bf16[256,512]{1,0:T(8,128)(2,1)S(1)} %collective-permute-done.18.refs_2_, ...), custom_call_target="tpu_custom_call" | custom-call | flops 1000 | bytes 1000 | tf_op jit(solution)/shard_map/product_own/pallas_call | solution.py:196
  105.6 9.1 %collective-permute-done.24.up_r = bf16[256,1024]{1,0:T(8,128)(2,1)S(1)} collective-permute-done((bf16[256,1024]{1,0:T(8,128)(2,1)S(1)}, bf16[256,1024]{1,0:T(8,128)(2,1)S(1)}, u32[]{:S(2)}, u32[]{:S(2)}) %collective-permute-start.24) | collective-permute-done | bytes 524320 | tf_op jit(solution)/shard_map/ppermute | solution.py:511
  114.6 10.1 %collective-permute-done.23.up_l = bf16[256,1024]{1,0:T(8,128)(2,1)S(1)} collective-permute-done((bf16[256,1024]{1,0:T(8,128)(2,1)S(1)}, bf16[256,1024]{1,0:T(8,128)(2,1)S(1)}, u32[]{:S(2)}, u32[]{:S(2)}) %collective-permute-start.23) | collective-permute-done | bytes 524320 | tf_op jit(solution)/shard_map/ppermute | solution.py:510
  124.8 3.8 %prefix_attention.1 = (bf16[1,256,2048]{2,1,0:T(8,128)(2,1)}, f32[16,72,128]{2,1,0:T(8,128)}) custom-call(s32[1]{0:T(128)S(6)} %copy.12.prompt_pages, f32[256,1024]{1,0:T(8,128)S(1)} %get-tuple-element.120.own_l, f32[256,1024]{1,0:T(8,128)S(1)} %get-tuple-element.121.own_r, bf16[256,1024]{1,0:T(8,128)(2,1)S(1)} %collective-permute-done.23.up_l, ...), custom_call_target="tpu_custom_call" | custom-call | flops 300000000 | bytes 6291456 | tf_op jit(solution)/shard_map/prefix_attention/pallas_call | solution.py:401
  128.5 7.0 %all-to-all-start = ((f32[16,72,128]{2,1,0:T(8,128)}), f32[16,72,128]{2,1,0:T(8,128)S(1)}, u32[]{:S(2)}, u32[]{:S(2)}) async-start(f32[16,72,128]{2,1,0:T(8,128)} %get-tuple-element.144), calls=%async_computation | async-start | bytes 1179648 | tf_op jit(solution)/shard_map/all_to_all | solution.py:524
  135.6 0.0 copy-start.1
  135.6 3.4 %copy-done.1 = bf16[1,1,16,128,2048]{4,3,2,1,0:T(8,128)(2,1)S(1)} copy-done((bf16[1,1,16,128,2048]{4,3,2,1,0:T(8,128)(2,1)S(1)}, bf16[1,1,16,128,2048]{4,3,2,1,0:T(8,128)(2,1)}, u32[]{:S(2)}) %copy-start.1) | copy-done | bytes 8388632
  139.0 0.2 local_attention.1.local
  139.2 7.2 %all-to-all-done.arrived = f32[16,72,128]{2,1,0:T(8,128)S(1)} async-done(((f32[16,72,128]{2,1,0:T(8,128)}), f32[16,72,128]{2,1,0:T(8,128)S(1)}, u32[]{:S(2)}, u32[]{:S(2)}) %all-to-all-start) | async-done | bytes 589856 | tf_op jit(solution)/shard_map/all_to_all | solution.py:524
  146.4 0.2 combine.1
  146.7 0.6 reshape.15
  (29 shorter events, 0.1 us)
Async XLA Ops:
  0.6 52.4 %copy-start = (bf16[1,4096,512]{2,1,0:T(8,128)(2,1)S(1)}, bf16[1,4096,512]{2,1,0:T(8,128)(2,1)}, u32[]{:S(2)}) copy-start(bf16[1,4096,512]{2,1,0:T(8,128)(2,1)} %param.10) | copy-start | bytes 12582916
  4.6 9.9 %collective-permute-start = (bf16[552,256]{1,0:T(8,128)(2,1)}, bf16[552,256]{1,0:T(8,128)(2,1)S(1)}, u32[]{:S(2)}, u32[]{:S(2)}) collective-permute-start(bf16[552,256]{1,0:T(8,128)(2,1)} %get-tuple-element.78), channel_id=1, source_target_pairs={{0,1},{1,2},{2,3},{3,0},{4,5},{5,6},{6,7},{7,4},{8,9},{9,10},{10,1... | collective-permute-start | bytes 847880 | tf_op jit(solution)/shard_map/ppermute | solution.py:456
  6.3 9.9 %collective-permute-start.1 = (bf16[552,256]{1,0:T(8,128)(2,1)}, bf16[552,256]{1,0:T(8,128)(2,1)S(1)}, u32[]{:S(2)}, u32[]{:S(2)}) collective-permute-start(bf16[552,256]{1,0:T(8,128)(2,1)} %get-tuple-element.78), channel_id=1, source_target_pairs={{0,3},{1,0},{2,1},{3,2},{4,7},{5,4},{6,5},{7,6},{8,11},{9,8},{10,9... | collective-permute-start | bytes 847880 | tf_op jit(solution)/shard_map/ppermute | solution.py:456
  7.9 13.8 %collective-permute-start.2 = (bf16[552,256]{1,0:T(8,128)(2,1)}, bf16[552,256]{1,0:T(8,128)(2,1)S(1)}, u32[]{:S(2)}, u32[]{:S(2)}) collective-permute-start(bf16[552,256]{1,0:T(8,128)(2,1)} %get-tuple-element.78), channel_id=1, source_target_pairs={{0,2},{1,3},{2,0},{3,1},{4,6},{5,7},{6,4},{7,5},{8,10},{9,11},{10,... | collective-permute-start | bytes 847880 | tf_op jit(solution)/shard_map/ppermute | solution.py:456
  12.9 50.9 %copy-start.4 = (bf16[2,256,512]{2,1,0:T(8,128)(2,1)S(1)}, bf16[2,256,512]{2,1,0:T(8,128)(2,1)}, u32[]{:S(2)}) copy-start(bf16[2,256,512]{2,1,0:T(8,128)(2,1)} %get-tuple-element.105) | copy-start | bytes 1572868
  22.9 17.4 %collective-permute-start.3 = (bf16[4,512,256]{2,1,0:T(8,128)(2,1)S(1)}, bf16[4,512,256]{2,1,0:T(8,128)(2,1)S(1)}, u32[]{:S(2)}, u32[]{:S(2)}) collective-permute-start(bf16[4,512,256]{2,1,0:T(8,128)(2,1)S(1)} %pad_maximum_fusion.refs_4_), channel_id=1, source_target_pairs={{0,32},{16,112},{32,64},{48,16},{64,96},{80,48},{96,0},{112,80},{1... | collective-permute-start | bytes 3145736 | tf_op jit(solution)/shard_map/ppermute | solution.py:471
  24.5 15.8 %collective-permute-start.4 = (bf16[4,512,256]{2,1,0:T(8,128)(2,1)S(1)}, bf16[4,512,256]{2,1,0:T(8,128)(2,1)S(1)}, u32[]{:S(2)}, u32[]{:S(2)}) collective-permute-start(bf16[4,512,256]{2,1,0:T(8,128)(2,1)S(1)} %pad_maximum_fusion.refs_4_), channel_id=1, source_target_pairs={{0,16},{16,0},{32,48},{48,32},{64,80},{80,64},{96,112},{112,96},{1... | collective-permute-start | bytes 3145736 | tf_op jit(solution)/shard_map/ppermute | solution.py:472
  24.7 10.0 %collective-permute-start.5 = (bf16[256,512]{1,0:T(8,128)(2,1)S(1)}, bf16[256,512]{1,0:T(8,128)(2,1)S(1)}, u32[]{:S(2)}, u32[]{:S(2)}) collective-permute-start(bf16[256,512]{1,0:T(8,128)(2,1)S(1)} %get-tuple-element.84), channel_id=1, source_target_pairs={{0,1},{1,2},{2,3},{3,0},{4,5},{5,6},{6,7},{7,4},{8,9},{9,10},{10,1... | collective-permute-start | bytes 786440 | tf_op jit(solution)/shard_map/ppermute | solution.py:463
  25.7 13.7 %collective-permute-start.6 = (bf16[256,512]{1,0:T(8,128)(2,1)S(1)}, bf16[256,512]{1,0:T(8,128)(2,1)S(1)}, u32[]{:S(2)}, u32[]{:S(2)}) collective-permute-start(bf16[256,512]{1,0:T(8,128)(2,1)S(1)} %get-tuple-element.85), channel_id=1, source_target_pairs={{0,3},{1,0},{2,1},{3,2},{4,7},{5,4},{6,5},{7,6},{8,11},{9,8},{10,9... | collective-permute-start | bytes 786440 | tf_op jit(solution)/shard_map/ppermute | solution.py:463
  27.9 12.4 %collective-permute-start.7 = (bf16[256,512]{1,0:T(8,128)(2,1)S(1)}, bf16[256,512]{1,0:T(8,128)(2,1)S(1)}, u32[]{:S(2)}, u32[]{:S(2)}) collective-permute-start(bf16[256,512]{1,0:T(8,128)(2,1)S(1)} %get-tuple-element.86), channel_id=1, source_target_pairs={{0,2},{1,3},{2,0},{3,1},{4,6},{5,7},{6,4},{7,5},{8,10},{9,11},{10,... | collective-permute-start | bytes 786440 | tf_op jit(solution)/shard_map/ppermute | solution.py:463
  40.3 17.9 %collective-permute-start.8 = (bf16[4,512,256]{2,1,0:T(8,128)(2,1)S(1)}, bf16[4,512,256]{2,1,0:T(8,128)(2,1)S(1)}, u32[]{:S(2)}, u32[]{:S(2)}) collective-permute-start(bf16[4,512,256]{2,1,0:T(8,128)(2,1)S(1)} %collective-permute-done.4.refs_5_), channel_id=1, source_target_pairs={{0,32},{16,112},{32,64},{48,16},{64,96},{80,48},{96,0},{112,80},{1... | collective-permute-start | bytes 3145736 | tf_op jit(solution)/shard_map/ppermute | solution.py:479
  41.9 15.2 %collective-permute-start.10 = (bf16[2,256,512]{2,1,0:T(8,128)(2,1)}, bf16[2,256,512]{2,1,0:T(8,128)(2,1)S(1)}, u32[]{:S(2)}, u32[]{:S(2)}) collective-permute-start(bf16[2,256,512]{2,1,0:T(8,128)(2,1)} %get-tuple-element.91), channel_id=1, source_target_pairs={{0,3},{1,0},{2,1},{3,2},{4,7},{5,4},{6,5},{7,6},{8,11},{9,8},{10,9... | collective-permute-start | bytes 1572872 | tf_op jit(solution)/shard_map/ppermute | solution.py:463
  44.7 13.5 %collective-permute-start.9 = (bf16[2,256,512]{2,1,0:T(8,128)(2,1)}, bf16[2,256,512]{2,1,0:T(8,128)(2,1)S(1)}, u32[]{:S(2)}, u32[]{:S(2)}) collective-permute-start(bf16[2,256,512]{2,1,0:T(8,128)(2,1)} %get-tuple-element.90), channel_id=1, source_target_pairs={{0,1},{1,2},{2,3},{3,0},{4,5},{5,6},{6,7},{7,4},{8,9},{9,10},{10,1... | collective-permute-start | bytes 1572872 | tf_op jit(solution)/shard_map/ppermute | solution.py:463
  44.7 6.5 %collective-permute-start.11 = (bf16[4,40,256]{2,1,0:T(8,128)(2,1)S(1)}, bf16[4,40,256]{2,1,0:T(8,128)(2,1)S(1)}, u32[]{:S(2)}, u32[]{:S(2)}) collective-permute-start(bf16[4,40,256]{2,1,0:T(8,128)(2,1)S(1)} %pad_maximum_fusion.1.refs_0_), channel_id=1, source_target_pairs={{0,4},{1,5},{2,6},{3,7},{4,8},{5,9},{6,10},{7,11},{8,12},{9,13},{1... | collective-permute-start | bytes 245768 | tf_op jit(solution)/shard_map/ppermute | solution.py:482
  46.6 6.5 %collective-permute-start.12 = (bf16[4,40,256]{2,1,0:T(8,128)(2,1)S(1)}, bf16[4,40,256]{2,1,0:T(8,128)(2,1)S(1)}, u32[]{:S(2)}, u32[]{:S(2)}) collective-permute-start(bf16[4,40,256]{2,1,0:T(8,128)(2,1)S(1)} %pad_maximum_fusion.1.refs_0_), channel_id=1, source_target_pairs={{0,12},{1,13},{2,14},{3,15},{4,0},{5,1},{6,2},{7,3},{8,4},{9,5},{1... | collective-permute-start | bytes 245768 | tf_op jit(solution)/shard_map/ppermute | solution.py:482
  51.2 5.9 %collective-permute-start.13 = (bf16[4,40,256]{2,1,0:T(8,128)(2,1)S(1)}, bf16[4,40,256]{2,1,0:T(8,128)(2,1)S(1)}, u32[]{:S(2)}, u32[]{:S(2)}) collective-permute-start(bf16[4,40,256]{2,1,0:T(8,128)(2,1)S(1)} %pad_maximum_fusion.1.refs_0_), channel_id=1, source_target_pairs={{0,8},{1,9},{2,10},{3,11},{4,12},{5,13},{6,14},{7,15},{8,0},{9,1},... | collective-permute-start | bytes 245768 | tf_op jit(solution)/shard_map/ppermute | solution.py:482
  58.2 19.3 %collective-permute-start.14 = (bf16[4,512,256]{2,1,0:T(8,128)(2,1)S(1)}, bf16[4,512,256]{2,1,0:T(8,128)(2,1)S(1)}, u32[]{:S(2)}, u32[]{:S(2)}) collective-permute-start(bf16[4,512,256]{2,1,0:T(8,128)(2,1)S(1)} %collective-permute-done.3.refs_6_), channel_id=1, source_target_pairs={{0,32},{16,112},{32,64},{48,16},{64,96},{80,48},{96,0},{112,80},{1... | collective-permute-start | bytes 3145736 | tf_op jit(solution)/shard_map/ppermute | solution.py:488
  59.8 14.7 %collective-permute-start.15 = (bf16[256,1024]{1,0:T(8,128)(2,1)S(1)}, bf16[256,1024]{1,0:T(8,128)(2,1)S(1)}, u32[]{:S(2)}, u32[]{:S(2)}) collective-permute-start(bf16[256,1024]{1,0:T(8,128)(2,1)S(1)} %product_far_l.1), channel_id=1, source_target_pairs={{0,8},{1,9},{2,10},{3,11},{4,12},{5,13},{6,14},{7,15},{8,0},{9,1},... | collective-permute-start | bytes 1572872 | tf_op jit(solution)/shard_map/ppermute | solution.py:493
  63.8 13.7 %collective-permute-start.16 = (bf16[2,256,512]{2,1,0:T(8,128)(2,1)S(1)}, bf16[2,256,512]{2,1,0:T(8,128)(2,1)S(1)}, u32[]{:S(2)}, u32[]{:S(2)}) collective-permute-start(bf16[2,256,512]{2,1,0:T(8,128)(2,1)S(1)} %copy-done.4), channel_id=1, source_target_pairs={{0,2},{1,3},{2,0},{3,1},{4,6},{5,7},{6,4},{7,5},{8,10},{9,11},{10,... | collective-permute-start | bytes 1572872 | tf_op jit(solution)/shard_map/ppermute | solution.py:490
  77.5 21.4 %slice-start = ((s8[8388608]{0:T(1024)(128)(4,1)}), s8[4194304]{0:T(1024)(128)(4,1)S(1)}, s32[]{:S(2)}) async-start(s8[8388608]{0:T(1024)(128)(4,1)} %bitcast.21), calls=%async_computation.1 | async-start | bytes 8388608
  77.5 3.8 %collective-permute-start.22 = (bf16[4,512,256]{2,1,0:T(8,128)(2,1)S(1)}, bf16[4,512,256]{2,1,0:T(8,128)(2,1)S(1)}, u32[]{:S(2)}, u32[]{:S(2)}) collective-permute-start(bf16[4,512,256]{2,1,0:T(8,128)(2,1)S(1)} %collective-permute-done.14.refs_10_.refs_6_), channel_id=1, source_target_pairs={{0,16},{16,0},{32,48},{48,32},{64,80},{80,64},{96,112},{112,96},{1... | collective-permute-start | bytes 3145736 | tf_op jit(solution)/shard_map/ppermute | solution.py:497
  77.5 6.2 %collective-permute-start.20 = (bf16[4,512,256]{2,1,0:T(8,128)(2,1)S(1)}, bf16[4,512,256]{2,1,0:T(8,128)(2,1)S(1)}, u32[]{:S(2)}, u32[]{:S(2)}) collective-permute-start(bf16[4,512,256]{2,1,0:T(8,128)(2,1)S(1)} %collective-permute-done.3.refs_6_), channel_id=1, source_target_pairs={{0,16},{16,0},{32,48},{48,32},{64,80},{80,64},{96,112},{112,96},{1... | collective-permute-start | bytes 3145736 | tf_op jit(solution)/shard_map/ppermute | solution.py:480
  78.0 5.7 %collective-permute-start.21 = (bf16[4,512,256]{2,1,0:T(8,128)(2,1)S(1)}, bf16[4,512,256]{2,1,0:T(8,128)(2,1)S(1)}, u32[]{:S(2)}, u32[]{:S(2)}) collective-permute-start(bf16[4,512,256]{2,1,0:T(8,128)(2,1)S(1)} %collective-permute-done.8.refs_7_), channel_id=1, source_target_pairs={{0,16},{16,0},{32,48},{48,32},{64,80},{80,64},{96,112},{112,96},{1... | collective-permute-start | bytes 3145736 | tf_op jit(solution)/shard_map/ppermute | solution.py:489
  78.1 15.5 %collective-permute-start.17 = (bf16[256,512]{1,0:T(8,128)(2,1)S(1)}, bf16[256,512]{1,0:T(8,128)(2,1)S(1)}, u32[]{:S(2)}, u32[]{:S(2)}) collective-permute-start(bf16[256,512]{1,0:T(8,128)(2,1)S(1)} %get-tuple-element.109), channel_id=1, source_target_pairs={{0,1},{1,2},{2,3},{3,0},{4,5},{5,6},{6,7},{7,4},{8,9},{9,10},{10,1... | collective-permute-start | bytes 786440 | tf_op jit(solution)/shard_map/ppermute | solution.py:463
  78.1 16.1 %collective-permute-start.18 = (bf16[256,512]{1,0:T(8,128)(2,1)S(1)}, bf16[256,512]{1,0:T(8,128)(2,1)S(1)}, u32[]{:S(2)}, u32[]{:S(2)}) collective-permute-start(bf16[256,512]{1,0:T(8,128)(2,1)S(1)} %get-tuple-element.110), channel_id=1, source_target_pairs={{0,3},{1,0},{2,1},{3,2},{4,7},{5,4},{6,5},{7,6},{8,11},{9,8},{10,9... | collective-permute-start | bytes 786440 | tf_op jit(solution)/shard_map/ppermute | solution.py:463
  81.3 13.9 %collective-permute-start.19 = (bf16[256,512]{1,0:T(8,128)(2,1)S(1)}, bf16[256,512]{1,0:T(8,128)(2,1)S(1)}, u32[]{:S(2)}, u32[]{:S(2)}) collective-permute-start(bf16[256,512]{1,0:T(8,128)(2,1)S(1)} %get-tuple-element.111), channel_id=1, source_target_pairs={{0,2},{1,3},{2,0},{3,1},{4,6},{5,7},{6,4},{7,5},{8,10},{9,11},{10,... | collective-permute-start | bytes 786440 | tf_op jit(solution)/shard_map/ppermute | solution.py:463
  83.7 15.2 %slice-start.1 = ((s8[8388608]{0:T(1024)(128)(4,1)}), s8[4194304]{0:T(1024)(128)(4,1)S(1)}, s32[]{:S(2)}) async-start(s8[8388608]{0:T(1024)(128)(4,1)} %bitcast.21), calls=%async_computation.2 | async-start | bytes 8388608
  87.3 27.3 %collective-permute-start.24 = (bf16[256,1024]{1,0:T(8,128)(2,1)S(1)}, bf16[256,1024]{1,0:T(8,128)(2,1)S(1)}, u32[]{:S(2)}, u32[]{:S(2)}) collective-permute-start(bf16[256,1024]{1,0:T(8,128)(2,1)S(1)} %get-tuple-element.130), channel_id=1, source_target_pairs={{0,4},{1,5},{2,6},{3,7},{4,8},{5,9},{6,10},{7,11},{8,12},{9,13},{1... | collective-permute-start | bytes 1572872 | tf_op jit(solution)/shard_map/ppermute | solution.py:511
  88.4 26.2 %collective-permute-start.26 = (bf16[256,1024]{1,0:T(8,128)(2,1)S(1)}, bf16[256,1024]{1,0:T(8,128)(2,1)S(1)}, u32[]{:S(2)}, u32[]{:S(2)}) collective-permute-start(bf16[256,1024]{1,0:T(8,128)(2,1)S(1)} %get-tuple-element.132), channel_id=1, source_target_pairs={{0,12},{1,13},{2,14},{3,15},{4,0},{5,1},{6,2},{7,3},{8,4},{9,5},{1... | collective-permute-start | bytes 1572872 | tf_op jit(solution)/shard_map/ppermute | solution.py:513
  93.6 21.0 %collective-permute-start.27 = (bf16[256,1024]{1,0:T(8,128)(2,1)S(1)}, bf16[256,1024]{1,0:T(8,128)(2,1)S(1)}, u32[]{:S(2)}, u32[]{:S(2)}) collective-permute-start(bf16[256,1024]{1,0:T(8,128)(2,1)S(1)} %product_far_r.1), channel_id=1, source_target_pairs={{0,8},{1,9},{2,10},{3,11},{4,12},{5,13},{6,14},{7,15},{8,0},{9,1},... | collective-permute-start | bytes 1572872 | tf_op jit(solution)/shard_map/ppermute | solution.py:515
  94.2 30.6 %collective-permute-start.23 = (bf16[256,1024]{1,0:T(8,128)(2,1)S(1)}, bf16[256,1024]{1,0:T(8,128)(2,1)S(1)}, u32[]{:S(2)}, u32[]{:S(2)}) collective-permute-start(bf16[256,1024]{1,0:T(8,128)(2,1)S(1)} %get-tuple-element.122), channel_id=1, source_target_pairs={{0,4},{1,5},{2,6},{3,7},{4,8},{5,9},{6,10},{7,11},{8,12},{9,13},{1... | collective-permute-start | bytes 1572872 | tf_op jit(solution)/shard_map/ppermute | solution.py:510
  95.2 29.6 %collective-permute-start.25 = (bf16[256,1024]{1,0:T(8,128)(2,1)S(1)}, bf16[256,1024]{1,0:T(8,128)(2,1)S(1)}, u32[]{:S(2)}, u32[]{:S(2)}) collective-permute-start(bf16[256,1024]{1,0:T(8,128)(2,1)S(1)} %get-tuple-element.131), channel_id=1, source_target_pairs={{0,12},{1,13},{2,14},{3,15},{4,0},{5,1},{6,2},{7,3},{8,4},{9,5},{1... | collective-permute-start | bytes 1572872 | tf_op jit(solution)/shard_map/ppermute | solution.py:512
  103.2 32.4 %copy-start.2 = (bf16[64,128]{1,0:T(8,128)(2,1)S(1)}, bf16[64,128]{1,0:T(8,128)(2,1)}, u32[]{:S(2)}) copy-start(bf16[64,128]{1,0:T(8,128)(2,1)} %get-tuple-element.145.query) | copy-start | bytes 49156
  103.2 32.4 %copy-start.3 = (bf16[1,1,2048]{2,1,0:T(2,128)(2,1)S(1)}, bf16[1,1,2048]{2,1,0:T(2,128)(2,1)}, u32[]{:S(2)}) copy-start(bf16[1,1,2048]{2,1,0:T(2,128)(2,1)} %param.13) | copy-start | bytes 12292
  128.5 17.9 %all-to-all-start = ((f32[16,72,128]{2,1,0:T(8,128)}), f32[16,72,128]{2,1,0:T(8,128)S(1)}, u32[]{:S(2)}, u32[]{:S(2)}) async-start(f32[16,72,128]{2,1,0:T(8,128)} %get-tuple-element.144), calls=%async_computation | async-start | bytes 1179648 | tf_op jit(solution)/shard_map/all_to_all | solution.py:524
  135.6 3.4 %copy-start.1 = (bf16[1,1,16,128,2048]{4,3,2,1,0:T(8,128)(2,1)S(1)}, bf16[1,1,16,128,2048]{4,3,2,1,0:T(8,128)(2,1)}, u32[]{:S(2)}) copy-start(bf16[1,1,16,128,2048]{4,3,2,1,0:T(8,128)(2,1)} %param.14) | copy-start | bytes 25165828

commit v3 on v1

--- a/solution.py
+++ b/solution.py
@@ -21,6 +21,7 @@
 KVW = 2048
 KEYS = GROUPS * HEAD_SIZE
 PACK = QUERY_HEADS + HEADS
+SENT = QUERY_HEADS + 16
 LOW = -1e30
 SCALE = 1.0 / math.sqrt(HEAD_SIZE)
 MIB = 1 << 20
@@ -54,48 +55,51 @@
     return jnp.where(at == lane, column, running)
 
 
-SENT = SLICE + QUERY_HEADS // 2 + 8
 HALF = QUERY_HEADS // 2
-
-
-def prepare_kernel(where, length, flag, weight, query, sent, own):
-    sent[:SLICE] = weight[...]
+BLOCK = HALF + 8
+
+
+def prepare_kernel(where, length, flag, query, sent, own):
     heads = [query[0, 0:1, h * HEAD_SIZE : (h + 1) * HEAD_SIZE].astype(F32) for h in range(QUERY_HEADS)]
     low, high = jnp.concatenate(heads[:HALF]), jnp.concatenate(heads[HALF:])
     own[:HALF] = low.astype(BF16)
     own[HALF:] = high.astype(BF16)
-    sent[SLICE : SLICE + HALF, :HEAD_SIZE] = low.astype(BF16)
-    sent[SLICE : SLICE + HALF, HEAD_SIZE:] = high.astype(BF16)
+    sent[:HALF, :HEAD_SIZE] = low.astype(BF16)
+    sent[:HALF, HEAD_SIZE:] = high.astype(BF16)
     plan = jnp.zeros((8, COLUMNS), F32)
     for c in range(CMAX):
         plan = put_lane(plan, c, where[0, 0, c].astype(F32))
     plan = put_lane(plan, CMAX, length[0, 0].astype(F32))
     plan = put_lane(plan, CMAX + 1, flag[0, 0].astype(F32))
-    sent[SLICE + HALF :] = plan.astype(BF16)
-
-
-def prepare(weight, query, where, length, flag):
+    sent[HALF:] = plan.astype(BF16)
+
+
+def prepare(query, where, length, flag):
     smem, vmem = pl.BlockSpec(memory_space=pltpu.SMEM), pl.BlockSpec(memory_space=pltpu.VMEM)
     return pl.pallas_call(
         prepare_kernel,
         out_shape=[
-            jax.ShapeDtypeStruct((SENT, COLUMNS), BF16),
+            jax.ShapeDtypeStruct((BLOCK, COLUMNS), BF16),
             jax.ShapeDtypeStruct((QUERY_HEADS, HEAD_SIZE), BF16),
         ],
-        in_specs=[smem] * 3 + [vmem] * 2,
+        in_specs=[smem] * 3 + [vmem],
         out_specs=[vmem, vmem],
         compiler_params=params(16),
         cost_estimate=cost(1000, 1000),
         name="prepare",
-    )(where, length, flag, weight, query)
+    )(where, length, flag, query)
 
 
 def unpack_kernel(*refs):
     arrived, (queries, by_group, slots, alive) = refs[:4], refs[4:]
     me = lax.axis_index("sample")
+
+    def block_of(r):
+        return arrived[r // 4][r % 4].astype(F32)
+
     plans = []
     for r in range(SAMPLES):
-        block = arrived[r // 4][r % 4].astype(F32)
+        block = block_of(r)
         for half in range(2):
             lanes = slice(half * HEAD_SIZE, (half + 1) * HEAD_SIZE)
             queries[r, half * HALF : (half + 1) * HALF] = block[:HALF, lanes].astype(BF16)
@@ -103,7 +107,7 @@
     for g in range(GROUPS):
         lanes = slice(g // 4 * HEAD_SIZE, (g // 4 + 1) * HEAD_SIZE)
         rows = slice(g % 4 * HEADS, (g % 4 + 1) * HEADS)
-        parts = [arrived[r // 4][r % 4].astype(F32)[rows, lanes] for r in range(SAMPLES)]
+        parts = [block_of(r)[rows, lanes] for r in range(SAMPLES)]
         by_group[g] = jnp.concatenate(parts).astype(BF16)
     plan = jnp.concatenate(plans)
     lane = lax.broadcasted_iota(jnp.int32, plan.shape, 1)
@@ -135,16 +139,19 @@
     )(*arrived)
 
 
-def pick_kernel(steps, states, *refs):
-    outs, sems = refs[:-1], refs[-1]
+STEPS = (0, 1, 3, 2)
+
+
+def pick_kernel(states, *refs):
+    outs, sems = refs[:8], refs[8]
     me = lax.axis_index("sample")
     z, x = me // 4, lax.rem(me, 4)
     copies = []
-    for i, step in enumerate(steps):
+    for i, step in enumerate(STEPS):
         column = lax.rem(x + step, 4)
         for k, up in enumerate((2, 1, 3)):
-            copies.append((states.at[lax.rem(z + up, 4), column], outs[2 * i].at[k]))
-        copies.append((states.at[z, column], outs[2 * i + 1]))
+            copies.append((states.at[lax.rem(z + up, 4), column], outs[i].at[k]))
+        copies.append((states.at[z, column], outs[4 + i]))
     copies = [pltpu.make_async_copy(src, dst, sems.at[n]) for n, (src, dst) in enumerate(copies)]
     for copy in copies:
         copy.start()
@@ -152,18 +159,17 @@
         copy.wait()
 
 
-def pick(states, steps, space, mib, name):
-    rest = jax.ShapeDtypeStruct((3, ROWS, SLICE), BF16)
-    own = jax.ShapeDtypeStruct((ROWS, SLICE), BF16)
-    return pl.pallas_call(
-        functools.partial(pick_kernel, steps),
-        out_shape=[rest, own] * len(steps),
+def pick(states):
+    return pl.pallas_call(
+        pick_kernel,
+        out_shape=[jax.ShapeDtypeStruct((3, ROWS, SLICE), BF16)] * 4
+        + [jax.ShapeDtypeStruct((ROWS, SLICE), BF16)] * 4,
         in_specs=[pl.BlockSpec(memory_space=pl.ANY)],
-        out_specs=[pl.BlockSpec(memory_space=space)] * (2 * len(steps)),
-        scratch_shapes=[pltpu.SemaphoreType.DMA((4 * len(steps),))],
-        compiler_params=params(mib),
-        cost_estimate=cost(1000, 1000),
-        name=name,
+        out_specs=[pl.BlockSpec(memory_space=pltpu.VMEM)] * 8,
+        scratch_shapes=[pltpu.SemaphoreType.DMA((16,))],
+        compiler_params=params(50),
+        cost_estimate=cost(1000, 1000),
+        name="pick_rows",
     )(states)
 
 
@@ -175,13 +181,13 @@
             for d in range(4):
                 left = states[d][...] if block is None else states[d][block]
                 total += jnp.dot(left, pieces[j][d], preferred_element_type=F32)
-            out = outs[2 * k + j // 4]
-            out[:, (j % 4) * COLUMNS : (j % 4 + 1) * COLUMNS] = total.astype(out.dtype)
+            out = outs[k]
+            out[:, j * COLUMNS : (j + 1) * COLUMNS] = total.astype(out.dtype)
 
 
 def product(states, pieces, blocks, kind, name):
     vmem = pl.BlockSpec(memory_space=pltpu.VMEM)
-    outs = [jax.ShapeDtypeStruct((ROWS, KVW // 2), kind)] * (2 * len(blocks))
+    outs = [jax.ShapeDtypeStruct((ROWS, KVW), kind)] * len(blocks)
     return pl.pallas_call(
         functools.partial(product_kernel, blocks),
         out_shape=outs,
@@ -191,6 +197,49 @@
         cost_estimate=cost(1000, 1000),
         name=name,
     )(*states, *pieces)
+
+
+def product_far_kernel(*refs):
+    states, pieces, outs = refs[:4], refs[4:12], refs[12:]
+    for j in range(8):
+        total = jnp.zeros((ROWS, COLUMNS), F32)
+        for d in range(4):
+            total += jnp.dot(states[d][0], pieces[j][d], preferred_element_type=F32)
+        outs[j // 4][:, (j % 4) * COLUMNS : (j % 4 + 1) * COLUMNS] = total.astype(BF16)
+
+
+def product_far(states, pieces):
+    vmem = pl.BlockSpec(memory_space=pltpu.VMEM)
+    return pl.pallas_call(
+        product_far_kernel,
+        out_shape=[jax.ShapeDtypeStruct((ROWS, KVW // 2), BF16)] * 2,
+        in_specs=[vmem] * 12,
+        out_specs=[vmem] * 2,
+        compiler_params=params(20),
+        cost_estimate=cost(1000, 1000),
+        name="product_far",
+    )(*states, *pieces)
+
+
+def relay_kernel(up, down, from_down, from_up, up_out, down_out):
+    half = KVW // 2
+    up_out[:, :half] = (up[:, :half].astype(F32) + from_down[...].astype(F32)).astype(BF16)
+    up_out[:, half:] = up[:, half:]
+    down_out[:, half:] = (down[:, half:].astype(F32) + from_up[...].astype(F32)).astype(BF16)
+    down_out[:, :half] = down[:, :half]
+
+
+def relay(up, down, from_down, from_up):
+    vmem = pl.BlockSpec(memory_space=pltpu.VMEM)
+    return pl.pallas_call(
+        relay_kernel,
+        out_shape=[jax.ShapeDtypeStruct((ROWS, KVW), BF16)] * 2,
+        in_specs=[vmem] * 4,
+        out_specs=[vmem] * 2,
+        compiler_params=params(20),
+        cost_estimate=cost(1000, 1000),
+        name="relay_sums",
+    )(up, down, from_down, from_up)
 
 
 def log_rows(logs):
@@ -335,7 +384,7 @@
 
 
 def prefix_kernel(
-    prompt_pages, own_l, own_r, up_l, up_r, down_l, down_r, queries, pool, cache, packed
+    prompt_pages, own, up, down, queries, pool, cache, packed
 ):
     me, prompt = lax.axis_index("sample"), lax.axis_index("prompt")
     z, x = me // 4, lax.rem(me, 4)
@@ -348,13 +397,12 @@
         2 * other + 1 - core, 2 * other + core, 2 * far + core, 2 * far + 1 - core,
     )
     for j in range(8):
-        lanes = slice((j % 4) * COLUMNS, (j % 4 + 1) * COLUMNS)
-        own, up, down = (own_l, up_l, down_l) if j < 4 else (own_r, up_r, down_r)
+        lanes = slice(j * COLUMNS, (j + 1) * COLUMNS)
         total = own[:, lanes] + up[:, lanes].astype(F32) + down[:, lanes].astype(F32)
         target = pl.ds(pl.multiple_of(columns[j] * COLUMNS, COLUMNS), COLUMNS)
         cache[0, :, target] = total.astype(BF16)
     sources = [
-        lax.rem(z + 4 - dz, 4) * 4 + lax.rem(x + 4 - dx, 4) for dz in (0, 1, 3, 2) for dx in (0, 1, 3, 2)
+        lax.rem(z + 4 - dz, 4) * 4 + lax.rem(x + 4 - dx, 4) for dx in STEPS for dz in STEPS
     ]
     live = lax.broadcasted_iota(jnp.int32, (SAMPLES * HEADS, ROWS), 1) < prompt_pages[0] * PAGE - me * ROWS
     logs = jnp.full((SAMPLES * HEADS, HEAD_SIZE), LOW, F32)
@@ -377,10 +425,19 @@
         both = here + there
         merged = mixture * (here / (total * both)) + pool_mixture * (there / both)
         for r, source in enumerate(sources):
-            packed[source, rows] = merged[r * HEADS : (r + 1) * HEADS]
+            packed[source, rows] = merged[r * HEADS : (r + 1) * HEADS].astype(BF16)
         logs = put_lane(logs, g, high + jnp.log(both))
+    first = logs.astype(BF16).astype(F32)
+    second = (logs - first).astype(BF16).astype(F32)
+    third = logs - first - second
+    terms = jnp.zeros((SAMPLES * HEADS, HEAD_SIZE), F32)
+    for g in range(GROUPS):
+        for t, term in enumerate((first, second, third)):
+            terms = put_lane(terms, t * GROUPS + g, term[:, g : g + 1])
+    padding = jnp.zeros((SENT - QUERY_HEADS - HEADS, HEAD_SIZE), F32)
     for r, source in enumerate(sources):
-        packed[source, QUERY_HEADS:] = logs[r * HEADS : (r + 1) * HEADS]
+        rows = jnp.concatenate([terms[r * HEADS : (r + 1) * HEADS], padding])
+        packed[source, QUERY_HEADS:] = rows.astype(BF16)
 
 
 def prefix_attention(prompt_pages, parts, queries, pool):
@@ -389,9 +446,9 @@
         prefix_kernel,
         out_shape=[
             jax.ShapeDtypeStruct((1, ROWS, KVW), BF16),
-            jax.ShapeDtypeStruct((SAMPLES, PACK, HEAD_SIZE), F32),
+            jax.ShapeDtypeStruct((SAMPLES, SENT, HEAD_SIZE), BF16),
         ],
-        in_specs=[smem] + [vmem] * 8,
+        in_specs=[smem] + [vmem] * 5,
         out_specs=[vmem, vmem],
         compiler_params=params(20),
         cost_estimate=cost(300_000_000, 6 * MIB),
@@ -400,15 +457,16 @@
 
 
 def combine_kernel(arrived, local, out):
+    terms = arrived[:, QUERY_HEADS:].astype(F32)
     for g in range(GROUPS):
         rows = slice(g * HEADS, (g + 1) * HEADS)
-        logs = arrived[:, QUERY_HEADS:, g : g + 1]
+        logs = sum(terms[:, :HEADS, lane : lane + 1] for lane in (g, g + GROUPS, g + 2 * GROUPS))
         local_log = local[QUERY_HEADS:, g : g + 1]
         high = jnp.maximum(jnp.max(logs, axis=0), local_log)
         shares = jnp.exp(logs - high[None])
         local_share = jnp.exp(local_log - high)
         total = jnp.sum(shares, axis=0) + local_share
-        mixture = jnp.sum(arrived[:, rows] * shares, axis=0) + local[rows] * local_share
+        mixture = jnp.sum(arrived[:, rows].astype(F32) * shares, axis=0) + local[rows] * local_share
         out[rows] = (mixture / total).astype(BF16)
 
 
@@ -439,68 +497,62 @@
 ):
     tie = lax.optimization_barrier
 
-    sent, query = prepare(kv_weight, queries, page_where, comp_pages, preempted)
-    along_x = [sent] + [lax.ppermute(sent, "sample", to) for to in (X_RIGHT, X_LEFT, X_FAR)]
-
+    weight_far = lax.ppermute(kv_weight, "sample", X_FAR)
+    weight_right = lax.ppermute(kv_weight, "sample", X_RIGHT)
+    weight_left = lax.ppermute(kv_weight, "sample", X_LEFT)
+    block, query = prepare(queries, page_where, comp_pages, preempted)
+    blocks = [block] + [lax.ppermute(block, "sample", to) for to in (Z_UP, Z_DOWN, Z_FAR)]
     states = prompt_states.reshape(4, 4, ROWS, SLICE)
-    to_right, last_right, to_left, last_left, to_far, last_far = pick(
-        states, (1, 3, 2), pl.ANY, 56, "pick_sent"
-    )
-    to_far, *along_x = tie((to_far, *along_x))
+    picked = pick(states)
+    slices, picked = tie(((kv_weight, weight_right, weight_left, weight_far), picked))
+    others, to_right, to_left, to_far = picked[:4]
     rows_far = lax.ppermute(to_far, "sample", X_FAR)
-    to_right, to_left, query, rows_far = tie((to_right, to_left, query, rows_far))
+    to_right, to_left, rows_far, blocks = tie((to_right, to_left, rows_far, blocks))
     rows_right = lax.ppermute(to_right, "sample", X_RIGHT)
     rows_left = lax.ppermute(to_left, "sample", X_LEFT)
-    last_right, last_left, last_far, rows_right = tie((last_right, last_left, last_far, rows_right))
-    own_states = [
-        lax.ppermute(last_right, "sample", X_RIGHT),
-        lax.ppermute(last_left, "sample", X_LEFT),
-        lax.ppermute(last_far, "sample", X_FAR),
+    of_column = jnp.stack(blocks)
+    everyone = [of_column] + [
+        lax.ppermute(of_column, "sample", to) for to in (X_RIGHT, X_LEFT, X_FAR)
     ]
 
-    of_row = jnp.stack([a[SLICE:] for a in along_x])
-    everyone = [of_row] + [lax.ppermute(of_row, "sample", to) for to in (Z_UP, Z_DOWN, Z_FAR)]
-
-    here = jnp.stack([a[:SLICE] for a in along_x])
+    here = jnp.stack(slices)
+    near = lax.ppermute(here, "prompt", Y_SPLIT)
     here_other = lax.ppermute(here, "prompt", SWAP)
-    near = lax.ppermute(here, "prompt", Y_SPLIT)
     near_other = lax.ppermute(here_other, "prompt", Y_SPLIT)
-    near, *everyone = tie((near, *everyone))
     far = lax.ppermute(near, "prompt", Y_SPLIT)
     near_swapped = lax.ppermute(near, "prompt", SWAP)
     near_other_swapped = lax.ppermute(near_other, "prompt", SWAP)
-
-    queries_all, by_group, slots, alive = unpack(everyone)
-    queries_all, rows_far = tie((queries_all, rows_far))
-    pool = pool_attention(slots, alive, queries_all, pool_pages[0, 0])
-    local_alive = jnp.where(preempted[0] > 0, 0, comp_pages[0])
-    query, here_other = tie((query, here_other))
-    local = local_attention(local_alive, query, new_kv[0], local_pages[0, 0])
-
-    far, pool, local, rows_right, rows_left = tie((far, pool, local, rows_right, rows_left))
+    far, rows_right, rows_left, everyone = tie((far, rows_right, rows_left, everyone))
     far_other = lax.ppermute(far, "prompt", SWAP)
+    others = [others, rows_right, rows_left, rows_far]
     pieces = [
         here, here_other, near, near_other,
         near_swapped, near_other_swapped, far, far_other,
     ]
 
-    mine_rows, mine_last = pick(states, (0,), pltpu.VMEM, 16, "pick_own")
-    rows = [mine_rows, rows_right, rows_left, rows_far]
-    far_l, far_r = product(rows, pieces, (0,), BF16, "product_far")
-    up_l, up_r, down_l, down_r = product(rows, pieces, (1, 2), BF16, "product_near")
-    own_l, own_r = product([mine_last] + own_states, pieces, (None,), F32, "product_own")
+    far_l, far_r = product_far(others, pieces)
+    mine, to_right, to_left, to_far = picked[4:]
+    to_right, to_left, to_far, far_l, far_r = tie((to_right, to_left, to_far, far_l, far_r))
+    mine = [
+        mine,
+        lax.ppermute(to_right, "sample", X_RIGHT),
+        lax.ppermute(to_left, "sample", X_LEFT),
+        lax.ppermute(to_far, "sample", X_FAR),
+    ]
     from_down = lax.ppermute(far_l, "sample", Z_UP)
     from_up = lax.ppermute(far_r, "sample", Z_DOWN)
-    up_l = (up_l.astype(F32) + from_down.astype(F32)).astype(BF16)
-    down_r = (down_r.astype(F32) + from_up.astype(F32)).astype(BF16)
-    sums = [
-        own_l,
-        own_r,
-        lax.ppermute(up_l, "sample", Z_UP),
-        lax.ppermute(up_r, "sample", Z_UP),
-        lax.ppermute(down_l, "sample", Z_DOWN),
-        lax.ppermute(down_r, "sample", Z_DOWN),
-    ]
+    up, down = product(others, pieces, (1, 2), BF16, "product_near")
+    up, down = relay(up, down, from_down, from_up)
+    sums = [lax.ppermute(up, "sample", Z_UP), lax.ppermute(down, "sample", Z_DOWN)]
+
+    everyone, query, up = tie((everyone, query, up))
+    queries_all, by_group, slots, alive = unpack(everyone)
+    pool = pool_attention(slots, alive, queries_all, pool_pages[0, 0])
+    local_alive = jnp.where(preempted[0] > 0, 0, comp_pages[0])
+    local = local_attention(local_alive, query, new_kv[0], local_pages[0, 0])
+    mine, pool, local = tie((mine, pool, local))
+    (own,) = product(mine, pieces, (None,), F32, "product_own")
+    sums = [own, *sums]
 
     cache, packed = prefix_attention(prompt_pages, sums, by_group, pool)
     arrived = lax.all_to_all(packed, "sample", split_axis=0, concat_axis=0, tiled=True)

time: 220 us -> 149 us (0.68)
  Pallas kernels: 115 us -> 24.7 us
  waiting for transfers between devices: 41.8 us -> 72.5 us
  blocking collectives: 17.8 us -> 12.2 us
  local copies, waits for them, and re-layouts: 6.47 us -> 2.06 us
    pallas_call x3 -> x4, Pallas kernels: 97.2 us -> 6.32 us  [the longest x1 3.15 us: pick(): pl.pallas_call(pick_kernel, out_shape=[jax.ShapeDtypeStruct((3, ROWS, SLI...]
    ppermute x13 -> x14, waiting for transfers between devices: 21.5 us -> 46.4 us  [the longest x3 21.1 us: per_device(): lax.ppermute(of_column, 'sample', to)]
    ppermute x1, waiting for transfers between devices: 0.01 us -> 13.7 us  [per_device(): near = lax.ppermute(here, 'prompt', Y_SPLIT)]
    ppermute x1, waiting for transfers between devices: 8.33 us -> 0.01 us  [per_device(): rows_right = lax.ppermute(to_right, 'sample', X_RIGHT)]
    ppermute x1, waiting for transfers between devices: 0.65 us -> 7.45 us  [per_device(): from_down = lax.ppermute(far_l, 'sample', Z_UP)]
    all_to_all x1, blocking collectives: 17.8 us -> 12.2 us  [per_device(): lax.all_to_all(packed, 'sample', split_axis=0, concat_axis=0, tiled=True)]
    unnamed x22 -> x14, local copies, waits for them, and re-layouts: 5.76 us -> 1.43 us
    ppermute x1, waiting for transfers between devices: 4.16 us -> 0.01 us  [per_device(): rows_far = lax.ppermute(to_far, 'sample', X_FAR)]
  transfers between devices with their start and end apart: 25 -> 26, of which waited for: 11 -> 17; matrix products, arithmetic and copies ran while one was open for 0% -> 0% of each run, Pallas kernels for 49% -> 12%
where the time goes in v3:
time: 149 us
  waiting for transfers between devices  72.5 us (49%)
  starting transfers between devices  33.6 us (23%)
  Pallas kernels  24.7 us (17%)
  blocking collectives  12.2 us (8%)
  between operations  2.79 us (2%)
  local copies, waits for them, and re-layouts  2.06 us (1%)
    ppermute x3, waiting for transfers between devices, per_device(): lax.ppermute(of_column, 'sample', to)  21.1 us
    ppermute x1, waiting for transfers between devices, per_device(): near = lax.ppermute(here, 'prompt', Y_SPLIT)  13.7 us
    all_to_all x1, blocking collectives, per_device(): lax.all_to_all(packed, 'sample', split_axis=0, concat_axis=0, tiled=True)  12.2 us
    ppermute x1, waiting for transfers between devices, per_device(): from_down = lax.ppermute(far_l, 'sample', Z_UP)  7.45 us
    pallas_call x2, Pallas kernels, product(): pl.pallas_call(functools.partial(product_kernel, blocks), out_shape=outs,...  6.8 us
    ppermute x3, starting transfers between devices, per_device(): lax.ppermute(block, 'sample', to)  6.23 us
    ppermute x1, waiting for transfers between devices, per_device(): weight_left = lax.ppermute(kv_weight, 'sample', X_LEFT)  6.05 us
    ppermute x1, waiting for transfers between devices, per_device(): lax.ppermute(down, 'sample', Z_DOWN)  5.24 us
  transfers between devices with their start and end apart: 26, of which 17 were waited for; matrix products, arithmetic and copies ran while one was open for 0% of the time, Pallas kernels for 12%

profile of v3, /device:TPU:0, one launch (start us, length us, event | category | flops | bytes accessed | tf_op | source)
XLA Modules:
  0.0 149.0 jit_solution(9926990327333773457)
XLA Ops:
  0.6 2.9 %collective-permute-start.1 = (bf16[512,256]{1,0:T(8,128)(2,1)}, bf16[512,256]{1,0:T(8,128)(2,1)S(1)}, u32[]{:S(2)}, u32[]{:S(2)}) collective-permute-start(bf16[512,256]{1,0:T(8,128)(2,1)} %param.11), channel_id=1, source_target_pairs={{0,3},{1,0},{2,1},{3,2},{4,7},{5,4},{6,5},{7,6},{8,11},{9,8},{10,9... | collective-permute-start | bytes 786440 | tf_op jit(solution)/shard_map/ppermute | solution.py:502
  3.5 0.0 collective-permute-start
  3.5 2.3 %collective-permute-start.2 = (bf16[512,256]{1,0:T(8,128)(2,1)}, bf16[512,256]{1,0:T(8,128)(2,1)S(1)}, u32[]{:S(2)}, u32[]{:S(2)}) collective-permute-start(bf16[512,256]{1,0:T(8,128)(2,1)} %param.11), channel_id=1, source_target_pairs={{0,2},{1,3},{2,0},{3,1},{4,6},{5,7},{6,4},{7,5},{8,10},{9,11},{10,... | collective-permute-start | bytes 786440 | tf_op jit(solution)/shard_map/ppermute | solution.py:500
  5.8 3.1 %pick_rows.1 = (bf16[3,256,512]{2,1,0:T(8,128)(2,1)S(1)}, bf16[3,256,512]{2,1,0:T(8,128)(2,1)S(1)}, bf16[3,256,512]{2,1,0:T(8,128)(2,1)S(1)}, bf16[3,256,512]{2,...) custom-call(bf16[4,4,256,512]{3,2,1,0:T(8,128)(2,1)} %bitcast.24), custom_call_target="tpu_custom_call" | custom-call | flops 1000 | bytes 1000 | tf_op jit(solution)/shard_map/pick_rows/pallas_call | solution.py:163
  9.0 6.0 %collective-permute-done.1 = bf16[512,256]{1,0:T(8,128)(2,1)S(1)} collective-permute-done((bf16[512,256]{1,0:T(8,128)(2,1)}, bf16[512,256]{1,0:T(8,128)(2,1)S(1)}, u32[]{:S(2)}, u32[]{:S(2)}) %collective-permute-start.1) | collective-permute-done | bytes 262176 | tf_op jit(solution)/shard_map/ppermute | solution.py:502
  15.0 3.3 %collective-permute-done = bf16[512,256]{1,0:T(8,128)(2,1)S(1)} collective-permute-done((bf16[512,256]{1,0:T(8,128)(2,1)}, bf16[512,256]{1,0:T(8,128)(2,1)S(1)}, u32[]{:S(2)}, u32[]{:S(2)}) %collective-permute-start) | collective-permute-done | bytes 262176 | tf_op jit(solution)/shard_map/ppermute | solution.py:501
  18.3 0.0 collective-permute-done.2
  18.3 1.1 pad_maximum_fusion.refs_4_
  19.4 1.6 %collective-permute-start.3 = (bf16[4,512,256]{2,1,0:T(8,128)(2,1)S(1)}, bf16[4,512,256]{2,1,0:T(8,128)(2,1)S(1)}, u32[]{:S(2)}, u32[]{:S(2)}) collective-permute-start(bf16[4,512,256]{2,1,0:T(8,128)(2,1)S(1)} %pad_maximum_fusion.refs_4_), channel_id=1, source_target_pairs={{0,32},{16,112},{32,64},{48,16},{64,96},{80,48},{96,0},{112,80},{1... | collective-permute-start | bytes 3145736 | tf_op jit(solution)/shard_map/ppermute | solution.py:519
  21.1 0.0 collective-permute-start.14
  21.1 0.8 collective-permute-start.5
  21.8 13.7 %collective-permute-done.3.refs_6_ = bf16[4,512,256]{2,1,0:T(8,128)(2,1)S(1)} collective-permute-done((bf16[4,512,256]{2,1,0:T(8,128)(2,1)S(1)}, bf16[4,512,256]{2,1,0:T(8,128)(2,1)S(1)}, u32[]{:S(2)}, u32[]{:S(2)}) %collective-permute-start.3) | collective-permute-done | bytes 1048608 | tf_op jit(solution)/shard_map/ppermute | solution.py:519
  35.5 0.4 collective-permute-start.4
  35.9 1.6 %collective-permute-start.15 = (bf16[4,512,256]{2,1,0:T(8,128)(2,1)S(1)}, bf16[4,512,256]{2,1,0:T(8,128)(2,1)S(1)}, u32[]{:S(2)}, u32[]{:S(2)}) collective-permute-start(bf16[4,512,256]{2,1,0:T(8,128)(2,1)S(1)} %collective-permute-done.14.refs_5_), channel_id=1, source_target_pairs={{0,32},{16,112},{32,64},{48,16},{64,96},{80,48},{96,0},{112,80},{1... | collective-permute-start | bytes 3145736 | tf_op jit(solution)/shard_map/ppermute | solution.py:521
  38.8 0.0 copy-start
  38.8 0.7 copy-done
  39.5 0.7 copy-done.2
  40.2 0.6 prepare.1
  40.8 4.0 %collective-permute-start.8 = (bf16[40,256]{1,0:T(8,128)(2,1)S(1)}, bf16[40,256]{1,0:T(8,128)(2,1)S(1)}, u32[]{:S(2)}, u32[]{:S(2)}) collective-permute-start(bf16[40,256]{1,0:T(8,128)(2,1)S(1)} %get-tuple-element.89), channel_id=1, source_target_pairs={{0,8},{1,9},{2,10},{3,11},{4,12},{5,13},{6,14},{7,15},{8,0},{9,1},... | collective-permute-start | bytes 61448 | tf_op jit(solution)/shard_map/ppermute | solution.py:504
  44.7 0.7 collective-permute-start.7
  45.4 1.0 collective-permute-done.8
  46.5 1.6 %collective-permute-start.6 = (bf16[40,256]{1,0:T(8,128)(2,1)S(1)}, bf16[40,256]{1,0:T(8,128)(2,1)S(1)}, u32[]{:S(2)}, u32[]{:S(2)}) collective-permute-start(bf16[40,256]{1,0:T(8,128)(2,1)S(1)} %get-tuple-element.89), channel_id=1, source_target_pairs={{0,4},{1,5},{2,6},{3,7},{4,8},{5,9},{6,10},{7,11},{8,12},{9,13},{1... | collective-permute-start | bytes 61448 | tf_op jit(solution)/shard_map/ppermute | solution.py:504
  48.0 0.5 collective-permute-done.7
  48.5 3.4 %collective-permute-done.6 = bf16[40,256]{1,0:T(8,128)(2,1)S(1)} collective-permute-done((bf16[40,256]{1,0:T(8,128)(2,1)S(1)}, bf16[40,256]{1,0:T(8,128)(2,1)S(1)}, u32[]{:S(2)}, u32[]{:S(2)}) %collective-permute-start.6) | collective-permute-done | bytes 20512 | tf_op jit(solution)/shard_map/ppermute | solution.py:504
  51.9 0.0 collective-permute-done.5.refs_3_
  51.9 0.0 collective-permute-start.9
  51.9 3.2 %collective-permute-start.10 = (bf16[3,256,512]{2,1,0:T(8,128)(2,1)S(1)}, bf16[3,256,512]{2,1,0:T(8,128)(2,1)S(1)}, u32[]{:S(2)}, u32[]{:S(2)}) collective-permute-start(bf16[3,256,512]{2,1,0:T(8,128)(2,1)S(1)} %get-tuple-element.88), channel_id=1, source_target_pairs={{0,3},{1,0},{2,1},{3,2},{4,7},{5,4},{6,5},{7,6},{8,11},{9,8},{10,9... | collective-permute-start | bytes 2359304 | tf_op jit(solution)/shard_map/ppermute | solution.py:512
  55.2 0.1 collective-permute-start.13
  55.3 15.0 %collective-permute-done.13.refs_3_ = bf16[4,40,256]{2,1,0:T(8,128)(2,1)S(1)} collective-permute-done((bf16[4,40,256]{2,1,0:T(8,128)(2,1)S(1)}, bf16[4,40,256]{2,1,0:T(8,128)(2,1)S(1)}, u32[]{:S(2)}, u32[]{:S(2)}) %collective-permute-start.13) | collective-permute-done | bytes 81952 | tf_op jit(solution)/shard_map/ppermute | solution.py:515
  70.3 2.1 %collective-permute-start.12 = (bf16[4,40,256]{2,1,0:T(8,128)(2,1)S(1)}, bf16[4,40,256]{2,1,0:T(8,128)(2,1)S(1)}, u32[]{:S(2)}, u32[]{:S(2)}) collective-permute-start(bf16[4,40,256]{2,1,0:T(8,128)(2,1)S(1)} %pad_maximum_fusion.1.refs_0_), channel_id=1, source_target_pairs={{0,3},{1,0},{2,1},{3,2},{4,7},{5,4},{6,5},{7,6},{8,11},{9,8},{10,9... | collective-permute-start | bytes 245768 | tf_op jit(solution)/shard_map/ppermute | solution.py:515
  72.4 2.4 %collective-permute-done.12.refs_2_ = bf16[4,40,256]{2,1,0:T(8,128)(2,1)S(1)} collective-permute-done((bf16[4,40,256]{2,1,0:T(8,128)(2,1)S(1)}, bf16[4,40,256]{2,1,0:T(8,128)(2,1)S(1)}, u32[]{:S(2)}, u32[]{:S(2)}) %collective-permute-start.12) | collective-permute-done | bytes 81952 | tf_op jit(solution)/shard_map/ppermute | solution.py:515
  74.7 2.0 %collective-permute-start.11 = (bf16[4,40,256]{2,1,0:T(8,128)(2,1)S(1)}, bf16[4,40,256]{2,1,0:T(8,128)(2,1)S(1)}, u32[]{:S(2)}, u32[]{:S(2)}) collective-permute-start(bf16[4,40,256]{2,1,0:T(8,128)(2,1)S(1)} %pad_maximum_fusion.1.refs_0_), channel_id=1, source_target_pairs={{0,1},{1,2},{2,3},{3,0},{4,5},{5,6},{6,7},{7,4},{8,9},{9,10},{10,1... | collective-permute-start | bytes 245768 | tf_op jit(solution)/shard_map/ppermute | solution.py:515
  76.7 3.7 %collective-permute-done.11.refs_1_ = bf16[4,40,256]{2,1,0:T(8,128)(2,1)S(1)} collective-permute-done((bf16[4,40,256]{2,1,0:T(8,128)(2,1)S(1)}, bf16[4,40,256]{2,1,0:T(8,128)(2,1)S(1)}, u32[]{:S(2)}, u32[]{:S(2)}) %collective-permute-start.11) | collective-permute-done | bytes 81952 | tf_op jit(solution)/shard_map/ppermute | solution.py:515
  80.4 0.0 collective-permute-start.16
  80.4 0.0 collective-permute-done.9.refs_1_
  80.5 0.6 collective-permute-start.17
  81.0 0.1 collective-permute-start.18
  81.1 2.0 %collective-permute-done.16.refs_8_ = bf16[4,512,256]{2,1,0:T(8,128)(2,1)S(1)} collective-permute-done((bf16[4,512,256]{2,1,0:T(8,128)(2,1)S(1)}, bf16[4,512,256]{2,1,0:T(8,128)(2,1)S(1)}, u32[]{:S(2)}, u32[]{:S(2)}) %collective-permute-start.16) | collective-permute-done | bytes 1048608 | tf_op jit(solution)/shard_map/ppermute | solution.py:523
  83.1 1.5 %collective-permute-done.17.refs_9_ = bf16[4,512,256]{2,1,0:T(8,128)(2,1)S(1)} collective-permute-done((bf16[4,512,256]{2,1,0:T(8,128)(2,1)S(1)}, bf16[4,512,256]{2,1,0:T(8,128)(2,1)S(1)}, u32[]{:S(2)}, u32[]{:S(2)}) %collective-permute-start.17) | collective-permute-done | bytes 1048608 | tf_op jit(solution)/shard_map/ppermute | solution.py:524
  84.6 1.5 %collective-permute-done.18.refs_11_ = bf16[4,512,256]{2,1,0:T(8,128)(2,1)S(1)} collective-permute-done((bf16[4,512,256]{2,1,0:T(8,128)(2,1)S(1)}, bf16[4,512,256]{2,1,0:T(8,128)(2,1)S(1)}, u32[]{:S(2)}, u32[]{:S(2)}) %collective-permute-start.18) | collective-permute-done | bytes 1048608 | tf_op jit(solution)/shard_map/ppermute | solution.py:526
  86.1 2.3 %product_far.1 = (bf16[256,1024]{1,0:T(8,128)(2,1)S(1)}, bf16[256,1024]{1,0:T(8,128)(2,1)S(1)}) custom-call(bf16[3,256,512]{2,1,0:T(8,128)(2,1)S(1)} %get-tuple-element.78.refs_0_, bf16[3,256,512]{2,1,0:T(8,128)(2,1)S(1)} %collective-permute-done.9.refs_1_, bf16[3,256,512]{2,1,0:T(8,128)(2,1)S(1)} %collective-permute-done.10.refs_2_, ...), custom_call_target="tpu_custom_call" | custom-call | flops 1000 | bytes 1000 | tf_op jit(solution)/shard_map/product_far/pallas_call | solution.py:213
  88.4 0.0 copy-start.1
  88.4 0.0 slice-start.3
  88.4 0.1 collective-permute-start.22
  88.5 3.2 %collective-permute-start.23 = (bf16[256,1024]{1,0:T(8,128)(2,1)S(1)}, bf16[256,1024]{1,0:T(8,128)(2,1)S(1)}, u32[]{:S(2)}, u32[]{:S(2)}) collective-permute-start(bf16[256,1024]{1,0:T(8,128)(2,1)S(1)} %get-tuple-element.110), channel_id=1, source_target_pairs={{0,12},{1,13},{2,14},{3,15},{4,0},{5,1},{6,2},{7,3},{8,4},{9,5},{1... | collective-permute-start | bytes 1572872 | tf_op jit(solution)/shard_map/ppermute | solution.py:543
  91.8 4.5 %product_near.1 = (bf16[256,2048]{1,0:T(8,128)(2,1)S(1)}, bf16[256,2048]{1,0:T(8,128)(2,1)S(1)}) custom-call(bf16[3,256,512]{2,1,0:T(8,128)(2,1)S(1)} %get-tuple-element.78.refs_0_, bf16[3,256,512]{2,1,0:T(8,128)(2,1)S(1)} %collective-permute-done.9.refs_1_, bf16[3,256,512]{2,1,0:T(8,128)(2,1)S(1)} %collective-permute-done.10.refs_2_, ...), custom_call_target="tpu_custom_call" | custom-call | flops 1000 | bytes 1000 | tf_op jit(solution)/shard_map/product_near/pallas_call | solution.py:191
  96.2 7.4 %collective-permute-done.22.from_down = bf16[256,1024]{1,0:T(8,128)(2,1)S(1)} collective-permute-done((bf16[256,1024]{1,0:T(8,128)(2,1)S(1)}, bf16[256,1024]{1,0:T(8,128)(2,1)S(1)}, u32[]{:S(2)}, u32[]{:S(2)}) %collective-permute-start.22) | collective-permute-done | bytes 524320 | tf_op jit(solution)/shard_map/ppermute | solution.py:542
  103.7 0.3 relay_sums.1
  104.0 3.0 %collective-permute-start.25 = (bf16[256,2048]{1,0:T(8,128)(2,1)S(1)}, bf16[256,2048]{1,0:T(8,128)(2,1)S(1)}, u32[]{:S(2)}, u32[]{:S(2)}) collective-permute-start(bf16[256,2048]{1,0:T(8,128)(2,1)S(1)} %get-tuple-element.124), channel_id=1, source_target_pairs={{0,12},{1,13},{2,14},{3,15},{4,0},{5,1},{6,2},{7,3},{8,4},{9,5},{1... | collective-permute-start | bytes 3145736 | tf_op jit(solution)/shard_map/ppermute | solution.py:546
  107.0 0.7 collective-permute-start.19
  107.7 2.5 %collective-permute-start.20 = (bf16[256,512]{1,0:T(8,128)(2,1)S(1)}, bf16[256,512]{1,0:T(8,128)(2,1)S(1)}, u32[]{:S(2)}, u32[]{:S(2)}) collective-permute-start(bf16[256,512]{1,0:T(8,128)(2,1)S(1)} %get-tuple-element.100), channel_id=1, source_target_pairs={{0,3},{1,0},{2,1},{3,2},{4,7},{5,4},{6,5},{7,6},{8,11},{9,8},{10,9... | collective-permute-start | bytes 786440 | tf_op jit(solution)/shard_map/ppermute | solution.py:539
  110.2 0.3 collective-permute-start.21
  111.2 2.2 %local_attention.1.local = f32[72,128]{1,0:T(8,128)S(1)} custom-call(s32[1]{0:T(128)} %bitcast.10.pages_alive, bf16[64,128]{1,0:T(8,128)(2,1)S(1)} %get-tuple-element.119.query, bf16[1,2048]{1,0:T(2,128)(2,1)S(1)} %bitcast.23, bf16[16,128,2048]{2,1,0:T(8,128)(2,1)S(1)} %bitcast.21), custom_call_target="tpu_custom_call" | custom-call | flops 1000 | bytes 1000 | tf_op jit(solution)/shard_map/local_attention/pallas_call | solution.py:362
  113.4 0.8 unpack.1
  114.3 4.3 %pool_attention.1.pool = f32[16,72,128]{2,1,0:T(8,128)S(1)} custom-call(s32[16]{0:T(128)S(1)} %get-tuple-element.116.slots, s32[16]{0:T(128)S(1)} %get-tuple-element.117.alive, bf16[16,64,128]{2,1,0:T(8,128)(2,1)S(1)} %get-tuple-element.118.query, bf16[16,128,2048]{2,1,0:T(8,128)(2,1)S(1)} %bitcast.15, bf16[16,128,2048]{2,1,0:T(8,128)(2,1)S(1)} %bitcast.16, ...), custom_call_target="tpu_custom_call" | custom-call | flops 1000 | bytes 1000 | tf_op jit(solution)/shard_map/pool_attention/pallas_call | solution.py:283
  118.6 1.5 collective-permute-done.20.refs_2_
  120.0 0.9 collective-permute-done.21.refs_3_
  121.0 2.3 %product_own.1.own = f32[256,2048]{1,0:T(8,128)S(1)} custom-call(bf16[256,512]{1,0:T(8,128)(2,1)S(1)} %get-tuple-element.120.refs_0_, bf16[256,512]{1,0:T(8,128)(2,1)S(1)} %collective-permute-done.19.refs_1_, bf16[256,512]{1,0:T(8,128)(2,1)S(1)} %collective-permute-done.20.refs_2_, bf16[256,512]{1,0:T(8,128)(2,1)S(1)} %collective-permute-done.21.refs_3_, ...), custom_call_target="tpu_custom_call" | custom-call | flops 1000 | bytes 1000 | tf_op jit(solution)/shard_map/product_own/pallas_call | solution.py:191
  123.3 5.2 %collective-permute-done.25.down = bf16[256,2048]{1,0:T(8,128)(2,1)S(1)} collective-permute-done((bf16[256,2048]{1,0:T(8,128)(2,1)S(1)}, bf16[256,2048]{1,0:T(8,128)(2,1)S(1)}, u32[]{:S(2)}, u32[]{:S(2)}) %collective-permute-start.25) | collective-permute-done | bytes 1048608 | tf_op jit(solution)/shard_map/ppermute | solution.py:546
  128.6 3.4 %collective-permute-done.24.up = bf16[256,2048]{1,0:T(8,128)(2,1)S(1)} collective-permute-done((bf16[256,2048]{1,0:T(8,128)(2,1)S(1)}, bf16[256,2048]{1,0:T(8,128)(2,1)S(1)}, u32[]{:S(2)}, u32[]{:S(2)}) %collective-permute-start.24) | collective-permute-done | bytes 1048608 | tf_op jit(solution)/shard_map/ppermute | solution.py:546
  132.0 3.9 %prefix_attention.1 = (bf16[1,256,2048]{2,1,0:T(8,128)(2,1)}, bf16[16,80,128]{2,1,0:T(8,128)(2,1)S(1)}) custom-call(s32[1]{0:T(128)S(6)} %copy.12.prompt_pages, f32[256,2048]{1,0:T(8,128)S(1)} %product_own.1.own, bf16[256,2048]{1,0:T(8,128)(2,1)S(1)} %collective-permute-done.24.up, bf16[256,2048]{1,0:T(8,128)(2,1)S(1)} %collective-permute-done.25.down, ...), custom_call_target="tpu_custom_call" | custom-call | flops 300000000 | bytes 6291456 | tf_op jit(solution)/shard_map/prefix_attention/pallas_call | solution.py:445
  135.8 12.2 %all_to_all.5.arrived = bf16[16,80,128]{2,1,0:T(8,128)(2,1)S(1)} all-to-all(bf16[16,80,128]{2,1,0:T(8,128)(2,1)S(1)} %get-tuple-element.128), channel_id=1, replica_groups=mesh['prompt'=8,'sample'=16] {'sample'}, dimensions={0} | all-to-all | bytes 655360 | tf_op jit(solution)/shard_map/all_to_all | solution.py:558
  148.1 0.3 combine.1
  148.4 0.6 reshape.15
  (19 shorter events, 0.0 us)
Async XLA Ops:
  0.6 14.4 %collective-permute-start.1 = (bf16[512,256]{1,0:T(8,128)(2,1)}, bf16[512,256]{1,0:T(8,128)(2,1)S(1)}, u32[]{:S(2)}, u32[]{:S(2)}) collective-permute-start(bf16[512,256]{1,0:T(8,128)(2,1)} %param.11), channel_id=1, source_target_pairs={{0,3},{1,0},{2,1},{3,2},{4,7},{5,4},{6,5},{7,6},{8,11},{9,8},{10,9... | collective-permute-start | bytes 786440 | tf_op jit(solution)/shard_map/ppermute | solution.py:502
  3.5 14.8 %collective-permute-start = (bf16[512,256]{1,0:T(8,128)(2,1)}, bf16[512,256]{1,0:T(8,128)(2,1)S(1)}, u32[]{:S(2)}, u32[]{:S(2)}) collective-permute-start(bf16[512,256]{1,0:T(8,128)(2,1)} %param.11), channel_id=1, source_target_pairs={{0,1},{1,2},{2,3},{3,0},{4,5},{5,6},{6,7},{7,4},{8,9},{9,10},{10,1... | collective-permute-start | bytes 786440 | tf_op jit(solution)/shard_map/ppermute | solution.py:501
  3.5 14.8 %collective-permute-start.2 = (bf16[512,256]{1,0:T(8,128)(2,1)}, bf16[512,256]{1,0:T(8,128)(2,1)S(1)}, u32[]{:S(2)}, u32[]{:S(2)}) collective-permute-start(bf16[512,256]{1,0:T(8,128)(2,1)} %param.11), channel_id=1, source_target_pairs={{0,2},{1,3},{2,0},{3,1},{4,6},{5,7},{6,4},{7,5},{8,10},{9,11},{10,... | collective-permute-start | bytes 786440 | tf_op jit(solution)/shard_map/ppermute | solution.py:500
  19.4 16.1 %collective-permute-start.3 = (bf16[4,512,256]{2,1,0:T(8,128)(2,1)S(1)}, bf16[4,512,256]{2,1,0:T(8,128)(2,1)S(1)}, u32[]{:S(2)}, u32[]{:S(2)}) collective-permute-start(bf16[4,512,256]{2,1,0:T(8,128)(2,1)S(1)} %pad_maximum_fusion.refs_4_), channel_id=1, source_target_pairs={{0,32},{16,112},{32,64},{48,16},{64,96},{80,48},{96,0},{112,80},{1... | collective-permute-start | bytes 3145736 | tf_op jit(solution)/shard_map/ppermute | solution.py:519
  21.1 14.8 %collective-permute-start.14 = (bf16[4,512,256]{2,1,0:T(8,128)(2,1)S(1)}, bf16[4,512,256]{2,1,0:T(8,128)(2,1)S(1)}, u32[]{:S(2)}, u32[]{:S(2)}) collective-permute-start(bf16[4,512,256]{2,1,0:T(8,128)(2,1)S(1)} %pad_maximum_fusion.refs_4_), channel_id=1, source_target_pairs={{0,16},{16,0},{32,48},{48,32},{64,80},{80,64},{96,112},{112,96},{1... | collective-permute-start | bytes 3145736 | tf_op jit(solution)/shard_map/ppermute | solution.py:520
  21.1 30.8 %collective-permute-start.5 = (bf16[3,256,512]{2,1,0:T(8,128)(2,1)}, bf16[3,256,512]{2,1,0:T(8,128)(2,1)S(1)}, u32[]{:S(2)}, u32[]{:S(2)}) collective-permute-start(bf16[3,256,512]{2,1,0:T(8,128)(2,1)} %get-tuple-element.85), channel_id=1, source_target_pairs={{0,2},{1,3},{2,0},{3,1},{4,6},{5,7},{6,4},{7,5},{8,10},{9,11},{10,... | collective-permute-start | bytes 2359304 | tf_op jit(solution)/shard_map/ppermute | solution.py:509
  35.5 44.9 %collective-permute-start.4 = (bf16[4,512,256]{2,1,0:T(8,128)(2,1)S(1)}, bf16[4,512,256]{2,1,0:T(8,128)(2,1)S(1)}, u32[]{:S(2)}, u32[]{:S(2)}) collective-permute-start(bf16[4,512,256]{2,1,0:T(8,128)(2,1)S(1)} %collective-permute-done.3.refs_6_), channel_id=1, source_target_pairs={{0,32},{16,112},{32,64},{48,16},{64,96},{80,48},{96,0},{112,80},{1... | collective-permute-start | bytes 3145736 | tf_op jit(solution)/shard_map/ppermute | solution.py:522
  35.9 44.6 %collective-permute-start.15 = (bf16[4,512,256]{2,1,0:T(8,128)(2,1)S(1)}, bf16[4,512,256]{2,1,0:T(8,128)(2,1)S(1)}, u32[]{:S(2)}, u32[]{:S(2)}) collective-permute-start(bf16[4,512,256]{2,1,0:T(8,128)(2,1)S(1)} %collective-permute-done.14.refs_5_), channel_id=1, source_target_pairs={{0,32},{16,112},{32,64},{48,16},{64,96},{80,48},{96,0},{112,80},{1... | collective-permute-start | bytes 3145736 | tf_op jit(solution)/shard_map/ppermute | solution.py:521
  38.8 0.8 copy-start
  39.5 0.7 copy-start.2
  40.8 5.7 %collective-permute-start.8 = (bf16[40,256]{1,0:T(8,128)(2,1)S(1)}, bf16[40,256]{1,0:T(8,128)(2,1)S(1)}, u32[]{:S(2)}, u32[]{:S(2)}) collective-permute-start(bf16[40,256]{1,0:T(8,128)(2,1)S(1)} %get-tuple-element.89), channel_id=1, source_target_pairs={{0,8},{1,9},{2,10},{3,11},{4,12},{5,13},{6,14},{7,15},{8,0},{9,1},... | collective-permute-start | bytes 61448 | tf_op jit(solution)/shard_map/ppermute | solution.py:504
  44.7 3.8 %collective-permute-start.7 = (bf16[40,256]{1,0:T(8,128)(2,1)S(1)}, bf16[40,256]{1,0:T(8,128)(2,1)S(1)}, u32[]{:S(2)}, u32[]{:S(2)}) collective-permute-start(bf16[40,256]{1,0:T(8,128)(2,1)S(1)} %get-tuple-element.89), channel_id=1, source_target_pairs={{0,12},{1,13},{2,14},{3,15},{4,0},{5,1},{6,2},{7,3},{8,4},{9,5},{1... | collective-permute-start | bytes 61448 | tf_op jit(solution)/shard_map/ppermute | solution.py:504
  46.5 5.4 %collective-permute-start.6 = (bf16[40,256]{1,0:T(8,128)(2,1)S(1)}, bf16[40,256]{1,0:T(8,128)(2,1)S(1)}, u32[]{:S(2)}, u32[]{:S(2)}) collective-permute-start(bf16[40,256]{1,0:T(8,128)(2,1)S(1)} %get-tuple-element.89), channel_id=1, source_target_pairs={{0,4},{1,5},{2,6},{3,7},{4,8},{5,9},{6,10},{7,11},{8,12},{9,13},{1... | collective-permute-start | bytes 61448 | tf_op jit(solution)/shard_map/ppermute | solution.py:504
  51.9 28.5 %collective-permute-start.9 = (bf16[3,256,512]{2,1,0:T(8,128)(2,1)S(1)}, bf16[3,256,512]{2,1,0:T(8,128)(2,1)S(1)}, u32[]{:S(2)}, u32[]{:S(2)}) collective-permute-start(bf16[3,256,512]{2,1,0:T(8,128)(2,1)S(1)} %get-tuple-element.87), channel_id=1, source_target_pairs={{0,1},{1,2},{2,3},{3,0},{4,5},{5,6},{6,7},{7,4},{8,9},{9,10},{10,1... | collective-permute-start | bytes 2359304 | tf_op jit(solution)/shard_map/ppermute | solution.py:511
  51.9 28.5 %collective-permute-start.10 = (bf16[3,256,512]{2,1,0:T(8,128)(2,1)S(1)}, bf16[3,256,512]{2,1,0:T(8,128)(2,1)S(1)}, u32[]{:S(2)}, u32[]{:S(2)}) collective-permute-start(bf16[3,256,512]{2,1,0:T(8,128)(2,1)S(1)} %get-tuple-element.88), channel_id=1, source_target_pairs={{0,3},{1,0},{2,1},{3,2},{4,7},{5,4},{6,5},{7,6},{8,11},{9,8},{10,9... | collective-permute-start | bytes 2359304 | tf_op jit(solution)/shard_map/ppermute | solution.py:512
  55.2 15.1 %collective-permute-start.13 = (bf16[4,40,256]{2,1,0:T(8,128)(2,1)S(1)}, bf16[4,40,256]{2,1,0:T(8,128)(2,1)S(1)}, u32[]{:S(2)}, u32[]{:S(2)}) collective-permute-start(bf16[4,40,256]{2,1,0:T(8,128)(2,1)S(1)} %pad_maximum_fusion.1.refs_0_), channel_id=1, source_target_pairs={{0,2},{1,3},{2,0},{3,1},{4,6},{5,7},{6,4},{7,5},{8,10},{9,11},{10,... | collective-permute-start | bytes 245768 | tf_op jit(solution)/shard_map/ppermute | solution.py:515
  70.3 4.4 %collective-permute-start.12 = (bf16[4,40,256]{2,1,0:T(8,128)(2,1)S(1)}, bf16[4,40,256]{2,1,0:T(8,128)(2,1)S(1)}, u32[]{:S(2)}, u32[]{:S(2)}) collective-permute-start(bf16[4,40,256]{2,1,0:T(8,128)(2,1)S(1)} %pad_maximum_fusion.1.refs_0_), channel_id=1, source_target_pairs={{0,3},{1,0},{2,1},{3,2},{4,7},{5,4},{6,5},{7,6},{8,11},{9,8},{10,9... | collective-permute-start | bytes 245768 | tf_op jit(solution)/shard_map/ppermute | solution.py:515
  74.7 5.7 %collective-permute-start.11 = (bf16[4,40,256]{2,1,0:T(8,128)(2,1)S(1)}, bf16[4,40,256]{2,1,0:T(8,128)(2,1)S(1)}, u32[]{:S(2)}, u32[]{:S(2)}) collective-permute-start(bf16[4,40,256]{2,1,0:T(8,128)(2,1)S(1)} %pad_maximum_fusion.1.refs_0_), channel_id=1, source_target_pairs={{0,1},{1,2},{2,3},{3,0},{4,5},{5,6},{6,7},{7,4},{8,9},{9,10},{10,1... | collective-permute-start | bytes 245768 | tf_op jit(solution)/shard_map/ppermute | solution.py:515
  80.4 2.7 %collective-permute-start.16 = (bf16[4,512,256]{2,1,0:T(8,128)(2,1)S(1)}, bf16[4,512,256]{2,1,0:T(8,128)(2,1)S(1)}, u32[]{:S(2)}, u32[]{:S(2)}) collective-permute-start(bf16[4,512,256]{2,1,0:T(8,128)(2,1)S(1)} %collective-permute-done.3.refs_6_), channel_id=1, source_target_pairs={{0,16},{16,0},{32,48},{48,32},{64,80},{80,64},{96,112},{112,96},{1... | collective-permute-start | bytes 3145736 | tf_op jit(solution)/shard_map/ppermute | solution.py:523
  80.5 4.1 %collective-permute-start.17 = (bf16[4,512,256]{2,1,0:T(8,128)(2,1)S(1)}, bf16[4,512,256]{2,1,0:T(8,128)(2,1)S(1)}, u32[]{:S(2)}, u32[]{:S(2)}) collective-permute-start(bf16[4,512,256]{2,1,0:T(8,128)(2,1)S(1)} %collective-permute-done.15.refs_7_), channel_id=1, source_target_pairs={{0,16},{16,0},{32,48},{48,32},{64,80},{80,64},{96,112},{112,96},{1... | collective-permute-start | bytes 3145736 | tf_op jit(solution)/shard_map/ppermute | solution.py:524
  81.0 5.0 %collective-permute-start.18 = (bf16[4,512,256]{2,1,0:T(8,128)(2,1)S(1)}, bf16[4,512,256]{2,1,0:T(8,128)(2,1)S(1)}, u32[]{:S(2)}, u32[]{:S(2)}) collective-permute-start(bf16[4,512,256]{2,1,0:T(8,128)(2,1)S(1)} %collective-permute-done.4.refs_10_), channel_id=1, source_target_pairs={{0,16},{16,0},{32,48},{48,32},{64,80},{80,64},{96,112},{112,96},{1... | collective-permute-start | bytes 3145736 | tf_op jit(solution)/shard_map/ppermute | solution.py:526
  86.1 25.1 %slice-start.2 = ((s8[8388608]{0:T(1024)(128)(4,1)}), s8[4194304]{0:T(1024)(128)(4,1)S(1)}, s32[]{:S(2)}) async-start(s8[8388608]{0:T(1024)(128)(4,1)} %bitcast.19), calls=%async_computation.3 | async-start | bytes 8388608
  88.4 22.7 %copy-start.1 = (bf16[1,1,2048]{2,1,0:T(2,128)(2,1)S(1)}, bf16[1,1,2048]{2,1,0:T(2,128)(2,1)}, u32[]{:S(2)}) copy-start(bf16[1,1,2048]{2,1,0:T(2,128)(2,1)} %param.13) | copy-start | bytes 12292
  88.4 22.7 %slice-start.3 = ((s8[8388608]{0:T(1024)(128)(4,1)}), s8[4194304]{0:T(1024)(128)(4,1)S(1)}, s32[]{:S(2)}) async-start(s8[8388608]{0:T(1024)(128)(4,1)} %bitcast.19), calls=%async_computation.4 | async-start | bytes 8388608
  88.4 15.2 %collective-permute-start.22 = (bf16[256,1024]{1,0:T(8,128)(2,1)S(1)}, bf16[256,1024]{1,0:T(8,128)(2,1)S(1)}, u32[]{:S(2)}, u32[]{:S(2)}) collective-permute-start(bf16[256,1024]{1,0:T(8,128)(2,1)S(1)} %get-tuple-element.109), channel_id=1, source_target_pairs={{0,4},{1,5},{2,6},{3,7},{4,8},{5,9},{6,10},{7,11},{8,12},{9,13},{1... | collective-permute-start | bytes 1572872 | tf_op jit(solution)/shard_map/ppermute | solution.py:542
  88.5 15.2 %collective-permute-start.23 = (bf16[256,1024]{1,0:T(8,128)(2,1)S(1)}, bf16[256,1024]{1,0:T(8,128)(2,1)S(1)}, u32[]{:S(2)}, u32[]{:S(2)}) collective-permute-start(bf16[256,1024]{1,0:T(8,128)(2,1)S(1)} %get-tuple-element.110), channel_id=1, source_target_pairs={{0,12},{1,13},{2,14},{3,15},{4,0},{5,1},{6,2},{7,3},{8,4},{9,5},{1... | collective-permute-start | bytes 1572872 | tf_op jit(solution)/shard_map/ppermute | solution.py:543
  91.8 22.5 %slice-start = ((s8[8388608]{0:T(1024)(128)(4,1)}), s8[4194304]{0:T(1024)(128)(4,1)S(1)}, s32[]{:S(2)}) async-start(s8[8388608]{0:T(1024)(128)(4,1)} %bitcast.13), calls=%async_computation.1 | async-start | bytes 8388608
  103.7 10.6 %slice-start.1 = ((s8[8388608]{0:T(1024)(128)(4,1)}), s8[4194304]{0:T(1024)(128)(4,1)S(1)}, s32[]{:S(2)}) async-start(s8[8388608]{0:T(1024)(128)(4,1)} %bitcast.13), calls=%async_computation.2 | async-start | bytes 8388608
  104.0 24.6 %collective-permute-start.25 = (bf16[256,2048]{1,0:T(8,128)(2,1)S(1)}, bf16[256,2048]{1,0:T(8,128)(2,1)S(1)}, u32[]{:S(2)}, u32[]{:S(2)}) collective-permute-start(bf16[256,2048]{1,0:T(8,128)(2,1)S(1)} %get-tuple-element.124), channel_id=1, source_target_pairs={{0,12},{1,13},{2,14},{3,15},{4,0},{5,1},{6,2},{7,3},{8,4},{9,5},{1... | collective-permute-start | bytes 3145736 | tf_op jit(solution)/shard_map/ppermute | solution.py:546
  107.0 25.0 %collective-permute-start.24 = (bf16[256,2048]{1,0:T(8,128)(2,1)S(1)}, bf16[256,2048]{1,0:T(8,128)(2,1)S(1)}, u32[]{:S(2)}, u32[]{:S(2)}) collective-permute-start(bf16[256,2048]{1,0:T(8,128)(2,1)S(1)} %get-tuple-element.111), channel_id=1, source_target_pairs={{0,4},{1,5},{2,6},{3,7},{4,8},{5,9},{6,10},{7,11},{8,12},{9,13},{1... | collective-permute-start | bytes 3145736 | tf_op jit(solution)/shard_map/ppermute | solution.py:546
  107.0 11.6 %collective-permute-start.19 = (bf16[256,512]{1,0:T(8,128)(2,1)S(1)}, bf16[256,512]{1,0:T(8,128)(2,1)S(1)}, u32[]{:S(2)}, u32[]{:S(2)}) collective-permute-start(bf16[256,512]{1,0:T(8,128)(2,1)S(1)} %get-tuple-element.99), channel_id=1, source_target_pairs={{0,1},{1,2},{2,3},{3,0},{4,5},{5,6},{6,7},{7,4},{8,9},{9,10},{10,1... | collective-permute-start | bytes 786440 | tf_op jit(solution)/shard_map/ppermute | solution.py:538
  107.7 12.3 %collective-permute-start.20 = (bf16[256,512]{1,0:T(8,128)(2,1)S(1)}, bf16[256,512]{1,0:T(8,128)(2,1)S(1)}, u32[]{:S(2)}, u32[]{:S(2)}) collective-permute-start(bf16[256,512]{1,0:T(8,128)(2,1)S(1)} %get-tuple-element.100), channel_id=1, source_target_pairs={{0,3},{1,0},{2,1},{3,2},{4,7},{5,4},{6,5},{7,6},{8,11},{9,8},{10,9... | collective-permute-start | bytes 786440 | tf_op jit(solution)/shard_map/ppermute | solution.py:539
  110.2 10.8 %collective-permute-start.21 = (bf16[256,512]{1,0:T(8,128)(2,1)S(1)}, bf16[256,512]{1,0:T(8,128)(2,1)S(1)}, u32[]{:S(2)}, u32[]{:S(2)}) collective-permute-start(bf16[256,512]{1,0:T(8,128)(2,1)S(1)} %get-tuple-element.101), channel_id=1, source_target_pairs={{0,2},{1,3},{2,0},{3,1},{4,6},{5,7},{6,4},{7,5},{8,10},{9,11},{10,... | collective-permute-start | bytes 786440 | tf_op jit(solution)/shard_map/ppermute | solution.py:540

commit v4 on v3

--- a/solution.py
+++ b/solution.py
@@ -95,7 +95,9 @@
     me = lax.axis_index("sample")
 
     def block_of(r):
-        return arrived[r // 4][r % 4].astype(F32)
+        rows = slice(3 * ROWS + r % 4 // 2 * BLOCK, 3 * ROWS + (r % 4 // 2 + 1) * BLOCK)
+        lanes = slice(r % 2 * COLUMNS, (r % 2 + 1) * COLUMNS)
+        return arrived[r // 4][rows, lanes].astype(F32)
 
     plans = []
     for r in range(SAMPLES):
@@ -143,34 +145,38 @@
 
 
 def pick_kernel(states, *refs):
-    outs, sems = refs[:8], refs[8]
+    blocks, outs, sems = refs[:4], refs[4:12], refs[12]
     me = lax.axis_index("sample")
     z, x = me // 4, lax.rem(me, 4)
     copies = []
     for i, step in enumerate(STEPS):
         column = lax.rem(x + step, 4)
         for k, up in enumerate((2, 1, 3)):
-            copies.append((states.at[lax.rem(z + up, 4), column], outs[i].at[k]))
+            copies.append((states.at[lax.rem(z + up, 4), column], outs[i].at[pl.ds(k * ROWS, ROWS)]))
         copies.append((states.at[z, column], outs[4 + i]))
     copies = [pltpu.make_async_copy(src, dst, sems.at[n]) for n, (src, dst) in enumerate(copies)]
     for copy in copies:
         copy.start()
+    for out in outs[:4]:
+        for r, block in enumerate(blocks):
+            rows = slice(3 * ROWS + r // 2 * BLOCK, 3 * ROWS + (r // 2 + 1) * BLOCK)
+            out[rows, r % 2 * COLUMNS : (r % 2 + 1) * COLUMNS] = block[...]
     for copy in copies:
         copy.wait()
 
 
-def pick(states):
+def pick(states, blocks):
     return pl.pallas_call(
         pick_kernel,
-        out_shape=[jax.ShapeDtypeStruct((3, ROWS, SLICE), BF16)] * 4
+        out_shape=[jax.ShapeDtypeStruct((3 * ROWS + 2 * BLOCK, SLICE), BF16)] * 4
         + [jax.ShapeDtypeStruct((ROWS, SLICE), BF16)] * 4,
-        in_specs=[pl.BlockSpec(memory_space=pl.ANY)],
+        in_specs=[pl.BlockSpec(memory_space=pl.ANY)] + [pl.BlockSpec(memory_space=pltpu.VMEM)] * 4,
         out_specs=[pl.BlockSpec(memory_space=pltpu.VMEM)] * 8,
         scratch_shapes=[pltpu.SemaphoreType.DMA((16,))],
         compiler_params=params(50),
         cost_estimate=cost(1000, 1000),
         name="pick_rows",
-    )(states)
+    )(states, *blocks)
 
 
 def product_kernel(blocks, *refs):
@@ -179,15 +185,15 @@
         for k, block in enumerate(blocks):
             total = jnp.zeros((ROWS, COLUMNS), F32)
             for d in range(4):
-                left = states[d][...] if block is None else states[d][block]
+                left = states[d][...] if block is None else states[d][block * ROWS : (block + 1) * ROWS]
                 total += jnp.dot(left, pieces[j][d], preferred_element_type=F32)
-            out = outs[k]
-            out[:, j * COLUMNS : (j + 1) * COLUMNS] = total.astype(out.dtype)
+            out = outs[2 * k + j // 4]
+            out[:, (j % 4) * COLUMNS : (j % 4 + 1) * COLUMNS] = total.astype(out.dtype)
 
 
 def product(states, pieces, blocks, kind, name):
     vmem = pl.BlockSpec(memory_space=pltpu.VMEM)
-    outs = [jax.ShapeDtypeStruct((ROWS, KVW), kind)] * len(blocks)
+    outs = [jax.ShapeDtypeStruct((ROWS, KVW // 2), kind)] * (2 * len(blocks))
     return pl.pallas_call(
         functools.partial(product_kernel, blocks),
         out_shape=outs,
@@ -204,7 +210,7 @@
     for j in range(8):
         total = jnp.zeros((ROWS, COLUMNS), F32)
         for d in range(4):
-            total += jnp.dot(states[d][0], pieces[j][d], preferred_element_type=F32)
+            total += jnp.dot(states[d][:ROWS], pieces[j][d], preferred_element_type=F32)
         outs[j // 4][:, (j % 4) * COLUMNS : (j % 4 + 1) * COLUMNS] = total.astype(BF16)
 
 
@@ -222,21 +228,18 @@
 
 
 def relay_kernel(up, down, from_down, from_up, up_out, down_out):
-    half = KVW // 2
-    up_out[:, :half] = (up[:, :half].astype(F32) + from_down[...].astype(F32)).astype(BF16)
-    up_out[:, half:] = up[:, half:]
-    down_out[:, half:] = (down[:, half:].astype(F32) + from_up[...].astype(F32)).astype(BF16)
-    down_out[:, :half] = down[:, :half]
+    up_out[...] = (up[...].astype(F32) + from_down[...].astype(F32)).astype(BF16)
+    down_out[...] = (down[...].astype(F32) + from_up[...].astype(F32)).astype(BF16)
 
 
 def relay(up, down, from_down, from_up):
     vmem = pl.BlockSpec(memory_space=pltpu.VMEM)
     return pl.pallas_call(
         relay_kernel,
-        out_shape=[jax.ShapeDtypeStruct((ROWS, KVW), BF16)] * 2,
+        out_shape=[jax.ShapeDtypeStruct((ROWS, KVW // 2), BF16)] * 2,
         in_specs=[vmem] * 4,
         out_specs=[vmem] * 2,
-        compiler_params=params(20),
+        compiler_params=params(16),
         cost_estimate=cost(1000, 1000),
         name="relay_sums",
     )(up, down, from_down, from_up)
@@ -384,7 +387,7 @@
 
 
 def prefix_kernel(
-    prompt_pages, own, up, down, queries, pool, cache, packed
+    prompt_pages, own_l, own_r, up_l, up_r, down_l, down_r, queries, pool, cache, packed
 ):
     me, prompt = lax.axis_index("sample"), lax.axis_index("prompt")
     z, x = me // 4, lax.rem(me, 4)
@@ -397,7 +400,8 @@
         2 * other + 1 - core, 2 * other + core, 2 * far + core, 2 * far + 1 - core,
     )
     for j in range(8):
-        lanes = slice(j * COLUMNS, (j + 1) * COLUMNS)
+        lanes = slice((j % 4) * COLUMNS, (j % 4 + 1) * COLUMNS)
+        own, up, down = (own_l, up_l, down_l) if j < 4 else (own_r, up_r, down_r)
         total = own[:, lanes] + up[:, lanes].astype(F32) + down[:, lanes].astype(F32)
         target = pl.ds(pl.multiple_of(columns[j] * COLUMNS, COLUMNS), COLUMNS)
         cache[0, :, target] = total.astype(BF16)
@@ -448,7 +452,7 @@
             jax.ShapeDtypeStruct((1, ROWS, KVW), BF16),
             jax.ShapeDtypeStruct((SAMPLES, SENT, HEAD_SIZE), BF16),
         ],
-        in_specs=[smem] + [vmem] * 5,
+        in_specs=[smem] + [vmem] * 8,
         out_specs=[vmem, vmem],
         compiler_params=params(20),
         cost_estimate=cost(300_000_000, 6 * MIB),
@@ -503,17 +507,13 @@
     block, query = prepare(queries, page_where, comp_pages, preempted)
     blocks = [block] + [lax.ppermute(block, "sample", to) for to in (Z_UP, Z_DOWN, Z_FAR)]
     states = prompt_states.reshape(4, 4, ROWS, SLICE)
-    picked = pick(states)
+    picked = pick(states, blocks)
     slices, picked = tie(((kv_weight, weight_right, weight_left, weight_far), picked))
     others, to_right, to_left, to_far = picked[:4]
     rows_far = lax.ppermute(to_far, "sample", X_FAR)
-    to_right, to_left, rows_far, blocks = tie((to_right, to_left, rows_far, blocks))
+    to_right, to_left, rows_far = tie((to_right, to_left, rows_far))
     rows_right = lax.ppermute(to_right, "sample", X_RIGHT)
     rows_left = lax.ppermute(to_left, "sample", X_LEFT)
-    of_column = jnp.stack(blocks)
-    everyone = [of_column] + [
-        lax.ppermute(of_column, "sample", to) for to in (X_RIGHT, X_LEFT, X_FAR)
-    ]
 
     here = jnp.stack(slices)
     near = lax.ppermute(here, "prompt", Y_SPLIT)
@@ -522,7 +522,7 @@
     far = lax.ppermute(near, "prompt", Y_SPLIT)
     near_swapped = lax.ppermute(near, "prompt", SWAP)
     near_other_swapped = lax.ppermute(near_other, "prompt", SWAP)
-    far, rows_right, rows_left, everyone = tie((far, rows_right, rows_left, everyone))
+    far, rows_right, rows_left = tie((far, rows_right, rows_left))
     far_other = lax.ppermute(far, "prompt", SWAP)
     others = [others, rows_right, rows_left, rows_far]
     pieces = [
@@ -541,18 +541,25 @@
     ]
     from_down = lax.ppermute(far_l, "sample", Z_UP)
     from_up = lax.ppermute(far_r, "sample", Z_DOWN)
-    up, down = product(others, pieces, (1, 2), BF16, "product_near")
-    up, down = relay(up, down, from_down, from_up)
-    sums = [lax.ppermute(up, "sample", Z_UP), lax.ppermute(down, "sample", Z_DOWN)]
-
-    everyone, query, up = tie((everyone, query, up))
-    queries_all, by_group, slots, alive = unpack(everyone)
+    up_l, up_r, down_l, down_r = product(others, pieces, (1, 2), BF16, "product_near")
+    up_r, down_l, from_down, from_up = (
+        lax.ppermute(up_r, "sample", Z_UP), lax.ppermute(down_l, "sample", Z_DOWN), from_down, from_up,
+    )
+    up_l, down_r = relay(up_l, down_r, from_down, from_up)
+    sums = [
+        lax.ppermute(up_l, "sample", Z_UP),
+        up_r,
+        down_l,
+        lax.ppermute(down_r, "sample", Z_DOWN),
+    ]
+
+    arrived, query, up_l = tie((others, query, up_l))
+    queries_all, by_group, slots, alive = unpack(arrived)
     pool = pool_attention(slots, alive, queries_all, pool_pages[0, 0])
     local_alive = jnp.where(preempted[0] > 0, 0, comp_pages[0])
     local = local_attention(local_alive, query, new_kv[0], local_pages[0, 0])
     mine, pool, local = tie((mine, pool, local))
-    (own,) = product(mine, pieces, (None,), F32, "product_own")
-    sums = [own, *sums]
+    sums = [*product(mine, pieces, (None,), F32, "product_own"), *sums]
 
     cache, packed = prefix_attention(prompt_pages, sums, by_group, pool)
     arrived = lax.all_to_all(packed, "sample", split_axis=0, concat_axis=0, tiled=True)

time: 149 us -> 138 us (0.926)
  waiting for transfers between devices: 72.5 us -> 63.6 us
  starting transfers between devices: 33.6 us -> 30.9 us
  blocking collectives: 12.2 us -> 14.3 us
  Pallas kernels: 24.7 us -> 22.7 us
    ppermute x5 -> x4, waiting for transfers between devices: 29.7 us -> 10.2 us  [the longest x1 8.7 us: per_device(): lax.ppermute(down_r, 'sample', Z_DOWN)]
    ppermute x1, waiting for transfers between devices: 0.01 us -> 18.9 us  [per_device(): rows_right = lax.ppermute(to_right, 'sample', X_RIGHT)]
    ppermute x1, waiting for transfers between devices: 0.01 us -> 7.05 us  [per_device(): rows_far = lax.ppermute(to_far, 'sample', X_FAR)]
    ppermute x1, waiting for transfers between devices: 6.05 us -> 0.01 us  [per_device(): weight_left = lax.ppermute(kv_weight, 'sample', X_LEFT)]
    ppermute x5 -> x4, starting transfers between devices: 7.16 us -> 3.16 us  [the longest x1 1.4 us: per_device(): lax.ppermute(down_r, 'sample', Z_DOWN)]
    ppermute x1, waiting for transfers between devices: 3.31 us -> 0.01 us  [per_device(): weight_right = lax.ppermute(kv_weight, 'sample', X_RIGHT)]
    ppermute x1, waiting for transfers between devices: 7.45 us -> 4.75 us  [per_device(): from_down = lax.ppermute(far_l, 'sample', Z_UP)]
    all_to_all x1, blocking collectives: 12.2 us -> 14.3 us  [per_device(): lax.all_to_all(packed, 'sample', split_axis=0, concat_axis=0, tiled=True)]
  transfers between devices with their start and end apart: 26 -> 25, of which waited for: 17 -> 13; matrix products, arithmetic and copies ran while one was open for 0% -> 0% of each run, Pallas kernels for 12% -> 12%
where the time goes in v4:
time: 138 us; the launch traced here: 137 us
  waiting for transfers between devices  63.6 us (46%)
  starting transfers between devices  30.9 us (22%)
  Pallas kernels  22.7 us (16%)
  blocking collectives  14.3 us (10%)
  between operations  2.81 us (2%)
  local copies, waits for them, and re-layouts  2.06 us (1%)
    ppermute x1, waiting for transfers between devices, per_device(): rows_right = lax.ppermute(to_right, 'sample', X_RIGHT)  18.9 us
    all_to_all x1, blocking collectives, per_device(): lax.all_to_all(packed, 'sample', split_axis=0, concat_axis=0, tiled=True)  14.3 us
    ppermute x1, waiting for transfers between devices, per_device(): near = lax.ppermute(here, 'prompt', Y_SPLIT)  13.2 us
    ppermute x1, waiting for transfers between devices, per_device(): lax.ppermute(down_r, 'sample', Z_DOWN)  8.7 us
    ppermute x1, waiting for transfers between devices, per_device(): rows_far = lax.ppermute(to_far, 'sample', X_FAR)  7.05 us
    pallas_call x2, Pallas kernels, product(): pl.pallas_call(functools.partial(product_kernel, blocks), out_shape=outs,...  6.81 us
    ppermute x3, starting transfers between devices, per_device(): lax.ppermute(block, 'sample', to)  6.23 us
    ppermute x3, waiting for transfers between devices, per_device(): lax.ppermute(block, 'sample', to)  4.93 us
  transfers between devices with their start and end apart: 25, of which 13 were waited for; matrix products, arithmetic and copies ran while one was open for 0% of the time, Pallas kernels for 12%

profile of v4, /device:TPU:0, one launch (start us, length us, event | category | flops | bytes accessed | tf_op | source)
XLA Modules:
  0.0 137.5 jit_solution(18189891502277536211)
XLA Ops:
  0.6 2.9 %collective-permute-start.1 = (bf16[512,256]{1,0:T(8,128)(2,1)}, bf16[512,256]{1,0:T(8,128)(2,1)S(1)}, u32[]{:S(2)}, u32[]{:S(2)}) collective-permute-start(bf16[512,256]{1,0:T(8,128)(2,1)} %param.11), channel_id=1, source_target_pairs={{0,3},{1,0},{2,1},{3,2},{4,7},{5,4},{6,5},{7,6},{8,11},{9,8},{10,9... | collective-permute-start | bytes 786440 | tf_op jit(solution)/shard_map/ppermute | solution.py:506
  3.5 0.0 collective-permute-start
  3.5 2.3 %collective-permute-start.2 = (bf16[512,256]{1,0:T(8,128)(2,1)}, bf16[512,256]{1,0:T(8,128)(2,1)S(1)}, u32[]{:S(2)}, u32[]{:S(2)}) collective-permute-start(bf16[512,256]{1,0:T(8,128)(2,1)} %param.11), channel_id=1, source_target_pairs={{0,2},{1,3},{2,0},{3,1},{4,6},{5,7},{6,4},{7,5},{8,10},{9,11},{10,... | collective-permute-start | bytes 786440 | tf_op jit(solution)/shard_map/ppermute | solution.py:504
  7.1 0.7 copy-done
  7.9 0.7 copy-done.2
  8.5 0.6 prepare.1
  9.1 4.0 %collective-permute-start.5 = (bf16[40,256]{1,0:T(8,128)(2,1)S(1)}, bf16[40,256]{1,0:T(8,128)(2,1)S(1)}, u32[]{:S(2)}, u32[]{:S(2)}) collective-permute-start(bf16[40,256]{1,0:T(8,128)(2,1)S(1)} %get-tuple-element.62.refs_0_), channel_id=1, source_target_pairs={{0,8},{1,9},{2,10},{3,11},{4,12},{5,13},{6,14},{7,15},{8,0},{9,1},... | collective-permute-start | bytes 61448 | tf_op jit(solution)/shard_map/ppermute | solution.py:508
  13.1 0.7 collective-permute-start.4
  13.8 1.0 collective-permute-done.5.refs_3_
  14.9 1.6 %collective-permute-start.3 = (bf16[40,256]{1,0:T(8,128)(2,1)S(1)}, bf16[40,256]{1,0:T(8,128)(2,1)S(1)}, u32[]{:S(2)}, u32[]{:S(2)}) collective-permute-start(bf16[40,256]{1,0:T(8,128)(2,1)S(1)} %get-tuple-element.62.refs_0_), channel_id=1, source_target_pairs={{0,4},{1,5},{2,6},{3,7},{4,8},{5,9},{6,10},{7,11},{8,12},{9,13},{1... | collective-permute-start | bytes 61448 | tf_op jit(solution)/shard_map/ppermute | solution.py:508
  16.4 0.5 collective-permute-done.4.refs_2_
  16.9 3.4 %collective-permute-done.3.refs_1_ = bf16[40,256]{1,0:T(8,128)(2,1)S(1)} collective-permute-done((bf16[40,256]{1,0:T(8,128)(2,1)S(1)}, bf16[40,256]{1,0:T(8,128)(2,1)S(1)}, u32[]{:S(2)}, u32[]{:S(2)}) %collective-permute-start.3) | collective-permute-done | bytes 20512 | tf_op jit(solution)/shard_map/ppermute | solution.py:508
  20.3 3.2 %pick_rows.1 = (bf16[848,512]{1,0:T(8,128)(2,1)S(1)}, bf16[848,512]{1,0:T(8,128)(2,1)S(1)}, bf16[848,512]{1,0:T(8,128)(2,1)S(1)}, bf16[848,512]{1,0:T(8,128)(2,1...) custom-call(bf16[4,4,256,512]{3,2,1,0:T(8,128)(2,1)} %bitcast.19, ...), custom_call_target="tpu_custom_call" | custom-call | flops 1000 | bytes 1000 | tf_op jit(solution)/shard_map/pick_rows/pallas_call | solution.py:169
  23.5 0.0 collective-permute-done.1
  23.5 0.0 collective-permute-done
  23.5 0.0 collective-permute-done.2
  23.5 1.1 pad_maximum_fusion.refs_4_
  24.6 1.6 %collective-permute-start.6 = (bf16[4,512,256]{2,1,0:T(8,128)(2,1)S(1)}, bf16[4,512,256]{2,1,0:T(8,128)(2,1)S(1)}, u32[]{:S(2)}, u32[]{:S(2)}) collective-permute-start(bf16[4,512,256]{2,1,0:T(8,128)(2,1)S(1)} %pad_maximum_fusion.refs_4_), channel_id=1, source_target_pairs={{0,32},{16,112},{32,64},{48,16},{64,96},{80,48},{96,0},{112,80},{1... | collective-permute-start | bytes 3145736 | tf_op jit(solution)/shard_map/ppermute | solution.py:519
  26.3 0.0 collective-permute-start.11
  26.3 1.2 collective-permute-start.8
  27.5 13.2 %collective-permute-done.6.refs_6_ = bf16[4,512,256]{2,1,0:T(8,128)(2,1)S(1)} collective-permute-done((bf16[4,512,256]{2,1,0:T(8,128)(2,1)S(1)}, bf16[4,512,256]{2,1,0:T(8,128)(2,1)S(1)}, u32[]{:S(2)}, u32[]{:S(2)}) %collective-permute-start.6) | collective-permute-done | bytes 1048608 | tf_op jit(solution)/shard_map/ppermute | solution.py:519
  40.7 0.4 collective-permute-start.7
  41.1 0.0 collective-permute-done.11.refs_5_
  41.1 1.6 %collective-permute-start.12 = (bf16[4,512,256]{2,1,0:T(8,128)(2,1)S(1)}, bf16[4,512,256]{2,1,0:T(8,128)(2,1)S(1)}, u32[]{:S(2)}, u32[]{:S(2)}) collective-permute-start(bf16[4,512,256]{2,1,0:T(8,128)(2,1)S(1)} %collective-permute-done.11.refs_5_), channel_id=1, source_target_pairs={{0,32},{16,112},{32,64},{48,16},{64,96},{80,48},{96,0},{112,80},{1... | collective-permute-start | bytes 3145736 | tf_op jit(solution)/shard_map/ppermute | solution.py:521
  42.6 7.0 %collective-permute-done.8.refs_3_ = bf16[848,512]{1,0:T(8,128)(2,1)S(1)} collective-permute-done((bf16[848,512]{1,0:T(8,128)(2,1)}, bf16[848,512]{1,0:T(8,128)(2,1)S(1)}, u32[]{:S(2)}, u32[]{:S(2)}) %collective-permute-start.8) | collective-permute-done | bytes 868384 | tf_op jit(solution)/shard_map/ppermute | solution.py:513
  49.7 1.8 %collective-permute-start.9 = (bf16[848,512]{1,0:T(8,128)(2,1)S(1)}, bf16[848,512]{1,0:T(8,128)(2,1)S(1)}, u32[]{:S(2)}, u32[]{:S(2)}) collective-permute-start(bf16[848,512]{1,0:T(8,128)(2,1)S(1)} %get-tuple-element.83), channel_id=1, source_target_pairs={{0,1},{1,2},{2,3},{3,0},{4,5},{5,6},{6,7},{7,4},{8,9},{9,10},{10,1... | collective-permute-start | bytes 2605064 | tf_op jit(solution)/shard_map/ppermute | solution.py:515
  51.5 1.4 %collective-permute-start.10 = (bf16[848,512]{1,0:T(8,128)(2,1)S(1)}, bf16[848,512]{1,0:T(8,128)(2,1)S(1)}, u32[]{:S(2)}, u32[]{:S(2)}) collective-permute-start(bf16[848,512]{1,0:T(8,128)(2,1)S(1)} %get-tuple-element.84), channel_id=1, source_target_pairs={{0,3},{1,0},{2,1},{3,2},{4,7},{5,4},{6,5},{7,6},{8,11},{9,8},{10,9... | collective-permute-start | bytes 2605064 | tf_op jit(solution)/shard_map/ppermute | solution.py:516
  52.9 0.0 collective-permute-start.13
  52.9 18.9 %collective-permute-done.9.refs_1_ = bf16[848,512]{1,0:T(8,128)(2,1)S(1)} collective-permute-done((bf16[848,512]{1,0:T(8,128)(2,1)S(1)}, bf16[848,512]{1,0:T(8,128)(2,1)S(1)}, u32[]{:S(2)}, u32[]{:S(2)}) %collective-permute-start.9) | collective-permute-done | bytes 868384 | tf_op jit(solution)/shard_map/ppermute | solution.py:515
  71.8 0.3 collective-permute-done.10.refs_2_
  72.1 0.0 collective-permute-done.7.refs_10_
  72.1 0.5 collective-permute-start.15
  72.7 2.1 %collective-permute-done.14.refs_9_ = bf16[4,512,256]{2,1,0:T(8,128)(2,1)S(1)} collective-permute-done((bf16[4,512,256]{2,1,0:T(8,128)(2,1)S(1)}, bf16[4,512,256]{2,1,0:T(8,128)(2,1)S(1)}, u32[]{:S(2)}, u32[]{:S(2)}) %collective-permute-start.14) | collective-permute-done | bytes 1048608 | tf_op jit(solution)/shard_map/ppermute | solution.py:524
  74.8 1.5 %collective-permute-done.15.refs_11_ = bf16[4,512,256]{2,1,0:T(8,128)(2,1)S(1)} collective-permute-done((bf16[4,512,256]{2,1,0:T(8,128)(2,1)S(1)}, bf16[4,512,256]{2,1,0:T(8,128)(2,1)S(1)}, u32[]{:S(2)}, u32[]{:S(2)}) %collective-permute-start.15) | collective-permute-done | bytes 1048608 | tf_op jit(solution)/shard_map/ppermute | solution.py:526
  76.3 2.3 %product_far.1 = (bf16[256,1024]{1,0:T(8,128)(2,1)S(1)}, bf16[256,1024]{1,0:T(8,128)(2,1)S(1)}) custom-call(bf16[848,512]{1,0:T(8,128)(2,1)S(1)} %get-tuple-element.100.refs_0_, bf16[848,512]{1,0:T(8,128)(2,1)S(1)} %collective-permute-done.9.refs_1_, bf16[848,512]{1,0:T(8,128)(2,1)S(1)} %collective-permute-done.10.refs_2_, ...), custom_call_target="tpu_custom_call" | custom-call | flops 1000 | bytes 1000 | tf_op jit(solution)/shard_map/product_far/pallas_call | solution.py:219
  78.6 0.0 slice-start.2
  78.7 0.0 slice-start.3
  78.7 0.0 copy-start.1
  78.7 0.1 collective-permute-start.19
  78.8 3.2 %collective-permute-start.20 = (bf16[256,1024]{1,0:T(8,128)(2,1)S(1)}, bf16[256,1024]{1,0:T(8,128)(2,1)S(1)}, u32[]{:S(2)}, u32[]{:S(2)}) collective-permute-start(bf16[256,1024]{1,0:T(8,128)(2,1)S(1)} %get-tuple-element.98), channel_id=1, source_target_pairs={{0,12},{1,13},{2,14},{3,15},{4,0},{5,1},{6,2},{7,3},{8,4},{9,5},{1... | collective-permute-start | bytes 1572872 | tf_op jit(solution)/shard_map/ppermute | solution.py:543
  82.0 0.4 collective-permute-start.16
  82.3 2.9 %collective-permute-start.17 = (bf16[256,512]{1,0:T(8,128)(2,1)S(1)}, bf16[256,512]{1,0:T(8,128)(2,1)S(1)}, u32[]{:S(2)}, u32[]{:S(2)}) collective-permute-start(bf16[256,512]{1,0:T(8,128)(2,1)S(1)} %get-tuple-element.92), channel_id=1, source_target_pairs={{0,3},{1,0},{2,1},{3,2},{4,7},{5,4},{6,5},{7,6},{8,11},{9,8},{10,9... | collective-permute-start | bytes 786440 | tf_op jit(solution)/shard_map/ppermute | solution.py:539
  85.2 4.5 %product_near.1 = (bf16[256,1024]{1,0:T(8,128)(2,1)S(1)}, bf16[256,1024]{1,0:T(8,128)(2,1)S(1)}, bf16[256,1024]{1,0:T(8,128)(2,1)S(1)}, bf16[256,1024]{1,0:T(8,128)(2,1)S(1)}) custom-call(bf16[848,512]{1,0:T(8,128)(2,1)S(1)} %get-tuple-element.100.refs_0_, bf16[848,512]{1,0:T(8,128)(2,1)S(1)} %collective-permute-done.9.refs_1_, ...), custom_call_target="tpu_custom_call" | custom-call | flops 1000 | bytes 1000 | tf_op jit(solution)/shard_map/product_near/pallas_call | solution.py:197
  89.7 0.3 collective-permute-start.22
  90.0 4.8 %collective-permute-done.19.from_down = bf16[256,1024]{1,0:T(8,128)(2,1)S(1)} collective-permute-done((bf16[256,1024]{1,0:T(8,128)(2,1)S(1)}, bf16[256,1024]{1,0:T(8,128)(2,1)S(1)}, u32[]{:S(2)}, u32[]{:S(2)}) %collective-permute-start.19) | collective-permute-done | bytes 524320 | tf_op jit(solution)/shard_map/ppermute | solution.py:542
  94.7 0.8 collective-permute-start.23
  95.5 0.0 collective-permute-done.20.from_up
  95.5 0.2 relay_sums.1
  95.8 1.4 %collective-permute-start.24 = (bf16[256,1024]{1,0:T(8,128)(2,1)S(1)}, bf16[256,1024]{1,0:T(8,128)(2,1)S(1)}, u32[]{:S(2)}, u32[]{:S(2)}) collective-permute-start(bf16[256,1024]{1,0:T(8,128)(2,1)S(1)} %get-tuple-element.116), channel_id=1, source_target_pairs={{0,12},{1,13},{2,14},{3,15},{4,0},{5,1},{6,2},{7,3},{8,4},{9,5},{1... | collective-permute-start | bytes 1572872 | tf_op jit(solution)/shard_map/ppermute | solution.py:553
  97.2 0.0 collective-permute-done.16.refs_1_
  97.2 0.7 collective-permute-start.21
  97.9 1.1 collective-permute-start.18
  99.7 0.8 unpack.1
  100.5 0.3 local_attention.1.local
  100.9 4.3 %pool_attention.1.pool = f32[16,72,128]{2,1,0:T(8,128)S(1)} custom-call(s32[16]{0:T(128)S(1)} %get-tuple-element.104.slots, s32[16]{0:T(128)S(1)} %get-tuple-element.105.alive, bf16[16,64,128]{2,1,0:T(8,128)(2,1)S(1)} %get-tuple-element.106.query, bf16[16,128,2048]{2,1,0:T(8,128)(2,1)S(1)} %bitcast.11, bf16[16,128,2048]{2,1,0:T(8,128)(2,1)S(1)} %bitcast.12, ...), custom_call_target="tpu_custom_call" | custom-call | flops 1000 | bytes 1000 | tf_op jit(solution)/shard_map/pool_attention/pallas_call | solution.py:286
  105.1 0.6 collective-permute-done.18.refs_3_
  105.8 2.3 %product_own.1 = (f32[256,1024]{1,0:T(8,128)S(1)}, f32[256,1024]{1,0:T(8,128)S(1)}) custom-call(bf16[256,512]{1,0:T(8,128)(2,1)S(1)} %get-tuple-element.108.refs_0_, bf16[256,512]{1,0:T(8,128)(2,1)S(1)} %collective-permute-done.16.refs_1_, bf16[256,512]{1,0:T(8,128)(2,1)S(1)} %collective-permute-done.17.refs_2_, ...), custom_call_target="tpu_custom_call" | custom-call | flops 1000 | bytes 1000 | tf_op jit(solution)/shard_map/product_own/pallas_call | solution.py:197
  108.1 1.5 %collective-permute-done.23.down_l = bf16[256,1024]{1,0:T(8,128)(2,1)S(1)} collective-permute-done((bf16[256,1024]{1,0:T(8,128)(2,1)S(1)}, bf16[256,1024]{1,0:T(8,128)(2,1)S(1)}, u32[]{:S(2)}, u32[]{:S(2)}) %collective-permute-start.23) | collective-permute-done | bytes 524320 | tf_op jit(solution)/shard_map/ppermute | solution.py:546
  109.6 8.7 %collective-permute-done.24.down_r = bf16[256,1024]{1,0:T(8,128)(2,1)S(1)} collective-permute-done((bf16[256,1024]{1,0:T(8,128)(2,1)S(1)}, bf16[256,1024]{1,0:T(8,128)(2,1)S(1)}, u32[]{:S(2)}, u32[]{:S(2)}) %collective-permute-start.24) | collective-permute-done | bytes 524320 | tf_op jit(solution)/shard_map/ppermute | solution.py:553
  118.3 0.0 collective-permute-done.21.up_l
  118.3 3.9 %prefix_attention.1 = (bf16[1,256,2048]{2,1,0:T(8,128)(2,1)}, bf16[16,80,128]{2,1,0:T(8,128)(2,1)S(1)}) custom-call(s32[1]{0:T(128)S(6)} %copy.12.prompt_pages, f32[256,1024]{1,0:T(8,128)S(1)} %get-tuple-element.112.own_l, f32[256,1024]{1,0:T(8,128)S(1)} %get-tuple-element.113.own_r, bf16[256,1024]{1,0:T(8,128)(2,1)S(1)} %collective-permute-done.21.up_l, ...), custom_call_target="tpu_custom_call" | custom-call | flops 300000000 | bytes 6291456 | tf_op jit(solution)/shard_map/prefix_attention/pallas_call | solution.py:449
  122.2 14.3 %all_to_all.5.arrived = bf16[16,80,128]{2,1,0:T(8,128)(2,1)S(1)} all-to-all(bf16[16,80,128]{2,1,0:T(8,128)(2,1)S(1)} %get-tuple-element.120), channel_id=1, replica_groups=mesh['prompt'=8,'sample'=16] {'sample'}, dimensions={0} | all-to-all | bytes 655360 | tf_op jit(solution)/shard_map/all_to_all | solution.py:565
  136.5 0.3 combine.1
  136.8 0.6 reshape.15
  (16 shorter events, 0.0 us)
Async XLA Ops:
  0.6 22.9 %collective-permute-start.1 = (bf16[512,256]{1,0:T(8,128)(2,1)}, bf16[512,256]{1,0:T(8,128)(2,1)S(1)}, u32[]{:S(2)}, u32[]{:S(2)}) collective-permute-start(bf16[512,256]{1,0:T(8,128)(2,1)} %param.11), channel_id=1, source_target_pairs={{0,3},{1,0},{2,1},{3,2},{4,7},{5,4},{6,5},{7,6},{8,11},{9,8},{10,9... | collective-permute-start | bytes 786440 | tf_op jit(solution)/shard_map/ppermute | solution.py:506
  3.5 20.0 %collective-permute-start = (bf16[512,256]{1,0:T(8,128)(2,1)}, bf16[512,256]{1,0:T(8,128)(2,1)S(1)}, u32[]{:S(2)}, u32[]{:S(2)}) collective-permute-start(bf16[512,256]{1,0:T(8,128)(2,1)} %param.11), channel_id=1, source_target_pairs={{0,1},{1,2},{2,3},{3,0},{4,5},{5,6},{6,7},{7,4},{8,9},{9,10},{10,1... | collective-permute-start | bytes 786440 | tf_op jit(solution)/shard_map/ppermute | solution.py:505
  3.5 20.0 %collective-permute-start.2 = (bf16[512,256]{1,0:T(8,128)(2,1)}, bf16[512,256]{1,0:T(8,128)(2,1)S(1)}, u32[]{:S(2)}, u32[]{:S(2)}) collective-permute-start(bf16[512,256]{1,0:T(8,128)(2,1)} %param.11), channel_id=1, source_target_pairs={{0,2},{1,3},{2,0},{3,1},{4,6},{5,7},{6,4},{7,5},{8,10},{9,11},{10,... | collective-permute-start | bytes 786440 | tf_op jit(solution)/shard_map/ppermute | solution.py:504
  7.1 0.8 copy-start
  7.9 0.7 copy-start.2
  9.1 5.7 %collective-permute-start.5 = (bf16[40,256]{1,0:T(8,128)(2,1)S(1)}, bf16[40,256]{1,0:T(8,128)(2,1)S(1)}, u32[]{:S(2)}, u32[]{:S(2)}) collective-permute-start(bf16[40,256]{1,0:T(8,128)(2,1)S(1)} %get-tuple-element.62.refs_0_), channel_id=1, source_target_pairs={{0,8},{1,9},{2,10},{3,11},{4,12},{5,13},{6,14},{7,15},{8,0},{9,1},... | collective-permute-start | bytes 61448 | tf_op jit(solution)/shard_map/ppermute | solution.py:508
  13.1 3.8 %collective-permute-start.4 = (bf16[40,256]{1,0:T(8,128)(2,1)S(1)}, bf16[40,256]{1,0:T(8,128)(2,1)S(1)}, u32[]{:S(2)}, u32[]{:S(2)}) collective-permute-start(bf16[40,256]{1,0:T(8,128)(2,1)S(1)} %get-tuple-element.62.refs_0_), channel_id=1, source_target_pairs={{0,12},{1,13},{2,14},{3,15},{4,0},{5,1},{6,2},{7,3},{8,4},{9,5},{1... | collective-permute-start | bytes 61448 | tf_op jit(solution)/shard_map/ppermute | solution.py:508
  14.9 5.4 %collective-permute-start.3 = (bf16[40,256]{1,0:T(8,128)(2,1)S(1)}, bf16[40,256]{1,0:T(8,128)(2,1)S(1)}, u32[]{:S(2)}, u32[]{:S(2)}) collective-permute-start(bf16[40,256]{1,0:T(8,128)(2,1)S(1)} %get-tuple-element.62.refs_0_), channel_id=1, source_target_pairs={{0,4},{1,5},{2,6},{3,7},{4,8},{5,9},{6,10},{7,11},{8,12},{9,13},{1... | collective-permute-start | bytes 61448 | tf_op jit(solution)/shard_map/ppermute | solution.py:508
  24.6 16.1 %collective-permute-start.6 = (bf16[4,512,256]{2,1,0:T(8,128)(2,1)S(1)}, bf16[4,512,256]{2,1,0:T(8,128)(2,1)S(1)}, u32[]{:S(2)}, u32[]{:S(2)}) collective-permute-start(bf16[4,512,256]{2,1,0:T(8,128)(2,1)S(1)} %pad_maximum_fusion.refs_4_), channel_id=1, source_target_pairs={{0,32},{16,112},{32,64},{48,16},{64,96},{80,48},{96,0},{112,80},{1... | collective-permute-start | bytes 3145736 | tf_op jit(solution)/shard_map/ppermute | solution.py:519
  26.3 14.8 %collective-permute-start.11 = (bf16[4,512,256]{2,1,0:T(8,128)(2,1)S(1)}, bf16[4,512,256]{2,1,0:T(8,128)(2,1)S(1)}, u32[]{:S(2)}, u32[]{:S(2)}) collective-permute-start(bf16[4,512,256]{2,1,0:T(8,128)(2,1)S(1)} %pad_maximum_fusion.refs_4_), channel_id=1, source_target_pairs={{0,16},{16,0},{32,48},{48,32},{64,80},{80,64},{96,112},{112,96},{1... | collective-permute-start | bytes 3145736 | tf_op jit(solution)/shard_map/ppermute | solution.py:520
  26.3 23.4 %collective-permute-start.8 = (bf16[848,512]{1,0:T(8,128)(2,1)}, bf16[848,512]{1,0:T(8,128)(2,1)S(1)}, u32[]{:S(2)}, u32[]{:S(2)}) collective-permute-start(bf16[848,512]{1,0:T(8,128)(2,1)} %get-tuple-element.82), channel_id=1, source_target_pairs={{0,2},{1,3},{2,0},{3,1},{4,6},{5,7},{6,4},{7,5},{8,10},{9,11},{10,... | collective-permute-start | bytes 2605064 | tf_op jit(solution)/shard_map/ppermute | solution.py:513
  40.7 31.4 %collective-permute-start.7 = (bf16[4,512,256]{2,1,0:T(8,128)(2,1)S(1)}, bf16[4,512,256]{2,1,0:T(8,128)(2,1)S(1)}, u32[]{:S(2)}, u32[]{:S(2)}) collective-permute-start(bf16[4,512,256]{2,1,0:T(8,128)(2,1)S(1)} %collective-permute-done.6.refs_6_), channel_id=1, source_target_pairs={{0,32},{16,112},{32,64},{48,16},{64,96},{80,48},{96,0},{112,80},{1... | collective-permute-start | bytes 3145736 | tf_op jit(solution)/shard_map/ppermute | solution.py:522
  41.1 31.1 %collective-permute-start.12 = (bf16[4,512,256]{2,1,0:T(8,128)(2,1)S(1)}, bf16[4,512,256]{2,1,0:T(8,128)(2,1)S(1)}, u32[]{:S(2)}, u32[]{:S(2)}) collective-permute-start(bf16[4,512,256]{2,1,0:T(8,128)(2,1)S(1)} %collective-permute-done.11.refs_5_), channel_id=1, source_target_pairs={{0,32},{16,112},{32,64},{48,16},{64,96},{80,48},{96,0},{112,80},{1... | collective-permute-start | bytes 3145736 | tf_op jit(solution)/shard_map/ppermute | solution.py:521
  49.7 22.1 %collective-permute-start.9 = (bf16[848,512]{1,0:T(8,128)(2,1)S(1)}, bf16[848,512]{1,0:T(8,128)(2,1)S(1)}, u32[]{:S(2)}, u32[]{:S(2)}) collective-permute-start(bf16[848,512]{1,0:T(8,128)(2,1)S(1)} %get-tuple-element.83), channel_id=1, source_target_pairs={{0,1},{1,2},{2,3},{3,0},{4,5},{5,6},{6,7},{7,4},{8,9},{9,10},{10,1... | collective-permute-start | bytes 2605064 | tf_op jit(solution)/shard_map/ppermute | solution.py:515
  51.5 20.6 %collective-permute-start.10 = (bf16[848,512]{1,0:T(8,128)(2,1)S(1)}, bf16[848,512]{1,0:T(8,128)(2,1)S(1)}, u32[]{:S(2)}, u32[]{:S(2)}) collective-permute-start(bf16[848,512]{1,0:T(8,128)(2,1)S(1)} %get-tuple-element.84), channel_id=1, source_target_pairs={{0,3},{1,0},{2,1},{3,2},{4,7},{5,4},{6,5},{7,6},{8,11},{9,8},{10,9... | collective-permute-start | bytes 2605064 | tf_op jit(solution)/shard_map/ppermute | solution.py:516
  52.9 19.7 %collective-permute-start.13 = (bf16[4,512,256]{2,1,0:T(8,128)(2,1)S(1)}, bf16[4,512,256]{2,1,0:T(8,128)(2,1)S(1)}, u32[]{:S(2)}, u32[]{:S(2)}) collective-permute-start(bf16[4,512,256]{2,1,0:T(8,128)(2,1)S(1)} %collective-permute-done.6.refs_6_), channel_id=1, source_target_pairs={{0,16},{16,0},{32,48},{48,32},{64,80},{80,64},{96,112},{112,96},{1... | collective-permute-start | bytes 3145736 | tf_op jit(solution)/shard_map/ppermute | solution.py:523
  72.1 2.7 %collective-permute-start.14 = (bf16[4,512,256]{2,1,0:T(8,128)(2,1)S(1)}, bf16[4,512,256]{2,1,0:T(8,128)(2,1)S(1)}, u32[]{:S(2)}, u32[]{:S(2)}) collective-permute-start(bf16[4,512,256]{2,1,0:T(8,128)(2,1)S(1)} %collective-permute-done.12.refs_7_), channel_id=1, source_target_pairs={{0,16},{16,0},{32,48},{48,32},{64,80},{80,64},{96,112},{112,96},{1... | collective-permute-start | bytes 3145736 | tf_op jit(solution)/shard_map/ppermute | solution.py:524
  72.1 4.2 %collective-permute-start.15 = (bf16[4,512,256]{2,1,0:T(8,128)(2,1)S(1)}, bf16[4,512,256]{2,1,0:T(8,128)(2,1)S(1)}, u32[]{:S(2)}, u32[]{:S(2)}) collective-permute-start(bf16[4,512,256]{2,1,0:T(8,128)(2,1)S(1)} %collective-permute-done.7.refs_10_), channel_id=1, source_target_pairs={{0,16},{16,0},{32,48},{48,32},{64,80},{80,64},{96,112},{112,96},{1... | collective-permute-start | bytes 3145736 | tf_op jit(solution)/shard_map/ppermute | solution.py:526
  78.6 21.9 %slice-start.2 = ((s8[8388608]{0:T(1024)(128)(4,1)}), s8[4194304]{0:T(1024)(128)(4,1)S(1)}, s32[]{:S(2)}) async-start(s8[8388608]{0:T(1024)(128)(4,1)} %bitcast.15), calls=%async_computation.3 | async-start | bytes 8388608
  78.7 21.9 %slice-start.3 = ((s8[8388608]{0:T(1024)(128)(4,1)}), s8[4194304]{0:T(1024)(128)(4,1)S(1)}, s32[]{:S(2)}) async-start(s8[8388608]{0:T(1024)(128)(4,1)} %bitcast.15), calls=%async_computation.4 | async-start | bytes 8388608
  78.7 21.9 %copy-start.1 = (bf16[1,1,2048]{2,1,0:T(2,128)(2,1)S(1)}, bf16[1,1,2048]{2,1,0:T(2,128)(2,1)}, u32[]{:S(2)}) copy-start(bf16[1,1,2048]{2,1,0:T(2,128)(2,1)} %param.13) | copy-start | bytes 12292
  78.7 16.1 %collective-permute-start.19 = (bf16[256,1024]{1,0:T(8,128)(2,1)S(1)}, bf16[256,1024]{1,0:T(8,128)(2,1)S(1)}, u32[]{:S(2)}, u32[]{:S(2)}) collective-permute-start(bf16[256,1024]{1,0:T(8,128)(2,1)S(1)} %get-tuple-element.97), channel_id=1, source_target_pairs={{0,4},{1,5},{2,6},{3,7},{4,8},{5,9},{6,10},{7,11},{8,12},{9,13},{1... | collective-permute-start | bytes 1572872 | tf_op jit(solution)/shard_map/ppermute | solution.py:542
  78.8 16.8 %collective-permute-start.20 = (bf16[256,1024]{1,0:T(8,128)(2,1)S(1)}, bf16[256,1024]{1,0:T(8,128)(2,1)S(1)}, u32[]{:S(2)}, u32[]{:S(2)}) collective-permute-start(bf16[256,1024]{1,0:T(8,128)(2,1)S(1)} %get-tuple-element.98), channel_id=1, source_target_pairs={{0,12},{1,13},{2,14},{3,15},{4,0},{5,1},{6,2},{7,3},{8,4},{9,5},{1... | collective-permute-start | bytes 1572872 | tf_op jit(solution)/shard_map/ppermute | solution.py:543
  82.0 15.2 %collective-permute-start.16 = (bf16[256,512]{1,0:T(8,128)(2,1)S(1)}, bf16[256,512]{1,0:T(8,128)(2,1)S(1)}, u32[]{:S(2)}, u32[]{:S(2)}) collective-permute-start(bf16[256,512]{1,0:T(8,128)(2,1)S(1)} %get-tuple-element.91), channel_id=1, source_target_pairs={{0,1},{1,2},{2,3},{3,0},{4,5},{5,6},{6,7},{7,4},{8,9},{9,10},{10,1... | collective-permute-start | bytes 786440 | tf_op jit(solution)/shard_map/ppermute | solution.py:538
  82.3 15.5 %collective-permute-start.17 = (bf16[256,512]{1,0:T(8,128)(2,1)S(1)}, bf16[256,512]{1,0:T(8,128)(2,1)S(1)}, u32[]{:S(2)}, u32[]{:S(2)}) collective-permute-start(bf16[256,512]{1,0:T(8,128)(2,1)S(1)} %get-tuple-element.92), channel_id=1, source_target_pairs={{0,3},{1,0},{2,1},{3,2},{4,7},{5,4},{6,5},{7,6},{8,11},{9,8},{10,9... | collective-permute-start | bytes 786440 | tf_op jit(solution)/shard_map/ppermute | solution.py:539
  85.2 15.6 %slice-start = ((s8[8388608]{0:T(1024)(128)(4,1)}), s8[4194304]{0:T(1024)(128)(4,1)S(1)}, s32[]{:S(2)}) async-start(s8[8388608]{0:T(1024)(128)(4,1)} %bitcast.9), calls=%async_computation.1 | async-start | bytes 8388608
  89.7 18.4 %collective-permute-start.22 = (bf16[256,1024]{1,0:T(8,128)(2,1)S(1)}, bf16[256,1024]{1,0:T(8,128)(2,1)S(1)}, u32[]{:S(2)}, u32[]{:S(2)}) collective-permute-start(bf16[256,1024]{1,0:T(8,128)(2,1)S(1)} %get-tuple-element.114), channel_id=1, source_target_pairs={{0,4},{1,5},{2,6},{3,7},{4,8},{5,9},{6,10},{7,11},{8,12},{9,13},{1... | collective-permute-start | bytes 1572872 | tf_op jit(solution)/shard_map/ppermute | solution.py:546
  94.7 14.9 %collective-permute-start.23 = (bf16[256,1024]{1,0:T(8,128)(2,1)S(1)}, bf16[256,1024]{1,0:T(8,128)(2,1)S(1)}, u32[]{:S(2)}, u32[]{:S(2)}) collective-permute-start(bf16[256,1024]{1,0:T(8,128)(2,1)S(1)} %get-tuple-element.115), channel_id=1, source_target_pairs={{0,12},{1,13},{2,14},{3,15},{4,0},{5,1},{6,2},{7,3},{8,4},{9,5},{1... | collective-permute-start | bytes 1572872 | tf_op jit(solution)/shard_map/ppermute | solution.py:546
  95.5 5.3 %slice-start.1 = ((s8[8388608]{0:T(1024)(128)(4,1)}), s8[4194304]{0:T(1024)(128)(4,1)S(1)}, s32[]{:S(2)}) async-start(s8[8388608]{0:T(1024)(128)(4,1)} %bitcast.9), calls=%async_computation.2 | async-start | bytes 8388608
  95.8 22.5 %collective-permute-start.24 = (bf16[256,1024]{1,0:T(8,128)(2,1)S(1)}, bf16[256,1024]{1,0:T(8,128)(2,1)S(1)}, u32[]{:S(2)}, u32[]{:S(2)}) collective-permute-start(bf16[256,1024]{1,0:T(8,128)(2,1)S(1)} %get-tuple-element.116), channel_id=1, source_target_pairs={{0,12},{1,13},{2,14},{3,15},{4,0},{5,1},{6,2},{7,3},{8,4},{9,5},{1... | collective-permute-start | bytes 1572872 | tf_op jit(solution)/shard_map/ppermute | solution.py:553
  97.2 21.1 %collective-permute-start.21 = (bf16[256,1024]{1,0:T(8,128)(2,1)S(1)}, bf16[256,1024]{1,0:T(8,128)(2,1)S(1)}, u32[]{:S(2)}, u32[]{:S(2)}) collective-permute-start(bf16[256,1024]{1,0:T(8,128)(2,1)S(1)} %get-tuple-element.99), channel_id=1, source_target_pairs={{0,4},{1,5},{2,6},{3,7},{4,8},{5,9},{6,10},{7,11},{8,12},{9,13},{1... | collective-permute-start | bytes 1572872 | tf_op jit(solution)/shard_map/ppermute | solution.py:550
  97.9 7.9 %collective-permute-start.18 = (bf16[256,512]{1,0:T(8,128)(2,1)S(1)}, bf16[256,512]{1,0:T(8,128)(2,1)S(1)}, u32[]{:S(2)}, u32[]{:S(2)}) collective-permute-start(bf16[256,512]{1,0:T(8,128)(2,1)S(1)} %get-tuple-element.93), channel_id=1, source_target_pairs={{0,2},{1,3},{2,0},{3,1},{4,6},{5,7},{6,4},{7,5},{8,10},{9,11},{10,... | collective-permute-start | bytes 786440 | tf_op jit(solution)/shard_map/ppermute | solution.py:540

commit v5 on v4

--- a/solution.py
+++ b/solution.py
@@ -91,13 +91,16 @@
 
 
 def unpack_kernel(*refs):
-    arrived, (queries, by_group, slots, alive) = refs[:4], refs[4:]
+    own, arrived, (queries, by_group, slots, alive) = refs[:4], refs[4:7], refs[7:]
     me = lax.axis_index("sample")
 
     def block_of(r):
-        rows = slice(3 * ROWS + r % 4 // 2 * BLOCK, 3 * ROWS + (r % 4 // 2 + 1) * BLOCK)
+        if r < 4:
+            return own[r][...].astype(F32)
+        source = arrived[r // 4 - 1]
+        first = source.shape[0] - 2 * BLOCK + r % 4 // 2 * BLOCK
         lanes = slice(r % 2 * COLUMNS, (r % 2 + 1) * COLUMNS)
-        return arrived[r // 4][rows, lanes].astype(F32)
+        return source[first : first + BLOCK, lanes].astype(F32)
 
     plans = []
     for r in range(SAMPLES):
@@ -123,7 +126,7 @@
         alive[r] = some[r, 0]
 
 
-def unpack(arrived):
+def unpack(own, arrived):
     smem, vmem = pl.BlockSpec(memory_space=pltpu.SMEM), pl.BlockSpec(memory_space=pltpu.VMEM)
     return pl.pallas_call(
         unpack_kernel,
@@ -133,49 +136,91 @@
             jax.ShapeDtypeStruct((SAMPLES,), jnp.int32),
             jax.ShapeDtypeStruct((SAMPLES,), jnp.int32),
         ],
-        in_specs=[vmem] * 4,
+        in_specs=[vmem] * 7,
         out_specs=[vmem, vmem, smem, smem],
         compiler_params=params(16),
         cost_estimate=cost(1000, 1000),
         name="unpack",
-    )(*arrived)
+    )(*own, *arrived)
 
 
 STEPS = (0, 1, 3, 2)
-
-
-def pick_kernel(states, *refs):
-    blocks, outs, sems = refs[:4], refs[4:12], refs[12]
+NEXT = (2, 1, 3, 0)
+
+
+def copy_rows(states, sems, wanted):
     me = lax.axis_index("sample")
     z, x = me // 4, lax.rem(me, 4)
-    copies = []
-    for i, step in enumerate(STEPS):
-        column = lax.rem(x + step, 4)
-        for k, up in enumerate((2, 1, 3)):
-            copies.append((states.at[lax.rem(z + up, 4), column], outs[i].at[pl.ds(k * ROWS, ROWS)]))
-        copies.append((states.at[z, column], outs[4 + i]))
-    copies = [pltpu.make_async_copy(src, dst, sems.at[n]) for n, (src, dst) in enumerate(copies)]
+    copies = [
+        pltpu.make_async_copy(
+            states.at[lax.rem(z + NEXT[k], 4), lax.rem(x + step, 4)], target, sems.at[n]
+        )
+        for n, (step, k, target) in enumerate(wanted)
+    ]
     for copy in copies:
         copy.start()
-    for out in outs[:4]:
-        for r, block in enumerate(blocks):
-            rows = slice(3 * ROWS + r // 2 * BLOCK, 3 * ROWS + (r // 2 + 1) * BLOCK)
-            out[rows, r % 2 * COLUMNS : (r % 2 + 1) * COLUMNS] = block[...]
+    return copies
+
+
+def block_rows(k):
+    return pl.ds(k * ROWS, ROWS)
+
+
+def pick_far_kernel(states, own, far, sems):
+    wanted = [(2, k, far.at[block_rows(k)]) for k in range(3)]
+    wanted += [(0, k, own.at[block_rows(k)]) for k in range(4)]
+    for copy in copy_rows(states, sems, wanted):
+        copy.wait()
+
+
+def pick_far(states):
+    vmem = pl.BlockSpec(memory_space=pltpu.VMEM)
+    return pl.pallas_call(
+        pick_far_kernel,
+        out_shape=[
+            jax.ShapeDtypeStruct((4 * ROWS, SLICE), BF16),
+            jax.ShapeDtypeStruct((3 * ROWS, SLICE), BF16),
+        ],
+        in_specs=[pl.BlockSpec(memory_space=pl.ANY)],
+        out_specs=[vmem] * 2,
+        scratch_shapes=[pltpu.SemaphoreType.DMA((7,))],
+        compiler_params=params(50),
+        cost_estimate=cost(1000, 1000),
+        name="pick_far",
+    )(states)
+
+
+def put_blocks(target, first, blocks):
+    for r, block in enumerate(blocks):
+        rows = slice(first + r // 2 * BLOCK, first + (r // 2 + 1) * BLOCK)
+        target[rows, r % 2 * COLUMNS : (r % 2 + 1) * COLUMNS] = block[...]
+
+
+def pick_near_kernel(states, *refs):
+    blocks, (right, left, last), sems = refs[:4], refs[4:7], refs[7]
+    wanted = [(1, k, right.at[block_rows(k)]) for k in range(4)]
+    wanted += [(3, k, left.at[block_rows(k)]) for k in range(4)]
+    wanted += [(2, 3, last.at[block_rows(0)])]
+    copies = copy_rows(states, sems, wanted)
+    put_blocks(right, 4 * ROWS, blocks)
+    put_blocks(left, 4 * ROWS, blocks)
+    put_blocks(last, ROWS, blocks)
     for copy in copies:
         copy.wait()
 
 
-def pick(states, blocks):
-    return pl.pallas_call(
-        pick_kernel,
-        out_shape=[jax.ShapeDtypeStruct((3 * ROWS + 2 * BLOCK, SLICE), BF16)] * 4
-        + [jax.ShapeDtypeStruct((ROWS, SLICE), BF16)] * 4,
-        in_specs=[pl.BlockSpec(memory_space=pl.ANY)] + [pl.BlockSpec(memory_space=pltpu.VMEM)] * 4,
-        out_specs=[pl.BlockSpec(memory_space=pltpu.VMEM)] * 8,
-        scratch_shapes=[pltpu.SemaphoreType.DMA((16,))],
-        compiler_params=params(50),
-        cost_estimate=cost(1000, 1000),
-        name="pick_rows",
+def pick_near(states, blocks):
+    vmem = pl.BlockSpec(memory_space=pltpu.VMEM)
+    return pl.pallas_call(
+        pick_near_kernel,
+        out_shape=[jax.ShapeDtypeStruct((4 * ROWS + 2 * BLOCK, SLICE), BF16)] * 2
+        + [jax.ShapeDtypeStruct((ROWS + 2 * BLOCK, SLICE), BF16)],
+        in_specs=[pl.BlockSpec(memory_space=pl.ANY)] + [vmem] * 4,
+        out_specs=[vmem] * 3,
+        scratch_shapes=[pltpu.SemaphoreType.DMA((9,))],
+        compiler_params=params(44),
+        cost_estimate=cost(1000, 1000),
+        name="pick_near",
     )(states, *blocks)
 
 
@@ -185,8 +230,10 @@
         for k, block in enumerate(blocks):
             total = jnp.zeros((ROWS, COLUMNS), F32)
             for d in range(4):
-                left = states[d][...] if block is None else states[d][block * ROWS : (block + 1) * ROWS]
-                total += jnp.dot(left, pieces[j][d], preferred_element_type=F32)
+                at = block[d] * ROWS
+                total += jnp.dot(
+                    states[d][at : at + ROWS], pieces[j][d], preferred_element_type=F32
+                )
             out = outs[2 * k + j // 4]
             out[:, (j % 4) * COLUMNS : (j % 4 + 1) * COLUMNS] = total.astype(out.dtype)
 
@@ -505,13 +552,14 @@
     weight_right = lax.ppermute(kv_weight, "sample", X_RIGHT)
     weight_left = lax.ppermute(kv_weight, "sample", X_LEFT)
     block, query = prepare(queries, page_where, comp_pages, preempted)
+    states = prompt_states.reshape(4, 4, ROWS, SLICE)
+    own_states, to_far = pick_far(states)
+    slices, own_states, to_far, block = tie(
+        ((kv_weight, weight_right, weight_left, weight_far), own_states, to_far, block)
+    )
     blocks = [block] + [lax.ppermute(block, "sample", to) for to in (Z_UP, Z_DOWN, Z_FAR)]
-    states = prompt_states.reshape(4, 4, ROWS, SLICE)
-    picked = pick(states, blocks)
-    slices, picked = tie(((kv_weight, weight_right, weight_left, weight_far), picked))
-    others, to_right, to_left, to_far = picked[:4]
+    to_right, to_left, last_far = pick_near(states, blocks)
     rows_far = lax.ppermute(to_far, "sample", X_FAR)
-    to_right, to_left, rows_far = tie((to_right, to_left, rows_far))
     rows_right = lax.ppermute(to_right, "sample", X_RIGHT)
     rows_left = lax.ppermute(to_left, "sample", X_LEFT)
 
@@ -519,32 +567,26 @@
     near = lax.ppermute(here, "prompt", Y_SPLIT)
     here_other = lax.ppermute(here, "prompt", SWAP)
     near_other = lax.ppermute(here_other, "prompt", Y_SPLIT)
+    near, near_other, rows_far = tie((near, near_other, rows_far))
     far = lax.ppermute(near, "prompt", Y_SPLIT)
     near_swapped = lax.ppermute(near, "prompt", SWAP)
     near_other_swapped = lax.ppermute(near_other, "prompt", SWAP)
     far, rows_right, rows_left = tie((far, rows_right, rows_left))
     far_other = lax.ppermute(far, "prompt", SWAP)
-    others = [others, rows_right, rows_left, rows_far]
+    others = [own_states, rows_right, rows_left, rows_far]
     pieces = [
         here, here_other, near, near_other,
         near_swapped, near_other_swapped, far, far_other,
     ]
 
     far_l, far_r = product_far(others, pieces)
-    mine, to_right, to_left, to_far = picked[4:]
-    to_right, to_left, to_far, far_l, far_r = tie((to_right, to_left, to_far, far_l, far_r))
-    mine = [
-        mine,
-        lax.ppermute(to_right, "sample", X_RIGHT),
-        lax.ppermute(to_left, "sample", X_LEFT),
-        lax.ppermute(to_far, "sample", X_FAR),
-    ]
+    last_far, rows_right = tie((last_far, rows_right))
+    last_far = lax.ppermute(last_far, "sample", X_FAR)
     from_down = lax.ppermute(far_l, "sample", Z_UP)
     from_up = lax.ppermute(far_r, "sample", Z_DOWN)
-    up_l, up_r, down_l, down_r = product(others, pieces, (1, 2), BF16, "product_near")
-    up_r, down_l, from_down, from_up = (
-        lax.ppermute(up_r, "sample", Z_UP), lax.ppermute(down_l, "sample", Z_DOWN), from_down, from_up,
-    )
+    up_l, up_r, down_l, down_r = product(others, pieces, ((1,) * 4, (2,) * 4), BF16, "product_near")
+    up_r, down_l, last_far = tie((up_r, down_l, last_far))
+    up_r, down_l = lax.ppermute(up_r, "sample", Z_UP), lax.ppermute(down_l, "sample", Z_DOWN)
     up_l, down_r = relay(up_l, down_r, from_down, from_up)
     sums = [
         lax.ppermute(up_l, "sample", Z_UP),
@@ -553,13 +595,13 @@
         lax.ppermute(down_r, "sample", Z_DOWN),
     ]
 
-    arrived, query, up_l = tie((others, query, up_l))
-    queries_all, by_group, slots, alive = unpack(arrived)
+    arrived, query, up_l = tie(([rows_right, rows_left, last_far], query, up_l))
+    queries_all, by_group, slots, alive = unpack(blocks, arrived)
     pool = pool_attention(slots, alive, queries_all, pool_pages[0, 0])
     local_alive = jnp.where(preempted[0] > 0, 0, comp_pages[0])
     local = local_attention(local_alive, query, new_kv[0], local_pages[0, 0])
-    mine, pool, local = tie((mine, pool, local))
-    sums = [*product(mine, pieces, (None,), F32, "product_own"), *sums]
+    mine, pool, local = tie(([own_states, *arrived], pool, local))
+    sums = [*product(mine, pieces, ((3, 3, 3, 0),), F32, "product_own"), *sums]
 
     cache, packed = prefix_attention(prompt_pages, sums, by_group, pool)
     arrived = lax.all_to_all(packed, "sample", split_axis=0, concat_axis=0, tiled=True)

time: 138 us -> 134 us (0.971)
  waiting for transfers between devices: 63.6 us -> 55.5 us
  local copies, waits for them, and re-layouts: 2.06 us -> 4.79 us
  starting transfers between devices: 30.9 us -> 33.2 us
    ppermute x1, waiting for transfers between devices: 13.2 us -> 0.01 us  [per_device(): near = lax.ppermute(here, 'prompt', Y_SPLIT)]
    ppermute x1, waiting for transfers between devices: 8.7 us -> 0.01 us  [per_device(): lax.ppermute(down_r, 'sample', Z_DOWN)]
    ppermute x1, waiting for transfers between devices: 0.01 us -> 6.66 us  [per_device(): lax.ppermute(up_l, 'sample', Z_UP)]
    ppermute x1, waiting for transfers between devices: 0.01 us -> 5.14 us  [per_device(): weight_far = lax.ppermute(kv_weight, 'sample', X_FAR)]
    ppermute x3 -> x1, waiting for transfers between devices: 0.62 us -> 5.38 us  [per_device(): last_far = lax.ppermute(last_far, 'sample', X_FAR)]
    ppermute x1, waiting for transfers between devices: 4.75 us -> 0.01 us  [per_device(): from_down = lax.ppermute(far_l, 'sample', Z_UP)]
    ppermute x3 -> x1, starting transfers between devices: 4.39 us -> 1.46 us  [per_device(): last_far = lax.ppermute(last_far, 'sample', X_FAR)]
    unnamed x14, local copies, waits for them, and re-layouts: 1.43 us -> 4.16 us
  transfers between devices with their start and end apart: 25 -> 23, of which waited for: 13 -> 11; matrix products, arithmetic and copies ran while one was open for 0% -> 0% of each run, Pallas kernels for 12% -> 11%
where the time goes in v5:
time: 134 us
  waiting for transfers between devices  55.5 us (41%)
  starting transfers between devices  33.2 us (25%)
  Pallas kernels  21.5 us (16%)
  blocking collectives  14.6 us (11%)
  local copies, waits for them, and re-layouts  4.79 us (4%)
  between operations  2.96 us (2%)
    ppermute x1, waiting for transfers between devices, per_device(): rows_right = lax.ppermute(to_right, 'sample', X_RIGHT)  20.7 us
    all_to_all x1, blocking collectives, per_device(): lax.all_to_all(packed, 'sample', split_axis=0, concat_axis=0, tiled=True)  14.6 us
    pallas_call x2, Pallas kernels, product(): pl.pallas_call(functools.partial(product_kernel, blocks), out_shape=outs,...  6.81 us
    ppermute x1, waiting for transfers between devices, per_device(): lax.ppermute(up_l, 'sample', Z_UP)  6.66 us
    ppermute x1, waiting for transfers between devices, per_device(): rows_far = lax.ppermute(to_far, 'sample', X_FAR)  6.17 us
    ppermute x3, starting transfers between devices, per_device(): lax.ppermute(block, 'sample', to)  6.07 us
    ppermute x1, waiting for transfers between devices, per_device(): last_far = lax.ppermute(last_far, 'sample', X_FAR)  5.38 us
    ppermute x1, waiting for transfers between devices, per_device(): weight_far = lax.ppermute(kv_weight, 'sample', X_FAR)  5.14 us
  transfers between devices with their start and end apart: 23, of which 11 were waited for; matrix products, arithmetic and copies ran while one was open for 0% of the time, Pallas kernels for 11%

profile of v5, /device:TPU:0, one launch (start us, length us, event | category | flops | bytes accessed | tf_op | source)
XLA Modules:
  0.0 133.6 jit_solution(7527463183509572174)
XLA Ops:
  0.6 1.6 %collective-permute-start = (bf16[512,256]{1,0:T(8,128)(2,1)}, bf16[512,256]{1,0:T(8,128)(2,1)S(1)}, u32[]{:S(2)}, u32[]{:S(2)}) collective-permute-start(bf16[512,256]{1,0:T(8,128)(2,1)} %param.11), channel_id=1, source_target_pairs={{0,1},{1,2},{2,3},{3,0},{4,5},{5,6},{6,7},{7,4},{8,9},{9,10},{10,1... | collective-permute-start | bytes 786440 | tf_op jit(solution)/shard_map/ppermute | solution.py:552
  2.3 1.7 %collective-permute-start.1 = (bf16[512,256]{1,0:T(8,128)(2,1)}, bf16[512,256]{1,0:T(8,128)(2,1)S(1)}, u32[]{:S(2)}, u32[]{:S(2)}) collective-permute-start(bf16[512,256]{1,0:T(8,128)(2,1)} %param.11), channel_id=1, source_target_pairs={{0,3},{1,0},{2,1},{3,2},{4,7},{5,4},{6,5},{7,6},{8,11},{9,8},{10,9... | collective-permute-start | bytes 786440 | tf_op jit(solution)/shard_map/ppermute | solution.py:553
  3.9 1.9 %collective-permute-start.2 = (bf16[512,256]{1,0:T(8,128)(2,1)}, bf16[512,256]{1,0:T(8,128)(2,1)S(1)}, u32[]{:S(2)}, u32[]{:S(2)}) collective-permute-start(bf16[512,256]{1,0:T(8,128)(2,1)} %param.11), channel_id=1, source_target_pairs={{0,2},{1,3},{2,0},{3,1},{4,6},{5,7},{6,4},{7,5},{8,10},{9,11},{10,... | collective-permute-start | bytes 786440 | tf_op jit(solution)/shard_map/ppermute | solution.py:551
  5.8 1.6 %pick_far.1 = (bf16[1024,512]{1,0:T(8,128)(2,1)S(1)}, bf16[768,512]{1,0:T(8,128)(2,1)S(1)}) custom-call(bf16[4,4,256,512]{3,2,1,0:T(8,128)(2,1)} %bitcast.15), custom_call_target="tpu_custom_call" | custom-call | flops 1000 | bytes 1000 | tf_op jit(solution)/shard_map/pick_far/pallas_call | solution.py:178
  9.0 0.0 copy-start.2
  9.0 0.7 copy-done.2
  9.7 0.6 prepare.1
  10.3 0.0 collective-permute-done
  10.3 1.4 %collective-permute-done.1 = bf16[512,256]{1,0:T(8,128)(2,1)S(1)} collective-permute-done((bf16[512,256]{1,0:T(8,128)(2,1)}, bf16[512,256]{1,0:T(8,128)(2,1)S(1)}, u32[]{:S(2)}, u32[]{:S(2)}) %collective-permute-start.1) | collective-permute-done | bytes 262176 | tf_op jit(solution)/shard_map/ppermute | solution.py:553
  11.7 5.1 %collective-permute-done.2 = bf16[512,256]{1,0:T(8,128)(2,1)S(1)} collective-permute-done((bf16[512,256]{1,0:T(8,128)(2,1)}, bf16[512,256]{1,0:T(8,128)(2,1)S(1)}, u32[]{:S(2)}, u32[]{:S(2)}) %collective-permute-start.2) | collective-permute-done | bytes 262176 | tf_op jit(solution)/shard_map/ppermute | solution.py:551
  16.9 1.1 pad_maximum_fusion.refs_4_
  17.9 0.1 collective-permute-start.7
  18.0 1.6 %collective-permute-start.6 = (bf16[4,512,256]{2,1,0:T(8,128)(2,1)S(1)}, bf16[4,512,256]{2,1,0:T(8,128)(2,1)S(1)}, u32[]{:S(2)}, u32[]{:S(2)}) collective-permute-start(bf16[4,512,256]{2,1,0:T(8,128)(2,1)S(1)} %pad_maximum_fusion.refs_4_), channel_id=1, source_target_pairs={{0,32},{16,112},{32,64},{48,16},{64,96},{80,48},{96,0},{112,80},{1... | collective-permute-start | bytes 3145736 | tf_op jit(solution)/shard_map/ppermute | solution.py:567
  19.7 1.0 collective-permute-done.7.refs_5_
  20.7 1.6 %collective-permute-start.8 = (bf16[4,512,256]{2,1,0:T(8,128)(2,1)S(1)}, bf16[4,512,256]{2,1,0:T(8,128)(2,1)S(1)}, u32[]{:S(2)}, u32[]{:S(2)}) collective-permute-start(bf16[4,512,256]{2,1,0:T(8,128)(2,1)S(1)} %collective-permute-done.7.refs_5_), channel_id=1, source_target_pairs={{0,32},{16,112},{32,64},{48,16},{64,96},{80,48},{96,0},{112,80},{1... | collective-permute-start | bytes 3145736 | tf_op jit(solution)/shard_map/ppermute | solution.py:569
  22.3 0.8 collective-permute-start.9
  23.1 1.9 %collective-permute-start.3 = (bf16[40,256]{1,0:T(8,128)(2,1)S(1)}, bf16[40,256]{1,0:T(8,128)(2,1)S(1)}, u32[]{:S(2)}, u32[]{:S(2)}) collective-permute-start(bf16[40,256]{1,0:T(8,128)(2,1)S(1)} %get-tuple-element.57.refs_0_), channel_id=1, source_target_pairs={{0,4},{1,5},{2,6},{3,7},{4,8},{5,9},{6,10},{7,11},{8,12},{9,13},{1... | collective-permute-start | bytes 61448 | tf_op jit(solution)/shard_map/ppermute | solution.py:560
  25.0 2.1 %collective-permute-start.4 = (bf16[40,256]{1,0:T(8,128)(2,1)S(1)}, bf16[40,256]{1,0:T(8,128)(2,1)S(1)}, u32[]{:S(2)}, u32[]{:S(2)}) collective-permute-start(bf16[40,256]{1,0:T(8,128)(2,1)S(1)} %get-tuple-element.57.refs_0_), channel_id=1, source_target_pairs={{0,12},{1,13},{2,14},{3,15},{4,0},{5,1},{6,2},{7,3},{8,4},{9,5},{1... | collective-permute-start | bytes 61448 | tf_op jit(solution)/shard_map/ppermute | solution.py:560
  27.1 1.8 %collective-permute-done.3.refs_1_ = bf16[40,256]{1,0:T(8,128)(2,1)S(1)} collective-permute-done((bf16[40,256]{1,0:T(8,128)(2,1)S(1)}, bf16[40,256]{1,0:T(8,128)(2,1)S(1)}, u32[]{:S(2)}, u32[]{:S(2)}) %collective-permute-start.3) | collective-permute-done | bytes 20512 | tf_op jit(solution)/shard_map/ppermute | solution.py:560
  28.9 2.0 %collective-permute-start.5 = (bf16[40,256]{1,0:T(8,128)(2,1)S(1)}, bf16[40,256]{1,0:T(8,128)(2,1)S(1)}, u32[]{:S(2)}, u32[]{:S(2)}) collective-permute-start(bf16[40,256]{1,0:T(8,128)(2,1)S(1)} %get-tuple-element.57.refs_0_), channel_id=1, source_target_pairs={{0,8},{1,9},{2,10},{3,11},{4,12},{5,13},{6,14},{7,15},{8,0},{9,1},... | collective-permute-start | bytes 61448 | tf_op jit(solution)/shard_map/ppermute | solution.py:560
  30.9 0.0 collective-permute-done.4.refs_2_
  30.9 3.2 %collective-permute-done.5.refs_3_ = bf16[40,256]{1,0:T(8,128)(2,1)S(1)} collective-permute-done((bf16[40,256]{1,0:T(8,128)(2,1)S(1)}, bf16[40,256]{1,0:T(8,128)(2,1)S(1)}, u32[]{:S(2)}, u32[]{:S(2)}) %collective-permute-start.5) | collective-permute-done | bytes 20512 | tf_op jit(solution)/shard_map/ppermute | solution.py:560
  34.2 0.3 pick_near.1
  34.5 2.1 %collective-permute-start.11 = (bf16[1104,512]{1,0:T(8,128)(2,1)S(1)}, bf16[1104,512]{1,0:T(8,128)(2,1)S(1)}, u32[]{:S(2)}, u32[]{:S(2)}) collective-permute-start(bf16[1104,512]{1,0:T(8,128)(2,1)S(1)} %get-tuple-element.65), channel_id=1, source_target_pairs={{0,1},{1,2},{2,3},{3,0},{4,5},{5,6},{6,7},{7,4},{8,9},{9,10},{10,1... | collective-permute-start | bytes 3391496 | tf_op jit(solution)/shard_map/ppermute | solution.py:563
  36.5 1.2 collective-permute-start.12
  37.8 6.2 %collective-permute-done.9.refs_3_ = bf16[768,512]{1,0:T(8,128)(2,1)S(1)} collective-permute-done((bf16[768,512]{1,0:T(8,128)(2,1)S(1)}, bf16[768,512]{1,0:T(8,128)(2,1)S(1)}, u32[]{:S(2)}, u32[]{:S(2)}) %collective-permute-start.9) | collective-permute-done | bytes 786464 | tf_op jit(solution)/shard_map/ppermute | solution.py:562
  43.9 0.0 collective-permute-done.6.refs_6_
  43.9 1.4 %collective-permute-done.8.refs_7_ = bf16[4,512,256]{2,1,0:T(8,128)(2,1)S(1)} collective-permute-done((bf16[4,512,256]{2,1,0:T(8,128)(2,1)S(1)}, bf16[4,512,256]{2,1,0:T(8,128)(2,1)S(1)}, u32[]{:S(2)}, u32[]{:S(2)}) %collective-permute-start.8) | collective-permute-done | bytes 1048608 | tf_op jit(solution)/shard_map/ppermute | solution.py:569
  45.3 0.5 collective-permute-start.10
  45.9 1.8 %collective-permute-start.13 = (bf16[4,512,256]{2,1,0:T(8,128)(2,1)S(1)}, bf16[4,512,256]{2,1,0:T(8,128)(2,1)S(1)}, u32[]{:S(2)}, u32[]{:S(2)}) collective-permute-start(bf16[4,512,256]{2,1,0:T(8,128)(2,1)S(1)} %collective-permute-done.6.refs_6_), channel_id=1, source_target_pairs={{0,16},{16,0},{32,48},{48,32},{64,80},{80,64},{96,112},{112,96},{1... | collective-permute-start | bytes 3145736 | tf_op jit(solution)/shard_map/ppermute | solution.py:572
  47.7 0.0 collective-permute-start.14
  47.7 20.7 %collective-permute-done.11.refs_1_.refs_4_ = bf16[1104,512]{1,0:T(8,128)(2,1)S(1)} collective-permute-done((bf16[1104,512]{1,0:T(8,128)(2,1)S(1)}, bf16[1104,512]{1,0:T(8,128)(2,1)S(1)}, u32[]{:S(2)}, u32[]{:S(2)}) %collective-permute-start.11) | collective-permute-done | bytes 1130528 | tf_op jit(solution)/shard_map/ppermute | solution.py:563
  68.4 0.0 collective-permute-done.12.refs_2_.refs_5_
  68.4 0.0 collective-permute-done.10.refs_10_
  68.4 0.0 collective-permute-start.15
  68.4 0.0 collective-permute-done.13.refs_8_
  68.4 0.0 collective-permute-done.14.refs_9_
  68.4 2.6 %collective-permute-done.15.refs_11_ = bf16[4,512,256]{2,1,0:T(8,128)(2,1)S(1)} collective-permute-done((bf16[4,512,256]{2,1,0:T(8,128)(2,1)S(1)}, bf16[4,512,256]{2,1,0:T(8,128)(2,1)S(1)}, u32[]{:S(2)}, u32[]{:S(2)}) %collective-permute-start.15) | collective-permute-done | bytes 1048608 | tf_op jit(solution)/shard_map/ppermute | solution.py:575
  71.1 2.3 %product_far.1 = (bf16[256,1024]{1,0:T(8,128)(2,1)S(1)}, bf16[256,1024]{1,0:T(8,128)(2,1)S(1)}) custom-call(bf16[1024,512]{1,0:T(8,128)(2,1)S(1)} %get-tuple-element.90.refs_0_, bf16[1104,512]{1,0:T(8,128)(2,1)S(1)} %collective-permute-done.11.refs_1_.refs_4_, bf16[1104,512]{1,0:T(8,128)(2,1)S(1)} %collective-permute-done.12.refs_2_.refs_5_, ...), custom_call_target="tpu_custom_call" | custom-call | flops 1000 | bytes 1000 | tf_op jit(solution)/shard_map/product_far/pallas_call | solution.py:266
  73.4 2.0 %collective-permute-start.17 = (bf16[256,1024]{1,0:T(8,128)(2,1)S(1)}, bf16[256,1024]{1,0:T(8,128)(2,1)S(1)}, u32[]{:S(2)}, u32[]{:S(2)}) collective-permute-start(bf16[256,1024]{1,0:T(8,128)(2,1)S(1)} %get-tuple-element.80), channel_id=1, source_target_pairs={{0,4},{1,5},{2,6},{3,7},{4,8},{5,9},{6,10},{7,11},{8,12},{9,13},{1... | collective-permute-start | bytes 1572872 | tf_op jit(solution)/shard_map/ppermute | solution.py:585
  75.4 2.2 %collective-permute-start.18 = (bf16[256,1024]{1,0:T(8,128)(2,1)S(1)}, bf16[256,1024]{1,0:T(8,128)(2,1)S(1)}, u32[]{:S(2)}, u32[]{:S(2)}) collective-permute-start(bf16[256,1024]{1,0:T(8,128)(2,1)S(1)} %get-tuple-element.81), channel_id=1, source_target_pairs={{0,12},{1,13},{2,14},{3,15},{4,0},{5,1},{6,2},{7,3},{8,4},{9,5},{1... | collective-permute-start | bytes 1572872 | tf_op jit(solution)/shard_map/ppermute | solution.py:586
  77.6 1.5 %collective-permute-start.16 = (bf16[336,512]{1,0:T(8,128)(2,1)S(1)}, bf16[336,512]{1,0:T(8,128)(2,1)S(1)}, u32[]{:S(2)}, u32[]{:S(2)}) collective-permute-start(bf16[336,512]{1,0:T(8,128)(2,1)S(1)} %get-tuple-element.75), channel_id=1, source_target_pairs={{0,2},{1,3},{2,0},{3,1},{4,6},{5,7},{6,4},{7,5},{8,10},{9,11},{10,... | collective-permute-start | bytes 1032200 | tf_op jit(solution)/shard_map/ppermute | solution.py:584
  79.1 4.5 %product_near.1 = (bf16[256,1024]{1,0:T(8,128)(2,1)S(1)}, bf16[256,1024]{1,0:T(8,128)(2,1)S(1)}, bf16[256,1024]{1,0:T(8,128)(2,1)S(1)}, bf16[256,1024]{1,0:T(8,128)(2,1)S(1)}) custom-call(bf16[1024,512]{1,0:T(8,128)(2,1)S(1)} %get-tuple-element.90.refs_0_, bf16[1104,512]{1,0:T(8,128)(2,1)S(1)} %collective-permute-done.11.refs_1_.refs_4_, ...), custom_call_target="tpu_custom_call" | custom-call | flops 1000 | bytes 1000 | tf_op jit(solution)/shard_map/product_near/pallas_call | solution.py:244
  83.5 5.4 %collective-permute-done.16.refs_6_.refs_3_ = bf16[336,512]{1,0:T(8,128)(2,1)S(1)} collective-permute-done((bf16[336,512]{1,0:T(8,128)(2,1)S(1)}, bf16[336,512]{1,0:T(8,128)(2,1)S(1)}, u32[]{:S(2)}, u32[]{:S(2)}) %collective-permute-start.16) | collective-permute-done | bytes 344096 | tf_op jit(solution)/shard_map/ppermute | solution.py:584
  88.9 0.0 collective-permute-start.20
  88.9 3.2 %collective-permute-start.21 = (bf16[256,1024]{1,0:T(8,128)(2,1)S(1)}, bf16[256,1024]{1,0:T(8,128)(2,1)S(1)}, u32[]{:S(2)}, u32[]{:S(2)}) collective-permute-start(bf16[256,1024]{1,0:T(8,128)(2,1)S(1)} %get-tuple-element.97), channel_id=1, source_target_pairs={{0,12},{1,13},{2,14},{3,15},{4,0},{5,1},{6,2},{7,3},{8,4},{9,5},{1... | collective-permute-start | bytes 1572872 | tf_op jit(solution)/shard_map/ppermute | solution.py:589
  92.2 0.0 collective-permute-done.17.from_down
  92.2 0.0 collective-permute-done.18.from_up
  92.2 0.2 relay_sums.1
  92.4 0.1 collective-permute-start.19
  92.5 3.2 %collective-permute-start.22 = (bf16[256,1024]{1,0:T(8,128)(2,1)S(1)}, bf16[256,1024]{1,0:T(8,128)(2,1)S(1)}, u32[]{:S(2)}, u32[]{:S(2)}) collective-permute-start(bf16[256,1024]{1,0:T(8,128)(2,1)S(1)} %get-tuple-element.98), channel_id=1, source_target_pairs={{0,12},{1,13},{2,14},{3,15},{4,0},{5,1},{6,2},{7,3},{8,4},{9,5},{1... | collective-permute-start | bytes 1572872 | tf_op jit(solution)/shard_map/ppermute | solution.py:595
  96.4 0.8 unpack.1
  97.2 0.0 copy-start.3
  97.2 4.3 %pool_attention.1.pool = f32[16,72,128]{2,1,0:T(8,128)S(1)} custom-call(s32[16]{0:T(128)S(1)} %get-tuple-element.86.slots, s32[16]{0:T(128)S(1)} %get-tuple-element.87.alive, bf16[16,64,128]{2,1,0:T(8,128)(2,1)S(1)} %get-tuple-element.88.query, bf16[16,128,2048]{2,1,0:T(8,128)(2,1)S(1)} %bitcast.11, bf16[16,128,2048]{2,1,0:T(8,128)(2,1)S(1)} %bitcast.12, ...), custom_call_target="tpu_custom_call" | custom-call | flops 1000 | bytes 1000 | tf_op jit(solution)/shard_map/pool_attention/pallas_call | solution.py:333
  101.5 3.4 %copy-done.1 = bf16[1,1,16,128,2048]{4,3,2,1,0:T(8,128)(2,1)S(1)} copy-done((bf16[1,1,16,128,2048]{4,3,2,1,0:T(8,128)(2,1)S(1)}, bf16[1,1,16,128,2048]{4,3,2,1,0:T(8,128)(2,1)}, u32[]{:S(2)}) %copy-start.1) | copy-done | bytes 8388632
  104.9 0.2 local_attention.1.local
  105.2 2.3 %product_own.1 = (f32[256,1024]{1,0:T(8,128)S(1)}, f32[256,1024]{1,0:T(8,128)S(1)}) custom-call(bf16[1024,512]{1,0:T(8,128)(2,1)S(1)} %get-tuple-element.90.refs_0_, bf16[1104,512]{1,0:T(8,128)(2,1)S(1)} %collective-permute-done.11.refs_1_.refs_4_, bf16[1104,512]{1,0:T(8,128)(2,1)S(1)} %collective-permute-done.12.refs_2_.refs_5_, ...), custom_call_target="tpu_custom_call" | custom-call | flops 1000 | bytes 1000 | tf_op jit(solution)/shard_map/product_own/pallas_call | solution.py:244
  107.5 0.0 collective-permute-done.21.down_l
  107.5 6.7 %collective-permute-done.19.up_l = bf16[256,1024]{1,0:T(8,128)(2,1)S(1)} collective-permute-done((bf16[256,1024]{1,0:T(8,128)(2,1)S(1)}, bf16[256,1024]{1,0:T(8,128)(2,1)S(1)}, u32[]{:S(2)}, u32[]{:S(2)}) %collective-permute-start.19) | collective-permute-done | bytes 524320 | tf_op jit(solution)/shard_map/ppermute | solution.py:592
  114.2 0.0 collective-permute-done.22.down_r
  114.2 3.9 %prefix_attention.1 = (bf16[1,256,2048]{2,1,0:T(8,128)(2,1)}, bf16[16,80,128]{2,1,0:T(8,128)(2,1)S(1)}) custom-call(s32[1]{0:T(128)S(6)} %copy.12.prompt_pages, f32[256,1024]{1,0:T(8,128)S(1)} %get-tuple-element.94.own_l, f32[256,1024]{1,0:T(8,128)S(1)} %get-tuple-element.95.own_r, bf16[256,1024]{1,0:T(8,128)(2,1)S(1)} %collective-permute-done.19.up_l, ...), custom_call_target="tpu_custom_call" | custom-call | flops 300000000 | bytes 6291456 | tf_op jit(solution)/shard_map/prefix_attention/pallas_call | solution.py:496
  118.1 14.6 %all_to_all.5.arrived = bf16[16,80,128]{2,1,0:T(8,128)(2,1)S(1)} all-to-all(bf16[16,80,128]{2,1,0:T(8,128)(2,1)S(1)} %get-tuple-element.102), channel_id=1, replica_groups=mesh['prompt'=8,'sample'=16] {'sample'}, dimensions={0} | all-to-all | bytes 655360 | tf_op jit(solution)/shard_map/all_to_all | solution.py:607
  132.6 0.3 combine.1
  133.0 0.6 reshape.15
  (12 shorter events, 0.0 us)
Async XLA Ops:
  0.6 9.7 %collective-permute-start = (bf16[512,256]{1,0:T(8,128)(2,1)}, bf16[512,256]{1,0:T(8,128)(2,1)S(1)}, u32[]{:S(2)}, u32[]{:S(2)}) collective-permute-start(bf16[512,256]{1,0:T(8,128)(2,1)} %param.11), channel_id=1, source_target_pairs={{0,1},{1,2},{2,3},{3,0},{4,5},{5,6},{6,7},{7,4},{8,9},{9,10},{10,1... | collective-permute-start | bytes 786440 | tf_op jit(solution)/shard_map/ppermute | solution.py:552
  2.3 9.4 %collective-permute-start.1 = (bf16[512,256]{1,0:T(8,128)(2,1)}, bf16[512,256]{1,0:T(8,128)(2,1)S(1)}, u32[]{:S(2)}, u32[]{:S(2)}) collective-permute-start(bf16[512,256]{1,0:T(8,128)(2,1)} %param.11), channel_id=1, source_target_pairs={{0,3},{1,0},{2,1},{3,2},{4,7},{5,4},{6,5},{7,6},{8,11},{9,8},{10,9... | collective-permute-start | bytes 786440 | tf_op jit(solution)/shard_map/ppermute | solution.py:553
  3.9 12.9 %collective-permute-start.2 = (bf16[512,256]{1,0:T(8,128)(2,1)}, bf16[512,256]{1,0:T(8,128)(2,1)S(1)}, u32[]{:S(2)}, u32[]{:S(2)}) collective-permute-start(bf16[512,256]{1,0:T(8,128)(2,1)} %param.11), channel_id=1, source_target_pairs={{0,2},{1,3},{2,0},{3,1},{4,6},{5,7},{6,4},{7,5},{8,10},{9,11},{10,... | collective-permute-start | bytes 786440 | tf_op jit(solution)/shard_map/ppermute | solution.py:551
  5.8 3.1 %copy-start.4 = (s32[1,1,16]{2,1,0:T(1,128)S(1)}, s32[1,1,16]{2,1,0:T(1,128)}, u32[]{:S(2)}) copy-start(s32[1,1,16]{2,1,0:T(1,128)} %where.1) | copy-start | bytes 196
  5.8 28.3 %copy-start = (bf16[1,4096,512]{2,1,0:T(8,128)(2,1)S(1)}, bf16[1,4096,512]{2,1,0:T(8,128)(2,1)}, u32[]{:S(2)}) copy-start(bf16[1,4096,512]{2,1,0:T(8,128)(2,1)} %param.10) | copy-start | bytes 12582916
  9.0 0.8 copy-start.2
  17.9 2.7 %collective-permute-start.7 = (bf16[4,512,256]{2,1,0:T(8,128)(2,1)S(1)}, bf16[4,512,256]{2,1,0:T(8,128)(2,1)S(1)}, u32[]{:S(2)}, u32[]{:S(2)}) collective-permute-start(bf16[4,512,256]{2,1,0:T(8,128)(2,1)S(1)} %pad_maximum_fusion.refs_4_), channel_id=1, source_target_pairs={{0,16},{16,0},{32,48},{48,32},{64,80},{80,64},{96,112},{112,96},{1... | collective-permute-start | bytes 3145736 | tf_op jit(solution)/shard_map/ppermute | solution.py:568
  18.0 25.9 %collective-permute-start.6 = (bf16[4,512,256]{2,1,0:T(8,128)(2,1)S(1)}, bf16[4,512,256]{2,1,0:T(8,128)(2,1)S(1)}, u32[]{:S(2)}, u32[]{:S(2)}) collective-permute-start(bf16[4,512,256]{2,1,0:T(8,128)(2,1)S(1)} %pad_maximum_fusion.refs_4_), channel_id=1, source_target_pairs={{0,32},{16,112},{32,64},{48,16},{64,96},{80,48},{96,0},{112,80},{1... | collective-permute-start | bytes 3145736 | tf_op jit(solution)/shard_map/ppermute | solution.py:567
  20.7 24.7 %collective-permute-start.8 = (bf16[4,512,256]{2,1,0:T(8,128)(2,1)S(1)}, bf16[4,512,256]{2,1,0:T(8,128)(2,1)S(1)}, u32[]{:S(2)}, u32[]{:S(2)}) collective-permute-start(bf16[4,512,256]{2,1,0:T(8,128)(2,1)S(1)} %collective-permute-done.7.refs_5_), channel_id=1, source_target_pairs={{0,32},{16,112},{32,64},{48,16},{64,96},{80,48},{96,0},{112,80},{1... | collective-permute-start | bytes 3145736 | tf_op jit(solution)/shard_map/ppermute | solution.py:569
  22.3 21.7 %collective-permute-start.9 = (bf16[768,512]{1,0:T(8,128)(2,1)S(1)}, bf16[768,512]{1,0:T(8,128)(2,1)S(1)}, u32[]{:S(2)}, u32[]{:S(2)}) collective-permute-start(bf16[768,512]{1,0:T(8,128)(2,1)S(1)} %get-tuple-element.63), channel_id=1, source_target_pairs={{0,2},{1,3},{2,0},{3,1},{4,6},{5,7},{6,4},{7,5},{8,10},{9,11},{10,... | collective-permute-start | bytes 2359304 | tf_op jit(solution)/shard_map/ppermute | solution.py:562
  23.1 5.8 %collective-permute-start.3 = (bf16[40,256]{1,0:T(8,128)(2,1)S(1)}, bf16[40,256]{1,0:T(8,128)(2,1)S(1)}, u32[]{:S(2)}, u32[]{:S(2)}) collective-permute-start(bf16[40,256]{1,0:T(8,128)(2,1)S(1)} %get-tuple-element.57.refs_0_), channel_id=1, source_target_pairs={{0,4},{1,5},{2,6},{3,7},{4,8},{5,9},{6,10},{7,11},{8,12},{9,13},{1... | collective-permute-start | bytes 61448 | tf_op jit(solution)/shard_map/ppermute | solution.py:560
  25.0 5.9 %collective-permute-start.4 = (bf16[40,256]{1,0:T(8,128)(2,1)S(1)}, bf16[40,256]{1,0:T(8,128)(2,1)S(1)}, u32[]{:S(2)}, u32[]{:S(2)}) collective-permute-start(bf16[40,256]{1,0:T(8,128)(2,1)S(1)} %get-tuple-element.57.refs_0_), channel_id=1, source_target_pairs={{0,12},{1,13},{2,14},{3,15},{4,0},{5,1},{6,2},{7,3},{8,4},{9,5},{1... | collective-permute-start | bytes 61448 | tf_op jit(solution)/shard_map/ppermute | solution.py:560
  28.9 5.3 %collective-permute-start.5 = (bf16[40,256]{1,0:T(8,128)(2,1)S(1)}, bf16[40,256]{1,0:T(8,128)(2,1)S(1)}, u32[]{:S(2)}, u32[]{:S(2)}) collective-permute-start(bf16[40,256]{1,0:T(8,128)(2,1)S(1)} %get-tuple-element.57.refs_0_), channel_id=1, source_target_pairs={{0,8},{1,9},{2,10},{3,11},{4,12},{5,13},{6,14},{7,15},{8,0},{9,1},... | collective-permute-start | bytes 61448 | tf_op jit(solution)/shard_map/ppermute | solution.py:560
  34.5 33.9 %collective-permute-start.11 = (bf16[1104,512]{1,0:T(8,128)(2,1)S(1)}, bf16[1104,512]{1,0:T(8,128)(2,1)S(1)}, u32[]{:S(2)}, u32[]{:S(2)}) collective-permute-start(bf16[1104,512]{1,0:T(8,128)(2,1)S(1)} %get-tuple-element.65), channel_id=1, source_target_pairs={{0,1},{1,2},{2,3},{3,0},{4,5},{5,6},{6,7},{7,4},{8,9},{9,10},{10,1... | collective-permute-start | bytes 3391496 | tf_op jit(solution)/shard_map/ppermute | solution.py:563
  36.5 31.9 %collective-permute-start.12 = (bf16[1104,512]{1,0:T(8,128)(2,1)S(1)}, bf16[1104,512]{1,0:T(8,128)(2,1)S(1)}, u32[]{:S(2)}, u32[]{:S(2)}) collective-permute-start(bf16[1104,512]{1,0:T(8,128)(2,1)S(1)} %get-tuple-element.66), channel_id=1, source_target_pairs={{0,3},{1,0},{2,1},{3,2},{4,7},{5,4},{6,5},{7,6},{8,11},{9,8},{10,9... | collective-permute-start | bytes 3391496 | tf_op jit(solution)/shard_map/ppermute | solution.py:564
  45.3 23.1 %collective-permute-start.10 = (bf16[4,512,256]{2,1,0:T(8,128)(2,1)S(1)}, bf16[4,512,256]{2,1,0:T(8,128)(2,1)S(1)}, u32[]{:S(2)}, u32[]{:S(2)}) collective-permute-start(bf16[4,512,256]{2,1,0:T(8,128)(2,1)S(1)} %collective-permute-done.6.refs_6_), channel_id=1, source_target_pairs={{0,32},{16,112},{32,64},{48,16},{64,96},{80,48},{96,0},{112,80},{1... | collective-permute-start | bytes 3145736 | tf_op jit(solution)/shard_map/ppermute | solution.py:571
  45.9 22.6 %collective-permute-start.13 = (bf16[4,512,256]{2,1,0:T(8,128)(2,1)S(1)}, bf16[4,512,256]{2,1,0:T(8,128)(2,1)S(1)}, u32[]{:S(2)}, u32[]{:S(2)}) collective-permute-start(bf16[4,512,256]{2,1,0:T(8,128)(2,1)S(1)} %collective-permute-done.6.refs_6_), channel_id=1, source_target_pairs={{0,16},{16,0},{32,48},{48,32},{64,80},{80,64},{96,112},{112,96},{1... | collective-permute-start | bytes 3145736 | tf_op jit(solution)/shard_map/ppermute | solution.py:572
  47.7 20.8 %collective-permute-start.14 = (bf16[4,512,256]{2,1,0:T(8,128)(2,1)S(1)}, bf16[4,512,256]{2,1,0:T(8,128)(2,1)S(1)}, u32[]{:S(2)}, u32[]{:S(2)}) collective-permute-start(bf16[4,512,256]{2,1,0:T(8,128)(2,1)S(1)} %collective-permute-done.8.refs_7_), channel_id=1, source_target_pairs={{0,16},{16,0},{32,48},{48,32},{64,80},{80,64},{96,112},{112,96},{1... | collective-permute-start | bytes 3145736 | tf_op jit(solution)/shard_map/ppermute | solution.py:573
  68.4 2.7 %collective-permute-start.15 = (bf16[4,512,256]{2,1,0:T(8,128)(2,1)S(1)}, bf16[4,512,256]{2,1,0:T(8,128)(2,1)S(1)}, u32[]{:S(2)}, u32[]{:S(2)}) collective-permute-start(bf16[4,512,256]{2,1,0:T(8,128)(2,1)S(1)} %collective-permute-done.10.refs_10_), channel_id=1, source_target_pairs={{0,16},{16,0},{32,48},{48,32},{64,80},{80,64},{96,112},{112,96},{1... | collective-permute-start | bytes 3145736 | tf_op jit(solution)/shard_map/ppermute | solution.py:575
  71.1 26.1 %slice-start = ((s8[8388608]{0:T(1024)(128)(4,1)}), s8[4194304]{0:T(1024)(128)(4,1)S(1)}, s32[]{:S(2)}) async-start(s8[8388608]{0:T(1024)(128)(4,1)} %bitcast.9), calls=%async_computation.1 | async-start | bytes 8388608
  73.4 18.8 %collective-permute-start.17 = (bf16[256,1024]{1,0:T(8,128)(2,1)S(1)}, bf16[256,1024]{1,0:T(8,128)(2,1)S(1)}, u32[]{:S(2)}, u32[]{:S(2)}) collective-permute-start(bf16[256,1024]{1,0:T(8,128)(2,1)S(1)} %get-tuple-element.80), channel_id=1, source_target_pairs={{0,4},{1,5},{2,6},{3,7},{4,8},{5,9},{6,10},{7,11},{8,12},{9,13},{1... | collective-permute-start | bytes 1572872 | tf_op jit(solution)/shard_map/ppermute | solution.py:585
  75.4 16.8 %collective-permute-start.18 = (bf16[256,1024]{1,0:T(8,128)(2,1)S(1)}, bf16[256,1024]{1,0:T(8,128)(2,1)S(1)}, u32[]{:S(2)}, u32[]{:S(2)}) collective-permute-start(bf16[256,1024]{1,0:T(8,128)(2,1)S(1)} %get-tuple-element.81), channel_id=1, source_target_pairs={{0,12},{1,13},{2,14},{3,15},{4,0},{5,1},{6,2},{7,3},{8,4},{9,5},{1... | collective-permute-start | bytes 1572872 | tf_op jit(solution)/shard_map/ppermute | solution.py:586
  77.6 19.6 %slice-start.1 = ((s8[8388608]{0:T(1024)(128)(4,1)}), s8[4194304]{0:T(1024)(128)(4,1)S(1)}, s32[]{:S(2)}) async-start(s8[8388608]{0:T(1024)(128)(4,1)} %bitcast.9), calls=%async_computation.2 | async-start | bytes 8388608
  77.6 11.3 %collective-permute-start.16 = (bf16[336,512]{1,0:T(8,128)(2,1)S(1)}, bf16[336,512]{1,0:T(8,128)(2,1)S(1)}, u32[]{:S(2)}, u32[]{:S(2)}) collective-permute-start(bf16[336,512]{1,0:T(8,128)(2,1)S(1)} %get-tuple-element.75), channel_id=1, source_target_pairs={{0,2},{1,3},{2,0},{3,1},{4,6},{5,7},{6,4},{7,5},{8,10},{9,11},{10,... | collective-permute-start | bytes 1032200 | tf_op jit(solution)/shard_map/ppermute | solution.py:584
  88.9 18.6 %collective-permute-start.20 = (bf16[256,1024]{1,0:T(8,128)(2,1)S(1)}, bf16[256,1024]{1,0:T(8,128)(2,1)S(1)}, u32[]{:S(2)}, u32[]{:S(2)}) collective-permute-start(bf16[256,1024]{1,0:T(8,128)(2,1)S(1)} %get-tuple-element.96), channel_id=1, source_target_pairs={{0,4},{1,5},{2,6},{3,7},{4,8},{5,9},{6,10},{7,11},{8,12},{9,13},{1... | collective-permute-start | bytes 1572872 | tf_op jit(solution)/shard_map/ppermute | solution.py:589
  88.9 18.6 %collective-permute-start.21 = (bf16[256,1024]{1,0:T(8,128)(2,1)S(1)}, bf16[256,1024]{1,0:T(8,128)(2,1)S(1)}, u32[]{:S(2)}, u32[]{:S(2)}) collective-permute-start(bf16[256,1024]{1,0:T(8,128)(2,1)S(1)} %get-tuple-element.97), channel_id=1, source_target_pairs={{0,12},{1,13},{2,14},{3,15},{4,0},{5,1},{6,2},{7,3},{8,4},{9,5},{1... | collective-permute-start | bytes 1572872 | tf_op jit(solution)/shard_map/ppermute | solution.py:589
  92.4 21.8 %collective-permute-start.19 = (bf16[256,1024]{1,0:T(8,128)(2,1)S(1)}, bf16[256,1024]{1,0:T(8,128)(2,1)S(1)}, u32[]{:S(2)}, u32[]{:S(2)}) collective-permute-start(bf16[256,1024]{1,0:T(8,128)(2,1)S(1)} %get-tuple-element.82), channel_id=1, source_target_pairs={{0,4},{1,5},{2,6},{3,7},{4,8},{5,9},{6,10},{7,11},{8,12},{9,13},{1... | collective-permute-start | bytes 1572872 | tf_op jit(solution)/shard_map/ppermute | solution.py:592
  92.5 21.7 %collective-permute-start.22 = (bf16[256,1024]{1,0:T(8,128)(2,1)S(1)}, bf16[256,1024]{1,0:T(8,128)(2,1)S(1)}, u32[]{:S(2)}, u32[]{:S(2)}) collective-permute-start(bf16[256,1024]{1,0:T(8,128)(2,1)S(1)} %get-tuple-element.98), channel_id=1, source_target_pairs={{0,12},{1,13},{2,14},{3,15},{4,0},{5,1},{6,2},{7,3},{8,4},{9,5},{1... | collective-permute-start | bytes 1572872 | tf_op jit(solution)/shard_map/ppermute | solution.py:595
  97.2 4.3 %copy-start.3 = (bf16[1,1,2048]{2,1,0:T(2,128)(2,1)S(1)}, bf16[1,1,2048]{2,1,0:T(2,128)(2,1)}, u32[]{:S(2)}) copy-start(bf16[1,1,2048]{2,1,0:T(2,128)(2,1)} %param.13) | copy-start | bytes 12292
  101.5 3.4 %copy-start.1 = (bf16[1,1,16,128,2048]{4,3,2,1,0:T(8,128)(2,1)S(1)}, bf16[1,1,16,128,2048]{4,3,2,1,0:T(8,128)(2,1)}, u32[]{:S(2)}) copy-start(bf16[1,1,16,128,2048]{4,3,2,1,0:T(8,128)(2,1)} %param.14) | copy-start | bytes 25165828

commit v6 on v5

--- a/solution.py
+++ b/solution.py
@@ -585,7 +585,6 @@
     from_down = lax.ppermute(far_l, "sample", Z_UP)
     from_up = lax.ppermute(far_r, "sample", Z_DOWN)
     up_l, up_r, down_l, down_r = product(others, pieces, ((1,) * 4, (2,) * 4), BF16, "product_near")
-    up_r, down_l, last_far = tie((up_r, down_l, last_far))
     up_r, down_l = lax.ppermute(up_r, "sample", Z_UP), lax.ppermute(down_l, "sample", Z_DOWN)
     up_l, down_r = relay(up_l, down_r, from_down, from_up)
     sums = [
@@ -595,11 +594,12 @@
         lax.ppermute(down_r, "sample", Z_DOWN),
     ]
 
-    arrived, query, up_l = tie(([rows_right, rows_left, last_far], query, up_l))
+    query, up_l = tie((query, up_l))
+    local_alive = jnp.where(preempted[0] > 0, 0, comp_pages[0])
+    local = local_attention(local_alive, query, new_kv[0], local_pages[0, 0])
+    arrived, local = tie(([rows_right, rows_left, last_far], local))
     queries_all, by_group, slots, alive = unpack(blocks, arrived)
     pool = pool_attention(slots, alive, queries_all, pool_pages[0, 0])
-    local_alive = jnp.where(preempted[0] > 0, 0, comp_pages[0])
-    local = local_attention(local_alive, query, new_kv[0], local_pages[0, 0])
     mine, pool, local = tie(([own_states, *arrived], pool, local))
     sums = [*product(mine, pieces, ((3, 3, 3, 0),), F32, "product_own"), *sums]
 

time: 134 us -> 132 us (0.985)
  waiting for transfers between devices: 55.5 us -> 53.3 us
    ppermute x1, waiting for transfers between devices: 6.66 us -> 0.88 us  [per_device(): lax.ppermute(up_l, 'sample', Z_UP)]
    ppermute x1, waiting for transfers between devices: 0.01 us -> 4.83 us  [per_device(): from_down = lax.ppermute(far_l, 'sample', Z_UP)]
    ppermute x1, starting transfers between devices: 0.08 us -> 1.96 us  [per_device(): lax.ppermute(up_l, 'sample', Z_UP)]
    ppermute x1, starting transfers between devices: 3.22 us -> 1.54 us  [per_device(): lax.ppermute(down_r, 'sample', Z_DOWN)]
  transfers between devices with their start and end apart: 23 -> 23, of which waited for: 11 -> 12; matrix products, arithmetic and copies ran while one was open for 0% -> 0% of each run, Pallas kernels for 11% -> 11%
where the time goes in v6:
time: 132 us
  waiting for transfers between devices  53.3 us (40%)
  starting transfers between devices  33.5 us (25%)
  Pallas kernels  21.4 us (16%)
  blocking collectives  14.6 us (11%)
  local copies, waits for them, and re-layouts  4.78 us (4%)
  between operations  2.97 us (2%)
    ppermute x1, waiting for transfers between devices, per_device(): rows_right = lax.ppermute(to_right, 'sample', X_RIGHT)  20.7 us
    all_to_all x1, blocking collectives, per_device(): lax.all_to_all(packed, 'sample', split_axis=0, concat_axis=0, tiled=True)  14.6 us
    pallas_call x2, Pallas kernels, product(): pl.pallas_call(functools.partial(product_kernel, blocks), out_shape=outs,...  6.81 us
    ppermute x1, waiting for transfers between devices, per_device(): rows_far = lax.ppermute(to_far, 'sample', X_FAR)  6.17 us
    ppermute x3, starting transfers between devices, per_device(): lax.ppermute(block, 'sample', to)  6.07 us
    ppermute x1, waiting for transfers between devices, per_device(): weight_far = lax.ppermute(kv_weight, 'sample', X_FAR)  5.14 us
    ppermute x3, waiting for transfers between devices, per_device(): lax.ppermute(block, 'sample', to)  5.01 us
    ppermute x1, waiting for transfers between devices, per_device(): from_down = lax.ppermute(far_l, 'sample', Z_UP)  4.83 us
  transfers between devices with their start and end apart: 23, of which 12 were waited for; matrix products, arithmetic and copies ran while one was open for 0% of the time, Pallas kernels for 11%

profile of v6, /device:TPU:0, one launch (start us, length us, event | category | flops | bytes accessed | tf_op | source)
XLA Modules:
  0.0 131.7 jit_solution(2912846408056726770)
XLA Ops:
  0.6 1.6 %collective-permute-start = (bf16[512,256]{1,0:T(8,128)(2,1)}, bf16[512,256]{1,0:T(8,128)(2,1)S(1)}, u32[]{:S(2)}, u32[]{:S(2)}) collective-permute-start(bf16[512,256]{1,0:T(8,128)(2,1)} %param.11), channel_id=1, source_target_pairs={{0,1},{1,2},{2,3},{3,0},{4,5},{5,6},{6,7},{7,4},{8,9},{9,10},{10,1... | collective-permute-start | bytes 786440 | tf_op jit(solution)/shard_map/ppermute | solution.py:552
  2.3 1.7 %collective-permute-start.1 = (bf16[512,256]{1,0:T(8,128)(2,1)}, bf16[512,256]{1,0:T(8,128)(2,1)S(1)}, u32[]{:S(2)}, u32[]{:S(2)}) collective-permute-start(bf16[512,256]{1,0:T(8,128)(2,1)} %param.11), channel_id=1, source_target_pairs={{0,3},{1,0},{2,1},{3,2},{4,7},{5,4},{6,5},{7,6},{8,11},{9,8},{10,9... | collective-permute-start | bytes 786440 | tf_op jit(solution)/shard_map/ppermute | solution.py:553
  3.9 1.9 %collective-permute-start.2 = (bf16[512,256]{1,0:T(8,128)(2,1)}, bf16[512,256]{1,0:T(8,128)(2,1)S(1)}, u32[]{:S(2)}, u32[]{:S(2)}) collective-permute-start(bf16[512,256]{1,0:T(8,128)(2,1)} %param.11), channel_id=1, source_target_pairs={{0,2},{1,3},{2,0},{3,1},{4,6},{5,7},{6,4},{7,5},{8,10},{9,11},{10,... | collective-permute-start | bytes 786440 | tf_op jit(solution)/shard_map/ppermute | solution.py:551
  5.8 1.6 %pick_far.1 = (bf16[1024,512]{1,0:T(8,128)(2,1)S(1)}, bf16[768,512]{1,0:T(8,128)(2,1)S(1)}) custom-call(bf16[4,4,256,512]{3,2,1,0:T(8,128)(2,1)} %bitcast.15), custom_call_target="tpu_custom_call" | custom-call | flops 1000 | bytes 1000 | tf_op jit(solution)/shard_map/pick_far/pallas_call | solution.py:178
  9.0 0.0 copy-start.2
  9.0 0.7 copy-done.2
  9.7 0.6 prepare.1
  10.3 0.0 collective-permute-done
  10.3 1.4 %collective-permute-done.1 = bf16[512,256]{1,0:T(8,128)(2,1)S(1)} collective-permute-done((bf16[512,256]{1,0:T(8,128)(2,1)}, bf16[512,256]{1,0:T(8,128)(2,1)S(1)}, u32[]{:S(2)}, u32[]{:S(2)}) %collective-permute-start.1) | collective-permute-done | bytes 262176 | tf_op jit(solution)/shard_map/ppermute | solution.py:553
  11.7 5.1 %collective-permute-done.2 = bf16[512,256]{1,0:T(8,128)(2,1)S(1)} collective-permute-done((bf16[512,256]{1,0:T(8,128)(2,1)}, bf16[512,256]{1,0:T(8,128)(2,1)S(1)}, u32[]{:S(2)}, u32[]{:S(2)}) %collective-permute-start.2) | collective-permute-done | bytes 262176 | tf_op jit(solution)/shard_map/ppermute | solution.py:551
  16.9 1.1 pad_maximum_fusion.refs_4_
  17.9 0.1 collective-permute-start.7
  18.0 1.6 %collective-permute-start.6 = (bf16[4,512,256]{2,1,0:T(8,128)(2,1)S(1)}, bf16[4,512,256]{2,1,0:T(8,128)(2,1)S(1)}, u32[]{:S(2)}, u32[]{:S(2)}) collective-permute-start(bf16[4,512,256]{2,1,0:T(8,128)(2,1)S(1)} %pad_maximum_fusion.refs_4_), channel_id=1, source_target_pairs={{0,32},{16,112},{32,64},{48,16},{64,96},{80,48},{96,0},{112,80},{1... | collective-permute-start | bytes 3145736 | tf_op jit(solution)/shard_map/ppermute | solution.py:567
  19.7 1.0 collective-permute-done.7.refs_5_
  20.7 1.6 %collective-permute-start.8 = (bf16[4,512,256]{2,1,0:T(8,128)(2,1)S(1)}, bf16[4,512,256]{2,1,0:T(8,128)(2,1)S(1)}, u32[]{:S(2)}, u32[]{:S(2)}) collective-permute-start(bf16[4,512,256]{2,1,0:T(8,128)(2,1)S(1)} %collective-permute-done.7.refs_5_), channel_id=1, source_target_pairs={{0,32},{16,112},{32,64},{48,16},{64,96},{80,48},{96,0},{112,80},{1... | collective-permute-start | bytes 3145736 | tf_op jit(solution)/shard_map/ppermute | solution.py:569
  22.3 0.8 collective-permute-start.9
  23.1 1.9 %collective-permute-start.3 = (bf16[40,256]{1,0:T(8,128)(2,1)S(1)}, bf16[40,256]{1,0:T(8,128)(2,1)S(1)}, u32[]{:S(2)}, u32[]{:S(2)}) collective-permute-start(bf16[40,256]{1,0:T(8,128)(2,1)S(1)} %get-tuple-element.55.refs_0_), channel_id=1, source_target_pairs={{0,4},{1,5},{2,6},{3,7},{4,8},{5,9},{6,10},{7,11},{8,12},{9,13},{1... | collective-permute-start | bytes 61448 | tf_op jit(solution)/shard_map/ppermute | solution.py:560
  25.0 2.1 %collective-permute-start.4 = (bf16[40,256]{1,0:T(8,128)(2,1)S(1)}, bf16[40,256]{1,0:T(8,128)(2,1)S(1)}, u32[]{:S(2)}, u32[]{:S(2)}) collective-permute-start(bf16[40,256]{1,0:T(8,128)(2,1)S(1)} %get-tuple-element.55.refs_0_), channel_id=1, source_target_pairs={{0,12},{1,13},{2,14},{3,15},{4,0},{5,1},{6,2},{7,3},{8,4},{9,5},{1... | collective-permute-start | bytes 61448 | tf_op jit(solution)/shard_map/ppermute | solution.py:560
  27.1 1.8 %collective-permute-done.3.refs_1_ = bf16[40,256]{1,0:T(8,128)(2,1)S(1)} collective-permute-done((bf16[40,256]{1,0:T(8,128)(2,1)S(1)}, bf16[40,256]{1,0:T(8,128)(2,1)S(1)}, u32[]{:S(2)}, u32[]{:S(2)}) %collective-permute-start.3) | collective-permute-done | bytes 20512 | tf_op jit(solution)/shard_map/ppermute | solution.py:560
  28.9 2.0 %collective-permute-start.5 = (bf16[40,256]{1,0:T(8,128)(2,1)S(1)}, bf16[40,256]{1,0:T(8,128)(2,1)S(1)}, u32[]{:S(2)}, u32[]{:S(2)}) collective-permute-start(bf16[40,256]{1,0:T(8,128)(2,1)S(1)} %get-tuple-element.55.refs_0_), channel_id=1, source_target_pairs={{0,8},{1,9},{2,10},{3,11},{4,12},{5,13},{6,14},{7,15},{8,0},{9,1},... | collective-permute-start | bytes 61448 | tf_op jit(solution)/shard_map/ppermute | solution.py:560
  30.9 0.0 collective-permute-done.4.refs_2_
  30.9 3.2 %collective-permute-done.5.refs_3_ = bf16[40,256]{1,0:T(8,128)(2,1)S(1)} collective-permute-done((bf16[40,256]{1,0:T(8,128)(2,1)S(1)}, bf16[40,256]{1,0:T(8,128)(2,1)S(1)}, u32[]{:S(2)}, u32[]{:S(2)}) %collective-permute-start.5) | collective-permute-done | bytes 20512 | tf_op jit(solution)/shard_map/ppermute | solution.py:560
  34.2 0.3 pick_near.1
  34.5 2.1 %collective-permute-start.11 = (bf16[1104,512]{1,0:T(8,128)(2,1)S(1)}, bf16[1104,512]{1,0:T(8,128)(2,1)S(1)}, u32[]{:S(2)}, u32[]{:S(2)}) collective-permute-start(bf16[1104,512]{1,0:T(8,128)(2,1)S(1)} %get-tuple-element.63), channel_id=1, source_target_pairs={{0,1},{1,2},{2,3},{3,0},{4,5},{5,6},{6,7},{7,4},{8,9},{9,10},{10,1... | collective-permute-start | bytes 3391496 | tf_op jit(solution)/shard_map/ppermute | solution.py:563
  36.5 1.2 collective-permute-start.12
  37.8 6.2 %collective-permute-done.9.refs_3_ = bf16[768,512]{1,0:T(8,128)(2,1)S(1)} collective-permute-done((bf16[768,512]{1,0:T(8,128)(2,1)S(1)}, bf16[768,512]{1,0:T(8,128)(2,1)S(1)}, u32[]{:S(2)}, u32[]{:S(2)}) %collective-permute-start.9) | collective-permute-done | bytes 786464 | tf_op jit(solution)/shard_map/ppermute | solution.py:562
  43.9 0.0 collective-permute-done.6.refs_6_
  43.9 1.4 %collective-permute-done.8.refs_7_ = bf16[4,512,256]{2,1,0:T(8,128)(2,1)S(1)} collective-permute-done((bf16[4,512,256]{2,1,0:T(8,128)(2,1)S(1)}, bf16[4,512,256]{2,1,0:T(8,128)(2,1)S(1)}, u32[]{:S(2)}, u32[]{:S(2)}) %collective-permute-start.8) | collective-permute-done | bytes 1048608 | tf_op jit(solution)/shard_map/ppermute | solution.py:569
  45.3 0.5 collective-permute-start.10
  45.9 1.8 %collective-permute-start.14 = (bf16[4,512,256]{2,1,0:T(8,128)(2,1)S(1)}, bf16[4,512,256]{2,1,0:T(8,128)(2,1)S(1)}, u32[]{:S(2)}, u32[]{:S(2)}) collective-permute-start(bf16[4,512,256]{2,1,0:T(8,128)(2,1)S(1)} %collective-permute-done.6.refs_6_), channel_id=1, source_target_pairs={{0,16},{16,0},{32,48},{48,32},{64,80},{80,64},{96,112},{112,96},{1... | collective-permute-start | bytes 3145736 | tf_op jit(solution)/shard_map/ppermute | solution.py:572
  47.7 0.0 collective-permute-start.15
  47.7 20.7 %collective-permute-done.11.refs_1_.refs_4_ = bf16[1104,512]{1,0:T(8,128)(2,1)S(1)} collective-permute-done((bf16[1104,512]{1,0:T(8,128)(2,1)S(1)}, bf16[1104,512]{1,0:T(8,128)(2,1)S(1)}, u32[]{:S(2)}, u32[]{:S(2)}) %collective-permute-start.11) | collective-permute-done | bytes 1130528 | tf_op jit(solution)/shard_map/ppermute | solution.py:563
  68.4 0.0 collective-permute-done.12.refs_2_.refs_5_
  68.4 0.0 collective-permute-done.10.refs_10_
  68.4 0.0 collective-permute-start.16
  68.4 0.0 collective-permute-done.14.refs_8_
  68.4 0.0 collective-permute-done.15.refs_9_
  68.4 2.6 %collective-permute-done.16.refs_11_ = bf16[4,512,256]{2,1,0:T(8,128)(2,1)S(1)} collective-permute-done((bf16[4,512,256]{2,1,0:T(8,128)(2,1)S(1)}, bf16[4,512,256]{2,1,0:T(8,128)(2,1)S(1)}, u32[]{:S(2)}, u32[]{:S(2)}) %collective-permute-start.16) | collective-permute-done | bytes 1048608 | tf_op jit(solution)/shard_map/ppermute | solution.py:575
  71.1 2.3 %product_far.1 = (bf16[256,1024]{1,0:T(8,128)(2,1)S(1)}, bf16[256,1024]{1,0:T(8,128)(2,1)S(1)}) custom-call(bf16[1024,512]{1,0:T(8,128)(2,1)S(1)} %get-tuple-element.86.refs_0_, bf16[1104,512]{1,0:T(8,128)(2,1)S(1)} %collective-permute-done.11.refs_1_.refs_4_, bf16[1104,512]{1,0:T(8,128)(2,1)S(1)} %collective-permute-done.12.refs_2_.refs_5_, ...), custom_call_target="tpu_custom_call" | custom-call | flops 1000 | bytes 1000 | tf_op jit(solution)/shard_map/product_far/pallas_call | solution.py:266
  73.4 2.0 %collective-permute-start.17 = (bf16[256,1024]{1,0:T(8,128)(2,1)S(1)}, bf16[256,1024]{1,0:T(8,128)(2,1)S(1)}, u32[]{:S(2)}, u32[]{:S(2)}) collective-permute-start(bf16[256,1024]{1,0:T(8,128)(2,1)S(1)} %get-tuple-element.75), channel_id=1, source_target_pairs={{0,4},{1,5},{2,6},{3,7},{4,8},{5,9},{6,10},{7,11},{8,12},{9,13},{1... | collective-permute-start | bytes 1572872 | tf_op jit(solution)/shard_map/ppermute | solution.py:585
  75.4 2.2 %collective-permute-start.18 = (bf16[256,1024]{1,0:T(8,128)(2,1)S(1)}, bf16[256,1024]{1,0:T(8,128)(2,1)S(1)}, u32[]{:S(2)}, u32[]{:S(2)}) collective-permute-start(bf16[256,1024]{1,0:T(8,128)(2,1)S(1)} %get-tuple-element.76), channel_id=1, source_target_pairs={{0,12},{1,13},{2,14},{3,15},{4,0},{5,1},{6,2},{7,3},{8,4},{9,5},{1... | collective-permute-start | bytes 1572872 | tf_op jit(solution)/shard_map/ppermute | solution.py:586
  77.6 4.5 %product_near.1 = (bf16[256,1024]{1,0:T(8,128)(2,1)S(1)}, bf16[256,1024]{1,0:T(8,128)(2,1)S(1)}, bf16[256,1024]{1,0:T(8,128)(2,1)S(1)}, bf16[256,1024]{1,0:T(8,128)(2,1)S(1)}) custom-call(bf16[1024,512]{1,0:T(8,128)(2,1)S(1)} %get-tuple-element.86.refs_0_, bf16[1104,512]{1,0:T(8,128)(2,1)S(1)} %collective-permute-done.11.refs_1_.refs_4_, ...), custom_call_target="tpu_custom_call" | custom-call | flops 1000 | bytes 1000 | tf_op jit(solution)/shard_map/product_near/pallas_call | solution.py:244
  82.1 0.1 collective-permute-start.20
  82.2 3.2 %collective-permute-start.21 = (bf16[256,1024]{1,0:T(8,128)(2,1)S(1)}, bf16[256,1024]{1,0:T(8,128)(2,1)S(1)}, u32[]{:S(2)}, u32[]{:S(2)}) collective-permute-start(bf16[256,1024]{1,0:T(8,128)(2,1)S(1)} %get-tuple-element.93), channel_id=1, source_target_pairs={{0,12},{1,13},{2,14},{3,15},{4,0},{5,1},{6,2},{7,3},{8,4},{9,5},{1... | collective-permute-start | bytes 1572872 | tf_op jit(solution)/shard_map/ppermute | solution.py:588
  85.4 4.8 %collective-permute-done.17.from_down = bf16[256,1024]{1,0:T(8,128)(2,1)S(1)} collective-permute-done((bf16[256,1024]{1,0:T(8,128)(2,1)S(1)}, bf16[256,1024]{1,0:T(8,128)(2,1)S(1)}, u32[]{:S(2)}, u32[]{:S(2)}) %collective-permute-start.17) | collective-permute-done | bytes 524320 | tf_op jit(solution)/shard_map/ppermute | solution.py:585
  90.2 0.0 collective-permute-done.18.from_up
  90.2 0.2 relay_sums.1
  90.5 2.0 %collective-permute-start.19 = (bf16[256,1024]{1,0:T(8,128)(2,1)S(1)}, bf16[256,1024]{1,0:T(8,128)(2,1)S(1)}, u32[]{:S(2)}, u32[]{:S(2)}) collective-permute-start(bf16[256,1024]{1,0:T(8,128)(2,1)S(1)} %get-tuple-element.77), channel_id=1, source_target_pairs={{0,4},{1,5},{2,6},{3,7},{4,8},{5,9},{6,10},{7,11},{8,12},{9,13},{1... | collective-permute-start | bytes 1572872 | tf_op jit(solution)/shard_map/ppermute | solution.py:591
  92.4 1.5 %collective-permute-start.22 = (bf16[256,1024]{1,0:T(8,128)(2,1)S(1)}, bf16[256,1024]{1,0:T(8,128)(2,1)S(1)}, u32[]{:S(2)}, u32[]{:S(2)}) collective-permute-start(bf16[256,1024]{1,0:T(8,128)(2,1)S(1)} %get-tuple-element.94), channel_id=1, source_target_pairs={{0,12},{1,13},{2,14},{3,15},{4,0},{5,1},{6,2},{7,3},{8,4},{9,5},{1... | collective-permute-start | bytes 1572872 | tf_op jit(solution)/shard_map/ppermute | solution.py:594
  94.0 1.5 %collective-permute-start.13 = (bf16[336,512]{1,0:T(8,128)(2,1)S(1)}, bf16[336,512]{1,0:T(8,128)(2,1)S(1)}, u32[]{:S(2)}, u32[]{:S(2)}) collective-permute-start(bf16[336,512]{1,0:T(8,128)(2,1)S(1)} %get-tuple-element.68), channel_id=1, source_target_pairs={{0,2},{1,3},{2,0},{3,1},{4,6},{5,7},{6,4},{7,5},{8,10},{9,11},{10,... | collective-permute-start | bytes 1032200 | tf_op jit(solution)/shard_map/ppermute | solution.py:584
  96.1 0.0 copy-start.1
  96.1 3.4 %copy-done.1 = bf16[1,1,16,128,2048]{4,3,2,1,0:T(8,128)(2,1)S(1)} copy-done((bf16[1,1,16,128,2048]{4,3,2,1,0:T(8,128)(2,1)S(1)}, bf16[1,1,16,128,2048]{4,3,2,1,0:T(8,128)(2,1)}, u32[]{:S(2)}) %copy-start.1) | copy-done | bytes 8388632
  99.5 0.2 local_attention.1.local
  99.7 4.1 %collective-permute-done.13.refs_6_.refs_3_ = bf16[336,512]{1,0:T(8,128)(2,1)S(1)} collective-permute-done((bf16[336,512]{1,0:T(8,128)(2,1)S(1)}, bf16[336,512]{1,0:T(8,128)(2,1)S(1)}, u32[]{:S(2)}, u32[]{:S(2)}) %collective-permute-start.13) | collective-permute-done | bytes 344096 | tf_op jit(solution)/shard_map/ppermute | solution.py:584
  103.8 0.8 unpack.1
  104.7 4.3 %pool_attention.1.pool = f32[16,72,128]{2,1,0:T(8,128)S(1)} custom-call(s32[16]{0:T(128)S(1)} %get-tuple-element.82.slots, s32[16]{0:T(128)S(1)} %get-tuple-element.83.alive, bf16[16,64,128]{2,1,0:T(8,128)(2,1)S(1)} %get-tuple-element.84.query, bf16[16,128,2048]{2,1,0:T(8,128)(2,1)S(1)} %bitcast.11, bf16[16,128,2048]{2,1,0:T(8,128)(2,1)S(1)} %bitcast.12, ...), custom_call_target="tpu_custom_call" | custom-call | flops 1000 | bytes 1000 | tf_op jit(solution)/shard_map/pool_attention/pallas_call | solution.py:333
  109.0 2.3 %product_own.1 = (f32[256,1024]{1,0:T(8,128)S(1)}, f32[256,1024]{1,0:T(8,128)S(1)}) custom-call(bf16[1024,512]{1,0:T(8,128)(2,1)S(1)} %get-tuple-element.86.refs_0_, bf16[1104,512]{1,0:T(8,128)(2,1)S(1)} %collective-permute-done.11.refs_1_.refs_4_, bf16[1104,512]{1,0:T(8,128)(2,1)S(1)} %collective-permute-done.12.refs_2_.refs_5_, ...), custom_call_target="tpu_custom_call" | custom-call | flops 1000 | bytes 1000 | tf_op jit(solution)/shard_map/product_own/pallas_call | solution.py:244
  111.3 0.0 collective-permute-done.20.up_r
  111.3 0.0 collective-permute-done.21.down_l
  111.3 0.9 collective-permute-done.19.up_l
  112.2 3.9 %prefix_attention.1 = (bf16[1,256,2048]{2,1,0:T(8,128)(2,1)}, bf16[16,80,128]{2,1,0:T(8,128)(2,1)S(1)}) custom-call(s32[1]{0:T(128)S(6)} %copy.12.prompt_pages, f32[256,1024]{1,0:T(8,128)S(1)} %get-tuple-element.90.own_l, f32[256,1024]{1,0:T(8,128)S(1)} %get-tuple-element.91.own_r, bf16[256,1024]{1,0:T(8,128)(2,1)S(1)} %collective-permute-done.19.up_l, ...), custom_call_target="tpu_custom_call" | custom-call | flops 300000000 | bytes 6291456 | tf_op jit(solution)/shard_map/prefix_attention/pallas_call | solution.py:496
  116.1 14.6 %all_to_all.5.arrived = bf16[16,80,128]{2,1,0:T(8,128)(2,1)S(1)} all-to-all(bf16[16,80,128]{2,1,0:T(8,128)(2,1)S(1)} %get-tuple-element.98), channel_id=1, replica_groups=mesh['prompt'=8,'sample'=16] {'sample'}, dimensions={0} | all-to-all | bytes 655360 | tf_op jit(solution)/shard_map/all_to_all | solution.py:607
  130.7 0.3 combine.1
  131.1 0.6 reshape.15
  (12 shorter events, 0.0 us)
Async XLA Ops:
  0.6 9.7 %collective-permute-start = (bf16[512,256]{1,0:T(8,128)(2,1)}, bf16[512,256]{1,0:T(8,128)(2,1)S(1)}, u32[]{:S(2)}, u32[]{:S(2)}) collective-permute-start(bf16[512,256]{1,0:T(8,128)(2,1)} %param.11), channel_id=1, source_target_pairs={{0,1},{1,2},{2,3},{3,0},{4,5},{5,6},{6,7},{7,4},{8,9},{9,10},{10,1... | collective-permute-start | bytes 786440 | tf_op jit(solution)/shard_map/ppermute | solution.py:552
  2.3 9.4 %collective-permute-start.1 = (bf16[512,256]{1,0:T(8,128)(2,1)}, bf16[512,256]{1,0:T(8,128)(2,1)S(1)}, u32[]{:S(2)}, u32[]{:S(2)}) collective-permute-start(bf16[512,256]{1,0:T(8,128)(2,1)} %param.11), channel_id=1, source_target_pairs={{0,3},{1,0},{2,1},{3,2},{4,7},{5,4},{6,5},{7,6},{8,11},{9,8},{10,9... | collective-permute-start | bytes 786440 | tf_op jit(solution)/shard_map/ppermute | solution.py:553
  3.9 12.9 %collective-permute-start.2 = (bf16[512,256]{1,0:T(8,128)(2,1)}, bf16[512,256]{1,0:T(8,128)(2,1)S(1)}, u32[]{:S(2)}, u32[]{:S(2)}) collective-permute-start(bf16[512,256]{1,0:T(8,128)(2,1)} %param.11), channel_id=1, source_target_pairs={{0,2},{1,3},{2,0},{3,1},{4,6},{5,7},{6,4},{7,5},{8,10},{9,11},{10,... | collective-permute-start | bytes 786440 | tf_op jit(solution)/shard_map/ppermute | solution.py:551
  5.8 3.1 %copy-start.4 = (s32[1,1,16]{2,1,0:T(1,128)S(1)}, s32[1,1,16]{2,1,0:T(1,128)}, u32[]{:S(2)}) copy-start(s32[1,1,16]{2,1,0:T(1,128)} %where.1) | copy-start | bytes 196
  5.8 28.3 %copy-start = (bf16[1,4096,512]{2,1,0:T(8,128)(2,1)S(1)}, bf16[1,4096,512]{2,1,0:T(8,128)(2,1)}, u32[]{:S(2)}) copy-start(bf16[1,4096,512]{2,1,0:T(8,128)(2,1)} %param.10) | copy-start | bytes 12582916
  9.0 0.8 copy-start.2
  17.9 2.7 %collective-permute-start.7 = (bf16[4,512,256]{2,1,0:T(8,128)(2,1)S(1)}, bf16[4,512,256]{2,1,0:T(8,128)(2,1)S(1)}, u32[]{:S(2)}, u32[]{:S(2)}) collective-permute-start(bf16[4,512,256]{2,1,0:T(8,128)(2,1)S(1)} %pad_maximum_fusion.refs_4_), channel_id=1, source_target_pairs={{0,16},{16,0},{32,48},{48,32},{64,80},{80,64},{96,112},{112,96},{1... | collective-permute-start | bytes 3145736 | tf_op jit(solution)/shard_map/ppermute | solution.py:568
  18.0 25.9 %collective-permute-start.6 = (bf16[4,512,256]{2,1,0:T(8,128)(2,1)S(1)}, bf16[4,512,256]{2,1,0:T(8,128)(2,1)S(1)}, u32[]{:S(2)}, u32[]{:S(2)}) collective-permute-start(bf16[4,512,256]{2,1,0:T(8,128)(2,1)S(1)} %pad_maximum_fusion.refs_4_), channel_id=1, source_target_pairs={{0,32},{16,112},{32,64},{48,16},{64,96},{80,48},{96,0},{112,80},{1... | collective-permute-start | bytes 3145736 | tf_op jit(solution)/shard_map/ppermute | solution.py:567
  20.7 24.7 %collective-permute-start.8 = (bf16[4,512,256]{2,1,0:T(8,128)(2,1)S(1)}, bf16[4,512,256]{2,1,0:T(8,128)(2,1)S(1)}, u32[]{:S(2)}, u32[]{:S(2)}) collective-permute-start(bf16[4,512,256]{2,1,0:T(8,128)(2,1)S(1)} %collective-permute-done.7.refs_5_), channel_id=1, source_target_pairs={{0,32},{16,112},{32,64},{48,16},{64,96},{80,48},{96,0},{112,80},{1... | collective-permute-start | bytes 3145736 | tf_op jit(solution)/shard_map/ppermute | solution.py:569
  22.3 21.7 %collective-permute-start.9 = (bf16[768,512]{1,0:T(8,128)(2,1)S(1)}, bf16[768,512]{1,0:T(8,128)(2,1)S(1)}, u32[]{:S(2)}, u32[]{:S(2)}) collective-permute-start(bf16[768,512]{1,0:T(8,128)(2,1)S(1)} %get-tuple-element.61), channel_id=1, source_target_pairs={{0,2},{1,3},{2,0},{3,1},{4,6},{5,7},{6,4},{7,5},{8,10},{9,11},{10,... | collective-permute-start | bytes 2359304 | tf_op jit(solution)/shard_map/ppermute | solution.py:562
  23.1 5.8 %collective-permute-start.3 = (bf16[40,256]{1,0:T(8,128)(2,1)S(1)}, bf16[40,256]{1,0:T(8,128)(2,1)S(1)}, u32[]{:S(2)}, u32[]{:S(2)}) collective-permute-start(bf16[40,256]{1,0:T(8,128)(2,1)S(1)} %get-tuple-element.55.refs_0_), channel_id=1, source_target_pairs={{0,4},{1,5},{2,6},{3,7},{4,8},{5,9},{6,10},{7,11},{8,12},{9,13},{1... | collective-permute-start | bytes 61448 | tf_op jit(solution)/shard_map/ppermute | solution.py:560
  25.0 5.9 %collective-permute-start.4 = (bf16[40,256]{1,0:T(8,128)(2,1)S(1)}, bf16[40,256]{1,0:T(8,128)(2,1)S(1)}, u32[]{:S(2)}, u32[]{:S(2)}) collective-permute-start(bf16[40,256]{1,0:T(8,128)(2,1)S(1)} %get-tuple-element.55.refs_0_), channel_id=1, source_target_pairs={{0,12},{1,13},{2,14},{3,15},{4,0},{5,1},{6,2},{7,3},{8,4},{9,5},{1... | collective-permute-start | bytes 61448 | tf_op jit(solution)/shard_map/ppermute | solution.py:560
  28.9 5.3 %collective-permute-start.5 = (bf16[40,256]{1,0:T(8,128)(2,1)S(1)}, bf16[40,256]{1,0:T(8,128)(2,1)S(1)}, u32[]{:S(2)}, u32[]{:S(2)}) collective-permute-start(bf16[40,256]{1,0:T(8,128)(2,1)S(1)} %get-tuple-element.55.refs_0_), channel_id=1, source_target_pairs={{0,8},{1,9},{2,10},{3,11},{4,12},{5,13},{6,14},{7,15},{8,0},{9,1},... | collective-permute-start | bytes 61448 | tf_op jit(solution)/shard_map/ppermute | solution.py:560
  34.5 33.9 %collective-permute-start.11 = (bf16[1104,512]{1,0:T(8,128)(2,1)S(1)}, bf16[1104,512]{1,0:T(8,128)(2,1)S(1)}, u32[]{:S(2)}, u32[]{:S(2)}) collective-permute-start(bf16[1104,512]{1,0:T(8,128)(2,1)S(1)} %get-tuple-element.63), channel_id=1, source_target_pairs={{0,1},{1,2},{2,3},{3,0},{4,5},{5,6},{6,7},{7,4},{8,9},{9,10},{10,1... | collective-permute-start | bytes 3391496 | tf_op jit(solution)/shard_map/ppermute | solution.py:563
  36.5 31.9 %collective-permute-start.12 = (bf16[1104,512]{1,0:T(8,128)(2,1)S(1)}, bf16[1104,512]{1,0:T(8,128)(2,1)S(1)}, u32[]{:S(2)}, u32[]{:S(2)}) collective-permute-start(bf16[1104,512]{1,0:T(8,128)(2,1)S(1)} %get-tuple-element.64), channel_id=1, source_target_pairs={{0,3},{1,0},{2,1},{3,2},{4,7},{5,4},{6,5},{7,6},{8,11},{9,8},{10,9... | collective-permute-start | bytes 3391496 | tf_op jit(solution)/shard_map/ppermute | solution.py:564
  45.3 23.1 %collective-permute-start.10 = (bf16[4,512,256]{2,1,0:T(8,128)(2,1)S(1)}, bf16[4,512,256]{2,1,0:T(8,128)(2,1)S(1)}, u32[]{:S(2)}, u32[]{:S(2)}) collective-permute-start(bf16[4,512,256]{2,1,0:T(8,128)(2,1)S(1)} %collective-permute-done.6.refs_6_), channel_id=1, source_target_pairs={{0,32},{16,112},{32,64},{48,16},{64,96},{80,48},{96,0},{112,80},{1... | collective-permute-start | bytes 3145736 | tf_op jit(solution)/shard_map/ppermute | solution.py:571
  45.9 22.6 %collective-permute-start.14 = (bf16[4,512,256]{2,1,0:T(8,128)(2,1)S(1)}, bf16[4,512,256]{2,1,0:T(8,128)(2,1)S(1)}, u32[]{:S(2)}, u32[]{:S(2)}) collective-permute-start(bf16[4,512,256]{2,1,0:T(8,128)(2,1)S(1)} %collective-permute-done.6.refs_6_), channel_id=1, source_target_pairs={{0,16},{16,0},{32,48},{48,32},{64,80},{80,64},{96,112},{112,96},{1... | collective-permute-start | bytes 3145736 | tf_op jit(solution)/shard_map/ppermute | solution.py:572
  47.7 20.8 %collective-permute-start.15 = (bf16[4,512,256]{2,1,0:T(8,128)(2,1)S(1)}, bf16[4,512,256]{2,1,0:T(8,128)(2,1)S(1)}, u32[]{:S(2)}, u32[]{:S(2)}) collective-permute-start(bf16[4,512,256]{2,1,0:T(8,128)(2,1)S(1)} %collective-permute-done.8.refs_7_), channel_id=1, source_target_pairs={{0,16},{16,0},{32,48},{48,32},{64,80},{80,64},{96,112},{112,96},{1... | collective-permute-start | bytes 3145736 | tf_op jit(solution)/shard_map/ppermute | solution.py:573
  68.4 2.7 %collective-permute-start.16 = (bf16[4,512,256]{2,1,0:T(8,128)(2,1)S(1)}, bf16[4,512,256]{2,1,0:T(8,128)(2,1)S(1)}, u32[]{:S(2)}, u32[]{:S(2)}) collective-permute-start(bf16[4,512,256]{2,1,0:T(8,128)(2,1)S(1)} %collective-permute-done.10.refs_10_), channel_id=1, source_target_pairs={{0,16},{16,0},{32,48},{48,32},{64,80},{80,64},{96,112},{112,96},{1... | collective-permute-start | bytes 3145736 | tf_op jit(solution)/shard_map/ppermute | solution.py:575
  73.4 16.8 %collective-permute-start.17 = (bf16[256,1024]{1,0:T(8,128)(2,1)S(1)}, bf16[256,1024]{1,0:T(8,128)(2,1)S(1)}, u32[]{:S(2)}, u32[]{:S(2)}) collective-permute-start(bf16[256,1024]{1,0:T(8,128)(2,1)S(1)} %get-tuple-element.75), channel_id=1, source_target_pairs={{0,4},{1,5},{2,6},{3,7},{4,8},{5,9},{6,10},{7,11},{8,12},{9,13},{1... | collective-permute-start | bytes 1572872 | tf_op jit(solution)/shard_map/ppermute | solution.py:585
  75.4 14.8 %collective-permute-start.18 = (bf16[256,1024]{1,0:T(8,128)(2,1)S(1)}, bf16[256,1024]{1,0:T(8,128)(2,1)S(1)}, u32[]{:S(2)}, u32[]{:S(2)}) collective-permute-start(bf16[256,1024]{1,0:T(8,128)(2,1)S(1)} %get-tuple-element.76), channel_id=1, source_target_pairs={{0,12},{1,13},{2,14},{3,15},{4,0},{5,1},{6,2},{7,3},{8,4},{9,5},{1... | collective-permute-start | bytes 1572872 | tf_op jit(solution)/shard_map/ppermute | solution.py:586
  77.6 18.5 %copy-start.3 = (bf16[1,1,2048]{2,1,0:T(2,128)(2,1)S(1)}, bf16[1,1,2048]{2,1,0:T(2,128)(2,1)}, u32[]{:S(2)}) copy-start(bf16[1,1,2048]{2,1,0:T(2,128)(2,1)} %param.13) | copy-start | bytes 12292
  77.6 27.0 %slice-start = ((s8[8388608]{0:T(1024)(128)(4,1)}), s8[4194304]{0:T(1024)(128)(4,1)S(1)}, s32[]{:S(2)}) async-start(s8[8388608]{0:T(1024)(128)(4,1)} %bitcast.9), calls=%async_computation.1 | async-start | bytes 8388608
  82.1 29.2 %collective-permute-start.20 = (bf16[256,1024]{1,0:T(8,128)(2,1)S(1)}, bf16[256,1024]{1,0:T(8,128)(2,1)S(1)}, u32[]{:S(2)}, u32[]{:S(2)}) collective-permute-start(bf16[256,1024]{1,0:T(8,128)(2,1)S(1)} %get-tuple-element.92), channel_id=1, source_target_pairs={{0,4},{1,5},{2,6},{3,7},{4,8},{5,9},{6,10},{7,11},{8,12},{9,13},{1... | collective-permute-start | bytes 1572872 | tf_op jit(solution)/shard_map/ppermute | solution.py:588
  82.2 29.1 %collective-permute-start.21 = (bf16[256,1024]{1,0:T(8,128)(2,1)S(1)}, bf16[256,1024]{1,0:T(8,128)(2,1)S(1)}, u32[]{:S(2)}, u32[]{:S(2)}) collective-permute-start(bf16[256,1024]{1,0:T(8,128)(2,1)S(1)} %get-tuple-element.93), channel_id=1, source_target_pairs={{0,12},{1,13},{2,14},{3,15},{4,0},{5,1},{6,2},{7,3},{8,4},{9,5},{1... | collective-permute-start | bytes 1572872 | tf_op jit(solution)/shard_map/ppermute | solution.py:588
  90.2 14.4 %slice-start.1 = ((s8[8388608]{0:T(1024)(128)(4,1)}), s8[4194304]{0:T(1024)(128)(4,1)S(1)}, s32[]{:S(2)}) async-start(s8[8388608]{0:T(1024)(128)(4,1)} %bitcast.9), calls=%async_computation.2 | async-start | bytes 8388608
  90.5 21.7 %collective-permute-start.19 = (bf16[256,1024]{1,0:T(8,128)(2,1)S(1)}, bf16[256,1024]{1,0:T(8,128)(2,1)S(1)}, u32[]{:S(2)}, u32[]{:S(2)}) collective-permute-start(bf16[256,1024]{1,0:T(8,128)(2,1)S(1)} %get-tuple-element.77), channel_id=1, source_target_pairs={{0,4},{1,5},{2,6},{3,7},{4,8},{5,9},{6,10},{7,11},{8,12},{9,13},{1... | collective-permute-start | bytes 1572872 | tf_op jit(solution)/shard_map/ppermute | solution.py:591
  92.4 19.8 %collective-permute-start.22 = (bf16[256,1024]{1,0:T(8,128)(2,1)S(1)}, bf16[256,1024]{1,0:T(8,128)(2,1)S(1)}, u32[]{:S(2)}, u32[]{:S(2)}) collective-permute-start(bf16[256,1024]{1,0:T(8,128)(2,1)S(1)} %get-tuple-element.94), channel_id=1, source_target_pairs={{0,12},{1,13},{2,14},{3,15},{4,0},{5,1},{6,2},{7,3},{8,4},{9,5},{1... | collective-permute-start | bytes 1572872 | tf_op jit(solution)/shard_map/ppermute | solution.py:594
  94.0 9.9 %collective-permute-start.13 = (bf16[336,512]{1,0:T(8,128)(2,1)S(1)}, bf16[336,512]{1,0:T(8,128)(2,1)S(1)}, u32[]{:S(2)}, u32[]{:S(2)}) collective-permute-start(bf16[336,512]{1,0:T(8,128)(2,1)S(1)} %get-tuple-element.68), channel_id=1, source_target_pairs={{0,2},{1,3},{2,0},{3,1},{4,6},{5,7},{6,4},{7,5},{8,10},{9,11},{10,... | collective-permute-start | bytes 1032200 | tf_op jit(solution)/shard_map/ppermute | solution.py:584
  96.1 3.4 %copy-start.1 = (bf16[1,1,16,128,2048]{4,3,2,1,0:T(8,128)(2,1)S(1)}, bf16[1,1,16,128,2048]{4,3,2,1,0:T(8,128)(2,1)}, u32[]{:S(2)}) copy-start(bf16[1,1,16,128,2048]{4,3,2,1,0:T(8,128)(2,1)} %param.14) | copy-start | bytes 25165828

commit v7 on v6

--- a/solution.py
+++ b/solution.py
@@ -197,13 +197,14 @@
 
 
 def pick_near_kernel(states, *refs):
-    blocks, (right, left, last), sems = refs[:4], refs[4:7], refs[7]
-    wanted = [(1, k, right.at[block_rows(k)]) for k in range(4)]
-    wanted += [(3, k, left.at[block_rows(k)]) for k in range(4)]
+    blocks, (first_right, first_left, right, left, last), sems = refs[:4], refs[4:9], refs[9]
+    wanted = [(1, 0, first_right), (3, 0, first_left)]
+    wanted += [(1, k + 1, right.at[block_rows(k)]) for k in range(3)]
+    wanted += [(3, k + 1, left.at[block_rows(k)]) for k in range(3)]
     wanted += [(2, 3, last.at[block_rows(0)])]
     copies = copy_rows(states, sems, wanted)
-    put_blocks(right, 4 * ROWS, blocks)
-    put_blocks(left, 4 * ROWS, blocks)
+    put_blocks(right, 3 * ROWS, blocks)
+    put_blocks(left, 3 * ROWS, blocks)
     put_blocks(last, ROWS, blocks)
     for copy in copies:
         copy.wait()
@@ -213,10 +214,11 @@
     vmem = pl.BlockSpec(memory_space=pltpu.VMEM)
     return pl.pallas_call(
         pick_near_kernel,
-        out_shape=[jax.ShapeDtypeStruct((4 * ROWS + 2 * BLOCK, SLICE), BF16)] * 2
+        out_shape=[jax.ShapeDtypeStruct((ROWS, SLICE), BF16)] * 2
+        + [jax.ShapeDtypeStruct((3 * ROWS + 2 * BLOCK, SLICE), BF16)] * 2
         + [jax.ShapeDtypeStruct((ROWS + 2 * BLOCK, SLICE), BF16)],
         in_specs=[pl.BlockSpec(memory_space=pl.ANY)] + [vmem] * 4,
-        out_specs=[vmem] * 3,
+        out_specs=[vmem] * 5,
         scratch_shapes=[pltpu.SemaphoreType.DMA((9,))],
         compiler_params=params(44),
         cost_estimate=cost(1000, 1000),
@@ -224,15 +226,19 @@
     )(states, *blocks)
 
 
+def weight_of(pieces, j, d):
+    return pieces[j][d] if j < 7 else pieces[7 + d // 2][d % 2]
+
+
 def product_kernel(blocks, *refs):
-    states, pieces, outs = refs[:4], refs[4:12], refs[12:]
+    states, pieces, outs = refs[:4], refs[4:13], refs[13:]
     for j in range(8):
         for k, block in enumerate(blocks):
             total = jnp.zeros((ROWS, COLUMNS), F32)
             for d in range(4):
                 at = block[d] * ROWS
                 total += jnp.dot(
-                    states[d][at : at + ROWS], pieces[j][d], preferred_element_type=F32
+                    states[d][at : at + ROWS], weight_of(pieces, j, d), preferred_element_type=F32
                 )
             out = outs[2 * k + j // 4]
             out[:, (j % 4) * COLUMNS : (j % 4 + 1) * COLUMNS] = total.astype(out.dtype)
@@ -244,7 +250,7 @@
     return pl.pallas_call(
         functools.partial(product_kernel, blocks),
         out_shape=outs,
-        in_specs=[vmem] * 12,
+        in_specs=[vmem] * 13,
         out_specs=[vmem] * len(outs),
         compiler_params=params(20),
         cost_estimate=cost(1000, 1000),
@@ -253,11 +259,13 @@
 
 
 def product_far_kernel(*refs):
-    states, pieces, outs = refs[:4], refs[4:12], refs[12:]
+    states, pieces, outs = refs[:4], refs[4:13], refs[13:]
     for j in range(8):
         total = jnp.zeros((ROWS, COLUMNS), F32)
         for d in range(4):
-            total += jnp.dot(states[d][:ROWS], pieces[j][d], preferred_element_type=F32)
+            total += jnp.dot(
+                states[d][:ROWS], weight_of(pieces, j, d), preferred_element_type=F32
+            )
         outs[j // 4][:, (j % 4) * COLUMNS : (j % 4 + 1) * COLUMNS] = total.astype(BF16)
 
 
@@ -266,7 +274,7 @@
     return pl.pallas_call(
         product_far_kernel,
         out_shape=[jax.ShapeDtypeStruct((ROWS, KVW // 2), BF16)] * 2,
-        in_specs=[vmem] * 12,
+        in_specs=[vmem] * 13,
         out_specs=[vmem] * 2,
         compiler_params=params(20),
         cost_estimate=cost(1000, 1000),
@@ -518,14 +526,17 @@
         local_share = jnp.exp(local_log - high)
         total = jnp.sum(shares, axis=0) + local_share
         mixture = jnp.sum(arrived[:, rows].astype(F32) * shares, axis=0) + local[rows] * local_share
-        out[rows] = (mixture / total).astype(BF16)
+        mixture = (mixture / total).astype(BF16)
+        for h in range(HEADS):
+            lanes = slice((g * HEADS + h) * HEAD_SIZE, (g * HEADS + h + 1) * HEAD_SIZE)
+            out[0, :, lanes] = mixture[h : h + 1]
 
 
 def combine(arrived, local):
     vmem = pl.BlockSpec(memory_space=pltpu.VMEM)
     return pl.pallas_call(
         combine_kernel,
-        out_shape=jax.ShapeDtypeStruct((QUERY_HEADS, HEAD_SIZE), BF16),
+        out_shape=jax.ShapeDtypeStruct((1, 1, QUERY_HEADS * HEAD_SIZE), BF16),
         in_specs=[vmem, vmem],
         out_specs=vmem,
         compiler_params=params(16),
@@ -558,8 +569,10 @@
         ((kv_weight, weight_right, weight_left, weight_far), own_states, to_far, block)
     )
     blocks = [block] + [lax.ppermute(block, "sample", to) for to in (Z_UP, Z_DOWN, Z_FAR)]
-    to_right, to_left, last_far = pick_near(states, blocks)
+    first_right, first_left, to_right, to_left, last_far = pick_near(states, blocks)
     rows_far = lax.ppermute(to_far, "sample", X_FAR)
+    first_right = lax.ppermute(first_right, "sample", X_RIGHT)
+    first_left = lax.ppermute(first_left, "sample", X_LEFT)
     rows_right = lax.ppermute(to_right, "sample", X_RIGHT)
     rows_left = lax.ppermute(to_left, "sample", X_LEFT)
 
@@ -567,24 +580,33 @@
     near = lax.ppermute(here, "prompt", Y_SPLIT)
     here_other = lax.ppermute(here, "prompt", SWAP)
     near_other = lax.ppermute(here_other, "prompt", Y_SPLIT)
-    near, near_other, rows_far = tie((near, near_other, rows_far))
+    near, near_other, rows_far, first_right, first_left = tie(
+        (near, near_other, rows_far, first_right, first_left)
+    )
     far = lax.ppermute(near, "prompt", Y_SPLIT)
     near_swapped = lax.ppermute(near, "prompt", SWAP)
     near_other_swapped = lax.ppermute(near_other, "prompt", SWAP)
-    far, rows_right, rows_left = tie((far, rows_right, rows_left))
-    far_other = lax.ppermute(far, "prompt", SWAP)
-    others = [own_states, rows_right, rows_left, rows_far]
+    query, near_swapped = tie((query, near_swapped))
+    local_alive = jnp.where(preempted[0] > 0, 0, comp_pages[0])
+    local = local_attention(local_alive, query, new_kv[0], local_pages[0, 0])
+    far, local = tie((far, local))
+    far_other = [lax.ppermute(half, "prompt", SWAP) for half in (far[:2], far[2:])]
     pieces = [
         here, here_other, near, near_other,
-        near_swapped, near_other_swapped, far, far_other,
+        near_swapped, near_other_swapped, far, *far_other,
     ]
 
-    far_l, far_r = product_far(others, pieces)
+    first_right, rows_right, rows_left = tie((first_right, rows_right, rows_left))
+
+    far_l, far_r = product_far([own_states, first_right, first_left, rows_far], pieces)
+    from_down = lax.ppermute(far_l, "sample", Z_UP)
+    from_up = lax.ppermute(far_r, "sample", Z_DOWN)
     last_far, rows_right = tie((last_far, rows_right))
     last_far = lax.ppermute(last_far, "sample", X_FAR)
-    from_down = lax.ppermute(far_l, "sample", Z_UP)
-    from_up = lax.ppermute(far_r, "sample", Z_DOWN)
-    up_l, up_r, down_l, down_r = product(others, pieces, ((1,) * 4, (2,) * 4), BF16, "product_near")
+    others = [own_states, rows_right, rows_left, rows_far]
+    up_l, up_r, down_l, down_r = product(
+        others, pieces, ((1, 0, 0, 1), (2, 1, 1, 2)), BF16, "product_near"
+    )
     up_r, down_l = lax.ppermute(up_r, "sample", Z_UP), lax.ppermute(down_l, "sample", Z_DOWN)
     up_l, down_r = relay(up_l, down_r, from_down, from_up)
     sums = [
@@ -594,19 +616,16 @@
         lax.ppermute(down_r, "sample", Z_DOWN),
     ]
 
-    query, up_l = tie((query, up_l))
-    local_alive = jnp.where(preempted[0] > 0, 0, comp_pages[0])
-    local = local_attention(local_alive, query, new_kv[0], local_pages[0, 0])
-    arrived, local = tie(([rows_right, rows_left, last_far], local))
+    arrived, up_l = tie(([rows_right, rows_left, last_far], up_l))
     queries_all, by_group, slots, alive = unpack(blocks, arrived)
     pool = pool_attention(slots, alive, queries_all, pool_pages[0, 0])
-    mine, pool, local = tie(([own_states, *arrived], pool, local))
-    sums = [*product(mine, pieces, ((3, 3, 3, 0),), F32, "product_own"), *sums]
+    mine, pool = tie(([own_states, *arrived], pool))
+    sums = [*product(mine, pieces, ((3, 2, 2, 0),), F32, "product_own"), *sums]
 
     cache, packed = prefix_attention(prompt_pages, sums, by_group, pool)
     arrived = lax.all_to_all(packed, "sample", split_axis=0, concat_axis=0, tiled=True)
     attended = combine(arrived, local)
-    return (cache, attended.reshape(1, 1, -1))
+    return (cache, attended)
 
 
 def solution(mesh):

time: 132 us -> 135 us (1.023)
  starting transfers between devices: 33.5 us -> 37.1 us
  waiting for transfers between devices: 53.3 us -> 50.1 us
    ppermute x1, waiting for transfers between devices: 20.7 us -> 6.96 us  [per_device(): rows_right = lax.ppermute(to_right, 'sample', X_RIGHT)]
    ppermute x1 -> x4, waiting for transfers between devices: 2.63 us -> 12 us  [the longest x1 12 us: per_device(): first_right = lax.ppermute(first_right, 'sample', X_RIGHT)]
    ppermute x1, waiting for transfers between devices: 0.01 us -> 7.22 us  [per_device(): far = lax.ppermute(near, 'prompt', Y_SPLIT)]
    ppermute x1, waiting for transfers between devices: 6.17 us -> 0.01 us  [per_device(): rows_far = lax.ppermute(to_far, 'sample', X_FAR)]
    ppermute x1 -> x4, starting transfers between devices: 0.02 us -> 3.89 us  [the longest x1 2.07 us: per_device(): first_right = lax.ppermute(first_right, 'sample', X_RIGHT)]
    ppermute x1, waiting for transfers between devices: 4.1 us -> 6.18 us  [per_device(): last_far = lax.ppermute(last_far, 'sample', X_FAR)]
    ppermute x1, starting transfers between devices: 1.78 us -> 0.1 us  [per_device(): near_swapped = lax.ppermute(near, 'prompt', SWAP)]
    ppermute x1, waiting for transfers between devices: 1.4 us -> 0.01 us  [per_device(): near_other = lax.ppermute(here_other, 'prompt', Y_SPLIT)]
  transfers between devices with their start and end apart: 23 -> 26, of which waited for: 12 -> 11; matrix products, arithmetic and copies ran while one was open for 0% -> 0% of each run, Pallas kernels for 11% -> 11%
where the time goes in v7:
time: 135 us; the launch traced here: 134 us
  waiting for transfers between devices  50.1 us (37%)
  starting transfers between devices  37.1 us (27%)
  Pallas kernels  21.9 us (16%)
  blocking collectives  15.5 us (11%)
  local copies, waits for them, and re-layouts  5.57 us (4%)
  between operations  2.8 us (2%)
    all_to_all x1, blocking collectives, per_device(): lax.all_to_all(packed, 'sample', split_axis=0, concat_axis=0, tiled=True)  15.5 us
    ppermute x1, waiting for transfers between devices, per_device(): first_right = lax.ppermute(first_right, 'sample', X_RIGHT)  12 us
    ppermute x1, waiting for transfers between devices, per_device(): far = lax.ppermute(near, 'prompt', Y_SPLIT)  7.22 us
    ppermute x1, waiting for transfers between devices, per_device(): rows_right = lax.ppermute(to_right, 'sample', X_RIGHT)  6.96 us
    pallas_call x2, Pallas kernels, product(): pl.pallas_call(functools.partial(product_kernel, blocks), out_shape=outs,...  6.82 us
    ppermute x1, waiting for transfers between devices, per_device(): last_far = lax.ppermute(last_far, 'sample', X_FAR)  6.18 us
    ppermute x3, starting transfers between devices, per_device(): lax.ppermute(block, 'sample', to)  6.07 us
    unnamed x14, local copies, waits for them, and re-layouts  5.5 us
  transfers between devices with their start and end apart: 26, of which 11 were waited for; matrix products, arithmetic and copies ran while one was open for 0% of the time, Pallas kernels for 11%

profile of v7, /device:TPU:0, one launch (start us, length us, event | category | flops | bytes accessed | tf_op | source)
XLA Modules:
  0.0 134.1 jit_solution(2866630675762787349)
XLA Ops:
  0.6 1.6 %collective-permute-start = (bf16[512,256]{1,0:T(8,128)(2,1)}, bf16[512,256]{1,0:T(8,128)(2,1)S(1)}, u32[]{:S(2)}, u32[]{:S(2)}) collective-permute-start(bf16[512,256]{1,0:T(8,128)(2,1)} %param.11), channel_id=1, source_target_pairs={{0,1},{1,2},{2,3},{3,0},{4,5},{5,6},{6,7},{7,4},{8,9},{9,10},{10,1... | collective-permute-start | bytes 786440 | tf_op jit(solution)/shard_map/ppermute | solution.py:563
  2.3 1.7 %collective-permute-start.1 = (bf16[512,256]{1,0:T(8,128)(2,1)}, bf16[512,256]{1,0:T(8,128)(2,1)S(1)}, u32[]{:S(2)}, u32[]{:S(2)}) collective-permute-start(bf16[512,256]{1,0:T(8,128)(2,1)} %param.11), channel_id=1, source_target_pairs={{0,3},{1,0},{2,1},{3,2},{4,7},{5,4},{6,5},{7,6},{8,11},{9,8},{10,9... | collective-permute-start | bytes 786440 | tf_op jit(solution)/shard_map/ppermute | solution.py:564
  3.9 1.9 %collective-permute-start.2 = (bf16[512,256]{1,0:T(8,128)(2,1)}, bf16[512,256]{1,0:T(8,128)(2,1)S(1)}, u32[]{:S(2)}, u32[]{:S(2)}) collective-permute-start(bf16[512,256]{1,0:T(8,128)(2,1)} %param.11), channel_id=1, source_target_pairs={{0,2},{1,3},{2,0},{3,1},{4,6},{5,7},{6,4},{7,5},{8,10},{9,11},{10,... | collective-permute-start | bytes 786440 | tf_op jit(solution)/shard_map/ppermute | solution.py:562
  5.8 1.5 %pick_far.1 = (bf16[1024,512]{1,0:T(8,128)(2,1)S(1)}, bf16[768,512]{1,0:T(8,128)(2,1)S(1)}) custom-call(bf16[4,4,256,512]{3,2,1,0:T(8,128)(2,1)} %bitcast.15), custom_call_target="tpu_custom_call" | custom-call | flops 1000 | bytes 1000 | tf_op jit(solution)/shard_map/pick_far/pallas_call | solution.py:178
  8.6 0.0 copy-start.2
  8.6 0.7 copy-done.2
  9.4 0.7 copy-done.4
  10.0 0.6 prepare.1
  10.6 1.1 collective-permute-done.1
  11.7 5.1 %collective-permute-done.2 = bf16[512,256]{1,0:T(8,128)(2,1)S(1)} collective-permute-done((bf16[512,256]{1,0:T(8,128)(2,1)}, bf16[512,256]{1,0:T(8,128)(2,1)S(1)}, u32[]{:S(2)}, u32[]{:S(2)}) %collective-permute-start.2) | collective-permute-done | bytes 262176 | tf_op jit(solution)/shard_map/ppermute | solution.py:562
  16.9 1.1 pad_maximum_fusion.refs_4_
  17.9 0.1 collective-permute-start.7
  18.0 1.6 %collective-permute-start.6 = (bf16[4,512,256]{2,1,0:T(8,128)(2,1)S(1)}, bf16[4,512,256]{2,1,0:T(8,128)(2,1)S(1)}, u32[]{:S(2)}, u32[]{:S(2)}) collective-permute-start(bf16[4,512,256]{2,1,0:T(8,128)(2,1)S(1)} %pad_maximum_fusion.refs_4_), channel_id=1, source_target_pairs={{0,32},{16,112},{32,64},{48,16},{64,96},{80,48},{96,0},{112,80},{1... | collective-permute-start | bytes 3145736 | tf_op jit(solution)/shard_map/ppermute | solution.py:580
  19.7 1.0 collective-permute-done.7.refs_5_
  20.7 1.6 %collective-permute-start.8 = (bf16[4,512,256]{2,1,0:T(8,128)(2,1)S(1)}, bf16[4,512,256]{2,1,0:T(8,128)(2,1)S(1)}, u32[]{:S(2)}, u32[]{:S(2)}) collective-permute-start(bf16[4,512,256]{2,1,0:T(8,128)(2,1)S(1)} %collective-permute-done.7.refs_5_), channel_id=1, source_target_pairs={{0,32},{16,112},{32,64},{48,16},{64,96},{80,48},{96,0},{112,80},{1... | collective-permute-start | bytes 3145736 | tf_op jit(solution)/shard_map/ppermute | solution.py:582
  22.3 0.8 collective-permute-start.9
  23.1 1.9 %collective-permute-start.3 = (bf16[40,256]{1,0:T(8,128)(2,1)S(1)}, bf16[40,256]{1,0:T(8,128)(2,1)S(1)}, u32[]{:S(2)}, u32[]{:S(2)}) collective-permute-start(bf16[40,256]{1,0:T(8,128)(2,1)S(1)} %get-tuple-element.60.refs_0_), channel_id=1, source_target_pairs={{0,4},{1,5},{2,6},{3,7},{4,8},{5,9},{6,10},{7,11},{8,12},{9,13},{1... | collective-permute-start | bytes 61448 | tf_op jit(solution)/shard_map/ppermute | solution.py:571
  25.0 2.1 %collective-permute-start.4 = (bf16[40,256]{1,0:T(8,128)(2,1)S(1)}, bf16[40,256]{1,0:T(8,128)(2,1)S(1)}, u32[]{:S(2)}, u32[]{:S(2)}) collective-permute-start(bf16[40,256]{1,0:T(8,128)(2,1)S(1)} %get-tuple-element.60.refs_0_), channel_id=1, source_target_pairs={{0,12},{1,13},{2,14},{3,15},{4,0},{5,1},{6,2},{7,3},{8,4},{9,5},{1... | collective-permute-start | bytes 61448 | tf_op jit(solution)/shard_map/ppermute | solution.py:571
  27.1 1.8 %collective-permute-done.3.refs_1_ = bf16[40,256]{1,0:T(8,128)(2,1)S(1)} collective-permute-done((bf16[40,256]{1,0:T(8,128)(2,1)S(1)}, bf16[40,256]{1,0:T(8,128)(2,1)S(1)}, u32[]{:S(2)}, u32[]{:S(2)}) %collective-permute-start.3) | collective-permute-done | bytes 20512 | tf_op jit(solution)/shard_map/ppermute | solution.py:571
  28.9 2.0 %collective-permute-start.5 = (bf16[40,256]{1,0:T(8,128)(2,1)S(1)}, bf16[40,256]{1,0:T(8,128)(2,1)S(1)}, u32[]{:S(2)}, u32[]{:S(2)}) collective-permute-start(bf16[40,256]{1,0:T(8,128)(2,1)S(1)} %get-tuple-element.60.refs_0_), channel_id=1, source_target_pairs={{0,8},{1,9},{2,10},{3,11},{4,12},{5,13},{6,14},{7,15},{8,0},{9,1},... | collective-permute-start | bytes 61448 | tf_op jit(solution)/shard_map/ppermute | solution.py:571
  30.9 3.2 %collective-permute-done.5.refs_3_ = bf16[40,256]{1,0:T(8,128)(2,1)S(1)} collective-permute-done((bf16[40,256]{1,0:T(8,128)(2,1)S(1)}, bf16[40,256]{1,0:T(8,128)(2,1)S(1)}, u32[]{:S(2)}, u32[]{:S(2)}) %collective-permute-start.5) | collective-permute-done | bytes 20512 | tf_op jit(solution)/shard_map/ppermute | solution.py:571
  34.2 0.3 pick_near.1
  34.5 2.1 %collective-permute-start.10 = (bf16[256,512]{1,0:T(8,128)(2,1)S(1)}, bf16[256,512]{1,0:T(8,128)(2,1)S(1)}, u32[]{:S(2)}, u32[]{:S(2)}) collective-permute-start(bf16[256,512]{1,0:T(8,128)(2,1)S(1)} %get-tuple-element.67), channel_id=1, source_target_pairs={{0,1},{1,2},{2,3},{3,0},{4,5},{5,6},{6,7},{7,4},{8,9},{9,10},{10,1... | collective-permute-start | bytes 786440 | tf_op jit(solution)/shard_map/ppermute | solution.py:574
  36.5 1.2 collective-permute-start.11
  37.8 12.0 %collective-permute-done.10.refs_1_ = bf16[256,512]{1,0:T(8,128)(2,1)S(1)} collective-permute-done((bf16[256,512]{1,0:T(8,128)(2,1)S(1)}, bf16[256,512]{1,0:T(8,128)(2,1)S(1)}, u32[]{:S(2)}, u32[]{:S(2)}) %collective-permute-start.10) | collective-permute-done | bytes 262176 | tf_op jit(solution)/shard_map/ppermute | solution.py:574
  49.8 0.0 collective-permute-done.9.refs_3_
  49.8 0.0 collective-permute-done.6.refs_6_
  49.8 0.0 collective-permute-done.8.refs_7_
  49.8 0.1 collective-permute-start.15
  49.9 0.1 collective-permute-start.17
  50.0 1.2 collective-permute-start.16
  51.2 1.1 collective-permute-start.12
  52.3 2.1 %collective-permute-start.13 = (bf16[848,512]{1,0:T(8,128)(2,1)S(1)}, bf16[848,512]{1,0:T(8,128)(2,1)S(1)}, u32[]{:S(2)}, u32[]{:S(2)}) collective-permute-start(bf16[848,512]{1,0:T(8,128)(2,1)S(1)} %get-tuple-element.71), channel_id=1, source_target_pairs={{0,3},{1,0},{2,1},{3,2},{4,7},{5,4},{6,5},{7,6},{8,11},{9,8},{10,9... | collective-permute-start | bytes 2605064 | tf_op jit(solution)/shard_map/ppermute | solution.py:577
  54.4 0.0 collective-permute-done.15.refs_8_
  54.4 3.4 %copy-done.1 = bf16[1,1,16,128,2048]{4,3,2,1,0:T(8,128)(2,1)S(1)} copy-done((bf16[1,1,16,128,2048]{4,3,2,1,0:T(8,128)(2,1)S(1)}, bf16[1,1,16,128,2048]{4,3,2,1,0:T(8,128)(2,1)}, u32[]{:S(2)}) %copy-start.1) | copy-done | bytes 8388632
  57.8 0.7 copy-done.3
  58.5 0.2 local_attention.1.local
  58.8 7.2 %collective-permute-done.17.refs_10_ = bf16[4,512,256]{2,1,0:T(8,128)(2,1)S(1)} collective-permute-done((bf16[4,512,256]{2,1,0:T(8,128)(2,1)S(1)}, bf16[4,512,256]{2,1,0:T(8,128)(2,1)S(1)}, u32[]{:S(2)}, u32[]{:S(2)}) %collective-permute-start.17) | collective-permute-done | bytes 1048608 | tf_op jit(solution)/shard_map/ppermute | solution.py:586
  66.0 0.1 fusion
  66.1 0.1 collective-permute-start.18
  66.2 0.5 collective-permute-start.19
  66.7 7.0 %collective-permute-done.12.refs_1_.refs_4_ = bf16[848,512]{1,0:T(8,128)(2,1)S(1)} collective-permute-done((bf16[848,512]{1,0:T(8,128)(2,1)S(1)}, bf16[848,512]{1,0:T(8,128)(2,1)S(1)}, u32[]{:S(2)}, u32[]{:S(2)}) %collective-permute-start.12) | collective-permute-done | bytes 868384 | tf_op jit(solution)/shard_map/ppermute | solution.py:576
  73.6 0.0 collective-permute-done.13.refs_2_.refs_5_
  73.6 0.0 collective-permute-done.16.refs_9_
  73.6 2.3 %product_far.1 = (bf16[256,1024]{1,0:T(8,128)(2,1)S(1)}, bf16[256,1024]{1,0:T(8,128)(2,1)S(1)}) custom-call(bf16[1024,512]{1,0:T(8,128)(2,1)S(1)} %get-tuple-element.96.refs_0_, bf16[256,512]{1,0:T(8,128)(2,1)S(1)} %collective-permute-done.10.refs_1_, bf16[256,512]{1,0:T(8,128)(2,1)S(1)} %collective-permute-done.11.refs_2_, ...), custom_call_target="tpu_custom_call" | custom-call | flops 1000 | bytes 1000 | tf_op jit(solution)/shard_map/product_far/pallas_call | solution.py:274
  76.0 0.0 slice-start
  76.0 2.0 %collective-permute-start.20 = (bf16[256,1024]{1,0:T(8,128)(2,1)S(1)}, bf16[256,1024]{1,0:T(8,128)(2,1)S(1)}, u32[]{:S(2)}, u32[]{:S(2)}) collective-permute-start(bf16[256,1024]{1,0:T(8,128)(2,1)S(1)} %get-tuple-element.87), channel_id=1, source_target_pairs={{0,4},{1,5},{2,6},{3,7},{4,8},{5,9},{6,10},{7,11},{8,12},{9,13},{1... | collective-permute-start | bytes 1572872 | tf_op jit(solution)/shard_map/ppermute | solution.py:602
  78.0 2.4 %collective-permute-start.21 = (bf16[256,1024]{1,0:T(8,128)(2,1)S(1)}, bf16[256,1024]{1,0:T(8,128)(2,1)S(1)}, u32[]{:S(2)}, u32[]{:S(2)}) collective-permute-start(bf16[256,1024]{1,0:T(8,128)(2,1)S(1)} %get-tuple-element.88), channel_id=1, source_target_pairs={{0,12},{1,13},{2,14},{3,15},{4,0},{5,1},{6,2},{7,3},{8,4},{9,5},{1... | collective-permute-start | bytes 1572872 | tf_op jit(solution)/shard_map/ppermute | solution.py:603
  80.4 4.5 %product_near.1 = (bf16[256,1024]{1,0:T(8,128)(2,1)S(1)}, bf16[256,1024]{1,0:T(8,128)(2,1)S(1)}, bf16[256,1024]{1,0:T(8,128)(2,1)S(1)}, bf16[256,1024]{1,0:T(8,128)(2,1)S(1)}) custom-call(bf16[1024,512]{1,0:T(8,128)(2,1)S(1)} %get-tuple-element.96.refs_0_, bf16[848,512]{1,0:T(8,128)(2,1)S(1)} %collective-permute-done.12.refs_1_.refs_4_, ...), custom_call_target="tpu_custom_call" | custom-call | flops 1000 | bytes 1000 | tf_op jit(solution)/shard_map/product_near/pallas_call | solution.py:250
  84.9 0.1 collective-permute-start.23
  84.9 3.2 %collective-permute-start.24 = (bf16[256,1024]{1,0:T(8,128)(2,1)S(1)}, bf16[256,1024]{1,0:T(8,128)(2,1)S(1)}, u32[]{:S(2)}, u32[]{:S(2)}) collective-permute-start(bf16[256,1024]{1,0:T(8,128)(2,1)S(1)} %get-tuple-element.103), channel_id=1, source_target_pairs={{0,12},{1,13},{2,14},{3,15},{4,0},{5,1},{6,2},{7,3},{8,4},{9,5},{1... | collective-permute-start | bytes 1572872 | tf_op jit(solution)/shard_map/ppermute | solution.py:610
  88.2 4.8 %collective-permute-done.20.from_down = bf16[256,1024]{1,0:T(8,128)(2,1)S(1)} collective-permute-done((bf16[256,1024]{1,0:T(8,128)(2,1)S(1)}, bf16[256,1024]{1,0:T(8,128)(2,1)S(1)}, u32[]{:S(2)}, u32[]{:S(2)}) %collective-permute-start.20) | collective-permute-done | bytes 524320 | tf_op jit(solution)/shard_map/ppermute | solution.py:602
  92.9 0.2 relay_sums.1
  93.2 1.9 %collective-permute-start.22 = (bf16[256,1024]{1,0:T(8,128)(2,1)S(1)}, bf16[256,1024]{1,0:T(8,128)(2,1)S(1)}, u32[]{:S(2)}, u32[]{:S(2)}) collective-permute-start(bf16[256,1024]{1,0:T(8,128)(2,1)S(1)} %get-tuple-element.89), channel_id=1, source_target_pairs={{0,4},{1,5},{2,6},{3,7},{4,8},{5,9},{6,10},{7,11},{8,12},{9,13},{1... | collective-permute-start | bytes 1572872 | tf_op jit(solution)/shard_map/ppermute | solution.py:613
  95.1 1.8 %collective-permute-start.25 = (bf16[256,1024]{1,0:T(8,128)(2,1)S(1)}, bf16[256,1024]{1,0:T(8,128)(2,1)S(1)}, u32[]{:S(2)}, u32[]{:S(2)}) collective-permute-start(bf16[256,1024]{1,0:T(8,128)(2,1)S(1)} %get-tuple-element.104), channel_id=1, source_target_pairs={{0,12},{1,13},{2,14},{3,15},{4,0},{5,1},{6,2},{7,3},{8,4},{9,5},{1... | collective-permute-start | bytes 1572872 | tf_op jit(solution)/shard_map/ppermute | solution.py:616
  96.8 1.9 %collective-permute-start.14 = (bf16[336,512]{1,0:T(8,128)(2,1)S(1)}, bf16[336,512]{1,0:T(8,128)(2,1)S(1)}, u32[]{:S(2)}, u32[]{:S(2)}) collective-permute-start(bf16[336,512]{1,0:T(8,128)(2,1)S(1)} %get-tuple-element.75), channel_id=1, source_target_pairs={{0,2},{1,3},{2,0},{3,1},{4,6},{5,7},{6,4},{7,5},{8,10},{9,11},{10,... | collective-permute-start | bytes 1032200 | tf_op jit(solution)/shard_map/ppermute | solution.py:605
  99.4 6.2 %collective-permute-done.14.refs_6_.refs_3_ = bf16[336,512]{1,0:T(8,128)(2,1)S(1)} collective-permute-done((bf16[336,512]{1,0:T(8,128)(2,1)S(1)}, bf16[336,512]{1,0:T(8,128)(2,1)S(1)}, u32[]{:S(2)}, u32[]{:S(2)}) %collective-permute-start.14) | collective-permute-done | bytes 344096 | tf_op jit(solution)/shard_map/ppermute | solution.py:605
  105.6 0.8 unpack.1
  106.4 4.3 %pool_attention.1.pool = f32[16,72,128]{2,1,0:T(8,128)S(1)} custom-call(s32[16]{0:T(128)S(1)} %get-tuple-element.93.slots, s32[16]{0:T(128)S(1)} %get-tuple-element.94.alive, bf16[16,64,128]{2,1,0:T(8,128)(2,1)S(1)} %get-tuple-element.95.query, bf16[16,128,2048]{2,1,0:T(8,128)(2,1)S(1)} %bitcast.11, bf16[16,128,2048]{2,1,0:T(8,128)(2,1)S(1)} %bitcast.12, ...), custom_call_target="tpu_custom_call" | custom-call | flops 1000 | bytes 1000 | tf_op jit(solution)/shard_map/pool_attention/pallas_call | solution.py:341
  110.7 2.3 %product_own.1 = (f32[256,1024]{1,0:T(8,128)S(1)}, f32[256,1024]{1,0:T(8,128)S(1)}) custom-call(bf16[1024,512]{1,0:T(8,128)(2,1)S(1)} %get-tuple-element.96.refs_0_, bf16[848,512]{1,0:T(8,128)(2,1)S(1)} %collective-permute-done.12.refs_1_.refs_4_, bf16[848,512]{1,0:T(8,128)(2,1)S(1)} %collective-permute-done.13.refs_2_.refs_5_, ...), custom_call_target="tpu_custom_call" | custom-call | flops 1000 | bytes 1000 | tf_op jit(solution)/shard_map/product_own/pallas_call | solution.py:250
  113.1 0.7 collective-permute-done.22.up_l
  113.8 3.8 %prefix_attention.1 = (bf16[1,256,2048]{2,1,0:T(8,128)(2,1)}, bf16[16,80,128]{2,1,0:T(8,128)(2,1)S(1)}) custom-call(s32[1]{0:T(128)S(6)} %copy.12.prompt_pages, f32[256,1024]{1,0:T(8,128)S(1)} %get-tuple-element.100.own_l, f32[256,1024]{1,0:T(8,128)S(1)} %get-tuple-element.101.own_r, bf16[256,1024]{1,0:T(8,128)(2,1)S(1)} %collective-permute-done.22.up_l, ...), custom_call_target="tpu_custom_call" | custom-call | flops 300000000 | bytes 6291456 | tf_op jit(solution)/shard_map/prefix_attention/pallas_call | solution.py:504
  117.7 15.5 %all_to_all.5.arrived = bf16[16,80,128]{2,1,0:T(8,128)(2,1)S(1)} all-to-all(bf16[16,80,128]{2,1,0:T(8,128)(2,1)S(1)} %get-tuple-element.108), channel_id=1, replica_groups=mesh['prompt'=8,'sample'=16] {'sample'}, dimensions={0} | all-to-all | bytes 655360 | tf_op jit(solution)/shard_map/all_to_all | solution.py:626
  133.1 1.0 combine.1
  (18 shorter events, 0.0 us)
Async XLA Ops:
  0.6 33.5 %copy-start = (bf16[1,4096,512]{2,1,0:T(8,128)(2,1)S(1)}, bf16[1,4096,512]{2,1,0:T(8,128)(2,1)}, u32[]{:S(2)}) copy-start(bf16[1,4096,512]{2,1,0:T(8,128)(2,1)} %param.10) | copy-start | bytes 12582916
  0.6 10.0 %collective-permute-start = (bf16[512,256]{1,0:T(8,128)(2,1)}, bf16[512,256]{1,0:T(8,128)(2,1)S(1)}, u32[]{:S(2)}, u32[]{:S(2)}) collective-permute-start(bf16[512,256]{1,0:T(8,128)(2,1)} %param.11), channel_id=1, source_target_pairs={{0,1},{1,2},{2,3},{3,0},{4,5},{5,6},{6,7},{7,4},{8,9},{9,10},{10,1... | collective-permute-start | bytes 786440 | tf_op jit(solution)/shard_map/ppermute | solution.py:563
  2.3 9.4 %collective-permute-start.1 = (bf16[512,256]{1,0:T(8,128)(2,1)}, bf16[512,256]{1,0:T(8,128)(2,1)S(1)}, u32[]{:S(2)}, u32[]{:S(2)}) collective-permute-start(bf16[512,256]{1,0:T(8,128)(2,1)} %param.11), channel_id=1, source_target_pairs={{0,3},{1,0},{2,1},{3,2},{4,7},{5,4},{6,5},{7,6},{8,11},{9,8},{10,9... | collective-permute-start | bytes 786440 | tf_op jit(solution)/shard_map/ppermute | solution.py:564
  3.9 12.9 %collective-permute-start.2 = (bf16[512,256]{1,0:T(8,128)(2,1)}, bf16[512,256]{1,0:T(8,128)(2,1)S(1)}, u32[]{:S(2)}, u32[]{:S(2)}) collective-permute-start(bf16[512,256]{1,0:T(8,128)(2,1)} %param.11), channel_id=1, source_target_pairs={{0,2},{1,3},{2,0},{3,1},{4,6},{5,7},{6,4},{7,5},{8,10},{9,11},{10,... | collective-permute-start | bytes 786440 | tf_op jit(solution)/shard_map/ppermute | solution.py:562
  8.6 0.8 copy-start.2
  9.4 0.7 copy-start.4
  17.9 2.7 %collective-permute-start.7 = (bf16[4,512,256]{2,1,0:T(8,128)(2,1)S(1)}, bf16[4,512,256]{2,1,0:T(8,128)(2,1)S(1)}, u32[]{:S(2)}, u32[]{:S(2)}) collective-permute-start(bf16[4,512,256]{2,1,0:T(8,128)(2,1)S(1)} %pad_maximum_fusion.refs_4_), channel_id=1, source_target_pairs={{0,16},{16,0},{32,48},{48,32},{64,80},{80,64},{96,112},{112,96},{1... | collective-permute-start | bytes 3145736 | tf_op jit(solution)/shard_map/ppermute | solution.py:581
  18.0 31.8 %collective-permute-start.6 = (bf16[4,512,256]{2,1,0:T(8,128)(2,1)S(1)}, bf16[4,512,256]{2,1,0:T(8,128)(2,1)S(1)}, u32[]{:S(2)}, u32[]{:S(2)}) collective-permute-start(bf16[4,512,256]{2,1,0:T(8,128)(2,1)S(1)} %pad_maximum_fusion.refs_4_), channel_id=1, source_target_pairs={{0,32},{16,112},{32,64},{48,16},{64,96},{80,48},{96,0},{112,80},{1... | collective-permute-start | bytes 3145736 | tf_op jit(solution)/shard_map/ppermute | solution.py:580
  20.7 29.1 %collective-permute-start.8 = (bf16[4,512,256]{2,1,0:T(8,128)(2,1)S(1)}, bf16[4,512,256]{2,1,0:T(8,128)(2,1)S(1)}, u32[]{:S(2)}, u32[]{:S(2)}) collective-permute-start(bf16[4,512,256]{2,1,0:T(8,128)(2,1)S(1)} %collective-permute-done.7.refs_5_), channel_id=1, source_target_pairs={{0,32},{16,112},{32,64},{48,16},{64,96},{80,48},{96,0},{112,80},{1... | collective-permute-start | bytes 3145736 | tf_op jit(solution)/shard_map/ppermute | solution.py:582
  22.3 27.5 %collective-permute-start.9 = (bf16[768,512]{1,0:T(8,128)(2,1)S(1)}, bf16[768,512]{1,0:T(8,128)(2,1)S(1)}, u32[]{:S(2)}, u32[]{:S(2)}) collective-permute-start(bf16[768,512]{1,0:T(8,128)(2,1)S(1)} %get-tuple-element.66), channel_id=1, source_target_pairs={{0,2},{1,3},{2,0},{3,1},{4,6},{5,7},{6,4},{7,5},{8,10},{9,11},{10,... | collective-permute-start | bytes 2359304 | tf_op jit(solution)/shard_map/ppermute | solution.py:573
  23.1 5.8 %collective-permute-start.3 = (bf16[40,256]{1,0:T(8,128)(2,1)S(1)}, bf16[40,256]{1,0:T(8,128)(2,1)S(1)}, u32[]{:S(2)}, u32[]{:S(2)}) collective-permute-start(bf16[40,256]{1,0:T(8,128)(2,1)S(1)} %get-tuple-element.60.refs_0_), channel_id=1, source_target_pairs={{0,4},{1,5},{2,6},{3,7},{4,8},{5,9},{6,10},{7,11},{8,12},{9,13},{1... | collective-permute-start | bytes 61448 | tf_op jit(solution)/shard_map/ppermute | solution.py:571
  25.0 5.9 %collective-permute-start.4 = (bf16[40,256]{1,0:T(8,128)(2,1)S(1)}, bf16[40,256]{1,0:T(8,128)(2,1)S(1)}, u32[]{:S(2)}, u32[]{:S(2)}) collective-permute-start(bf16[40,256]{1,0:T(8,128)(2,1)S(1)} %get-tuple-element.60.refs_0_), channel_id=1, source_target_pairs={{0,12},{1,13},{2,14},{3,15},{4,0},{5,1},{6,2},{7,3},{8,4},{9,5},{1... | collective-permute-start | bytes 61448 | tf_op jit(solution)/shard_map/ppermute | solution.py:571
  28.9 5.3 %collective-permute-start.5 = (bf16[40,256]{1,0:T(8,128)(2,1)S(1)}, bf16[40,256]{1,0:T(8,128)(2,1)S(1)}, u32[]{:S(2)}, u32[]{:S(2)}) collective-permute-start(bf16[40,256]{1,0:T(8,128)(2,1)S(1)} %get-tuple-element.60.refs_0_), channel_id=1, source_target_pairs={{0,8},{1,9},{2,10},{3,11},{4,12},{5,13},{6,14},{7,15},{8,0},{9,1},... | collective-permute-start | bytes 61448 | tf_op jit(solution)/shard_map/ppermute | solution.py:571
  34.5 15.3 %collective-permute-start.10 = (bf16[256,512]{1,0:T(8,128)(2,1)S(1)}, bf16[256,512]{1,0:T(8,128)(2,1)S(1)}, u32[]{:S(2)}, u32[]{:S(2)}) collective-permute-start(bf16[256,512]{1,0:T(8,128)(2,1)S(1)} %get-tuple-element.67), channel_id=1, source_target_pairs={{0,1},{1,2},{2,3},{3,0},{4,5},{5,6},{6,7},{7,4},{8,9},{9,10},{10,1... | collective-permute-start | bytes 786440 | tf_op jit(solution)/shard_map/ppermute | solution.py:574
  36.5 13.3 %collective-permute-start.11 = (bf16[256,512]{1,0:T(8,128)(2,1)S(1)}, bf16[256,512]{1,0:T(8,128)(2,1)S(1)}, u32[]{:S(2)}, u32[]{:S(2)}) collective-permute-start(bf16[256,512]{1,0:T(8,128)(2,1)S(1)} %get-tuple-element.68), channel_id=1, source_target_pairs={{0,3},{1,0},{2,1},{3,2},{4,7},{5,4},{6,5},{7,6},{8,11},{9,8},{10,9... | collective-permute-start | bytes 786440 | tf_op jit(solution)/shard_map/ppermute | solution.py:575
  49.8 4.6 %collective-permute-start.15 = (bf16[4,512,256]{2,1,0:T(8,128)(2,1)S(1)}, bf16[4,512,256]{2,1,0:T(8,128)(2,1)S(1)}, u32[]{:S(2)}, u32[]{:S(2)}) collective-permute-start(bf16[4,512,256]{2,1,0:T(8,128)(2,1)S(1)} %collective-permute-done.6.refs_6_), channel_id=1, source_target_pairs={{0,16},{16,0},{32,48},{48,32},{64,80},{80,64},{96,112},{112,96},{1... | collective-permute-start | bytes 3145736 | tf_op jit(solution)/shard_map/ppermute | solution.py:587
  49.9 16.1 %collective-permute-start.17 = (bf16[4,512,256]{2,1,0:T(8,128)(2,1)S(1)}, bf16[4,512,256]{2,1,0:T(8,128)(2,1)S(1)}, u32[]{:S(2)}, u32[]{:S(2)}) collective-permute-start(bf16[4,512,256]{2,1,0:T(8,128)(2,1)S(1)} %collective-permute-done.6.refs_6_), channel_id=1, source_target_pairs={{0,32},{16,112},{32,64},{48,16},{64,96},{80,48},{96,0},{112,80},{1... | collective-permute-start | bytes 3145736 | tf_op jit(solution)/shard_map/ppermute | solution.py:586
  50.0 23.6 %collective-permute-start.16 = (bf16[4,512,256]{2,1,0:T(8,128)(2,1)S(1)}, bf16[4,512,256]{2,1,0:T(8,128)(2,1)S(1)}, u32[]{:S(2)}, u32[]{:S(2)}) collective-permute-start(bf16[4,512,256]{2,1,0:T(8,128)(2,1)S(1)} %collective-permute-done.8.refs_7_), channel_id=1, source_target_pairs={{0,16},{16,0},{32,48},{48,32},{64,80},{80,64},{96,112},{112,96},{1... | collective-permute-start | bytes 3145736 | tf_op jit(solution)/shard_map/ppermute | solution.py:588
  51.2 22.4 %collective-permute-start.12 = (bf16[848,512]{1,0:T(8,128)(2,1)S(1)}, bf16[848,512]{1,0:T(8,128)(2,1)S(1)}, u32[]{:S(2)}, u32[]{:S(2)}) collective-permute-start(bf16[848,512]{1,0:T(8,128)(2,1)S(1)} %get-tuple-element.70), channel_id=1, source_target_pairs={{0,1},{1,2},{2,3},{3,0},{4,5},{5,6},{6,7},{7,4},{8,9},{9,10},{10,1... | collective-permute-start | bytes 2605064 | tf_op jit(solution)/shard_map/ppermute | solution.py:576
  52.3 21.3 %collective-permute-start.13 = (bf16[848,512]{1,0:T(8,128)(2,1)S(1)}, bf16[848,512]{1,0:T(8,128)(2,1)S(1)}, u32[]{:S(2)}, u32[]{:S(2)}) collective-permute-start(bf16[848,512]{1,0:T(8,128)(2,1)S(1)} %get-tuple-element.71), channel_id=1, source_target_pairs={{0,3},{1,0},{2,1},{3,2},{4,7},{5,4},{6,5},{7,6},{8,11},{9,8},{10,9... | collective-permute-start | bytes 2605064 | tf_op jit(solution)/shard_map/ppermute | solution.py:577
  54.4 3.4 %copy-start.1 = (bf16[1,1,16,128,2048]{4,3,2,1,0:T(8,128)(2,1)S(1)}, bf16[1,1,16,128,2048]{4,3,2,1,0:T(8,128)(2,1)}, u32[]{:S(2)}) copy-start(bf16[1,1,16,128,2048]{4,3,2,1,0:T(8,128)(2,1)} %param.14) | copy-start | bytes 25165828
  57.8 0.7 copy-start.3
  66.1 7.6 %collective-permute-start.18 = (bf16[2,512,256]{2,1,0:T(8,128)(2,1)S(1)}, bf16[2,512,256]{2,1,0:T(8,128)(2,1)S(1)}, u32[]{:S(2)}, u32[]{:S(2)}) collective-permute-start(bf16[2,512,256]{2,1,0:T(8,128)(2,1)S(1)} %get-tuple-element.111), channel_id=1, source_target_pairs={{0,16},{16,0},{32,48},{48,32},{64,80},{80,64},{96,112},{112,96},{1... | collective-permute-start | bytes 1572872 | tf_op jit(solution)/shard_map/ppermute | solution.py:593
  66.2 7.5 %collective-permute-start.19 = (bf16[2,512,256]{2,1,0:T(8,128)(2,1)S(1)}, bf16[2,512,256]{2,1,0:T(8,128)(2,1)S(1)}, u32[]{:S(2)}, u32[]{:S(2)}) collective-permute-start(bf16[2,512,256]{2,1,0:T(8,128)(2,1)S(1)} %get-tuple-element.110), channel_id=1, source_target_pairs={{0,16},{16,0},{32,48},{48,32},{64,80},{80,64},{96,112},{112,96},{1... | collective-permute-start | bytes 1572872 | tf_op jit(solution)/shard_map/ppermute | solution.py:593
  76.0 30.4 %slice-start = ((s8[8388608]{0:T(1024)(128)(4,1)}), s8[4194304]{0:T(1024)(128)(4,1)S(1)}, s32[]{:S(2)}) async-start(s8[8388608]{0:T(1024)(128)(4,1)} %bitcast.9), calls=%async_computation.1 | async-start | bytes 8388608
  76.0 17.0 %collective-permute-start.20 = (bf16[256,1024]{1,0:T(8,128)(2,1)S(1)}, bf16[256,1024]{1,0:T(8,128)(2,1)S(1)}, u32[]{:S(2)}, u32[]{:S(2)}) collective-permute-start(bf16[256,1024]{1,0:T(8,128)(2,1)S(1)} %get-tuple-element.87), channel_id=1, source_target_pairs={{0,4},{1,5},{2,6},{3,7},{4,8},{5,9},{6,10},{7,11},{8,12},{9,13},{1... | collective-permute-start | bytes 1572872 | tf_op jit(solution)/shard_map/ppermute | solution.py:602
  78.0 15.0 %collective-permute-start.21 = (bf16[256,1024]{1,0:T(8,128)(2,1)S(1)}, bf16[256,1024]{1,0:T(8,128)(2,1)S(1)}, u32[]{:S(2)}, u32[]{:S(2)}) collective-permute-start(bf16[256,1024]{1,0:T(8,128)(2,1)S(1)} %get-tuple-element.88), channel_id=1, source_target_pairs={{0,12},{1,13},{2,14},{3,15},{4,0},{5,1},{6,2},{7,3},{8,4},{9,5},{1... | collective-permute-start | bytes 1572872 | tf_op jit(solution)/shard_map/ppermute | solution.py:603
  80.4 26.1 %slice-start.1 = ((s8[8388608]{0:T(1024)(128)(4,1)}), s8[4194304]{0:T(1024)(128)(4,1)S(1)}, s32[]{:S(2)}) async-start(s8[8388608]{0:T(1024)(128)(4,1)} %bitcast.9), calls=%async_computation.2 | async-start | bytes 8388608
  84.9 28.2 %collective-permute-start.23 = (bf16[256,1024]{1,0:T(8,128)(2,1)S(1)}, bf16[256,1024]{1,0:T(8,128)(2,1)S(1)}, u32[]{:S(2)}, u32[]{:S(2)}) collective-permute-start(bf16[256,1024]{1,0:T(8,128)(2,1)S(1)} %get-tuple-element.102), channel_id=1, source_target_pairs={{0,4},{1,5},{2,6},{3,7},{4,8},{5,9},{6,10},{7,11},{8,12},{9,13},{1... | collective-permute-start | bytes 1572872 | tf_op jit(solution)/shard_map/ppermute | solution.py:610
  84.9 28.1 %collective-permute-start.24 = (bf16[256,1024]{1,0:T(8,128)(2,1)S(1)}, bf16[256,1024]{1,0:T(8,128)(2,1)S(1)}, u32[]{:S(2)}, u32[]{:S(2)}) collective-permute-start(bf16[256,1024]{1,0:T(8,128)(2,1)S(1)} %get-tuple-element.103), channel_id=1, source_target_pairs={{0,12},{1,13},{2,14},{3,15},{4,0},{5,1},{6,2},{7,3},{8,4},{9,5},{1... | collective-permute-start | bytes 1572872 | tf_op jit(solution)/shard_map/ppermute | solution.py:610
  93.2 20.6 %collective-permute-start.22 = (bf16[256,1024]{1,0:T(8,128)(2,1)S(1)}, bf16[256,1024]{1,0:T(8,128)(2,1)S(1)}, u32[]{:S(2)}, u32[]{:S(2)}) collective-permute-start(bf16[256,1024]{1,0:T(8,128)(2,1)S(1)} %get-tuple-element.89), channel_id=1, source_target_pairs={{0,4},{1,5},{2,6},{3,7},{4,8},{5,9},{6,10},{7,11},{8,12},{9,13},{1... | collective-permute-start | bytes 1572872 | tf_op jit(solution)/shard_map/ppermute | solution.py:613
  95.1 18.7 %collective-permute-start.25 = (bf16[256,1024]{1,0:T(8,128)(2,1)S(1)}, bf16[256,1024]{1,0:T(8,128)(2,1)S(1)}, u32[]{:S(2)}, u32[]{:S(2)}) collective-permute-start(bf16[256,1024]{1,0:T(8,128)(2,1)S(1)} %get-tuple-element.104), channel_id=1, source_target_pairs={{0,12},{1,13},{2,14},{3,15},{4,0},{5,1},{6,2},{7,3},{8,4},{9,5},{1... | collective-permute-start | bytes 1572872 | tf_op jit(solution)/shard_map/ppermute | solution.py:616
  96.8 8.8 %collective-permute-start.14 = (bf16[336,512]{1,0:T(8,128)(2,1)S(1)}, bf16[336,512]{1,0:T(8,128)(2,1)S(1)}, u32[]{:S(2)}, u32[]{:S(2)}) collective-permute-start(bf16[336,512]{1,0:T(8,128)(2,1)S(1)} %get-tuple-element.75), channel_id=1, source_target_pairs={{0,2},{1,3},{2,0},{3,1},{4,6},{5,7},{6,4},{7,5},{8,10},{9,11},{10,... | collective-permute-start | bytes 1032200 | tf_op jit(solution)/shard_map/ppermute | solution.py:605

commit v8 on v6

--- a/solution.py
+++ b/solution.py
@@ -197,14 +197,14 @@
 
 
 def pick_near_kernel(states, *refs):
-    blocks, (right, left, last), sems = refs[:4], refs[4:7], refs[7]
+    blocks, (right, left, last_far), sems = refs[:4], refs[4:7], refs[7]
     wanted = [(1, k, right.at[block_rows(k)]) for k in range(4)]
     wanted += [(3, k, left.at[block_rows(k)]) for k in range(4)]
-    wanted += [(2, 3, last.at[block_rows(0)])]
+    wanted += [(2, 3, last_far.at[block_rows(0)])]
     copies = copy_rows(states, sems, wanted)
     put_blocks(right, 4 * ROWS, blocks)
     put_blocks(left, 4 * ROWS, blocks)
-    put_blocks(last, ROWS, blocks)
+    put_blocks(last_far, ROWS, blocks)
     for copy in copies:
         copy.wait()
 
@@ -257,7 +257,9 @@
     for j in range(8):
         total = jnp.zeros((ROWS, COLUMNS), F32)
         for d in range(4):
-            total += jnp.dot(states[d][:ROWS], pieces[j][d], preferred_element_type=F32)
+            total += jnp.dot(
+                states[d][:ROWS], pieces[j][d], preferred_element_type=F32
+            )
         outs[j // 4][:, (j % 4) * COLUMNS : (j % 4 + 1) * COLUMNS] = total.astype(BF16)
 
 
@@ -518,14 +520,17 @@
         local_share = jnp.exp(local_log - high)
         total = jnp.sum(shares, axis=0) + local_share
         mixture = jnp.sum(arrived[:, rows].astype(F32) * shares, axis=0) + local[rows] * local_share
-        out[rows] = (mixture / total).astype(BF16)
+        mixture = (mixture / total).astype(BF16)
+        for h in range(HEADS):
+            lanes = slice((g * HEADS + h) * HEAD_SIZE, (g * HEADS + h + 1) * HEAD_SIZE)
+            out[0, :, lanes] = mixture[h : h + 1]
 
 
 def combine(arrived, local):
     vmem = pl.BlockSpec(memory_space=pltpu.VMEM)
     return pl.pallas_call(
         combine_kernel,
-        out_shape=jax.ShapeDtypeStruct((QUERY_HEADS, HEAD_SIZE), BF16),
+        out_shape=jax.ShapeDtypeStruct((1, 1, QUERY_HEADS * HEAD_SIZE), BF16),
         in_specs=[vmem, vmem],
         out_specs=vmem,
         compiler_params=params(16),
@@ -571,21 +576,25 @@
     far = lax.ppermute(near, "prompt", Y_SPLIT)
     near_swapped = lax.ppermute(near, "prompt", SWAP)
     near_other_swapped = lax.ppermute(near_other, "prompt", SWAP)
-    far, rows_right, rows_left = tie((far, rows_right, rows_left))
+    local_alive = jnp.where(preempted[0] > 0, 0, comp_pages[0])
+    local = local_attention(local_alive, query, new_kv[0], local_pages[0, 0])
+    far, rows_right, rows_left, local = tie((far, rows_right, rows_left, local))
     far_other = lax.ppermute(far, "prompt", SWAP)
+    pieces = [
+        here, here_other, near, near_other, near_swapped, near_other_swapped, far, far_other,
+    ]
     others = [own_states, rows_right, rows_left, rows_far]
-    pieces = [
-        here, here_other, near, near_other,
-        near_swapped, near_other_swapped, far, far_other,
-    ]
 
     far_l, far_r = product_far(others, pieces)
+    from_down = lax.ppermute(far_l, "sample", Z_UP)
+    from_up = lax.ppermute(far_r, "sample", Z_DOWN)
     last_far, rows_right = tie((last_far, rows_right))
     last_far = lax.ppermute(last_far, "sample", X_FAR)
-    from_down = lax.ppermute(far_l, "sample", Z_UP)
-    from_up = lax.ppermute(far_r, "sample", Z_DOWN)
-    up_l, up_r, down_l, down_r = product(others, pieces, ((1,) * 4, (2,) * 4), BF16, "product_near")
+    up_l, up_r, down_l, down_r = product(
+        others, pieces, ((1,) * 4, (2,) * 4), BF16, "product_near"
+    )
     up_r, down_l = lax.ppermute(up_r, "sample", Z_UP), lax.ppermute(down_l, "sample", Z_DOWN)
+    from_down, from_up, last_far = tie((from_down, from_up, last_far))
     up_l, down_r = relay(up_l, down_r, from_down, from_up)
     sums = [
         lax.ppermute(up_l, "sample", Z_UP),
@@ -594,19 +603,16 @@
         lax.ppermute(down_r, "sample", Z_DOWN),
     ]
 
-    query, up_l = tie((query, up_l))
-    local_alive = jnp.where(preempted[0] > 0, 0, comp_pages[0])
-    local = local_attention(local_alive, query, new_kv[0], local_pages[0, 0])
-    arrived, local = tie(([rows_right, rows_left, last_far], local))
+    arrived, up_l = tie(([rows_right, rows_left, last_far], up_l))
     queries_all, by_group, slots, alive = unpack(blocks, arrived)
     pool = pool_attention(slots, alive, queries_all, pool_pages[0, 0])
-    mine, pool, local = tie(([own_states, *arrived], pool, local))
+    mine, pool = tie(([own_states, *arrived], pool))
     sums = [*product(mine, pieces, ((3, 3, 3, 0),), F32, "product_own"), *sums]
 
     cache, packed = prefix_attention(prompt_pages, sums, by_group, pool)
     arrived = lax.all_to_all(packed, "sample", split_axis=0, concat_axis=0, tiled=True)
     attended = combine(arrived, local)
-    return (cache, attended.reshape(1, 1, -1))
+    return (cache, attended)
 
 
 def solution(mesh):

time: 132 us -> 132 us (level)
    ppermute x1, waiting for transfers between devices: 0.88 us -> 10.1 us  [per_device(): lax.ppermute(up_l, 'sample', Z_UP)]
    ppermute x1, waiting for transfers between devices: 20.7 us -> 16.9 us  [per_device(): rows_right = lax.ppermute(to_right, 'sample', X_RIGHT)]
    ppermute x1, waiting for transfers between devices: 4.83 us -> 1.29 us  [per_device(): from_down = lax.ppermute(far_l, 'sample', Z_UP)]
    ppermute x1, waiting for transfers between devices: 4.1 us -> 2.07 us  [per_device(): last_far = lax.ppermute(last_far, 'sample', X_FAR)]
where the time goes in v8:
time: 132 us
  waiting for transfers between devices  53.2 us (40%)
  starting transfers between devices  33.7 us (26%)
  Pallas kernels  22 us (17%)
  blocking collectives  14.6 us (11%)
  local copies, waits for them, and re-layouts  4.16 us (3%)
  between operations  2.95 us (2%)
    ppermute x1, waiting for transfers between devices, per_device(): rows_right = lax.ppermute(to_right, 'sample', X_RIGHT)  16.9 us
    all_to_all x1, blocking collectives, per_device(): lax.all_to_all(packed, 'sample', split_axis=0, concat_axis=0, tiled=True)  14.6 us
    ppermute x1, waiting for transfers between devices, per_device(): lax.ppermute(up_l, 'sample', Z_UP)  10.1 us
    pallas_call x2, Pallas kernels, product(): pl.pallas_call(functools.partial(product_kernel, blocks), out_shape=outs,...  6.81 us
    ppermute x1, waiting for transfers between devices, per_device(): rows_far = lax.ppermute(to_far, 'sample', X_FAR)  6.17 us
    ppermute x3, starting transfers between devices, per_device(): lax.ppermute(block, 'sample', to)  6.07 us
    ppermute x1, waiting for transfers between devices, per_device(): weight_far = lax.ppermute(kv_weight, 'sample', X_FAR)  5.14 us
    ppermute x3, waiting for transfers between devices, per_device(): lax.ppermute(block, 'sample', to)  5.01 us
  transfers between devices with their start and end apart: 23, of which 12 were waited for; matrix products, arithmetic and copies ran while one was open for 0% of the time, Pallas kernels for 11%

profile of v8, /device:TPU:0, one launch (start us, length us, event | category | flops | bytes accessed | tf_op | source)
XLA Modules:
  0.0 131.7 jit_solution(2209216698378791318)
XLA Ops:
  0.6 1.6 %collective-permute-start = (bf16[512,256]{1,0:T(8,128)(2,1)}, bf16[512,256]{1,0:T(8,128)(2,1)S(1)}, u32[]{:S(2)}, u32[]{:S(2)}) collective-permute-start(bf16[512,256]{1,0:T(8,128)(2,1)} %param.11), channel_id=1, source_target_pairs={{0,1},{1,2},{2,3},{3,0},{4,5},{5,6},{6,7},{7,4},{8,9},{9,10},{10,1... | collective-permute-start | bytes 786440 | tf_op jit(solution)/shard_map/ppermute | solution.py:557
  2.3 1.7 %collective-permute-start.1 = (bf16[512,256]{1,0:T(8,128)(2,1)}, bf16[512,256]{1,0:T(8,128)(2,1)S(1)}, u32[]{:S(2)}, u32[]{:S(2)}) collective-permute-start(bf16[512,256]{1,0:T(8,128)(2,1)} %param.11), channel_id=1, source_target_pairs={{0,3},{1,0},{2,1},{3,2},{4,7},{5,4},{6,5},{7,6},{8,11},{9,8},{10,9... | collective-permute-start | bytes 786440 | tf_op jit(solution)/shard_map/ppermute | solution.py:558
  3.9 1.9 %collective-permute-start.2 = (bf16[512,256]{1,0:T(8,128)(2,1)}, bf16[512,256]{1,0:T(8,128)(2,1)S(1)}, u32[]{:S(2)}, u32[]{:S(2)}) collective-permute-start(bf16[512,256]{1,0:T(8,128)(2,1)} %param.11), channel_id=1, source_target_pairs={{0,2},{1,3},{2,0},{3,1},{4,6},{5,7},{6,4},{7,5},{8,10},{9,11},{10,... | collective-permute-start | bytes 786440 | tf_op jit(solution)/shard_map/ppermute | solution.py:556
  5.8 1.6 %pick_far.1 = (bf16[1024,512]{1,0:T(8,128)(2,1)S(1)}, bf16[768,512]{1,0:T(8,128)(2,1)S(1)}) custom-call(bf16[4,4,256,512]{3,2,1,0:T(8,128)(2,1)} %bitcast.15), custom_call_target="tpu_custom_call" | custom-call | flops 1000 | bytes 1000 | tf_op jit(solution)/shard_map/pick_far/pallas_call | solution.py:178
  9.0 0.0 copy-start.2
  9.0 0.7 copy-done.2
  9.7 0.6 prepare.1
  10.3 0.0 collective-permute-done
  10.3 1.4 %collective-permute-done.1 = bf16[512,256]{1,0:T(8,128)(2,1)S(1)} collective-permute-done((bf16[512,256]{1,0:T(8,128)(2,1)}, bf16[512,256]{1,0:T(8,128)(2,1)S(1)}, u32[]{:S(2)}, u32[]{:S(2)}) %collective-permute-start.1) | collective-permute-done | bytes 262176 | tf_op jit(solution)/shard_map/ppermute | solution.py:558
  11.7 5.1 %collective-permute-done.2 = bf16[512,256]{1,0:T(8,128)(2,1)S(1)} collective-permute-done((bf16[512,256]{1,0:T(8,128)(2,1)}, bf16[512,256]{1,0:T(8,128)(2,1)S(1)}, u32[]{:S(2)}, u32[]{:S(2)}) %collective-permute-start.2) | collective-permute-done | bytes 262176 | tf_op jit(solution)/shard_map/ppermute | solution.py:556
  16.9 1.1 pad_maximum_fusion.refs_4_
  17.9 0.0 copy-start.3
  17.9 0.1 collective-permute-start.7
  18.0 1.6 %collective-permute-start.6 = (bf16[4,512,256]{2,1,0:T(8,128)(2,1)S(1)}, bf16[4,512,256]{2,1,0:T(8,128)(2,1)S(1)}, u32[]{:S(2)}, u32[]{:S(2)}) collective-permute-start(bf16[4,512,256]{2,1,0:T(8,128)(2,1)S(1)} %pad_maximum_fusion.refs_4_), channel_id=1, source_target_pairs={{0,32},{16,112},{32,64},{48,16},{64,96},{80,48},{96,0},{112,80},{1... | collective-permute-start | bytes 3145736 | tf_op jit(solution)/shard_map/ppermute | solution.py:572
  19.7 1.0 collective-permute-done.7.refs_5_
  20.7 1.6 %collective-permute-start.8 = (bf16[4,512,256]{2,1,0:T(8,128)(2,1)S(1)}, bf16[4,512,256]{2,1,0:T(8,128)(2,1)S(1)}, u32[]{:S(2)}, u32[]{:S(2)}) collective-permute-start(bf16[4,512,256]{2,1,0:T(8,128)(2,1)S(1)} %collective-permute-done.7.refs_5_), channel_id=1, source_target_pairs={{0,32},{16,112},{32,64},{48,16},{64,96},{80,48},{96,0},{112,80},{1... | collective-permute-start | bytes 3145736 | tf_op jit(solution)/shard_map/ppermute | solution.py:574
  22.3 0.8 collective-permute-start.9
  23.1 1.9 %collective-permute-start.3 = (bf16[40,256]{1,0:T(8,128)(2,1)S(1)}, bf16[40,256]{1,0:T(8,128)(2,1)S(1)}, u32[]{:S(2)}, u32[]{:S(2)}) collective-permute-start(bf16[40,256]{1,0:T(8,128)(2,1)S(1)} %get-tuple-element.56.refs_0_), channel_id=1, source_target_pairs={{0,4},{1,5},{2,6},{3,7},{4,8},{5,9},{6,10},{7,11},{8,12},{9,13},{1... | collective-permute-start | bytes 61448 | tf_op jit(solution)/shard_map/ppermute | solution.py:565
  25.0 2.1 %collective-permute-start.4 = (bf16[40,256]{1,0:T(8,128)(2,1)S(1)}, bf16[40,256]{1,0:T(8,128)(2,1)S(1)}, u32[]{:S(2)}, u32[]{:S(2)}) collective-permute-start(bf16[40,256]{1,0:T(8,128)(2,1)S(1)} %get-tuple-element.56.refs_0_), channel_id=1, source_target_pairs={{0,12},{1,13},{2,14},{3,15},{4,0},{5,1},{6,2},{7,3},{8,4},{9,5},{1... | collective-permute-start | bytes 61448 | tf_op jit(solution)/shard_map/ppermute | solution.py:565
  27.1 1.8 %collective-permute-done.3.refs_1_ = bf16[40,256]{1,0:T(8,128)(2,1)S(1)} collective-permute-done((bf16[40,256]{1,0:T(8,128)(2,1)S(1)}, bf16[40,256]{1,0:T(8,128)(2,1)S(1)}, u32[]{:S(2)}, u32[]{:S(2)}) %collective-permute-start.3) | collective-permute-done | bytes 20512 | tf_op jit(solution)/shard_map/ppermute | solution.py:565
  28.9 2.0 %collective-permute-start.5 = (bf16[40,256]{1,0:T(8,128)(2,1)S(1)}, bf16[40,256]{1,0:T(8,128)(2,1)S(1)}, u32[]{:S(2)}, u32[]{:S(2)}) collective-permute-start(bf16[40,256]{1,0:T(8,128)(2,1)S(1)} %get-tuple-element.56.refs_0_), channel_id=1, source_target_pairs={{0,8},{1,9},{2,10},{3,11},{4,12},{5,13},{6,14},{7,15},{8,0},{9,1},... | collective-permute-start | bytes 61448 | tf_op jit(solution)/shard_map/ppermute | solution.py:565
  30.9 0.0 collective-permute-done.4.refs_2_
  30.9 3.2 %collective-permute-done.5.refs_3_ = bf16[40,256]{1,0:T(8,128)(2,1)S(1)} collective-permute-done((bf16[40,256]{1,0:T(8,128)(2,1)S(1)}, bf16[40,256]{1,0:T(8,128)(2,1)S(1)}, u32[]{:S(2)}, u32[]{:S(2)}) %collective-permute-start.5) | collective-permute-done | bytes 20512 | tf_op jit(solution)/shard_map/ppermute | solution.py:565
  34.2 0.3 pick_near.1
  34.5 2.1 %collective-permute-start.11 = (bf16[1104,512]{1,0:T(8,128)(2,1)S(1)}, bf16[1104,512]{1,0:T(8,128)(2,1)S(1)}, u32[]{:S(2)}, u32[]{:S(2)}) collective-permute-start(bf16[1104,512]{1,0:T(8,128)(2,1)S(1)} %get-tuple-element.64), channel_id=1, source_target_pairs={{0,1},{1,2},{2,3},{3,0},{4,5},{5,6},{6,7},{7,4},{8,9},{9,10},{10,1... | collective-permute-start | bytes 3391496 | tf_op jit(solution)/shard_map/ppermute | solution.py:568
  36.5 1.2 collective-permute-start.12
  37.8 6.2 %collective-permute-done.9.refs_3_ = bf16[768,512]{1,0:T(8,128)(2,1)S(1)} collective-permute-done((bf16[768,512]{1,0:T(8,128)(2,1)S(1)}, bf16[768,512]{1,0:T(8,128)(2,1)S(1)}, u32[]{:S(2)}, u32[]{:S(2)}) %collective-permute-start.9) | collective-permute-done | bytes 786464 | tf_op jit(solution)/shard_map/ppermute | solution.py:567
  44.0 0.0 collective-permute-done.6.refs_6_
  44.0 1.4 %collective-permute-done.8.refs_7_ = bf16[4,512,256]{2,1,0:T(8,128)(2,1)S(1)} collective-permute-done((bf16[4,512,256]{2,1,0:T(8,128)(2,1)S(1)}, bf16[4,512,256]{2,1,0:T(8,128)(2,1)S(1)}, u32[]{:S(2)}, u32[]{:S(2)}) %collective-permute-start.8) | collective-permute-done | bytes 1048608 | tf_op jit(solution)/shard_map/ppermute | solution.py:574
  45.4 0.5 collective-permute-start.10
  45.9 3.4 %copy-done.1 = bf16[1,1,16,128,2048]{4,3,2,1,0:T(8,128)(2,1)S(1)} copy-done((bf16[1,1,16,128,2048]{4,3,2,1,0:T(8,128)(2,1)S(1)}, bf16[1,1,16,128,2048]{4,3,2,1,0:T(8,128)(2,1)}, u32[]{:S(2)}) %copy-start.1) | copy-done | bytes 8388632
  49.3 0.2 local_attention.1.local
  49.5 1.9 %collective-permute-start.13 = (bf16[4,512,256]{2,1,0:T(8,128)(2,1)S(1)}, bf16[4,512,256]{2,1,0:T(8,128)(2,1)S(1)}, u32[]{:S(2)}, u32[]{:S(2)}) collective-permute-start(bf16[4,512,256]{2,1,0:T(8,128)(2,1)S(1)} %collective-permute-done.6.refs_6_), channel_id=1, source_target_pairs={{0,16},{16,0},{32,48},{48,32},{64,80},{80,64},{96,112},{112,96},{1... | collective-permute-start | bytes 3145736 | tf_op jit(solution)/shard_map/ppermute | solution.py:577
  51.4 0.1 collective-permute-start.14
  51.5 16.9 %collective-permute-done.11.refs_1_.refs_4_ = bf16[1104,512]{1,0:T(8,128)(2,1)S(1)} collective-permute-done((bf16[1104,512]{1,0:T(8,128)(2,1)S(1)}, bf16[1104,512]{1,0:T(8,128)(2,1)S(1)}, u32[]{:S(2)}, u32[]{:S(2)}) %collective-permute-start.11) | collective-permute-done | bytes 1130528 | tf_op jit(solution)/shard_map/ppermute | solution.py:568
  68.4 0.0 collective-permute-done.12.refs_2_.refs_5_
  68.4 0.0 collective-permute-done.10.refs_10_
  68.4 0.0 collective-permute-start.15
  68.4 0.0 collective-permute-done.13.refs_8_
  68.4 0.0 collective-permute-done.14.refs_9_
  68.5 2.6 %collective-permute-done.15.refs_11_ = bf16[4,512,256]{2,1,0:T(8,128)(2,1)S(1)} collective-permute-done((bf16[4,512,256]{2,1,0:T(8,128)(2,1)S(1)}, bf16[4,512,256]{2,1,0:T(8,128)(2,1)S(1)}, u32[]{:S(2)}, u32[]{:S(2)}) %collective-permute-start.15) | collective-permute-done | bytes 1048608 | tf_op jit(solution)/shard_map/ppermute | solution.py:582
  71.1 2.3 %product_far.1 = (bf16[256,1024]{1,0:T(8,128)(2,1)S(1)}, bf16[256,1024]{1,0:T(8,128)(2,1)S(1)}) custom-call(bf16[1024,512]{1,0:T(8,128)(2,1)S(1)} %get-tuple-element.88.refs_0_, bf16[1104,512]{1,0:T(8,128)(2,1)S(1)} %collective-permute-done.11.refs_1_.refs_4_, bf16[1104,512]{1,0:T(8,128)(2,1)S(1)} %collective-permute-done.12.refs_2_.refs_5_, ...), custom_call_target="tpu_custom_call" | custom-call | flops 1000 | bytes 1000 | tf_op jit(solution)/shard_map/product_far/pallas_call | solution.py:268
  73.4 2.0 %collective-permute-start.16 = (bf16[256,1024]{1,0:T(8,128)(2,1)S(1)}, bf16[256,1024]{1,0:T(8,128)(2,1)S(1)}, u32[]{:S(2)}, u32[]{:S(2)}) collective-permute-start(bf16[256,1024]{1,0:T(8,128)(2,1)S(1)} %get-tuple-element.73), channel_id=1, source_target_pairs={{0,4},{1,5},{2,6},{3,7},{4,8},{5,9},{6,10},{7,11},{8,12},{9,13},{1... | collective-permute-start | bytes 1572872 | tf_op jit(solution)/shard_map/ppermute | solution.py:589
  75.4 2.2 %collective-permute-start.17 = (bf16[256,1024]{1,0:T(8,128)(2,1)S(1)}, bf16[256,1024]{1,0:T(8,128)(2,1)S(1)}, u32[]{:S(2)}, u32[]{:S(2)}) collective-permute-start(bf16[256,1024]{1,0:T(8,128)(2,1)S(1)} %get-tuple-element.74), channel_id=1, source_target_pairs={{0,12},{1,13},{2,14},{3,15},{4,0},{5,1},{6,2},{7,3},{8,4},{9,5},{1... | collective-permute-start | bytes 1572872 | tf_op jit(solution)/shard_map/ppermute | solution.py:590
  77.6 1.5 %collective-permute-start.18 = (bf16[336,512]{1,0:T(8,128)(2,1)S(1)}, bf16[336,512]{1,0:T(8,128)(2,1)S(1)}, u32[]{:S(2)}, u32[]{:S(2)}) collective-permute-start(bf16[336,512]{1,0:T(8,128)(2,1)S(1)} %get-tuple-element.75), channel_id=1, source_target_pairs={{0,2},{1,3},{2,0},{3,1},{4,6},{5,7},{6,4},{7,5},{8,10},{9,11},{10,... | collective-permute-start | bytes 1032200 | tf_op jit(solution)/shard_map/ppermute | solution.py:592
  79.1 4.5 %product_near.1 = (bf16[256,1024]{1,0:T(8,128)(2,1)S(1)}, bf16[256,1024]{1,0:T(8,128)(2,1)S(1)}, bf16[256,1024]{1,0:T(8,128)(2,1)S(1)}, bf16[256,1024]{1,0:T(8,128)(2,1)S(1)}) custom-call(bf16[1024,512]{1,0:T(8,128)(2,1)S(1)} %get-tuple-element.88.refs_0_, bf16[1104,512]{1,0:T(8,128)(2,1)S(1)} %collective-permute-done.11.refs_1_.refs_4_, ...), custom_call_target="tpu_custom_call" | custom-call | flops 1000 | bytes 1000 | tf_op jit(solution)/shard_map/product_near/pallas_call | solution.py:244
  83.6 0.1 collective-permute-start.20
  83.6 3.2 %collective-permute-start.21 = (bf16[256,1024]{1,0:T(8,128)(2,1)S(1)}, bf16[256,1024]{1,0:T(8,128)(2,1)S(1)}, u32[]{:S(2)}, u32[]{:S(2)}) collective-permute-start(bf16[256,1024]{1,0:T(8,128)(2,1)S(1)} %get-tuple-element.95), channel_id=1, source_target_pairs={{0,12},{1,13},{2,14},{3,15},{4,0},{5,1},{6,2},{7,3},{8,4},{9,5},{1... | collective-permute-start | bytes 1572872 | tf_op jit(solution)/shard_map/ppermute | solution.py:596
  86.9 2.1 %collective-permute-done.18.refs_6_.refs_3_ = bf16[336,512]{1,0:T(8,128)(2,1)S(1)} collective-permute-done((bf16[336,512]{1,0:T(8,128)(2,1)S(1)}, bf16[336,512]{1,0:T(8,128)(2,1)S(1)}, u32[]{:S(2)}, u32[]{:S(2)}) %collective-permute-start.18) | collective-permute-done | bytes 344096 | tf_op jit(solution)/shard_map/ppermute | solution.py:592
  88.9 1.3 collective-permute-done.16.from_down
  90.2 0.0 collective-permute-done.17.from_up
  90.2 0.2 relay_sums.1
  90.5 2.0 %collective-permute-start.19 = (bf16[256,1024]{1,0:T(8,128)(2,1)S(1)}, bf16[256,1024]{1,0:T(8,128)(2,1)S(1)}, u32[]{:S(2)}, u32[]{:S(2)}) collective-permute-start(bf16[256,1024]{1,0:T(8,128)(2,1)S(1)} %get-tuple-element.81), channel_id=1, source_target_pairs={{0,4},{1,5},{2,6},{3,7},{4,8},{5,9},{6,10},{7,11},{8,12},{9,13},{1... | collective-permute-start | bytes 1572872 | tf_op jit(solution)/shard_map/ppermute | solution.py:600
  92.4 1.5 %collective-permute-start.22 = (bf16[256,1024]{1,0:T(8,128)(2,1)S(1)}, bf16[256,1024]{1,0:T(8,128)(2,1)S(1)}, u32[]{:S(2)}, u32[]{:S(2)}) collective-permute-start(bf16[256,1024]{1,0:T(8,128)(2,1)S(1)} %get-tuple-element.96), channel_id=1, source_target_pairs={{0,12},{1,13},{2,14},{3,15},{4,0},{5,1},{6,2},{7,3},{8,4},{9,5},{1... | collective-permute-start | bytes 1572872 | tf_op jit(solution)/shard_map/ppermute | solution.py:603
  94.6 0.8 unpack.1
  95.5 4.3 %pool_attention.1.pool = f32[16,72,128]{2,1,0:T(8,128)S(1)} custom-call(s32[16]{0:T(128)S(1)} %get-tuple-element.85.slots, s32[16]{0:T(128)S(1)} %get-tuple-element.86.alive, bf16[16,64,128]{2,1,0:T(8,128)(2,1)S(1)} %get-tuple-element.87.query, bf16[16,128,2048]{2,1,0:T(8,128)(2,1)S(1)} %bitcast.11, bf16[16,128,2048]{2,1,0:T(8,128)(2,1)S(1)} %bitcast.12, ...), custom_call_target="tpu_custom_call" | custom-call | flops 1000 | bytes 1000 | tf_op jit(solution)/shard_map/pool_attention/pallas_call | solution.py:335
  99.8 2.3 %product_own.1 = (f32[256,1024]{1,0:T(8,128)S(1)}, f32[256,1024]{1,0:T(8,128)S(1)}) custom-call(bf16[1024,512]{1,0:T(8,128)(2,1)S(1)} %get-tuple-element.88.refs_0_, bf16[1104,512]{1,0:T(8,128)(2,1)S(1)} %collective-permute-done.11.refs_1_.refs_4_, bf16[1104,512]{1,0:T(8,128)(2,1)S(1)} %collective-permute-done.12.refs_2_.refs_5_, ...), custom_call_target="tpu_custom_call" | custom-call | flops 1000 | bytes 1000 | tf_op jit(solution)/shard_map/product_own/pallas_call | solution.py:244
  102.1 0.0 collective-permute-done.20.up_r
  102.1 0.0 collective-permute-done.21.down_l
  102.1 10.1 %collective-permute-done.19.up_l = bf16[256,1024]{1,0:T(8,128)(2,1)S(1)} collective-permute-done((bf16[256,1024]{1,0:T(8,128)(2,1)S(1)}, bf16[256,1024]{1,0:T(8,128)(2,1)S(1)}, u32[]{:S(2)}, u32[]{:S(2)}) %collective-permute-start.19) | collective-permute-done | bytes 524320 | tf_op jit(solution)/shard_map/ppermute | solution.py:600
  112.2 0.0 collective-permute-done.22.down_r
  112.2 3.9 %prefix_attention.1 = (bf16[1,256,2048]{2,1,0:T(8,128)(2,1)}, bf16[16,80,128]{2,1,0:T(8,128)(2,1)S(1)}) custom-call(s32[1]{0:T(128)S(6)} %copy.12.prompt_pages, f32[256,1024]{1,0:T(8,128)S(1)} %get-tuple-element.92.own_l, f32[256,1024]{1,0:T(8,128)S(1)} %get-tuple-element.93.own_r, bf16[256,1024]{1,0:T(8,128)(2,1)S(1)} %collective-permute-done.19.up_l, ...), custom_call_target="tpu_custom_call" | custom-call | flops 300000000 | bytes 6291456 | tf_op jit(solution)/shard_map/prefix_attention/pallas_call | solution.py:498
  116.1 14.6 %all_to_all.5.arrived = bf16[16,80,128]{2,1,0:T(8,128)(2,1)S(1)} all-to-all(bf16[16,80,128]{2,1,0:T(8,128)(2,1)S(1)} %get-tuple-element.100), channel_id=1, replica_groups=mesh['prompt'=8,'sample'=16] {'sample'}, dimensions={0} | all-to-all | bytes 655360 | tf_op jit(solution)/shard_map/all_to_all | solution.py:613
  130.7 1.0 combine.1
  (11 shorter events, 0.0 us)
Async XLA Ops:
  0.6 9.7 %collective-permute-start = (bf16[512,256]{1,0:T(8,128)(2,1)}, bf16[512,256]{1,0:T(8,128)(2,1)S(1)}, u32[]{:S(2)}, u32[]{:S(2)}) collective-permute-start(bf16[512,256]{1,0:T(8,128)(2,1)} %param.11), channel_id=1, source_target_pairs={{0,1},{1,2},{2,3},{3,0},{4,5},{5,6},{6,7},{7,4},{8,9},{9,10},{10,1... | collective-permute-start | bytes 786440 | tf_op jit(solution)/shard_map/ppermute | solution.py:557
  2.3 9.4 %collective-permute-start.1 = (bf16[512,256]{1,0:T(8,128)(2,1)}, bf16[512,256]{1,0:T(8,128)(2,1)S(1)}, u32[]{:S(2)}, u32[]{:S(2)}) collective-permute-start(bf16[512,256]{1,0:T(8,128)(2,1)} %param.11), channel_id=1, source_target_pairs={{0,3},{1,0},{2,1},{3,2},{4,7},{5,4},{6,5},{7,6},{8,11},{9,8},{10,9... | collective-permute-start | bytes 786440 | tf_op jit(solution)/shard_map/ppermute | solution.py:558
  3.9 12.9 %collective-permute-start.2 = (bf16[512,256]{1,0:T(8,128)(2,1)}, bf16[512,256]{1,0:T(8,128)(2,1)S(1)}, u32[]{:S(2)}, u32[]{:S(2)}) collective-permute-start(bf16[512,256]{1,0:T(8,128)(2,1)} %param.11), channel_id=1, source_target_pairs={{0,2},{1,3},{2,0},{3,1},{4,6},{5,7},{6,4},{7,5},{8,10},{9,11},{10,... | collective-permute-start | bytes 786440 | tf_op jit(solution)/shard_map/ppermute | solution.py:556
  5.8 3.1 %copy-start.4 = (s32[1,1,16]{2,1,0:T(1,128)S(1)}, s32[1,1,16]{2,1,0:T(1,128)}, u32[]{:S(2)}) copy-start(s32[1,1,16]{2,1,0:T(1,128)} %where.1) | copy-start | bytes 196
  5.8 28.3 %copy-start = (bf16[1,4096,512]{2,1,0:T(8,128)(2,1)S(1)}, bf16[1,4096,512]{2,1,0:T(8,128)(2,1)}, u32[]{:S(2)}) copy-start(bf16[1,4096,512]{2,1,0:T(8,128)(2,1)} %param.10) | copy-start | bytes 12582916
  9.0 0.8 copy-start.2
  17.9 27.9 %copy-start.3 = (bf16[1,1,2048]{2,1,0:T(2,128)(2,1)S(1)}, bf16[1,1,2048]{2,1,0:T(2,128)(2,1)}, u32[]{:S(2)}) copy-start(bf16[1,1,2048]{2,1,0:T(2,128)(2,1)} %param.13) | copy-start | bytes 12292
  17.9 2.7 %collective-permute-start.7 = (bf16[4,512,256]{2,1,0:T(8,128)(2,1)S(1)}, bf16[4,512,256]{2,1,0:T(8,128)(2,1)S(1)}, u32[]{:S(2)}, u32[]{:S(2)}) collective-permute-start(bf16[4,512,256]{2,1,0:T(8,128)(2,1)S(1)} %pad_maximum_fusion.refs_4_), channel_id=1, source_target_pairs={{0,16},{16,0},{32,48},{48,32},{64,80},{80,64},{96,112},{112,96},{1... | collective-permute-start | bytes 3145736 | tf_op jit(solution)/shard_map/ppermute | solution.py:573
  18.0 25.9 %collective-permute-start.6 = (bf16[4,512,256]{2,1,0:T(8,128)(2,1)S(1)}, bf16[4,512,256]{2,1,0:T(8,128)(2,1)S(1)}, u32[]{:S(2)}, u32[]{:S(2)}) collective-permute-start(bf16[4,512,256]{2,1,0:T(8,128)(2,1)S(1)} %pad_maximum_fusion.refs_4_), channel_id=1, source_target_pairs={{0,32},{16,112},{32,64},{48,16},{64,96},{80,48},{96,0},{112,80},{1... | collective-permute-start | bytes 3145736 | tf_op jit(solution)/shard_map/ppermute | solution.py:572
  20.7 24.7 %collective-permute-start.8 = (bf16[4,512,256]{2,1,0:T(8,128)(2,1)S(1)}, bf16[4,512,256]{2,1,0:T(8,128)(2,1)S(1)}, u32[]{:S(2)}, u32[]{:S(2)}) collective-permute-start(bf16[4,512,256]{2,1,0:T(8,128)(2,1)S(1)} %collective-permute-done.7.refs_5_), channel_id=1, source_target_pairs={{0,32},{16,112},{32,64},{48,16},{64,96},{80,48},{96,0},{112,80},{1... | collective-permute-start | bytes 3145736 | tf_op jit(solution)/shard_map/ppermute | solution.py:574
  22.3 21.7 %collective-permute-start.9 = (bf16[768,512]{1,0:T(8,128)(2,1)S(1)}, bf16[768,512]{1,0:T(8,128)(2,1)S(1)}, u32[]{:S(2)}, u32[]{:S(2)}) collective-permute-start(bf16[768,512]{1,0:T(8,128)(2,1)S(1)} %get-tuple-element.62), channel_id=1, source_target_pairs={{0,2},{1,3},{2,0},{3,1},{4,6},{5,7},{6,4},{7,5},{8,10},{9,11},{10,... | collective-permute-start | bytes 2359304 | tf_op jit(solution)/shard_map/ppermute | solution.py:567
  23.1 5.8 %collective-permute-start.3 = (bf16[40,256]{1,0:T(8,128)(2,1)S(1)}, bf16[40,256]{1,0:T(8,128)(2,1)S(1)}, u32[]{:S(2)}, u32[]{:S(2)}) collective-permute-start(bf16[40,256]{1,0:T(8,128)(2,1)S(1)} %get-tuple-element.56.refs_0_), channel_id=1, source_target_pairs={{0,4},{1,5},{2,6},{3,7},{4,8},{5,9},{6,10},{7,11},{8,12},{9,13},{1... | collective-permute-start | bytes 61448 | tf_op jit(solution)/shard_map/ppermute | solution.py:565
  25.0 5.9 %collective-permute-start.4 = (bf16[40,256]{1,0:T(8,128)(2,1)S(1)}, bf16[40,256]{1,0:T(8,128)(2,1)S(1)}, u32[]{:S(2)}, u32[]{:S(2)}) collective-permute-start(bf16[40,256]{1,0:T(8,128)(2,1)S(1)} %get-tuple-element.56.refs_0_), channel_id=1, source_target_pairs={{0,12},{1,13},{2,14},{3,15},{4,0},{5,1},{6,2},{7,3},{8,4},{9,5},{1... | collective-permute-start | bytes 61448 | tf_op jit(solution)/shard_map/ppermute | solution.py:565
  28.9 5.3 %collective-permute-start.5 = (bf16[40,256]{1,0:T(8,128)(2,1)S(1)}, bf16[40,256]{1,0:T(8,128)(2,1)S(1)}, u32[]{:S(2)}, u32[]{:S(2)}) collective-permute-start(bf16[40,256]{1,0:T(8,128)(2,1)S(1)} %get-tuple-element.56.refs_0_), channel_id=1, source_target_pairs={{0,8},{1,9},{2,10},{3,11},{4,12},{5,13},{6,14},{7,15},{8,0},{9,1},... | collective-permute-start | bytes 61448 | tf_op jit(solution)/shard_map/ppermute | solution.py:565
  34.5 33.9 %collective-permute-start.11 = (bf16[1104,512]{1,0:T(8,128)(2,1)S(1)}, bf16[1104,512]{1,0:T(8,128)(2,1)S(1)}, u32[]{:S(2)}, u32[]{:S(2)}) collective-permute-start(bf16[1104,512]{1,0:T(8,128)(2,1)S(1)} %get-tuple-element.64), channel_id=1, source_target_pairs={{0,1},{1,2},{2,3},{3,0},{4,5},{5,6},{6,7},{7,4},{8,9},{9,10},{10,1... | collective-permute-start | bytes 3391496 | tf_op jit(solution)/shard_map/ppermute | solution.py:568
  36.5 31.9 %collective-permute-start.12 = (bf16[1104,512]{1,0:T(8,128)(2,1)S(1)}, bf16[1104,512]{1,0:T(8,128)(2,1)S(1)}, u32[]{:S(2)}, u32[]{:S(2)}) collective-permute-start(bf16[1104,512]{1,0:T(8,128)(2,1)S(1)} %get-tuple-element.65), channel_id=1, source_target_pairs={{0,3},{1,0},{2,1},{3,2},{4,7},{5,4},{6,5},{7,6},{8,11},{9,8},{10,9... | collective-permute-start | bytes 3391496 | tf_op jit(solution)/shard_map/ppermute | solution.py:569
  45.4 23.1 %collective-permute-start.10 = (bf16[4,512,256]{2,1,0:T(8,128)(2,1)S(1)}, bf16[4,512,256]{2,1,0:T(8,128)(2,1)S(1)}, u32[]{:S(2)}, u32[]{:S(2)}) collective-permute-start(bf16[4,512,256]{2,1,0:T(8,128)(2,1)S(1)} %collective-permute-done.6.refs_6_), channel_id=1, source_target_pairs={{0,32},{16,112},{32,64},{48,16},{64,96},{80,48},{96,0},{112,80},{1... | collective-permute-start | bytes 3145736 | tf_op jit(solution)/shard_map/ppermute | solution.py:576
  45.9 3.4 %copy-start.1 = (bf16[1,1,16,128,2048]{4,3,2,1,0:T(8,128)(2,1)S(1)}, bf16[1,1,16,128,2048]{4,3,2,1,0:T(8,128)(2,1)}, u32[]{:S(2)}) copy-start(bf16[1,1,16,128,2048]{4,3,2,1,0:T(8,128)(2,1)} %param.14) | copy-start | bytes 25165828
  49.5 18.9 %collective-permute-start.13 = (bf16[4,512,256]{2,1,0:T(8,128)(2,1)S(1)}, bf16[4,512,256]{2,1,0:T(8,128)(2,1)S(1)}, u32[]{:S(2)}, u32[]{:S(2)}) collective-permute-start(bf16[4,512,256]{2,1,0:T(8,128)(2,1)S(1)} %collective-permute-done.6.refs_6_), channel_id=1, source_target_pairs={{0,16},{16,0},{32,48},{48,32},{64,80},{80,64},{96,112},{112,96},{1... | collective-permute-start | bytes 3145736 | tf_op jit(solution)/shard_map/ppermute | solution.py:577
  51.4 17.1 %collective-permute-start.14 = (bf16[4,512,256]{2,1,0:T(8,128)(2,1)S(1)}, bf16[4,512,256]{2,1,0:T(8,128)(2,1)S(1)}, u32[]{:S(2)}, u32[]{:S(2)}) collective-permute-start(bf16[4,512,256]{2,1,0:T(8,128)(2,1)S(1)} %collective-permute-done.8.refs_7_), channel_id=1, source_target_pairs={{0,16},{16,0},{32,48},{48,32},{64,80},{80,64},{96,112},{112,96},{1... | collective-permute-start | bytes 3145736 | tf_op jit(solution)/shard_map/ppermute | solution.py:578
  68.4 2.7 %collective-permute-start.15 = (bf16[4,512,256]{2,1,0:T(8,128)(2,1)S(1)}, bf16[4,512,256]{2,1,0:T(8,128)(2,1)S(1)}, u32[]{:S(2)}, u32[]{:S(2)}) collective-permute-start(bf16[4,512,256]{2,1,0:T(8,128)(2,1)S(1)} %collective-permute-done.10.refs_10_), channel_id=1, source_target_pairs={{0,16},{16,0},{32,48},{48,32},{64,80},{80,64},{96,112},{112,96},{1... | collective-permute-start | bytes 3145736 | tf_op jit(solution)/shard_map/ppermute | solution.py:582
  71.1 24.4 %slice-start = ((s8[8388608]{0:T(1024)(128)(4,1)}), s8[4194304]{0:T(1024)(128)(4,1)S(1)}, s32[]{:S(2)}) async-start(s8[8388608]{0:T(1024)(128)(4,1)} %bitcast.9), calls=%async_computation.1 | async-start | bytes 8388608
  73.4 16.8 %collective-permute-start.16 = (bf16[256,1024]{1,0:T(8,128)(2,1)S(1)}, bf16[256,1024]{1,0:T(8,128)(2,1)S(1)}, u32[]{:S(2)}, u32[]{:S(2)}) collective-permute-start(bf16[256,1024]{1,0:T(8,128)(2,1)S(1)} %get-tuple-element.73), channel_id=1, source_target_pairs={{0,4},{1,5},{2,6},{3,7},{4,8},{5,9},{6,10},{7,11},{8,12},{9,13},{1... | collective-permute-start | bytes 1572872 | tf_op jit(solution)/shard_map/ppermute | solution.py:589
  75.4 14.8 %collective-permute-start.17 = (bf16[256,1024]{1,0:T(8,128)(2,1)S(1)}, bf16[256,1024]{1,0:T(8,128)(2,1)S(1)}, u32[]{:S(2)}, u32[]{:S(2)}) collective-permute-start(bf16[256,1024]{1,0:T(8,128)(2,1)S(1)} %get-tuple-element.74), channel_id=1, source_target_pairs={{0,12},{1,13},{2,14},{3,15},{4,0},{5,1},{6,2},{7,3},{8,4},{9,5},{1... | collective-permute-start | bytes 1572872 | tf_op jit(solution)/shard_map/ppermute | solution.py:590
  77.6 17.9 %slice-start.1 = ((s8[8388608]{0:T(1024)(128)(4,1)}), s8[4194304]{0:T(1024)(128)(4,1)S(1)}, s32[]{:S(2)}) async-start(s8[8388608]{0:T(1024)(128)(4,1)} %bitcast.9), calls=%async_computation.2 | async-start | bytes 8388608
  77.6 11.3 %collective-permute-start.18 = (bf16[336,512]{1,0:T(8,128)(2,1)S(1)}, bf16[336,512]{1,0:T(8,128)(2,1)S(1)}, u32[]{:S(2)}, u32[]{:S(2)}) collective-permute-start(bf16[336,512]{1,0:T(8,128)(2,1)S(1)} %get-tuple-element.75), channel_id=1, source_target_pairs={{0,2},{1,3},{2,0},{3,1},{4,6},{5,7},{6,4},{7,5},{8,10},{9,11},{10,... | collective-permute-start | bytes 1032200 | tf_op jit(solution)/shard_map/ppermute | solution.py:592
  83.6 18.6 %collective-permute-start.20 = (bf16[256,1024]{1,0:T(8,128)(2,1)S(1)}, bf16[256,1024]{1,0:T(8,128)(2,1)S(1)}, u32[]{:S(2)}, u32[]{:S(2)}) collective-permute-start(bf16[256,1024]{1,0:T(8,128)(2,1)S(1)} %get-tuple-element.94), channel_id=1, source_target_pairs={{0,4},{1,5},{2,6},{3,7},{4,8},{5,9},{6,10},{7,11},{8,12},{9,13},{1... | collective-permute-start | bytes 1572872 | tf_op jit(solution)/shard_map/ppermute | solution.py:596
  83.6 18.5 %collective-permute-start.21 = (bf16[256,1024]{1,0:T(8,128)(2,1)S(1)}, bf16[256,1024]{1,0:T(8,128)(2,1)S(1)}, u32[]{:S(2)}, u32[]{:S(2)}) collective-permute-start(bf16[256,1024]{1,0:T(8,128)(2,1)S(1)} %get-tuple-element.95), channel_id=1, source_target_pairs={{0,12},{1,13},{2,14},{3,15},{4,0},{5,1},{6,2},{7,3},{8,4},{9,5},{1... | collective-permute-start | bytes 1572872 | tf_op jit(solution)/shard_map/ppermute | solution.py:596
  90.5 21.7 %collective-permute-start.19 = (bf16[256,1024]{1,0:T(8,128)(2,1)S(1)}, bf16[256,1024]{1,0:T(8,128)(2,1)S(1)}, u32[]{:S(2)}, u32[]{:S(2)}) collective-permute-start(bf16[256,1024]{1,0:T(8,128)(2,1)S(1)} %get-tuple-element.81), channel_id=1, source_target_pairs={{0,4},{1,5},{2,6},{3,7},{4,8},{5,9},{6,10},{7,11},{8,12},{9,13},{1... | collective-permute-start | bytes 1572872 | tf_op jit(solution)/shard_map/ppermute | solution.py:600
  92.4 19.8 %collective-permute-start.22 = (bf16[256,1024]{1,0:T(8,128)(2,1)S(1)}, bf16[256,1024]{1,0:T(8,128)(2,1)S(1)}, u32[]{:S(2)}, u32[]{:S(2)}) collective-permute-start(bf16[256,1024]{1,0:T(8,128)(2,1)S(1)} %get-tuple-element.96), channel_id=1, source_target_pairs={{0,12},{1,13},{2,14},{3,15},{4,0},{5,1},{6,2},{7,3},{8,4},{9,5},{1... | collective-permute-start | bytes 1572872 | tf_op jit(solution)/shard_map/ppermute | solution.py:603

commit v9 on v8

--- a/solution.py
+++ b/solution.py
@@ -197,13 +197,13 @@
 
 
 def pick_near_kernel(states, *refs):
-    blocks, (right, left, last_far), sems = refs[:4], refs[4:7], refs[7]
-    wanted = [(1, k, right.at[block_rows(k)]) for k in range(4)]
-    wanted += [(3, k, left.at[block_rows(k)]) for k in range(4)]
-    wanted += [(2, 3, last_far.at[block_rows(0)])]
+    blocks, (right, left, last_right, last_left, last_far), sems = refs[:4], refs[4:9], refs[9]
+    wanted = [(1, k, right.at[block_rows(k)]) for k in range(3)]
+    wanted += [(3, k, left.at[block_rows(k)]) for k in range(3)]
+    wanted += [(1, 3, last_right), (3, 3, last_left), (2, 3, last_far.at[block_rows(0)])]
     copies = copy_rows(states, sems, wanted)
-    put_blocks(right, 4 * ROWS, blocks)
-    put_blocks(left, 4 * ROWS, blocks)
+    put_blocks(right, 3 * ROWS, blocks)
+    put_blocks(left, 3 * ROWS, blocks)
     put_blocks(last_far, ROWS, blocks)
     for copy in copies:
         copy.wait()
@@ -213,10 +213,11 @@
     vmem = pl.BlockSpec(memory_space=pltpu.VMEM)
     return pl.pallas_call(
         pick_near_kernel,
-        out_shape=[jax.ShapeDtypeStruct((4 * ROWS + 2 * BLOCK, SLICE), BF16)] * 2
+        out_shape=[jax.ShapeDtypeStruct((3 * ROWS + 2 * BLOCK, SLICE), BF16)] * 2
+        + [jax.ShapeDtypeStruct((ROWS, SLICE), BF16)] * 2
         + [jax.ShapeDtypeStruct((ROWS + 2 * BLOCK, SLICE), BF16)],
         in_specs=[pl.BlockSpec(memory_space=pl.ANY)] + [vmem] * 4,
-        out_specs=[vmem] * 3,
+        out_specs=[vmem] * 5,
         scratch_shapes=[pltpu.SemaphoreType.DMA((9,))],
         compiler_params=params(44),
         cost_estimate=cost(1000, 1000),
@@ -224,15 +225,19 @@
     )(states, *blocks)
 
 
+def weight_of(pieces, j, d):
+    return pieces[j][d] if j < 6 else pieces[2 * j - 6 + d // 2][d % 2]
+
+
 def product_kernel(blocks, *refs):
-    states, pieces, outs = refs[:4], refs[4:12], refs[12:]
+    states, pieces, outs = refs[:4], refs[4:14], refs[14:]
     for j in range(8):
         for k, block in enumerate(blocks):
             total = jnp.zeros((ROWS, COLUMNS), F32)
             for d in range(4):
                 at = block[d] * ROWS
                 total += jnp.dot(
-                    states[d][at : at + ROWS], pieces[j][d], preferred_element_type=F32
+                    states[d][at : at + ROWS], weight_of(pieces, j, d), preferred_element_type=F32
                 )
             out = outs[2 * k + j // 4]
             out[:, (j % 4) * COLUMNS : (j % 4 + 1) * COLUMNS] = total.astype(out.dtype)
@@ -244,7 +249,7 @@
     return pl.pallas_call(
         functools.partial(product_kernel, blocks),
         out_shape=outs,
-        in_specs=[vmem] * 12,
+        in_specs=[vmem] * 14,
         out_specs=[vmem] * len(outs),
         compiler_params=params(20),
         cost_estimate=cost(1000, 1000),
@@ -253,12 +258,12 @@
 
 
 def product_far_kernel(*refs):
-    states, pieces, outs = refs[:4], refs[4:12], refs[12:]
+    states, pieces, outs = refs[:4], refs[4:14], refs[14:]
     for j in range(8):
         total = jnp.zeros((ROWS, COLUMNS), F32)
         for d in range(4):
             total += jnp.dot(
-                states[d][:ROWS], pieces[j][d], preferred_element_type=F32
+                states[d][:ROWS], weight_of(pieces, j, d), preferred_element_type=F32
             )
         outs[j // 4][:, (j % 4) * COLUMNS : (j % 4 + 1) * COLUMNS] = total.astype(BF16)
 
@@ -268,7 +273,7 @@
     return pl.pallas_call(
         product_far_kernel,
         out_shape=[jax.ShapeDtypeStruct((ROWS, KVW // 2), BF16)] * 2,
-        in_specs=[vmem] * 12,
+        in_specs=[vmem] * 14,
         out_specs=[vmem] * 2,
         compiler_params=params(20),
         cost_estimate=cost(1000, 1000),
@@ -563,7 +568,7 @@
         ((kv_weight, weight_right, weight_left, weight_far), own_states, to_far, block)
     )
     blocks = [block] + [lax.ppermute(block, "sample", to) for to in (Z_UP, Z_DOWN, Z_FAR)]
-    to_right, to_left, last_far = pick_near(states, blocks)
+    to_right, to_left, last_right, last_left, last_far = pick_near(states, blocks)
     rows_far = lax.ppermute(to_far, "sample", X_FAR)
     rows_right = lax.ppermute(to_right, "sample", X_RIGHT)
     rows_left = lax.ppermute(to_left, "sample", X_LEFT)
@@ -572,16 +577,16 @@
     near = lax.ppermute(here, "prompt", Y_SPLIT)
     here_other = lax.ppermute(here, "prompt", SWAP)
     near_other = lax.ppermute(here_other, "prompt", Y_SPLIT)
-    near, near_other, rows_far = tie((near, near_other, rows_far))
-    far = lax.ppermute(near, "prompt", Y_SPLIT)
+    local_alive = jnp.where(preempted[0] > 0, 0, comp_pages[0])
+    local = local_attention(local_alive, query, new_kv[0], local_pages[0, 0])
+    near, near_other, rows_far, local = tie((near, near_other, rows_far, local))
+    far = [lax.ppermute(half, "prompt", Y_SPLIT) for half in (near[:2], near[2:])]
     near_swapped = lax.ppermute(near, "prompt", SWAP)
     near_other_swapped = lax.ppermute(near_other, "prompt", SWAP)
-    local_alive = jnp.where(preempted[0] > 0, 0, comp_pages[0])
-    local = local_attention(local_alive, query, new_kv[0], local_pages[0, 0])
-    far, rows_right, rows_left, local = tie((far, rows_right, rows_left, local))
-    far_other = lax.ppermute(far, "prompt", SWAP)
+    far, rows_right, rows_left = tie((far, rows_right, rows_left))
+    far_other = [lax.ppermute(half, "prompt", SWAP) for half in far]
     pieces = [
-        here, here_other, near, near_other, near_swapped, near_other_swapped, far, far_other,
+        here, here_other, near, near_other, near_swapped, near_other_swapped, *far, *far_other,
     ]
     others = [own_states, rows_right, rows_left, rows_far]
 
@@ -606,8 +611,10 @@
     arrived, up_l = tie(([rows_right, rows_left, last_far], up_l))
     queries_all, by_group, slots, alive = unpack(blocks, arrived)
     pool = pool_attention(slots, alive, queries_all, pool_pages[0, 0])
-    mine, pool = tie(([own_states, *arrived], pool))
-    sums = [*product(mine, pieces, ((3, 3, 3, 0),), F32, "product_own"), *sums]
+    last_right = lax.ppermute(last_right, "sample", X_RIGHT)
+    last_left = lax.ppermute(last_left, "sample", X_LEFT)
+    mine, pool = tie(([own_states, last_right, last_left, last_far], pool))
+    sums = [*product(mine, pieces, ((3, 0, 0, 0),), F32, "product_own"), *sums]
 
     cache, packed = prefix_attention(prompt_pages, sums, by_group, pool)
     arrived = lax.all_to_all(packed, "sample", split_axis=0, concat_axis=0, tiled=True)

time: 132 us -> 127 us (0.962)
  waiting for transfers between devices: 53.2 us -> 47 us
  Pallas kernels: 22 us -> 24.6 us
  blocking collectives: 14.6 us -> 13 us
  local copies, waits for them, and re-layouts: 4.16 us -> 5.57 us
    ppermute x1, waiting for transfers between devices: 6.17 us -> 0.01 us  [per_device(): rows_far = lax.ppermute(to_far, 'sample', X_FAR)]
    ppermute x1, waiting for transfers between devices: 2.07 us -> 6.57 us  [per_device(): last_far = lax.ppermute(last_far, 'sample', X_FAR)]
    ppermute x1, waiting for transfers between devices: 10.1 us -> 7.08 us  [per_device(): lax.ppermute(up_l, 'sample', Z_UP)]
    pallas_call x1, Pallas kernels: 0.24 us -> 2.91 us  [local_attention(): pl.pallas_call(local_kernel, out_shape=jax.ShapeDtypeStruct((PACK, HEAD_S...]
    ppermute x2 -> x6, starting transfers between devices: 0.54 us -> 3.19 us  [the longest x2 2.01 us: per_device(): lax.ppermute(half, 'prompt', Y_SPLIT)]
    ppermute x2 -> x6, waiting for transfers between devices: 2.63 us -> 4.8 us  [the longest x2 3.46 us: per_device(): far_other = [lax.ppermute(half, 'prompt', SWAP) for half in far]]
    ppermute x1, waiting for transfers between devices: 16.9 us -> 14.9 us  [per_device(): rows_right = lax.ppermute(to_right, 'sample', X_RIGHT)]
    ppermute x1, starting transfers between devices: 1.96 us -> 0.11 us  [per_device(): lax.ppermute(up_l, 'sample', Z_UP)]
  transfers between devices with their start and end apart: 23 -> 27, of which waited for: 12 -> 13; matrix products, arithmetic and copies ran while one was open for 0% -> 0% of each run, Pallas kernels for 11% -> 14%
where the time goes in v9:
time: 127 us
  waiting for transfers between devices  47 us (37%)
  starting transfers between devices  32.8 us (26%)
  Pallas kernels  24.6 us (19%)
  blocking collectives  13 us (10%)
  local copies, waits for them, and re-layouts  5.57 us (4%)
  between operations  2.79 us (2%)
    ppermute x1, waiting for transfers between devices, per_device(): rows_right = lax.ppermute(to_right, 'sample', X_RIGHT)  14.9 us
    all_to_all x1, blocking collectives, per_device(): lax.all_to_all(packed, 'sample', split_axis=0, concat_axis=0, tiled=True)  13 us
    ppermute x1, waiting for transfers between devices, per_device(): lax.ppermute(up_l, 'sample', Z_UP)  7.08 us
    pallas_call x2, Pallas kernels, product(): pl.pallas_call(functools.partial(product_kernel, blocks), out_shape=outs,...  6.81 us
    ppermute x1, waiting for transfers between devices, per_device(): last_far = lax.ppermute(last_far, 'sample', X_FAR)  6.57 us
    ppermute x3, starting transfers between devices, per_device(): lax.ppermute(block, 'sample', to)  6.07 us
    unnamed x14, local copies, waits for them, and re-layouts  5.5 us
    ppermute x1, waiting for transfers between devices, per_device(): weight_far = lax.ppermute(kv_weight, 'sample', X_FAR)  5.14 us
  transfers between devices with their start and end apart: 27, of which 13 were waited for; matrix products, arithmetic and copies ran while one was open for 0% of the time, Pallas kernels for 14%

profile of v9, /device:TPU:0, one launch (start us, length us, event | category | flops | bytes accessed | tf_op | source)
XLA Modules:
  0.0 126.8 jit_solution(15620494601469229482)
XLA Ops:
  0.6 1.6 %collective-permute-start = (bf16[512,256]{1,0:T(8,128)(2,1)}, bf16[512,256]{1,0:T(8,128)(2,1)S(1)}, u32[]{:S(2)}, u32[]{:S(2)}) collective-permute-start(bf16[512,256]{1,0:T(8,128)(2,1)} %param.11), channel_id=1, source_target_pairs={{0,1},{1,2},{2,3},{3,0},{4,5},{5,6},{6,7},{7,4},{8,9},{9,10},{10,1... | collective-permute-start | bytes 786440 | tf_op jit(solution)/shard_map/ppermute | solution.py:562
  2.3 1.7 %collective-permute-start.1 = (bf16[512,256]{1,0:T(8,128)(2,1)}, bf16[512,256]{1,0:T(8,128)(2,1)S(1)}, u32[]{:S(2)}, u32[]{:S(2)}) collective-permute-start(bf16[512,256]{1,0:T(8,128)(2,1)} %param.11), channel_id=1, source_target_pairs={{0,3},{1,0},{2,1},{3,2},{4,7},{5,4},{6,5},{7,6},{8,11},{9,8},{10,9... | collective-permute-start | bytes 786440 | tf_op jit(solution)/shard_map/ppermute | solution.py:563
  3.9 1.9 %collective-permute-start.2 = (bf16[512,256]{1,0:T(8,128)(2,1)}, bf16[512,256]{1,0:T(8,128)(2,1)S(1)}, u32[]{:S(2)}, u32[]{:S(2)}) collective-permute-start(bf16[512,256]{1,0:T(8,128)(2,1)} %param.11), channel_id=1, source_target_pairs={{0,2},{1,3},{2,0},{3,1},{4,6},{5,7},{6,4},{7,5},{8,10},{9,11},{10,... | collective-permute-start | bytes 786440 | tf_op jit(solution)/shard_map/ppermute | solution.py:561
  5.8 1.5 %pick_far.1 = (bf16[1024,512]{1,0:T(8,128)(2,1)S(1)}, bf16[768,512]{1,0:T(8,128)(2,1)S(1)}) custom-call(bf16[4,4,256,512]{3,2,1,0:T(8,128)(2,1)} %bitcast.15), custom_call_target="tpu_custom_call" | custom-call | flops 1000 | bytes 1000 | tf_op jit(solution)/shard_map/pick_far/pallas_call | solution.py:178
  8.6 0.0 copy-start.2
  8.6 0.7 copy-done.2
  9.4 0.7 copy-done.4
  10.0 0.6 prepare.1
  10.6 1.1 collective-permute-done.1
  11.7 5.1 %collective-permute-done.2 = bf16[512,256]{1,0:T(8,128)(2,1)S(1)} collective-permute-done((bf16[512,256]{1,0:T(8,128)(2,1)}, bf16[512,256]{1,0:T(8,128)(2,1)S(1)}, u32[]{:S(2)}, u32[]{:S(2)}) %collective-permute-start.2) | collective-permute-done | bytes 262176 | tf_op jit(solution)/shard_map/ppermute | solution.py:561
  16.9 1.1 pad_maximum_fusion.refs_4_
  17.9 0.1 collective-permute-start.9
  18.0 1.6 %collective-permute-start.8 = (bf16[4,512,256]{2,1,0:T(8,128)(2,1)S(1)}, bf16[4,512,256]{2,1,0:T(8,128)(2,1)S(1)}, u32[]{:S(2)}, u32[]{:S(2)}) collective-permute-start(bf16[4,512,256]{2,1,0:T(8,128)(2,1)S(1)} %pad_maximum_fusion.refs_4_), channel_id=1, source_target_pairs={{0,32},{16,112},{32,64},{48,16},{64,96},{80,48},{96,0},{112,80},{1... | collective-permute-start | bytes 3145736 | tf_op jit(solution)/shard_map/ppermute | solution.py:577
  19.7 1.0 collective-permute-done.9.refs_5_
  20.7 1.6 %collective-permute-start.10 = (bf16[4,512,256]{2,1,0:T(8,128)(2,1)S(1)}, bf16[4,512,256]{2,1,0:T(8,128)(2,1)S(1)}, u32[]{:S(2)}, u32[]{:S(2)}) collective-permute-start(bf16[4,512,256]{2,1,0:T(8,128)(2,1)S(1)} %collective-permute-done.9.refs_5_), channel_id=1, source_target_pairs={{0,32},{16,112},{32,64},{48,16},{64,96},{80,48},{96,0},{112,80},{1... | collective-permute-start | bytes 3145736 | tf_op jit(solution)/shard_map/ppermute | solution.py:579
  22.3 0.8 collective-permute-start.11
  23.1 1.9 %collective-permute-start.3 = (bf16[40,256]{1,0:T(8,128)(2,1)S(1)}, bf16[40,256]{1,0:T(8,128)(2,1)S(1)}, u32[]{:S(2)}, u32[]{:S(2)}) collective-permute-start(bf16[40,256]{1,0:T(8,128)(2,1)S(1)} %get-tuple-element.59.refs_0_), channel_id=1, source_target_pairs={{0,4},{1,5},{2,6},{3,7},{4,8},{5,9},{6,10},{7,11},{8,12},{9,13},{1... | collective-permute-start | bytes 61448 | tf_op jit(solution)/shard_map/ppermute | solution.py:570
  25.0 2.1 %collective-permute-start.4 = (bf16[40,256]{1,0:T(8,128)(2,1)S(1)}, bf16[40,256]{1,0:T(8,128)(2,1)S(1)}, u32[]{:S(2)}, u32[]{:S(2)}) collective-permute-start(bf16[40,256]{1,0:T(8,128)(2,1)S(1)} %get-tuple-element.59.refs_0_), channel_id=1, source_target_pairs={{0,12},{1,13},{2,14},{3,15},{4,0},{5,1},{6,2},{7,3},{8,4},{9,5},{1... | collective-permute-start | bytes 61448 | tf_op jit(solution)/shard_map/ppermute | solution.py:570
  27.1 1.8 %collective-permute-done.3.refs_1_ = bf16[40,256]{1,0:T(8,128)(2,1)S(1)} collective-permute-done((bf16[40,256]{1,0:T(8,128)(2,1)S(1)}, bf16[40,256]{1,0:T(8,128)(2,1)S(1)}, u32[]{:S(2)}, u32[]{:S(2)}) %collective-permute-start.3) | collective-permute-done | bytes 20512 | tf_op jit(solution)/shard_map/ppermute | solution.py:570
  28.9 2.0 %collective-permute-start.5 = (bf16[40,256]{1,0:T(8,128)(2,1)S(1)}, bf16[40,256]{1,0:T(8,128)(2,1)S(1)}, u32[]{:S(2)}, u32[]{:S(2)}) collective-permute-start(bf16[40,256]{1,0:T(8,128)(2,1)S(1)} %get-tuple-element.59.refs_0_), channel_id=1, source_target_pairs={{0,8},{1,9},{2,10},{3,11},{4,12},{5,13},{6,14},{7,15},{8,0},{9,1},... | collective-permute-start | bytes 61448 | tf_op jit(solution)/shard_map/ppermute | solution.py:570
  30.9 3.2 %collective-permute-done.5.refs_3_ = bf16[40,256]{1,0:T(8,128)(2,1)S(1)} collective-permute-done((bf16[40,256]{1,0:T(8,128)(2,1)S(1)}, bf16[40,256]{1,0:T(8,128)(2,1)S(1)}, u32[]{:S(2)}, u32[]{:S(2)}) %collective-permute-start.5) | collective-permute-done | bytes 20512 | tf_op jit(solution)/shard_map/ppermute | solution.py:570
  34.2 0.3 pick_near.1
  34.5 2.1 %collective-permute-start.14 = (bf16[848,512]{1,0:T(8,128)(2,1)S(1)}, bf16[848,512]{1,0:T(8,128)(2,1)S(1)}, u32[]{:S(2)}, u32[]{:S(2)}) collective-permute-start(bf16[848,512]{1,0:T(8,128)(2,1)S(1)} %get-tuple-element.69), channel_id=1, source_target_pairs={{0,1},{1,2},{2,3},{3,0},{4,5},{5,6},{6,7},{7,4},{8,9},{9,10},{10,1... | collective-permute-start | bytes 2605064 | tf_op jit(solution)/shard_map/ppermute | solution.py:573
  36.5 1.2 collective-permute-start.15
  37.8 3.4 %copy-done.1 = bf16[1,1,16,128,2048]{4,3,2,1,0:T(8,128)(2,1)S(1)} copy-done((bf16[1,1,16,128,2048]{4,3,2,1,0:T(8,128)(2,1)S(1)}, bf16[1,1,16,128,2048]{4,3,2,1,0:T(8,128)(2,1)}, u32[]{:S(2)}) %copy-start.1) | copy-done | bytes 8388632
  41.2 0.7 copy-done.3
  41.9 2.9 %local_attention.1.local = f32[72,128]{1,0:T(8,128)S(1)} custom-call(s32[1]{0:T(128)} %bitcast.5.pages_alive, bf16[64,128]{1,0:T(8,128)(2,1)S(1)} %get-tuple-element.67.query, bf16[1,2048]{1,0:T(2,128)(2,1)S(1)} %bitcast.18, bf16[16,128,2048]{2,1,0:T(8,128)(2,1)S(1)} %bitcast.17), custom_call_target="tpu_custom_call" | custom-call | flops 1000 | bytes 1000 | tf_op jit(solution)/shard_map/local_attention/pallas_call | solution.py:419
  44.8 0.6 collective-permute-done.10.refs_7_
  45.4 0.1 fusion
  45.4 0.6 collective-permute-start.12
  46.0 1.4 %collective-permute-start.13 = (bf16[2,512,256]{2,1,0:T(8,128)(2,1)S(1)}, bf16[2,512,256]{2,1,0:T(8,128)(2,1)S(1)}, u32[]{:S(2)}, u32[]{:S(2)}) collective-permute-start(bf16[2,512,256]{2,1,0:T(8,128)(2,1)S(1)} %get-tuple-element.108), channel_id=1, source_target_pairs={{0,32},{16,112},{32,64},{48,16},{64,96},{80,48},{96,0},{112,80},{1... | collective-permute-start | bytes 1572872 | tf_op jit(solution)/shard_map/ppermute | solution.py:583
  47.4 0.4 collective-permute-start.16
  47.9 14.9 %collective-permute-done.14.refs_1_.refs_4_ = bf16[848,512]{1,0:T(8,128)(2,1)S(1)} collective-permute-done((bf16[848,512]{1,0:T(8,128)(2,1)S(1)}, bf16[848,512]{1,0:T(8,128)(2,1)S(1)}, u32[]{:S(2)}, u32[]{:S(2)}) %collective-permute-start.14) | collective-permute-done | bytes 868384 | tf_op jit(solution)/shard_map/ppermute | solution.py:573
  62.8 0.0 collective-permute-start.17
  62.8 0.0 collective-permute-done.15.refs_2_.refs_5_
  62.8 0.0 collective-permute-done.12.refs_10_
  62.8 0.0 collective-permute-done.13.refs_11_
  62.8 0.6 collective-permute-start.18
  63.4 0.1 collective-permute-start.19
  63.5 2.7 %collective-permute-done.18.refs_12_ = bf16[2,512,256]{2,1,0:T(8,128)(2,1)S(1)} collective-permute-done((bf16[2,512,256]{2,1,0:T(8,128)(2,1)S(1)}, bf16[2,512,256]{2,1,0:T(8,128)(2,1)S(1)}, u32[]{:S(2)}, u32[]{:S(2)}) %collective-permute-start.18) | collective-permute-done | bytes 524320 | tf_op jit(solution)/shard_map/ppermute | solution.py:587
  66.2 0.7 collective-permute-done.19.refs_13_
  67.0 2.3 %product_far.1 = (bf16[256,1024]{1,0:T(8,128)(2,1)S(1)}, bf16[256,1024]{1,0:T(8,128)(2,1)S(1)}) custom-call(bf16[1024,512]{1,0:T(8,128)(2,1)S(1)} %get-tuple-element.94.refs_0_, bf16[848,512]{1,0:T(8,128)(2,1)S(1)} %collective-permute-done.14.refs_1_.refs_4_, bf16[848,512]{1,0:T(8,128)(2,1)S(1)} %collective-permute-done.15.refs_2_.refs_5_, ...), custom_call_target="tpu_custom_call" | custom-call | flops 1000 | bytes 1000 | tf_op jit(solution)/shard_map/product_far/pallas_call | solution.py:273
  69.3 0.0 slice-start
  69.3 2.0 %collective-permute-start.20 = (bf16[256,1024]{1,0:T(8,128)(2,1)S(1)}, bf16[256,1024]{1,0:T(8,128)(2,1)S(1)}, u32[]{:S(2)}, u32[]{:S(2)}) collective-permute-start(bf16[256,1024]{1,0:T(8,128)(2,1)S(1)} %get-tuple-element.77), channel_id=1, source_target_pairs={{0,4},{1,5},{2,6},{3,7},{4,8},{5,9},{6,10},{7,11},{8,12},{9,13},{1... | collective-permute-start | bytes 1572872 | tf_op jit(solution)/shard_map/ppermute | solution.py:594
  71.3 2.2 %collective-permute-start.21 = (bf16[256,1024]{1,0:T(8,128)(2,1)S(1)}, bf16[256,1024]{1,0:T(8,128)(2,1)S(1)}, u32[]{:S(2)}, u32[]{:S(2)}) collective-permute-start(bf16[256,1024]{1,0:T(8,128)(2,1)S(1)} %get-tuple-element.78), channel_id=1, source_target_pairs={{0,12},{1,13},{2,14},{3,15},{4,0},{5,1},{6,2},{7,3},{8,4},{9,5},{1... | collective-permute-start | bytes 1572872 | tf_op jit(solution)/shard_map/ppermute | solution.py:595
  73.5 0.8 collective-permute-start.22
  74.3 0.5 collective-permute-start.6
  74.8 4.5 %product_near.1 = (bf16[256,1024]{1,0:T(8,128)(2,1)S(1)}, bf16[256,1024]{1,0:T(8,128)(2,1)S(1)}, bf16[256,1024]{1,0:T(8,128)(2,1)S(1)}, bf16[256,1024]{1,0:T(8,128)(2,1)S(1)}) custom-call(bf16[1024,512]{1,0:T(8,128)(2,1)S(1)} %get-tuple-element.94.refs_0_, bf16[848,512]{1,0:T(8,128)(2,1)S(1)} %collective-permute-done.14.refs_1_.refs_4_, ...), custom_call_target="tpu_custom_call" | custom-call | flops 1000 | bytes 1000 | tf_op jit(solution)/shard_map/product_near/pallas_call | solution.py:249
  79.3 0.1 collective-permute-start.24
  79.4 6.6 %collective-permute-done.22.refs_6_.refs_3_ = bf16[336,512]{1,0:T(8,128)(2,1)S(1)} collective-permute-done((bf16[336,512]{1,0:T(8,128)(2,1)S(1)}, bf16[336,512]{1,0:T(8,128)(2,1)S(1)}, u32[]{:S(2)}, u32[]{:S(2)}) %collective-permute-start.22) | collective-permute-done | bytes 344096 | tf_op jit(solution)/shard_map/ppermute | solution.py:597
  86.0 2.0 %collective-permute-start.25 = (bf16[256,1024]{1,0:T(8,128)(2,1)S(1)}, bf16[256,1024]{1,0:T(8,128)(2,1)S(1)}, u32[]{:S(2)}, u32[]{:S(2)}) collective-permute-start(bf16[256,1024]{1,0:T(8,128)(2,1)S(1)} %get-tuple-element.101), channel_id=1, source_target_pairs={{0,12},{1,13},{2,14},{3,15},{4,0},{5,1},{6,2},{7,3},{8,4},{9,5},{1... | collective-permute-start | bytes 1572872 | tf_op jit(solution)/shard_map/ppermute | solution.py:601
  88.0 0.2 relay_sums.1
  88.2 0.1 collective-permute-start.23
  88.3 3.2 %collective-permute-start.26 = (bf16[256,1024]{1,0:T(8,128)(2,1)S(1)}, bf16[256,1024]{1,0:T(8,128)(2,1)S(1)}, u32[]{:S(2)}, u32[]{:S(2)}) collective-permute-start(bf16[256,1024]{1,0:T(8,128)(2,1)S(1)} %get-tuple-element.102), channel_id=1, source_target_pairs={{0,12},{1,13},{2,14},{3,15},{4,0},{5,1},{6,2},{7,3},{8,4},{9,5},{1... | collective-permute-start | bytes 1572872 | tf_op jit(solution)/shard_map/ppermute | solution.py:608
  92.2 0.8 unpack.1
  93.0 4.3 %pool_attention.1.pool = f32[16,72,128]{2,1,0:T(8,128)S(1)} custom-call(s32[16]{0:T(128)S(1)} %get-tuple-element.91.slots, s32[16]{0:T(128)S(1)} %get-tuple-element.92.alive, bf16[16,64,128]{2,1,0:T(8,128)(2,1)S(1)} %get-tuple-element.93.query, bf16[16,128,2048]{2,1,0:T(8,128)(2,1)S(1)} %bitcast.11, bf16[16,128,2048]{2,1,0:T(8,128)(2,1)S(1)} %bitcast.12, ...), custom_call_target="tpu_custom_call" | custom-call | flops 1000 | bytes 1000 | tf_op jit(solution)/shard_map/pool_attention/pallas_call | solution.py:340
  97.3 1.3 %collective-permute-done.7.refs_2_ = bf16[256,512]{1,0:T(8,128)(2,1)S(1)} collective-permute-done((bf16[256,512]{1,0:T(8,128)(2,1)S(1)}, bf16[256,512]{1,0:T(8,128)(2,1)S(1)}, u32[]{:S(2)}, u32[]{:S(2)}) %collective-permute-start.7) | collective-permute-done | bytes 262176 | tf_op jit(solution)/shard_map/ppermute | solution.py:615
  98.7 2.3 %product_own.1 = (f32[256,1024]{1,0:T(8,128)S(1)}, f32[256,1024]{1,0:T(8,128)S(1)}) custom-call(bf16[1024,512]{1,0:T(8,128)(2,1)S(1)} %get-tuple-element.94.refs_0_, bf16[256,512]{1,0:T(8,128)(2,1)S(1)} %collective-permute-done.6.refs_1_, bf16[256,512]{1,0:T(8,128)(2,1)S(1)} %collective-permute-done.7.refs_2_, ...), custom_call_target="tpu_custom_call" | custom-call | flops 1000 | bytes 1000 | tf_op jit(solution)/shard_map/product_own/pallas_call | solution.py:249
  101.0 0.0 collective-permute-done.25.down_l
  101.0 7.1 %collective-permute-done.23.up_l = bf16[256,1024]{1,0:T(8,128)(2,1)S(1)} collective-permute-done((bf16[256,1024]{1,0:T(8,128)(2,1)S(1)}, bf16[256,1024]{1,0:T(8,128)(2,1)S(1)}, u32[]{:S(2)}, u32[]{:S(2)}) %collective-permute-start.23) | collective-permute-done | bytes 524320 | tf_op jit(solution)/shard_map/ppermute | solution.py:605
  108.1 0.8 collective-permute-done.26.down_r
  108.9 3.9 %prefix_attention.1 = (bf16[1,256,2048]{2,1,0:T(8,128)(2,1)}, bf16[16,80,128]{2,1,0:T(8,128)(2,1)S(1)}) custom-call(s32[1]{0:T(128)S(6)} %copy.12.prompt_pages, f32[256,1024]{1,0:T(8,128)S(1)} %get-tuple-element.98.own_l, f32[256,1024]{1,0:T(8,128)S(1)} %get-tuple-element.99.own_r, bf16[256,1024]{1,0:T(8,128)(2,1)S(1)} %collective-permute-done.23.up_l, ...), custom_call_target="tpu_custom_call" | custom-call | flops 300000000 | bytes 6291456 | tf_op jit(solution)/shard_map/prefix_attention/pallas_call | solution.py:503
  112.8 13.0 %all_to_all.5.arrived = bf16[16,80,128]{2,1,0:T(8,128)(2,1)S(1)} all-to-all(bf16[16,80,128]{2,1,0:T(8,128)(2,1)S(1)} %get-tuple-element.106), channel_id=1, replica_groups=mesh['prompt'=8,'sample'=16] {'sample'}, dimensions={0} | all-to-all | bytes 655360 | tf_op jit(solution)/shard_map/all_to_all | solution.py:620
  125.8 1.0 combine.1
  (20 shorter events, 0.0 us)
Async XLA Ops:
  0.6 33.5 %copy-start = (bf16[1,4096,512]{2,1,0:T(8,128)(2,1)S(1)}, bf16[1,4096,512]{2,1,0:T(8,128)(2,1)}, u32[]{:S(2)}) copy-start(bf16[1,4096,512]{2,1,0:T(8,128)(2,1)} %param.10) | copy-start | bytes 12582916
  0.6 10.0 %collective-permute-start = (bf16[512,256]{1,0:T(8,128)(2,1)}, bf16[512,256]{1,0:T(8,128)(2,1)S(1)}, u32[]{:S(2)}, u32[]{:S(2)}) collective-permute-start(bf16[512,256]{1,0:T(8,128)(2,1)} %param.11), channel_id=1, source_target_pairs={{0,1},{1,2},{2,3},{3,0},{4,5},{5,6},{6,7},{7,4},{8,9},{9,10},{10,1... | collective-permute-start | bytes 786440 | tf_op jit(solution)/shard_map/ppermute | solution.py:562
  2.3 9.4 %collective-permute-start.1 = (bf16[512,256]{1,0:T(8,128)(2,1)}, bf16[512,256]{1,0:T(8,128)(2,1)S(1)}, u32[]{:S(2)}, u32[]{:S(2)}) collective-permute-start(bf16[512,256]{1,0:T(8,128)(2,1)} %param.11), channel_id=1, source_target_pairs={{0,3},{1,0},{2,1},{3,2},{4,7},{5,4},{6,5},{7,6},{8,11},{9,8},{10,9... | collective-permute-start | bytes 786440 | tf_op jit(solution)/shard_map/ppermute | solution.py:563
  3.9 12.9 %collective-permute-start.2 = (bf16[512,256]{1,0:T(8,128)(2,1)}, bf16[512,256]{1,0:T(8,128)(2,1)S(1)}, u32[]{:S(2)}, u32[]{:S(2)}) collective-permute-start(bf16[512,256]{1,0:T(8,128)(2,1)} %param.11), channel_id=1, source_target_pairs={{0,2},{1,3},{2,0},{3,1},{4,6},{5,7},{6,4},{7,5},{8,10},{9,11},{10,... | collective-permute-start | bytes 786440 | tf_op jit(solution)/shard_map/ppermute | solution.py:561
  8.6 0.8 copy-start.2
  9.4 0.7 copy-start.4
  17.9 2.7 %collective-permute-start.9 = (bf16[4,512,256]{2,1,0:T(8,128)(2,1)S(1)}, bf16[4,512,256]{2,1,0:T(8,128)(2,1)S(1)}, u32[]{:S(2)}, u32[]{:S(2)}) collective-permute-start(bf16[4,512,256]{2,1,0:T(8,128)(2,1)S(1)} %pad_maximum_fusion.refs_4_), channel_id=1, source_target_pairs={{0,16},{16,0},{32,48},{48,32},{64,80},{80,64},{96,112},{112,96},{1... | collective-permute-start | bytes 3145736 | tf_op jit(solution)/shard_map/ppermute | solution.py:578
  18.0 26.8 %collective-permute-start.8 = (bf16[4,512,256]{2,1,0:T(8,128)(2,1)S(1)}, bf16[4,512,256]{2,1,0:T(8,128)(2,1)S(1)}, u32[]{:S(2)}, u32[]{:S(2)}) collective-permute-start(bf16[4,512,256]{2,1,0:T(8,128)(2,1)S(1)} %pad_maximum_fusion.refs_4_), channel_id=1, source_target_pairs={{0,32},{16,112},{32,64},{48,16},{64,96},{80,48},{96,0},{112,80},{1... | collective-permute-start | bytes 3145736 | tf_op jit(solution)/shard_map/ppermute | solution.py:577
  20.7 24.7 %collective-permute-start.10 = (bf16[4,512,256]{2,1,0:T(8,128)(2,1)S(1)}, bf16[4,512,256]{2,1,0:T(8,128)(2,1)S(1)}, u32[]{:S(2)}, u32[]{:S(2)}) collective-permute-start(bf16[4,512,256]{2,1,0:T(8,128)(2,1)S(1)} %collective-permute-done.9.refs_5_), channel_id=1, source_target_pairs={{0,32},{16,112},{32,64},{48,16},{64,96},{80,48},{96,0},{112,80},{1... | collective-permute-start | bytes 3145736 | tf_op jit(solution)/shard_map/ppermute | solution.py:579
  22.3 22.5 %collective-permute-start.11 = (bf16[768,512]{1,0:T(8,128)(2,1)S(1)}, bf16[768,512]{1,0:T(8,128)(2,1)S(1)}, u32[]{:S(2)}, u32[]{:S(2)}) collective-permute-start(bf16[768,512]{1,0:T(8,128)(2,1)S(1)} %get-tuple-element.66), channel_id=1, source_target_pairs={{0,2},{1,3},{2,0},{3,1},{4,6},{5,7},{6,4},{7,5},{8,10},{9,11},{10,... | collective-permute-start | bytes 2359304 | tf_op jit(solution)/shard_map/ppermute | solution.py:572
  23.1 5.8 %collective-permute-start.3 = (bf16[40,256]{1,0:T(8,128)(2,1)S(1)}, bf16[40,256]{1,0:T(8,128)(2,1)S(1)}, u32[]{:S(2)}, u32[]{:S(2)}) collective-permute-start(bf16[40,256]{1,0:T(8,128)(2,1)S(1)} %get-tuple-element.59.refs_0_), channel_id=1, source_target_pairs={{0,4},{1,5},{2,6},{3,7},{4,8},{5,9},{6,10},{7,11},{8,12},{9,13},{1... | collective-permute-start | bytes 61448 | tf_op jit(solution)/shard_map/ppermute | solution.py:570
  25.0 5.9 %collective-permute-start.4 = (bf16[40,256]{1,0:T(8,128)(2,1)S(1)}, bf16[40,256]{1,0:T(8,128)(2,1)S(1)}, u32[]{:S(2)}, u32[]{:S(2)}) collective-permute-start(bf16[40,256]{1,0:T(8,128)(2,1)S(1)} %get-tuple-element.59.refs_0_), channel_id=1, source_target_pairs={{0,12},{1,13},{2,14},{3,15},{4,0},{5,1},{6,2},{7,3},{8,4},{9,5},{1... | collective-permute-start | bytes 61448 | tf_op jit(solution)/shard_map/ppermute | solution.py:570
  28.9 5.3 %collective-permute-start.5 = (bf16[40,256]{1,0:T(8,128)(2,1)S(1)}, bf16[40,256]{1,0:T(8,128)(2,1)S(1)}, u32[]{:S(2)}, u32[]{:S(2)}) collective-permute-start(bf16[40,256]{1,0:T(8,128)(2,1)S(1)} %get-tuple-element.59.refs_0_), channel_id=1, source_target_pairs={{0,8},{1,9},{2,10},{3,11},{4,12},{5,13},{6,14},{7,15},{8,0},{9,1},... | collective-permute-start | bytes 61448 | tf_op jit(solution)/shard_map/ppermute | solution.py:570
  34.5 28.3 %collective-permute-start.14 = (bf16[848,512]{1,0:T(8,128)(2,1)S(1)}, bf16[848,512]{1,0:T(8,128)(2,1)S(1)}, u32[]{:S(2)}, u32[]{:S(2)}) collective-permute-start(bf16[848,512]{1,0:T(8,128)(2,1)S(1)} %get-tuple-element.69), channel_id=1, source_target_pairs={{0,1},{1,2},{2,3},{3,0},{4,5},{5,6},{6,7},{7,4},{8,9},{9,10},{10,1... | collective-permute-start | bytes 2605064 | tf_op jit(solution)/shard_map/ppermute | solution.py:573
  36.5 26.3 %collective-permute-start.15 = (bf16[848,512]{1,0:T(8,128)(2,1)S(1)}, bf16[848,512]{1,0:T(8,128)(2,1)S(1)}, u32[]{:S(2)}, u32[]{:S(2)}) collective-permute-start(bf16[848,512]{1,0:T(8,128)(2,1)S(1)} %get-tuple-element.70), channel_id=1, source_target_pairs={{0,3},{1,0},{2,1},{3,2},{4,7},{5,4},{6,5},{7,6},{8,11},{9,8},{10,9... | collective-permute-start | bytes 2605064 | tf_op jit(solution)/shard_map/ppermute | solution.py:574
  37.8 3.4 %copy-start.1 = (bf16[1,1,16,128,2048]{4,3,2,1,0:T(8,128)(2,1)S(1)}, bf16[1,1,16,128,2048]{4,3,2,1,0:T(8,128)(2,1)}, u32[]{:S(2)}) copy-start(bf16[1,1,16,128,2048]{4,3,2,1,0:T(8,128)(2,1)} %param.14) | copy-start | bytes 25165828
  41.2 0.7 copy-start.3
  45.4 17.4 %collective-permute-start.12 = (bf16[2,512,256]{2,1,0:T(8,128)(2,1)S(1)}, bf16[2,512,256]{2,1,0:T(8,128)(2,1)S(1)}, u32[]{:S(2)}, u32[]{:S(2)}) collective-permute-start(bf16[2,512,256]{2,1,0:T(8,128)(2,1)S(1)} %get-tuple-element.109), channel_id=1, source_target_pairs={{0,32},{16,112},{32,64},{48,16},{64,96},{80,48},{96,0},{112,80},{1... | collective-permute-start | bytes 1572872 | tf_op jit(solution)/shard_map/ppermute | solution.py:583
  46.0 16.8 %collective-permute-start.13 = (bf16[2,512,256]{2,1,0:T(8,128)(2,1)S(1)}, bf16[2,512,256]{2,1,0:T(8,128)(2,1)S(1)}, u32[]{:S(2)}, u32[]{:S(2)}) collective-permute-start(bf16[2,512,256]{2,1,0:T(8,128)(2,1)S(1)} %get-tuple-element.108), channel_id=1, source_target_pairs={{0,32},{16,112},{32,64},{48,16},{64,96},{80,48},{96,0},{112,80},{1... | collective-permute-start | bytes 1572872 | tf_op jit(solution)/shard_map/ppermute | solution.py:583
  47.4 19.5 %collective-permute-start.16 = (bf16[4,512,256]{2,1,0:T(8,128)(2,1)S(1)}, bf16[4,512,256]{2,1,0:T(8,128)(2,1)S(1)}, u32[]{:S(2)}, u32[]{:S(2)}) collective-permute-start(bf16[4,512,256]{2,1,0:T(8,128)(2,1)S(1)} %collective-permute-done.8.refs_6_), channel_id=1, source_target_pairs={{0,16},{16,0},{32,48},{48,32},{64,80},{80,64},{96,112},{112,96},{1... | collective-permute-start | bytes 3145736 | tf_op jit(solution)/shard_map/ppermute | solution.py:584
  62.8 4.2 %collective-permute-start.17 = (bf16[4,512,256]{2,1,0:T(8,128)(2,1)S(1)}, bf16[4,512,256]{2,1,0:T(8,128)(2,1)S(1)}, u32[]{:S(2)}, u32[]{:S(2)}) collective-permute-start(bf16[4,512,256]{2,1,0:T(8,128)(2,1)S(1)} %collective-permute-done.10.refs_7_), channel_id=1, source_target_pairs={{0,16},{16,0},{32,48},{48,32},{64,80},{80,64},{96,112},{112,96},{1... | collective-permute-start | bytes 3145736 | tf_op jit(solution)/shard_map/ppermute | solution.py:585
  62.8 3.4 %collective-permute-start.18 = (bf16[2,512,256]{2,1,0:T(8,128)(2,1)S(1)}, bf16[2,512,256]{2,1,0:T(8,128)(2,1)S(1)}, u32[]{:S(2)}, u32[]{:S(2)}) collective-permute-start(bf16[2,512,256]{2,1,0:T(8,128)(2,1)S(1)} %collective-permute-done.12.refs_10_), channel_id=1, source_target_pairs={{0,16},{16,0},{32,48},{48,32},{64,80},{80,64},{96,112},{112,96},{1... | collective-permute-start | bytes 1572872 | tf_op jit(solution)/shard_map/ppermute | solution.py:587
  63.4 3.6 %collective-permute-start.19 = (bf16[2,512,256]{2,1,0:T(8,128)(2,1)S(1)}, bf16[2,512,256]{2,1,0:T(8,128)(2,1)S(1)}, u32[]{:S(2)}, u32[]{:S(2)}) collective-permute-start(bf16[2,512,256]{2,1,0:T(8,128)(2,1)S(1)} %collective-permute-done.13.refs_11_), channel_id=1, source_target_pairs={{0,16},{16,0},{32,48},{48,32},{64,80},{80,64},{96,112},{112,96},{1... | collective-permute-start | bytes 1572872 | tf_op jit(solution)/shard_map/ppermute | solution.py:587
  69.3 23.7 %slice-start = ((s8[8388608]{0:T(1024)(128)(4,1)}), s8[4194304]{0:T(1024)(128)(4,1)S(1)}, s32[]{:S(2)}) async-start(s8[8388608]{0:T(1024)(128)(4,1)} %bitcast.9), calls=%async_computation.1 | async-start | bytes 8388608
  69.3 18.7 %collective-permute-start.20 = (bf16[256,1024]{1,0:T(8,128)(2,1)S(1)}, bf16[256,1024]{1,0:T(8,128)(2,1)S(1)}, u32[]{:S(2)}, u32[]{:S(2)}) collective-permute-start(bf16[256,1024]{1,0:T(8,128)(2,1)S(1)} %get-tuple-element.77), channel_id=1, source_target_pairs={{0,4},{1,5},{2,6},{3,7},{4,8},{5,9},{6,10},{7,11},{8,12},{9,13},{1... | collective-permute-start | bytes 1572872 | tf_op jit(solution)/shard_map/ppermute | solution.py:594
  71.3 16.7 %collective-permute-start.21 = (bf16[256,1024]{1,0:T(8,128)(2,1)S(1)}, bf16[256,1024]{1,0:T(8,128)(2,1)S(1)}, u32[]{:S(2)}, u32[]{:S(2)}) collective-permute-start(bf16[256,1024]{1,0:T(8,128)(2,1)S(1)} %get-tuple-element.78), channel_id=1, source_target_pairs={{0,12},{1,13},{2,14},{3,15},{4,0},{5,1},{6,2},{7,3},{8,4},{9,5},{1... | collective-permute-start | bytes 1572872 | tf_op jit(solution)/shard_map/ppermute | solution.py:595
  73.5 12.5 %collective-permute-start.22 = (bf16[336,512]{1,0:T(8,128)(2,1)S(1)}, bf16[336,512]{1,0:T(8,128)(2,1)S(1)}, u32[]{:S(2)}, u32[]{:S(2)}) collective-permute-start(bf16[336,512]{1,0:T(8,128)(2,1)S(1)} %get-tuple-element.80), channel_id=1, source_target_pairs={{0,2},{1,3},{2,0},{3,1},{4,6},{5,7},{6,4},{7,5},{8,10},{9,11},{10,... | collective-permute-start | bytes 1032200 | tf_op jit(solution)/shard_map/ppermute | solution.py:597
  74.3 18.7 %slice-start.1 = ((s8[8388608]{0:T(1024)(128)(4,1)}), s8[4194304]{0:T(1024)(128)(4,1)S(1)}, s32[]{:S(2)}) async-start(s8[8388608]{0:T(1024)(128)(4,1)} %bitcast.9), calls=%async_computation.2 | async-start | bytes 8388608
  74.3 17.2 %collective-permute-start.6 = (bf16[256,512]{1,0:T(8,128)(2,1)S(1)}, bf16[256,512]{1,0:T(8,128)(2,1)S(1)}, u32[]{:S(2)}, u32[]{:S(2)}) collective-permute-start(bf16[256,512]{1,0:T(8,128)(2,1)S(1)} %get-tuple-element.60), channel_id=1, source_target_pairs={{0,1},{1,2},{2,3},{3,0},{4,5},{5,6},{6,7},{7,4},{8,9},{9,10},{10,1... | collective-permute-start | bytes 786440 | tf_op jit(solution)/shard_map/ppermute | solution.py:614
  79.3 21.7 %collective-permute-start.24 = (bf16[256,1024]{1,0:T(8,128)(2,1)S(1)}, bf16[256,1024]{1,0:T(8,128)(2,1)S(1)}, u32[]{:S(2)}, u32[]{:S(2)}) collective-permute-start(bf16[256,1024]{1,0:T(8,128)(2,1)S(1)} %get-tuple-element.100), channel_id=1, source_target_pairs={{0,4},{1,5},{2,6},{3,7},{4,8},{5,9},{6,10},{7,11},{8,12},{9,13},{1... | collective-permute-start | bytes 1572872 | tf_op jit(solution)/shard_map/ppermute | solution.py:601
  86.0 15.0 %collective-permute-start.25 = (bf16[256,1024]{1,0:T(8,128)(2,1)S(1)}, bf16[256,1024]{1,0:T(8,128)(2,1)S(1)}, u32[]{:S(2)}, u32[]{:S(2)}) collective-permute-start(bf16[256,1024]{1,0:T(8,128)(2,1)S(1)} %get-tuple-element.101), channel_id=1, source_target_pairs={{0,12},{1,13},{2,14},{3,15},{4,0},{5,1},{6,2},{7,3},{8,4},{9,5},{1... | collective-permute-start | bytes 1572872 | tf_op jit(solution)/shard_map/ppermute | solution.py:601
  88.2 19.9 %collective-permute-start.23 = (bf16[256,1024]{1,0:T(8,128)(2,1)S(1)}, bf16[256,1024]{1,0:T(8,128)(2,1)S(1)}, u32[]{:S(2)}, u32[]{:S(2)}) collective-permute-start(bf16[256,1024]{1,0:T(8,128)(2,1)S(1)} %get-tuple-element.87), channel_id=1, source_target_pairs={{0,4},{1,5},{2,6},{3,7},{4,8},{5,9},{6,10},{7,11},{8,12},{9,13},{1... | collective-permute-start | bytes 1572872 | tf_op jit(solution)/shard_map/ppermute | solution.py:605
  88.3 20.6 %collective-permute-start.26 = (bf16[256,1024]{1,0:T(8,128)(2,1)S(1)}, bf16[256,1024]{1,0:T(8,128)(2,1)S(1)}, u32[]{:S(2)}, u32[]{:S(2)}) collective-permute-start(bf16[256,1024]{1,0:T(8,128)(2,1)S(1)} %get-tuple-element.102), channel_id=1, source_target_pairs={{0,12},{1,13},{2,14},{3,15},{4,0},{5,1},{6,2},{7,3},{8,4},{9,5},{1... | collective-permute-start | bytes 1572872 | tf_op jit(solution)/shard_map/ppermute | solution.py:608
  91.5 7.1 %collective-permute-start.7 = (bf16[256,512]{1,0:T(8,128)(2,1)S(1)}, bf16[256,512]{1,0:T(8,128)(2,1)S(1)}, u32[]{:S(2)}, u32[]{:S(2)}) collective-permute-start(bf16[256,512]{1,0:T(8,128)(2,1)S(1)} %get-tuple-element.61), channel_id=1, source_target_pairs={{0,3},{1,0},{2,1},{3,2},{4,7},{5,4},{6,5},{7,6},{8,11},{9,8},{10,9... | collective-permute-start | bytes 786440 | tf_op jit(solution)/shard_map/ppermute | solution.py:615

commit v10 on v9

--- a/solution.py
+++ b/solution.py
@@ -148,6 +148,9 @@
 NEXT = (2, 1, 3, 0)
 
 
+PAD = 16
+
+
 def copy_rows(states, sems, wanted):
     me = lax.axis_index("sample")
     z, x = me // 4, lax.rem(me, 4)
@@ -167,9 +170,11 @@
 
 
 def pick_far_kernel(states, own, far, sems):
-    wanted = [(2, k, far.at[block_rows(k)]) for k in range(3)]
+    wanted = [(2, k, far.at[block_rows(k)]) for k in range(4)]
     wanted += [(0, k, own.at[block_rows(k)]) for k in range(4)]
-    for copy in copy_rows(states, sems, wanted):
+    copies = copy_rows(states, sems, wanted)
+    far[4 * ROWS :] = jnp.zeros((PAD, SLICE), BF16)
+    for copy in copies:
         copy.wait()
 
 
@@ -179,11 +184,11 @@
         pick_far_kernel,
         out_shape=[
             jax.ShapeDtypeStruct((4 * ROWS, SLICE), BF16),
-            jax.ShapeDtypeStruct((3 * ROWS, SLICE), BF16),
+            jax.ShapeDtypeStruct((4 * ROWS + PAD, SLICE), BF16),
         ],
         in_specs=[pl.BlockSpec(memory_space=pl.ANY)],
         out_specs=[vmem] * 2,
-        scratch_shapes=[pltpu.SemaphoreType.DMA((7,))],
+        scratch_shapes=[pltpu.SemaphoreType.DMA((8,))],
         compiler_params=params(50),
         cost_estimate=cost(1000, 1000),
         name="pick_far",
@@ -197,14 +202,14 @@
 
 
 def pick_near_kernel(states, *refs):
-    blocks, (right, left, last_right, last_left, last_far), sems = refs[:4], refs[4:9], refs[9]
+    blocks, (right, left, last_right, last_left, far_blocks), sems = refs[:4], refs[4:9], refs[9]
     wanted = [(1, k, right.at[block_rows(k)]) for k in range(3)]
     wanted += [(3, k, left.at[block_rows(k)]) for k in range(3)]
-    wanted += [(1, 3, last_right), (3, 3, last_left), (2, 3, last_far.at[block_rows(0)])]
+    wanted += [(1, 3, last_right), (3, 3, last_left)]
     copies = copy_rows(states, sems, wanted)
     put_blocks(right, 3 * ROWS, blocks)
     put_blocks(left, 3 * ROWS, blocks)
-    put_blocks(last_far, ROWS, blocks)
+    put_blocks(far_blocks, 0, blocks)
     for copy in copies:
         copy.wait()
 
@@ -215,10 +220,10 @@
         pick_near_kernel,
         out_shape=[jax.ShapeDtypeStruct((3 * ROWS + 2 * BLOCK, SLICE), BF16)] * 2
         + [jax.ShapeDtypeStruct((ROWS, SLICE), BF16)] * 2
-        + [jax.ShapeDtypeStruct((ROWS + 2 * BLOCK, SLICE), BF16)],
+        + [jax.ShapeDtypeStruct((2 * BLOCK, SLICE), BF16)],
         in_specs=[pl.BlockSpec(memory_space=pl.ANY)] + [vmem] * 4,
         out_specs=[vmem] * 5,
-        scratch_shapes=[pltpu.SemaphoreType.DMA((9,))],
+        scratch_shapes=[pltpu.SemaphoreType.DMA((8,))],
         compiler_params=params(44),
         cost_estimate=cost(1000, 1000),
         name="pick_near",
@@ -257,27 +262,26 @@
     )(*states, *pieces)
 
 
-def product_far_kernel(*refs):
-    states, pieces, outs = refs[:4], refs[4:14], refs[14:]
-    for j in range(8):
+def product_far_kernel(first, *refs):
+    states, pieces, out = refs[:4], refs[4:-1], refs[-1]
+    for j in range(4):
         total = jnp.zeros((ROWS, COLUMNS), F32)
         for d in range(4):
-            total += jnp.dot(
-                states[d][:ROWS], weight_of(pieces, j, d), preferred_element_type=F32
-            )
-        outs[j // 4][:, (j % 4) * COLUMNS : (j % 4 + 1) * COLUMNS] = total.astype(BF16)
-
-
-def product_far(states, pieces):
+            part = pieces[j][d] if first + j < 6 else weight_of((None,) * 4 + pieces, first + j, d)
+            total += jnp.dot(states[d][:ROWS], part, preferred_element_type=F32)
+        out[:, j * COLUMNS : (j + 1) * COLUMNS] = total.astype(BF16)
+
+
+def product_far(states, pieces, first, name):
     vmem = pl.BlockSpec(memory_space=pltpu.VMEM)
     return pl.pallas_call(
-        product_far_kernel,
-        out_shape=[jax.ShapeDtypeStruct((ROWS, KVW // 2), BF16)] * 2,
-        in_specs=[vmem] * 14,
-        out_specs=[vmem] * 2,
+        functools.partial(product_far_kernel, first),
+        out_shape=jax.ShapeDtypeStruct((ROWS, KVW // 2), BF16),
+        in_specs=[vmem] * (4 + len(pieces)),
+        out_specs=vmem,
         compiler_params=params(20),
         cost_estimate=cost(1000, 1000),
-        name="product_far",
+        name=name,
     )(*states, *pieces)
 
 
@@ -568,7 +572,7 @@
         ((kv_weight, weight_right, weight_left, weight_far), own_states, to_far, block)
     )
     blocks = [block] + [lax.ppermute(block, "sample", to) for to in (Z_UP, Z_DOWN, Z_FAR)]
-    to_right, to_left, last_right, last_left, last_far = pick_near(states, blocks)
+    to_right, to_left, last_right, last_left, far_blocks = pick_near(states, blocks)
     rows_far = lax.ppermute(to_far, "sample", X_FAR)
     rows_right = lax.ppermute(to_right, "sample", X_RIGHT)
     rows_left = lax.ppermute(to_left, "sample", X_LEFT)
@@ -590,16 +594,19 @@
     ]
     others = [own_states, rows_right, rows_left, rows_far]
 
-    far_l, far_r = product_far(others, pieces)
+    far_l = product_far(others, pieces[:4], 0, "product_far_l")
+    far_other[0], far_l = tie((far_other[0], far_l))
+    pieces[8] = far_other[0]
+    far_r = product_far(others, pieces[4:], 4, "product_far_r")
     from_down = lax.ppermute(far_l, "sample", Z_UP)
     from_up = lax.ppermute(far_r, "sample", Z_DOWN)
-    last_far, rows_right = tie((last_far, rows_right))
-    last_far = lax.ppermute(last_far, "sample", X_FAR)
+    far_blocks, rows_right = tie((far_blocks, rows_right))
+    far_blocks = lax.ppermute(far_blocks, "sample", X_FAR)
     up_l, up_r, down_l, down_r = product(
         others, pieces, ((1,) * 4, (2,) * 4), BF16, "product_near"
     )
     up_r, down_l = lax.ppermute(up_r, "sample", Z_UP), lax.ppermute(down_l, "sample", Z_DOWN)
-    from_down, from_up, last_far = tie((from_down, from_up, last_far))
+    from_down, from_up, far_blocks = tie((from_down, from_up, far_blocks))
     up_l, down_r = relay(up_l, down_r, from_down, from_up)
     sums = [
         lax.ppermute(up_l, "sample", Z_UP),
@@ -608,13 +615,13 @@
         lax.ppermute(down_r, "sample", Z_DOWN),
     ]
 
-    arrived, up_l = tie(([rows_right, rows_left, last_far], up_l))
+    arrived, up_l = tie(([rows_right, rows_left, far_blocks], up_l))
     queries_all, by_group, slots, alive = unpack(blocks, arrived)
     pool = pool_attention(slots, alive, queries_all, pool_pages[0, 0])
     last_right = lax.ppermute(last_right, "sample", X_RIGHT)
     last_left = lax.ppermute(last_left, "sample", X_LEFT)
-    mine, pool = tie(([own_states, last_right, last_left, last_far], pool))
-    sums = [*product(mine, pieces, ((3, 0, 0, 0),), F32, "product_own"), *sums]
+    mine, pool = tie(([own_states, last_right, last_left, rows_far], pool))
+    sums = [*product(mine, pieces, ((3, 0, 0, 3),), F32, "product_own"), *sums]
 
     cache, packed = prefix_attention(prompt_pages, sums, by_group, pool)
     arrived = lax.all_to_all(packed, "sample", split_axis=0, concat_axis=0, tiled=True)

time: 127 us -> 128 us (level)
  waiting for transfers between devices: 47 us -> 50.5 us
  Pallas kernels: 24.6 us -> 22.1 us
  starting transfers between devices: 32.8 us -> 35.1 us
  blocking collectives: 13 us -> 11.6 us
  local copies, waits for them, and re-layouts: 5.57 us -> 4.22 us
    ppermute x1, waiting for transfers between devices: 6.57 us -> 0.79 us  [per_device(): far_blocks = lax.ppermute(far_blocks, 'sample', X_FAR)]
    ppermute x1, waiting for transfers between devices: 0.01 us -> 5.42 us  [per_device(): rows_far = lax.ppermute(to_far, 'sample', X_FAR)]
    ppermute x1, waiting for transfers between devices: 0.01 us -> 3.73 us  [per_device(): from_down = lax.ppermute(far_l, 'sample', Z_UP)]
    pallas_call x1, Pallas kernels: 2.91 us -> 0.24 us  [local_attention(): pl.pallas_call(local_kernel, out_shape=jax.ShapeDtypeStruct((PACK, HEAD_S...]
    ppermute x1, waiting for transfers between devices: 0.01 us -> 2.17 us  [per_device(): from_up = lax.ppermute(far_r, 'sample', Z_DOWN)]
    ppermute x1, starting transfers between devices: 1.99 us -> 0.01 us  [per_device(): from_down = lax.ppermute(far_l, 'sample', Z_UP)]
    ppermute x1, waiting for transfers between devices: 7.08 us -> 9.03 us  [per_device(): lax.ppermute(up_l, 'sample', Z_UP)]
    ppermute x1, starting transfers between devices: 2.2 us -> 4.11 us  [per_device(): from_up = lax.ppermute(far_r, 'sample', Z_DOWN)]
  transfers between devices with their start and end apart: 27 -> 27, of which waited for: 13 -> 14; matrix products, arithmetic and copies ran while one was open for 0% -> 0% of each run, Pallas kernels for 14% -> 13%
where the time goes in v10:
time: 128 us; the launch traced here: 127 us
  waiting for transfers between devices  50.5 us (39%)
  starting transfers between devices  35.1 us (27%)
  Pallas kernels  22.1 us (17%)
  blocking collectives  11.6 us (9%)
  local copies, waits for them, and re-layouts  4.22 us (3%)
  between operations  2.8 us (2%)
    ppermute x1, waiting for transfers between devices, per_device(): rows_right = lax.ppermute(to_right, 'sample', X_RIGHT)  14.8 us
    all_to_all x1, blocking collectives, per_device(): lax.all_to_all(packed, 'sample', split_axis=0, concat_axis=0, tiled=True)  11.6 us
    ppermute x1, waiting for transfers between devices, per_device(): lax.ppermute(up_l, 'sample', Z_UP)  9.03 us
    pallas_call x2, Pallas kernels, product(): pl.pallas_call(functools.partial(product_kernel, blocks), out_shape=outs,...  6.81 us
    ppermute x3, starting transfers between devices, per_device(): lax.ppermute(block, 'sample', to)  5.9 us
    ppermute x1, waiting for transfers between devices, per_device(): rows_far = lax.ppermute(to_far, 'sample', X_FAR)  5.42 us
    ppermute x3, waiting for transfers between devices, per_device(): lax.ppermute(block, 'sample', to)  5.18 us
    ppermute x1, waiting for transfers between devices, per_device(): weight_far = lax.ppermute(kv_weight, 'sample', X_FAR)  5.14 us
  transfers between devices with their start and end apart: 27, of which 14 were waited for; matrix products, arithmetic and copies ran while one was open for 0% of the time, Pallas kernels for 13%

profile of v10, /device:TPU:0, one launch (start us, length us, event | category | flops | bytes accessed | tf_op | source)
XLA Modules:
  0.0 127.4 jit_solution(13707146857706713021)
XLA Ops:
  0.6 1.6 %collective-permute-start = (bf16[512,256]{1,0:T(8,128)(2,1)}, bf16[512,256]{1,0:T(8,128)(2,1)S(1)}, u32[]{:S(2)}, u32[]{:S(2)}) collective-permute-start(bf16[512,256]{1,0:T(8,128)(2,1)} %param.11), channel_id=1, source_target_pairs={{0,1},{1,2},{2,3},{3,0},{4,5},{5,6},{6,7},{7,4},{8,9},{9,10},{10,1... | collective-permute-start | bytes 786440 | tf_op jit(solution)/shard_map/ppermute | solution.py:566
  2.3 1.7 %collective-permute-start.1 = (bf16[512,256]{1,0:T(8,128)(2,1)}, bf16[512,256]{1,0:T(8,128)(2,1)S(1)}, u32[]{:S(2)}, u32[]{:S(2)}) collective-permute-start(bf16[512,256]{1,0:T(8,128)(2,1)} %param.11), channel_id=1, source_target_pairs={{0,3},{1,0},{2,1},{3,2},{4,7},{5,4},{6,5},{7,6},{8,11},{9,8},{10,9... | collective-permute-start | bytes 786440 | tf_op jit(solution)/shard_map/ppermute | solution.py:567
  4.0 1.9 %collective-permute-start.2 = (bf16[512,256]{1,0:T(8,128)(2,1)}, bf16[512,256]{1,0:T(8,128)(2,1)S(1)}, u32[]{:S(2)}, u32[]{:S(2)}) collective-permute-start(bf16[512,256]{1,0:T(8,128)(2,1)} %param.11), channel_id=1, source_target_pairs={{0,2},{1,3},{2,0},{3,1},{4,6},{5,7},{6,4},{7,5},{8,10},{9,11},{10,... | collective-permute-start | bytes 786440 | tf_op jit(solution)/shard_map/ppermute | solution.py:565
  5.9 1.6 %pick_far.1 = (bf16[1024,512]{1,0:T(8,128)(2,1)S(1)}, bf16[1040,512]{1,0:T(8,128)(2,1)S(1)}) custom-call(bf16[4,4,256,512]{3,2,1,0:T(8,128)(2,1)} %bitcast.15), custom_call_target="tpu_custom_call" | custom-call | flops 1000 | bytes 1000 | tf_op jit(solution)/shard_map/pick_far/pallas_call | solution.py:183
  8.7 0.0 copy-start.2
  8.7 0.7 copy-done.2
  9.5 0.6 prepare.1
  10.1 0.0 collective-permute-done
  10.1 1.6 %collective-permute-done.1 = bf16[512,256]{1,0:T(8,128)(2,1)S(1)} collective-permute-done((bf16[512,256]{1,0:T(8,128)(2,1)}, bf16[512,256]{1,0:T(8,128)(2,1)S(1)}, u32[]{:S(2)}, u32[]{:S(2)}) %collective-permute-start.1) | collective-permute-done | bytes 262176 | tf_op jit(solution)/shard_map/ppermute | solution.py:567
  11.7 5.1 %collective-permute-done.2 = bf16[512,256]{1,0:T(8,128)(2,1)S(1)} collective-permute-done((bf16[512,256]{1,0:T(8,128)(2,1)}, bf16[512,256]{1,0:T(8,128)(2,1)S(1)}, u32[]{:S(2)}, u32[]{:S(2)}) %collective-permute-start.2) | collective-permute-done | bytes 262176 | tf_op jit(solution)/shard_map/ppermute | solution.py:565
  16.9 1.1 pad_maximum_fusion.refs_4_
  18.0 0.1 collective-permute-start.9
  18.0 0.9 collective-permute-start.11
  19.0 1.6 %collective-permute-start.8 = (bf16[4,512,256]{2,1,0:T(8,128)(2,1)S(1)}, bf16[4,512,256]{2,1,0:T(8,128)(2,1)S(1)}, u32[]{:S(2)}, u32[]{:S(2)}) collective-permute-start(bf16[4,512,256]{2,1,0:T(8,128)(2,1)S(1)} %pad_maximum_fusion.refs_4_), channel_id=1, source_target_pairs={{0,32},{16,112},{32,64},{48,16},{64,96},{80,48},{96,0},{112,80},{1... | collective-permute-start | bytes 3145736 | tf_op jit(solution)/shard_map/ppermute | solution.py:581
  20.5 0.2 collective-permute-done.9.refs_5_
  20.7 1.6 %collective-permute-start.10 = (bf16[4,512,256]{2,1,0:T(8,128)(2,1)S(1)}, bf16[4,512,256]{2,1,0:T(8,128)(2,1)S(1)}, u32[]{:S(2)}, u32[]{:S(2)}) collective-permute-start(bf16[4,512,256]{2,1,0:T(8,128)(2,1)S(1)} %collective-permute-done.9.refs_5_), channel_id=1, source_target_pairs={{0,32},{16,112},{32,64},{48,16},{64,96},{80,48},{96,0},{112,80},{1... | collective-permute-start | bytes 3145736 | tf_op jit(solution)/shard_map/ppermute | solution.py:583
  22.3 1.9 %collective-permute-start.3 = (bf16[40,256]{1,0:T(8,128)(2,1)S(1)}, bf16[40,256]{1,0:T(8,128)(2,1)S(1)}, u32[]{:S(2)}, u32[]{:S(2)}) collective-permute-start(bf16[40,256]{1,0:T(8,128)(2,1)S(1)} %get-tuple-element.59.refs_0_), channel_id=1, source_target_pairs={{0,4},{1,5},{2,6},{3,7},{4,8},{5,9},{6,10},{7,11},{8,12},{9,13},{1... | collective-permute-start | bytes 61448 | tf_op jit(solution)/shard_map/ppermute | solution.py:574
  24.2 2.1 %collective-permute-start.4 = (bf16[40,256]{1,0:T(8,128)(2,1)S(1)}, bf16[40,256]{1,0:T(8,128)(2,1)S(1)}, u32[]{:S(2)}, u32[]{:S(2)}) collective-permute-start(bf16[40,256]{1,0:T(8,128)(2,1)S(1)} %get-tuple-element.59.refs_0_), channel_id=1, source_target_pairs={{0,12},{1,13},{2,14},{3,15},{4,0},{5,1},{6,2},{7,3},{8,4},{9,5},{1... | collective-permute-start | bytes 61448 | tf_op jit(solution)/shard_map/ppermute | solution.py:574
  26.3 1.8 %collective-permute-done.3.refs_1_ = bf16[40,256]{1,0:T(8,128)(2,1)S(1)} collective-permute-done((bf16[40,256]{1,0:T(8,128)(2,1)S(1)}, bf16[40,256]{1,0:T(8,128)(2,1)S(1)}, u32[]{:S(2)}, u32[]{:S(2)}) %collective-permute-start.3) | collective-permute-done | bytes 20512 | tf_op jit(solution)/shard_map/ppermute | solution.py:574
  28.1 1.9 %collective-permute-start.5 = (bf16[40,256]{1,0:T(8,128)(2,1)S(1)}, bf16[40,256]{1,0:T(8,128)(2,1)S(1)}, u32[]{:S(2)}, u32[]{:S(2)}) collective-permute-start(bf16[40,256]{1,0:T(8,128)(2,1)S(1)} %get-tuple-element.59.refs_0_), channel_id=1, source_target_pairs={{0,8},{1,9},{2,10},{3,11},{4,12},{5,13},{6,14},{7,15},{8,0},{9,1},... | collective-permute-start | bytes 61448 | tf_op jit(solution)/shard_map/ppermute | solution.py:574
  29.9 0.0 collective-permute-done.4.refs_2_
  29.9 3.4 %collective-permute-done.5.refs_3_ = bf16[40,256]{1,0:T(8,128)(2,1)S(1)} collective-permute-done((bf16[40,256]{1,0:T(8,128)(2,1)S(1)}, bf16[40,256]{1,0:T(8,128)(2,1)S(1)}, u32[]{:S(2)}, u32[]{:S(2)}) %collective-permute-start.5) | collective-permute-done | bytes 20512 | tf_op jit(solution)/shard_map/ppermute | solution.py:574
  33.4 0.3 pick_near.1
  33.6 2.0 %collective-permute-start.14 = (bf16[848,512]{1,0:T(8,128)(2,1)S(1)}, bf16[848,512]{1,0:T(8,128)(2,1)S(1)}, u32[]{:S(2)}, u32[]{:S(2)}) collective-permute-start(bf16[848,512]{1,0:T(8,128)(2,1)S(1)} %get-tuple-element.71), channel_id=1, source_target_pairs={{0,1},{1,2},{2,3},{3,0},{4,5},{5,6},{6,7},{7,4},{8,9},{9,10},{10,1... | collective-permute-start | bytes 2605064 | tf_op jit(solution)/shard_map/ppermute | solution.py:577
  35.7 1.3 collective-permute-start.15
  36.9 3.4 %copy-done.1 = bf16[1,1,16,128,2048]{4,3,2,1,0:T(8,128)(2,1)S(1)} copy-done((bf16[1,1,16,128,2048]{4,3,2,1,0:T(8,128)(2,1)S(1)}, bf16[1,1,16,128,2048]{4,3,2,1,0:T(8,128)(2,1)}, u32[]{:S(2)}) %copy-start.1) | copy-done | bytes 8388632
  40.3 0.2 local_attention.1.local
  40.6 5.4 %collective-permute-done.11.refs_3_ = bf16[1040,512]{1,0:T(8,128)(2,1)S(1)} collective-permute-done((bf16[1040,512]{1,0:T(8,128)(2,1)S(1)}, bf16[1040,512]{1,0:T(8,128)(2,1)S(1)}, u32[]{:S(2)}, u32[]{:S(2)}) %collective-permute-start.11) | collective-permute-done | bytes 1064992 | tf_op jit(solution)/shard_map/ppermute | solution.py:576
  46.0 0.2 collective-permute-done.10.refs_7_
  46.2 0.1 fusion
  46.3 1.4 %collective-permute-start.12 = (bf16[2,512,256]{2,1,0:T(8,128)(2,1)S(1)}, bf16[2,512,256]{2,1,0:T(8,128)(2,1)S(1)}, u32[]{:S(2)}, u32[]{:S(2)}) collective-permute-start(bf16[2,512,256]{2,1,0:T(8,128)(2,1)S(1)} %get-tuple-element.109), channel_id=1, source_target_pairs={{0,32},{16,112},{32,64},{48,16},{64,96},{80,48},{96,0},{112,80},{1... | collective-permute-start | bytes 1572872 | tf_op jit(solution)/shard_map/ppermute | solution.py:587
  47.7 1.6 %collective-permute-start.13 = (bf16[2,512,256]{2,1,0:T(8,128)(2,1)S(1)}, bf16[2,512,256]{2,1,0:T(8,128)(2,1)S(1)}, u32[]{:S(2)}, u32[]{:S(2)}) collective-permute-start(bf16[2,512,256]{2,1,0:T(8,128)(2,1)S(1)} %get-tuple-element.108), channel_id=1, source_target_pairs={{0,32},{16,112},{32,64},{48,16},{64,96},{80,48},{96,0},{112,80},{1... | collective-permute-start | bytes 1572872 | tf_op jit(solution)/shard_map/ppermute | solution.py:587
  49.3 14.8 %collective-permute-done.14.refs_1_.refs_4_ = bf16[848,512]{1,0:T(8,128)(2,1)S(1)} collective-permute-done((bf16[848,512]{1,0:T(8,128)(2,1)S(1)}, bf16[848,512]{1,0:T(8,128)(2,1)S(1)}, u32[]{:S(2)}, u32[]{:S(2)}) %collective-permute-start.14) | collective-permute-done | bytes 868384 | tf_op jit(solution)/shard_map/ppermute | solution.py:577
  64.1 0.0 collective-permute-start.19
  64.1 0.0 collective-permute-done.15.refs_2_.refs_5_
  64.1 0.0 collective-permute-done.12.refs_6_.refs_10_
  64.1 0.0 collective-permute-done.13.refs_7_.refs_11_
  64.1 0.6 collective-permute-start.16
  64.7 0.1 collective-permute-start.20
  64.8 1.2 product_far_l.1
  66.0 1.5 %collective-permute-done.16.refs_8_.refs_12_ = bf16[2,512,256]{2,1,0:T(8,128)(2,1)S(1)} collective-permute-done((bf16[2,512,256]{2,1,0:T(8,128)(2,1)S(1)}, bf16[2,512,256]{2,1,0:T(8,128)(2,1)S(1)}, u32[]{:S(2)}, u32[]{:S(2)}) %collective-permute-start.16) | collective-permute-done | bytes 524320 | tf_op jit(solution)/shard_map/ppermute | solution.py:591
  67.5 0.7 collective-permute-done.20.refs_9_.refs_13_
  68.2 0.0 collective-permute-done.18.refs_4_.refs_8_
  68.3 1.2 product_far_r.1
  69.5 4.1 %collective-permute-start.21 = (bf16[256,1024]{1,0:T(8,128)(2,1)S(1)}, bf16[256,1024]{1,0:T(8,128)(2,1)S(1)}, u32[]{:S(2)}, u32[]{:S(2)}) collective-permute-start(bf16[256,1024]{1,0:T(8,128)(2,1)S(1)} %product_far_r.1), channel_id=1, source_target_pairs={{0,12},{1,13},{2,14},{3,15},{4,0},{5,1},{6,2},{7,3},{8,4},{9,5},{1... | collective-permute-start | bytes 1572872 | tf_op jit(solution)/shard_map/ppermute | solution.py:602
  73.6 0.8 collective-permute-start.22
  74.5 0.6 collective-permute-start.6
  75.1 4.5 %product_near.1 = (bf16[256,1024]{1,0:T(8,128)(2,1)S(1)}, bf16[256,1024]{1,0:T(8,128)(2,1)S(1)}, bf16[256,1024]{1,0:T(8,128)(2,1)S(1)}, bf16[256,1024]{1,0:T(8,128)(2,1)S(1)}) custom-call(bf16[1024,512]{1,0:T(8,128)(2,1)S(1)} %get-tuple-element.94.refs_0_, bf16[848,512]{1,0:T(8,128)(2,1)S(1)} %collective-permute-done.14.refs_1_.refs_4_, ...), custom_call_target="tpu_custom_call" | custom-call | flops 1000 | bytes 1000 | tf_op jit(solution)/shard_map/product_near/pallas_call | solution.py:254
  79.6 0.1 collective-permute-start.24
  79.7 0.8 collective-permute-done.22.refs_6_
  80.5 3.3 %collective-permute-start.25 = (bf16[256,1024]{1,0:T(8,128)(2,1)S(1)}, bf16[256,1024]{1,0:T(8,128)(2,1)S(1)}, u32[]{:S(2)}, u32[]{:S(2)}) collective-permute-start(bf16[256,1024]{1,0:T(8,128)(2,1)S(1)} %get-tuple-element.101), channel_id=1, source_target_pairs={{0,12},{1,13},{2,14},{3,15},{4,0},{5,1},{6,2},{7,3},{8,4},{9,5},{1... | collective-permute-start | bytes 1572872 | tf_op jit(solution)/shard_map/ppermute | solution.py:608
  83.7 2.2 %collective-permute-done.21.from_up = bf16[256,1024]{1,0:T(8,128)(2,1)S(1)} collective-permute-done((bf16[256,1024]{1,0:T(8,128)(2,1)S(1)}, bf16[256,1024]{1,0:T(8,128)(2,1)S(1)}, u32[]{:S(2)}, u32[]{:S(2)}) %collective-permute-start.21) | collective-permute-done | bytes 524320 | tf_op jit(solution)/shard_map/ppermute | solution.py:602
  85.9 3.7 %collective-permute-done.17.from_down = bf16[256,1024]{1,0:T(8,128)(2,1)S(1)} collective-permute-done((bf16[256,1024]{1,0:T(8,128)(2,1)S(1)}, bf16[256,1024]{1,0:T(8,128)(2,1)S(1)}, u32[]{:S(2)}, u32[]{:S(2)}) %collective-permute-start.17) | collective-permute-done | bytes 524320 | tf_op jit(solution)/shard_map/ppermute | solution.py:601
  89.6 0.2 relay_sums.1
  89.9 0.1 collective-permute-start.23
  90.0 3.2 %collective-permute-start.26 = (bf16[256,1024]{1,0:T(8,128)(2,1)S(1)}, bf16[256,1024]{1,0:T(8,128)(2,1)S(1)}, u32[]{:S(2)}, u32[]{:S(2)}) collective-permute-start(bf16[256,1024]{1,0:T(8,128)(2,1)S(1)} %get-tuple-element.102), channel_id=1, source_target_pairs={{0,12},{1,13},{2,14},{3,15},{4,0},{5,1},{6,2},{7,3},{8,4},{9,5},{1... | collective-permute-start | bytes 1572872 | tf_op jit(solution)/shard_map/ppermute | solution.py:615
  93.2 0.6 collective-permute-start.7
  94.4 0.8 unpack.1
  95.3 4.3 %pool_attention.1.pool = f32[16,72,128]{2,1,0:T(8,128)S(1)} custom-call(s32[16]{0:T(128)S(1)} %get-tuple-element.91.slots, s32[16]{0:T(128)S(1)} %get-tuple-element.92.alive, bf16[16,64,128]{2,1,0:T(8,128)(2,1)S(1)} %get-tuple-element.93.query, bf16[16,128,2048]{2,1,0:T(8,128)(2,1)S(1)} %bitcast.11, bf16[16,128,2048]{2,1,0:T(8,128)(2,1)S(1)} %bitcast.12, ...), custom_call_target="tpu_custom_call" | custom-call | flops 1000 | bytes 1000 | tf_op jit(solution)/shard_map/pool_attention/pallas_call | solution.py:344
  99.6 2.3 %product_own.1 = (f32[256,1024]{1,0:T(8,128)S(1)}, f32[256,1024]{1,0:T(8,128)S(1)}) custom-call(bf16[1024,512]{1,0:T(8,128)(2,1)S(1)} %get-tuple-element.94.refs_0_, bf16[256,512]{1,0:T(8,128)(2,1)S(1)} %collective-permute-done.6.refs_1_, bf16[256,512]{1,0:T(8,128)(2,1)S(1)} %collective-permute-done.7.refs_2_, ...), custom_call_target="tpu_custom_call" | custom-call | flops 1000 | bytes 1000 | tf_op jit(solution)/shard_map/product_own/pallas_call | solution.py:254
  102.0 9.0 %collective-permute-done.23.up_l = bf16[256,1024]{1,0:T(8,128)(2,1)S(1)} collective-permute-done((bf16[256,1024]{1,0:T(8,128)(2,1)S(1)}, bf16[256,1024]{1,0:T(8,128)(2,1)S(1)}, u32[]{:S(2)}, u32[]{:S(2)}) %collective-permute-start.23) | collective-permute-done | bytes 524320 | tf_op jit(solution)/shard_map/ppermute | solution.py:612
  111.0 3.9 %prefix_attention.1 = (bf16[1,256,2048]{2,1,0:T(8,128)(2,1)}, bf16[16,80,128]{2,1,0:T(8,128)(2,1)S(1)}) custom-call(s32[1]{0:T(128)S(6)} %copy.12.prompt_pages, f32[256,1024]{1,0:T(8,128)S(1)} %get-tuple-element.98.own_l, f32[256,1024]{1,0:T(8,128)S(1)} %get-tuple-element.99.own_r, bf16[256,1024]{1,0:T(8,128)(2,1)S(1)} %collective-permute-done.23.up_l, ...), custom_call_target="tpu_custom_call" | custom-call | flops 300000000 | bytes 6291456 | tf_op jit(solution)/shard_map/prefix_attention/pallas_call | solution.py:507
  114.8 11.6 %all_to_all.5.arrived = bf16[16,80,128]{2,1,0:T(8,128)(2,1)S(1)} all-to-all(bf16[16,80,128]{2,1,0:T(8,128)(2,1)S(1)} %get-tuple-element.106), channel_id=1, replica_groups=mesh['prompt'=8,'sample'=16] {'sample'}, dimensions={0} | all-to-all | bytes 655360 | tf_op jit(solution)/shard_map/all_to_all | solution.py:627
  126.5 1.0 combine.1
  (21 shorter events, 0.0 us)
Async XLA Ops:
  0.6 32.7 %copy-start = (bf16[1,4096,512]{2,1,0:T(8,128)(2,1)S(1)}, bf16[1,4096,512]{2,1,0:T(8,128)(2,1)}, u32[]{:S(2)}) copy-start(bf16[1,4096,512]{2,1,0:T(8,128)(2,1)} %param.10) | copy-start | bytes 12582916
  0.6 8.1 %copy-start.4 = (s32[1,1,16]{2,1,0:T(1,128)S(1)}, s32[1,1,16]{2,1,0:T(1,128)}, u32[]{:S(2)}) copy-start(s32[1,1,16]{2,1,0:T(1,128)} %where.1) | copy-start | bytes 196
  0.6 9.4 %collective-permute-start = (bf16[512,256]{1,0:T(8,128)(2,1)}, bf16[512,256]{1,0:T(8,128)(2,1)S(1)}, u32[]{:S(2)}, u32[]{:S(2)}) collective-permute-start(bf16[512,256]{1,0:T(8,128)(2,1)} %param.11), channel_id=1, source_target_pairs={{0,1},{1,2},{2,3},{3,0},{4,5},{5,6},{6,7},{7,4},{8,9},{9,10},{10,1... | collective-permute-start | bytes 786440 | tf_op jit(solution)/shard_map/ppermute | solution.py:566
  2.3 9.4 %collective-permute-start.1 = (bf16[512,256]{1,0:T(8,128)(2,1)}, bf16[512,256]{1,0:T(8,128)(2,1)S(1)}, u32[]{:S(2)}, u32[]{:S(2)}) collective-permute-start(bf16[512,256]{1,0:T(8,128)(2,1)} %param.11), channel_id=1, source_target_pairs={{0,3},{1,0},{2,1},{3,2},{4,7},{5,4},{6,5},{7,6},{8,11},{9,8},{10,9... | collective-permute-start | bytes 786440 | tf_op jit(solution)/shard_map/ppermute | solution.py:567
  4.0 12.9 %collective-permute-start.2 = (bf16[512,256]{1,0:T(8,128)(2,1)}, bf16[512,256]{1,0:T(8,128)(2,1)S(1)}, u32[]{:S(2)}, u32[]{:S(2)}) collective-permute-start(bf16[512,256]{1,0:T(8,128)(2,1)} %param.11), channel_id=1, source_target_pairs={{0,2},{1,3},{2,0},{3,1},{4,6},{5,7},{6,4},{7,5},{8,10},{9,11},{10,... | collective-permute-start | bytes 786440 | tf_op jit(solution)/shard_map/ppermute | solution.py:565
  8.7 0.8 copy-start.2
  9.5 27.4 %copy-start.3 = (bf16[1,1,2048]{2,1,0:T(2,128)(2,1)S(1)}, bf16[1,1,2048]{2,1,0:T(2,128)(2,1)}, u32[]{:S(2)}) copy-start(bf16[1,1,2048]{2,1,0:T(2,128)(2,1)} %param.13) | copy-start | bytes 12292
  18.0 2.7 %collective-permute-start.9 = (bf16[4,512,256]{2,1,0:T(8,128)(2,1)S(1)}, bf16[4,512,256]{2,1,0:T(8,128)(2,1)S(1)}, u32[]{:S(2)}, u32[]{:S(2)}) collective-permute-start(bf16[4,512,256]{2,1,0:T(8,128)(2,1)S(1)} %pad_maximum_fusion.refs_4_), channel_id=1, source_target_pairs={{0,16},{16,0},{32,48},{48,32},{64,80},{80,64},{96,112},{112,96},{1... | collective-permute-start | bytes 3145736 | tf_op jit(solution)/shard_map/ppermute | solution.py:582
  18.0 27.9 %collective-permute-start.11 = (bf16[1040,512]{1,0:T(8,128)(2,1)S(1)}, bf16[1040,512]{1,0:T(8,128)(2,1)S(1)}, u32[]{:S(2)}, u32[]{:S(2)}) collective-permute-start(bf16[1040,512]{1,0:T(8,128)(2,1)S(1)} %get-tuple-element.66), channel_id=1, source_target_pairs={{0,2},{1,3},{2,0},{3,1},{4,6},{5,7},{6,4},{7,5},{8,10},{9,11},{10,... | collective-permute-start | bytes 3194888 | tf_op jit(solution)/shard_map/ppermute | solution.py:576
  19.0 21.6 %collective-permute-start.8 = (bf16[4,512,256]{2,1,0:T(8,128)(2,1)S(1)}, bf16[4,512,256]{2,1,0:T(8,128)(2,1)S(1)}, u32[]{:S(2)}, u32[]{:S(2)}) collective-permute-start(bf16[4,512,256]{2,1,0:T(8,128)(2,1)S(1)} %pad_maximum_fusion.refs_4_), channel_id=1, source_target_pairs={{0,32},{16,112},{32,64},{48,16},{64,96},{80,48},{96,0},{112,80},{1... | collective-permute-start | bytes 3145736 | tf_op jit(solution)/shard_map/ppermute | solution.py:581
  20.7 25.5 %collective-permute-start.10 = (bf16[4,512,256]{2,1,0:T(8,128)(2,1)S(1)}, bf16[4,512,256]{2,1,0:T(8,128)(2,1)S(1)}, u32[]{:S(2)}, u32[]{:S(2)}) collective-permute-start(bf16[4,512,256]{2,1,0:T(8,128)(2,1)S(1)} %collective-permute-done.9.refs_5_), channel_id=1, source_target_pairs={{0,32},{16,112},{32,64},{48,16},{64,96},{80,48},{96,0},{112,80},{1... | collective-permute-start | bytes 3145736 | tf_op jit(solution)/shard_map/ppermute | solution.py:583
  22.3 5.8 %collective-permute-start.3 = (bf16[40,256]{1,0:T(8,128)(2,1)S(1)}, bf16[40,256]{1,0:T(8,128)(2,1)S(1)}, u32[]{:S(2)}, u32[]{:S(2)}) collective-permute-start(bf16[40,256]{1,0:T(8,128)(2,1)S(1)} %get-tuple-element.59.refs_0_), channel_id=1, source_target_pairs={{0,4},{1,5},{2,6},{3,7},{4,8},{5,9},{6,10},{7,11},{8,12},{9,13},{1... | collective-permute-start | bytes 61448 | tf_op jit(solution)/shard_map/ppermute | solution.py:574
  24.2 5.7 %collective-permute-start.4 = (bf16[40,256]{1,0:T(8,128)(2,1)S(1)}, bf16[40,256]{1,0:T(8,128)(2,1)S(1)}, u32[]{:S(2)}, u32[]{:S(2)}) collective-permute-start(bf16[40,256]{1,0:T(8,128)(2,1)S(1)} %get-tuple-element.59.refs_0_), channel_id=1, source_target_pairs={{0,12},{1,13},{2,14},{3,15},{4,0},{5,1},{6,2},{7,3},{8,4},{9,5},{1... | collective-permute-start | bytes 61448 | tf_op jit(solution)/shard_map/ppermute | solution.py:574
  28.1 5.3 %collective-permute-start.5 = (bf16[40,256]{1,0:T(8,128)(2,1)S(1)}, bf16[40,256]{1,0:T(8,128)(2,1)S(1)}, u32[]{:S(2)}, u32[]{:S(2)}) collective-permute-start(bf16[40,256]{1,0:T(8,128)(2,1)S(1)} %get-tuple-element.59.refs_0_), channel_id=1, source_target_pairs={{0,8},{1,9},{2,10},{3,11},{4,12},{5,13},{6,14},{7,15},{8,0},{9,1},... | collective-permute-start | bytes 61448 | tf_op jit(solution)/shard_map/ppermute | solution.py:574
  33.6 30.5 %collective-permute-start.14 = (bf16[848,512]{1,0:T(8,128)(2,1)S(1)}, bf16[848,512]{1,0:T(8,128)(2,1)S(1)}, u32[]{:S(2)}, u32[]{:S(2)}) collective-permute-start(bf16[848,512]{1,0:T(8,128)(2,1)S(1)} %get-tuple-element.71), channel_id=1, source_target_pairs={{0,1},{1,2},{2,3},{3,0},{4,5},{5,6},{6,7},{7,4},{8,9},{9,10},{10,1... | collective-permute-start | bytes 2605064 | tf_op jit(solution)/shard_map/ppermute | solution.py:577
  35.7 28.5 %collective-permute-start.15 = (bf16[848,512]{1,0:T(8,128)(2,1)S(1)}, bf16[848,512]{1,0:T(8,128)(2,1)S(1)}, u32[]{:S(2)}, u32[]{:S(2)}) collective-permute-start(bf16[848,512]{1,0:T(8,128)(2,1)S(1)} %get-tuple-element.72), channel_id=1, source_target_pairs={{0,3},{1,0},{2,1},{3,2},{4,7},{5,4},{6,5},{7,6},{8,11},{9,8},{10,9... | collective-permute-start | bytes 2605064 | tf_op jit(solution)/shard_map/ppermute | solution.py:578
  36.9 3.4 %copy-start.1 = (bf16[1,1,16,128,2048]{4,3,2,1,0:T(8,128)(2,1)S(1)}, bf16[1,1,16,128,2048]{4,3,2,1,0:T(8,128)(2,1)}, u32[]{:S(2)}) copy-start(bf16[1,1,16,128,2048]{4,3,2,1,0:T(8,128)(2,1)} %param.14) | copy-start | bytes 25165828
  46.3 17.8 %collective-permute-start.12 = (bf16[2,512,256]{2,1,0:T(8,128)(2,1)S(1)}, bf16[2,512,256]{2,1,0:T(8,128)(2,1)S(1)}, u32[]{:S(2)}, u32[]{:S(2)}) collective-permute-start(bf16[2,512,256]{2,1,0:T(8,128)(2,1)S(1)} %get-tuple-element.109), channel_id=1, source_target_pairs={{0,32},{16,112},{32,64},{48,16},{64,96},{80,48},{96,0},{112,80},{1... | collective-permute-start | bytes 1572872 | tf_op jit(solution)/shard_map/ppermute | solution.py:587
  47.7 16.4 %collective-permute-start.13 = (bf16[2,512,256]{2,1,0:T(8,128)(2,1)S(1)}, bf16[2,512,256]{2,1,0:T(8,128)(2,1)S(1)}, u32[]{:S(2)}, u32[]{:S(2)}) collective-permute-start(bf16[2,512,256]{2,1,0:T(8,128)(2,1)S(1)} %get-tuple-element.108), channel_id=1, source_target_pairs={{0,32},{16,112},{32,64},{48,16},{64,96},{80,48},{96,0},{112,80},{1... | collective-permute-start | bytes 1572872 | tf_op jit(solution)/shard_map/ppermute | solution.py:587
  49.3 19.0 %collective-permute-start.18 = (bf16[4,512,256]{2,1,0:T(8,128)(2,1)S(1)}, bf16[4,512,256]{2,1,0:T(8,128)(2,1)S(1)}, u32[]{:S(2)}, u32[]{:S(2)}) collective-permute-start(bf16[4,512,256]{2,1,0:T(8,128)(2,1)S(1)} %collective-permute-done.8.refs_6_), channel_id=1, source_target_pairs={{0,16},{16,0},{32,48},{48,32},{64,80},{80,64},{96,112},{112,96},{1... | collective-permute-start | bytes 3145736 | tf_op jit(solution)/shard_map/ppermute | solution.py:588
  64.1 4.2 %collective-permute-start.19 = (bf16[4,512,256]{2,1,0:T(8,128)(2,1)S(1)}, bf16[4,512,256]{2,1,0:T(8,128)(2,1)S(1)}, u32[]{:S(2)}, u32[]{:S(2)}) collective-permute-start(bf16[4,512,256]{2,1,0:T(8,128)(2,1)S(1)} %collective-permute-done.10.refs_7_), channel_id=1, source_target_pairs={{0,16},{16,0},{32,48},{48,32},{64,80},{80,64},{96,112},{112,96},{1... | collective-permute-start | bytes 3145736 | tf_op jit(solution)/shard_map/ppermute | solution.py:589
  64.1 3.4 %collective-permute-start.16 = (bf16[2,512,256]{2,1,0:T(8,128)(2,1)S(1)}, bf16[2,512,256]{2,1,0:T(8,128)(2,1)S(1)}, u32[]{:S(2)}, u32[]{:S(2)}) collective-permute-start(bf16[2,512,256]{2,1,0:T(8,128)(2,1)S(1)} %collective-permute-done.12.refs_6_.refs_10_), channel_id=1, source_target_pairs={{0,16},{16,0},{32,48},{48,32},{64,80},{80,64},{96,112},{112,96},{1... | collective-permute-start | bytes 1572872 | tf_op jit(solution)/shard_map/ppermute | solution.py:591
  64.7 3.6 %collective-permute-start.20 = (bf16[2,512,256]{2,1,0:T(8,128)(2,1)S(1)}, bf16[2,512,256]{2,1,0:T(8,128)(2,1)S(1)}, u32[]{:S(2)}, u32[]{:S(2)}) collective-permute-start(bf16[2,512,256]{2,1,0:T(8,128)(2,1)S(1)} %collective-permute-done.13.refs_7_.refs_11_), channel_id=1, source_target_pairs={{0,16},{16,0},{32,48},{48,32},{64,80},{80,64},{96,112},{112,96},{1... | collective-permute-start | bytes 1572872 | tf_op jit(solution)/shard_map/ppermute | solution.py:591
  69.5 16.4 %collective-permute-start.21 = (bf16[256,1024]{1,0:T(8,128)(2,1)S(1)}, bf16[256,1024]{1,0:T(8,128)(2,1)S(1)}, u32[]{:S(2)}, u32[]{:S(2)}) collective-permute-start(bf16[256,1024]{1,0:T(8,128)(2,1)S(1)} %product_far_r.1), channel_id=1, source_target_pairs={{0,12},{1,13},{2,14},{3,15},{4,0},{5,1},{6,2},{7,3},{8,4},{9,5},{1... | collective-permute-start | bytes 1572872 | tf_op jit(solution)/shard_map/ppermute | solution.py:602
  73.6 16.0 %collective-permute-start.17 = (bf16[256,1024]{1,0:T(8,128)(2,1)S(1)}, bf16[256,1024]{1,0:T(8,128)(2,1)S(1)}, u32[]{:S(2)}, u32[]{:S(2)}) collective-permute-start(bf16[256,1024]{1,0:T(8,128)(2,1)S(1)} %product_far_l.1), channel_id=1, source_target_pairs={{0,4},{1,5},{2,6},{3,7},{4,8},{5,9},{6,10},{7,11},{8,12},{9,13},{1... | collective-permute-start | bytes 1572872 | tf_op jit(solution)/shard_map/ppermute | solution.py:601
  73.6 6.8 %collective-permute-start.22 = (bf16[80,512]{1,0:T(8,128)(2,1)S(1)}, bf16[80,512]{1,0:T(8,128)(2,1)S(1)}, u32[]{:S(2)}, u32[]{:S(2)}) collective-permute-start(bf16[80,512]{1,0:T(8,128)(2,1)S(1)} %get-tuple-element.81), channel_id=1, source_target_pairs={{0,2},{1,3},{2,0},{3,1},{4,6},{5,7},{6,4},{7,5},{8,10},{9,11},{10,... | collective-permute-start | bytes 245768 | tf_op jit(solution)/shard_map/ppermute | solution.py:604
  74.4 20.8 %slice-start = ((s8[8388608]{0:T(1024)(128)(4,1)}), s8[4194304]{0:T(1024)(128)(4,1)S(1)}, s32[]{:S(2)}) async-start(s8[8388608]{0:T(1024)(128)(4,1)} %bitcast.9), calls=%async_computation.1 | async-start | bytes 8388608
  74.5 20.8 %slice-start.1 = ((s8[8388608]{0:T(1024)(128)(4,1)}), s8[4194304]{0:T(1024)(128)(4,1)S(1)}, s32[]{:S(2)}) async-start(s8[8388608]{0:T(1024)(128)(4,1)} %bitcast.9), calls=%async_computation.2 | async-start | bytes 8388608
  74.5 18.7 %collective-permute-start.6 = (bf16[256,512]{1,0:T(8,128)(2,1)S(1)}, bf16[256,512]{1,0:T(8,128)(2,1)S(1)}, u32[]{:S(2)}, u32[]{:S(2)}) collective-permute-start(bf16[256,512]{1,0:T(8,128)(2,1)S(1)} %get-tuple-element.60), channel_id=1, source_target_pairs={{0,1},{1,2},{2,3},{3,0},{4,5},{5,6},{6,7},{7,4},{8,9},{9,10},{10,1... | collective-permute-start | bytes 786440 | tf_op jit(solution)/shard_map/ppermute | solution.py:621
  79.6 22.4 %collective-permute-start.24 = (bf16[256,1024]{1,0:T(8,128)(2,1)S(1)}, bf16[256,1024]{1,0:T(8,128)(2,1)S(1)}, u32[]{:S(2)}, u32[]{:S(2)}) collective-permute-start(bf16[256,1024]{1,0:T(8,128)(2,1)S(1)} %get-tuple-element.100), channel_id=1, source_target_pairs={{0,4},{1,5},{2,6},{3,7},{4,8},{5,9},{6,10},{7,11},{8,12},{9,13},{1... | collective-permute-start | bytes 1572872 | tf_op jit(solution)/shard_map/ppermute | solution.py:608
  80.5 21.5 %collective-permute-start.25 = (bf16[256,1024]{1,0:T(8,128)(2,1)S(1)}, bf16[256,1024]{1,0:T(8,128)(2,1)S(1)}, u32[]{:S(2)}, u32[]{:S(2)}) collective-permute-start(bf16[256,1024]{1,0:T(8,128)(2,1)S(1)} %get-tuple-element.101), channel_id=1, source_target_pairs={{0,12},{1,13},{2,14},{3,15},{4,0},{5,1},{6,2},{7,3},{8,4},{9,5},{1... | collective-permute-start | bytes 1572872 | tf_op jit(solution)/shard_map/ppermute | solution.py:608
  89.9 21.1 %collective-permute-start.23 = (bf16[256,1024]{1,0:T(8,128)(2,1)S(1)}, bf16[256,1024]{1,0:T(8,128)(2,1)S(1)}, u32[]{:S(2)}, u32[]{:S(2)}) collective-permute-start(bf16[256,1024]{1,0:T(8,128)(2,1)S(1)} %get-tuple-element.87), channel_id=1, source_target_pairs={{0,4},{1,5},{2,6},{3,7},{4,8},{5,9},{6,10},{7,11},{8,12},{9,13},{1... | collective-permute-start | bytes 1572872 | tf_op jit(solution)/shard_map/ppermute | solution.py:612
  90.0 21.0 %collective-permute-start.26 = (bf16[256,1024]{1,0:T(8,128)(2,1)S(1)}, bf16[256,1024]{1,0:T(8,128)(2,1)S(1)}, u32[]{:S(2)}, u32[]{:S(2)}) collective-permute-start(bf16[256,1024]{1,0:T(8,128)(2,1)S(1)} %get-tuple-element.102), channel_id=1, source_target_pairs={{0,12},{1,13},{2,14},{3,15},{4,0},{5,1},{6,2},{7,3},{8,4},{9,5},{1... | collective-permute-start | bytes 1572872 | tf_op jit(solution)/shard_map/ppermute | solution.py:615
  93.2 6.4 %collective-permute-start.7 = (bf16[256,512]{1,0:T(8,128)(2,1)S(1)}, bf16[256,512]{1,0:T(8,128)(2,1)S(1)}, u32[]{:S(2)}, u32[]{:S(2)}) collective-permute-start(bf16[256,512]{1,0:T(8,128)(2,1)S(1)} %get-tuple-element.61), channel_id=1, source_target_pairs={{0,3},{1,0},{2,1},{3,2},{4,7},{5,4},{6,5},{7,6},{8,11},{9,8},{10,9... | collective-permute-start | bytes 786440 | tf_op jit(solution)/shard_map/ppermute | solution.py:622

commit v11 on v10

--- a/solution.py
+++ b/solution.py
@@ -205,10 +205,10 @@
     blocks, (right, left, last_right, last_left, far_blocks), sems = refs[:4], refs[4:9], refs[9]
     wanted = [(1, k, right.at[block_rows(k)]) for k in range(3)]
     wanted += [(3, k, left.at[block_rows(k)]) for k in range(3)]
-    wanted += [(1, 3, last_right), (3, 3, last_left)]
+    wanted += [(1, 3, last_right.at[block_rows(0)]), (3, 3, last_left.at[block_rows(0)])]
     copies = copy_rows(states, sems, wanted)
-    put_blocks(right, 3 * ROWS, blocks)
-    put_blocks(left, 3 * ROWS, blocks)
+    put_blocks(last_right, ROWS, blocks)
+    put_blocks(last_left, ROWS, blocks)
     put_blocks(far_blocks, 0, blocks)
     for copy in copies:
         copy.wait()
@@ -218,8 +218,8 @@
     vmem = pl.BlockSpec(memory_space=pltpu.VMEM)
     return pl.pallas_call(
         pick_near_kernel,
-        out_shape=[jax.ShapeDtypeStruct((3 * ROWS + 2 * BLOCK, SLICE), BF16)] * 2
-        + [jax.ShapeDtypeStruct((ROWS, SLICE), BF16)] * 2
+        out_shape=[jax.ShapeDtypeStruct((3 * ROWS, SLICE), BF16)] * 2
+        + [jax.ShapeDtypeStruct((ROWS + 2 * BLOCK, SLICE), BF16)] * 2
         + [jax.ShapeDtypeStruct((2 * BLOCK, SLICE), BF16)],
         in_specs=[pl.BlockSpec(memory_space=pl.ANY)] + [vmem] * 4,
         out_specs=[vmem] * 5,
@@ -492,10 +492,9 @@
     first = logs.astype(BF16).astype(F32)
     second = (logs - first).astype(BF16).astype(F32)
     third = logs - first - second
-    terms = jnp.zeros((SAMPLES * HEADS, HEAD_SIZE), F32)
-    for g in range(GROUPS):
-        for t, term in enumerate((first, second, third)):
-            terms = put_lane(terms, t * GROUPS + g, term[:, g : g + 1])
+    lane = lax.broadcasted_iota(jnp.int32, logs.shape, 1)
+    later = jnp.where(lane < 2 * GROUPS, pltpu.roll(second, GROUPS, 1), pltpu.roll(third, 2 * GROUPS, 1))
+    terms = jnp.where(lane < GROUPS, first, jnp.where(lane < 3 * GROUPS, later, 0.0))
     padding = jnp.zeros((SENT - QUERY_HEADS - HEADS, HEAD_SIZE), F32)
     for r, source in enumerate(sources):
         rows = jnp.concatenate([terms[r * HEADS : (r + 1) * HEADS], padding])
@@ -615,11 +614,10 @@
         lax.ppermute(down_r, "sample", Z_DOWN),
     ]
 
-    arrived, up_l = tie(([rows_right, rows_left, far_blocks], up_l))
-    queries_all, by_group, slots, alive = unpack(blocks, arrived)
-    pool = pool_attention(slots, alive, queries_all, pool_pages[0, 0])
     last_right = lax.ppermute(last_right, "sample", X_RIGHT)
     last_left = lax.ppermute(last_left, "sample", X_LEFT)
+    queries_all, by_group, slots, alive = unpack(blocks, [last_right, last_left, far_blocks])
+    pool = pool_attention(slots, alive, queries_all, pool_pages[0, 0])
     mine, pool = tie(([own_states, last_right, last_left, rows_far], pool))
     sums = [*product(mine, pieces, ((3, 0, 0, 3),), F32, "product_own"), *sums]
 

time: 128 us -> 127 us (level)
  waiting for transfers between devices: 50.5 us -> 46.6 us
  blocking collectives: 11.6 us -> 13.8 us
  starting transfers between devices: 35.1 us -> 37.2 us
    ppermute x1, waiting for transfers between devices: 9.03 us -> 3.03 us  [per_device(): lax.ppermute(up_l, 'sample', Z_UP)]
    ppermute x1, waiting for transfers between devices: 0.01 us -> 5.1 us  [per_device(): last_left = lax.ppermute(last_left, 'sample', X_LEFT)]
    ppermute x1, waiting for transfers between devices: 0.79 us -> 5.08 us  [per_device(): far_blocks = lax.ppermute(far_blocks, 'sample', X_FAR)]
    ppermute x1, waiting for transfers between devices: 3.73 us -> 0.43 us  [per_device(): from_down = lax.ppermute(far_l, 'sample', Z_UP)]
    ppermute x1, waiting for transfers between devices: 2.17 us -> 0.01 us  [per_device(): from_up = lax.ppermute(far_r, 'sample', Z_DOWN)]
    all_to_all x1, blocking collectives: 11.6 us -> 13.8 us  [per_device(): lax.all_to_all(packed, 'sample', split_axis=0, concat_axis=0, tiled=True)]
    ppermute x1, waiting for transfers between devices: 14.8 us -> 13 us  [per_device(): rows_right = lax.ppermute(to_right, 'sample', X_RIGHT)]
    ppermute x1, starting transfers between devices: 0.83 us -> 2.44 us  [per_device(): far_blocks = lax.ppermute(far_blocks, 'sample', X_FAR)]
where the time goes in v11:
time: 127 us
  waiting for transfers between devices  46.6 us (37%)
  starting transfers between devices  37.2 us (29%)
  Pallas kernels  21.1 us (17%)
  blocking collectives  13.8 us (11%)
  local copies, waits for them, and re-layouts  4.22 us (3%)
  between operations  2.8 us (2%)
    all_to_all x1, blocking collectives, per_device(): lax.all_to_all(packed, 'sample', split_axis=0, concat_axis=0, tiled=True)  13.8 us
    ppermute x1, waiting for transfers between devices, per_device(): rows_right = lax.ppermute(to_right, 'sample', X_RIGHT)  13 us
    pallas_call x2, Pallas kernels, product(): pl.pallas_call(functools.partial(product_kernel, blocks), out_shape=outs,...  6.81 us
    ppermute x3, starting transfers between devices, per_device(): lax.ppermute(block, 'sample', to)  5.9 us
    ppermute x1, waiting for transfers between devices, per_device(): rows_far = lax.ppermute(to_far, 'sample', X_FAR)  5.36 us
    ppermute x3, waiting for transfers between devices, per_device(): lax.ppermute(block, 'sample', to)  5.18 us
    ppermute x1, waiting for transfers between devices, per_device(): weight_far = lax.ppermute(kv_weight, 'sample', X_FAR)  5.14 us
    ppermute x1, waiting for transfers between devices, per_device(): last_left = lax.ppermute(last_left, 'sample', X_LEFT)  5.1 us
  transfers between devices with their start and end apart: 27, of which 14 were waited for; matrix products, arithmetic and copies ran while one was open for 0% of the time, Pallas kernels for 13%

profile of v11, /device:TPU:0, one launch (start us, length us, event | category | flops | bytes accessed | tf_op | source)
XLA Modules:
  0.0 126.9 jit_solution(9611379378182308734)
XLA Ops:
  0.6 1.6 %collective-permute-start = (bf16[512,256]{1,0:T(8,128)(2,1)}, bf16[512,256]{1,0:T(8,128)(2,1)S(1)}, u32[]{:S(2)}, u32[]{:S(2)}) collective-permute-start(bf16[512,256]{1,0:T(8,128)(2,1)} %param.11), channel_id=1, source_target_pairs={{0,1},{1,2},{2,3},{3,0},{4,5},{5,6},{6,7},{7,4},{8,9},{9,10},{10,1... | collective-permute-start | bytes 786440 | tf_op jit(solution)/shard_map/ppermute | solution.py:565
  2.3 1.7 %collective-permute-start.1 = (bf16[512,256]{1,0:T(8,128)(2,1)}, bf16[512,256]{1,0:T(8,128)(2,1)S(1)}, u32[]{:S(2)}, u32[]{:S(2)}) collective-permute-start(bf16[512,256]{1,0:T(8,128)(2,1)} %param.11), channel_id=1, source_target_pairs={{0,3},{1,0},{2,1},{3,2},{4,7},{5,4},{6,5},{7,6},{8,11},{9,8},{10,9... | collective-permute-start | bytes 786440 | tf_op jit(solution)/shard_map/ppermute | solution.py:566
  4.0 1.9 %collective-permute-start.2 = (bf16[512,256]{1,0:T(8,128)(2,1)}, bf16[512,256]{1,0:T(8,128)(2,1)S(1)}, u32[]{:S(2)}, u32[]{:S(2)}) collective-permute-start(bf16[512,256]{1,0:T(8,128)(2,1)} %param.11), channel_id=1, source_target_pairs={{0,2},{1,3},{2,0},{3,1},{4,6},{5,7},{6,4},{7,5},{8,10},{9,11},{10,... | collective-permute-start | bytes 786440 | tf_op jit(solution)/shard_map/ppermute | solution.py:564
  5.9 1.6 %pick_far.1 = (bf16[1024,512]{1,0:T(8,128)(2,1)S(1)}, bf16[1040,512]{1,0:T(8,128)(2,1)S(1)}) custom-call(bf16[4,4,256,512]{3,2,1,0:T(8,128)(2,1)} %bitcast.15), custom_call_target="tpu_custom_call" | custom-call | flops 1000 | bytes 1000 | tf_op jit(solution)/shard_map/pick_far/pallas_call | solution.py:183
  8.7 0.0 copy-start.2
  8.7 0.7 copy-done.2
  9.5 0.6 prepare.1
  10.1 0.0 collective-permute-done
  10.1 1.6 %collective-permute-done.1 = bf16[512,256]{1,0:T(8,128)(2,1)S(1)} collective-permute-done((bf16[512,256]{1,0:T(8,128)(2,1)}, bf16[512,256]{1,0:T(8,128)(2,1)S(1)}, u32[]{:S(2)}, u32[]{:S(2)}) %collective-permute-start.1) | collective-permute-done | bytes 262176 | tf_op jit(solution)/shard_map/ppermute | solution.py:566
  11.7 5.1 %collective-permute-done.2 = bf16[512,256]{1,0:T(8,128)(2,1)S(1)} collective-permute-done((bf16[512,256]{1,0:T(8,128)(2,1)}, bf16[512,256]{1,0:T(8,128)(2,1)S(1)}, u32[]{:S(2)}, u32[]{:S(2)}) %collective-permute-start.2) | collective-permute-done | bytes 262176 | tf_op jit(solution)/shard_map/ppermute | solution.py:564
  16.9 1.1 pad_maximum_fusion.refs_4_
  18.0 0.1 collective-permute-start.9
  18.0 0.9 collective-permute-start.11
  19.0 1.6 %collective-permute-start.8 = (bf16[4,512,256]{2,1,0:T(8,128)(2,1)S(1)}, bf16[4,512,256]{2,1,0:T(8,128)(2,1)S(1)}, u32[]{:S(2)}, u32[]{:S(2)}) collective-permute-start(bf16[4,512,256]{2,1,0:T(8,128)(2,1)S(1)} %pad_maximum_fusion.refs_4_), channel_id=1, source_target_pairs={{0,32},{16,112},{32,64},{48,16},{64,96},{80,48},{96,0},{112,80},{1... | collective-permute-start | bytes 3145736 | tf_op jit(solution)/shard_map/ppermute | solution.py:580
  20.5 0.2 collective-permute-done.9.refs_5_
  20.7 1.6 %collective-permute-start.10 = (bf16[4,512,256]{2,1,0:T(8,128)(2,1)S(1)}, bf16[4,512,256]{2,1,0:T(8,128)(2,1)S(1)}, u32[]{:S(2)}, u32[]{:S(2)}) collective-permute-start(bf16[4,512,256]{2,1,0:T(8,128)(2,1)S(1)} %collective-permute-done.9.refs_5_), channel_id=1, source_target_pairs={{0,32},{16,112},{32,64},{48,16},{64,96},{80,48},{96,0},{112,80},{1... | collective-permute-start | bytes 3145736 | tf_op jit(solution)/shard_map/ppermute | solution.py:582
  22.3 1.9 %collective-permute-start.3 = (bf16[40,256]{1,0:T(8,128)(2,1)S(1)}, bf16[40,256]{1,0:T(8,128)(2,1)S(1)}, u32[]{:S(2)}, u32[]{:S(2)}) collective-permute-start(bf16[40,256]{1,0:T(8,128)(2,1)S(1)} %get-tuple-element.55.refs_0_), channel_id=1, source_target_pairs={{0,4},{1,5},{2,6},{3,7},{4,8},{5,9},{6,10},{7,11},{8,12},{9,13},{1... | collective-permute-start | bytes 61448 | tf_op jit(solution)/shard_map/ppermute | solution.py:573
  24.2 2.1 %collective-permute-start.4 = (bf16[40,256]{1,0:T(8,128)(2,1)S(1)}, bf16[40,256]{1,0:T(8,128)(2,1)S(1)}, u32[]{:S(2)}, u32[]{:S(2)}) collective-permute-start(bf16[40,256]{1,0:T(8,128)(2,1)S(1)} %get-tuple-element.55.refs_0_), channel_id=1, source_target_pairs={{0,12},{1,13},{2,14},{3,15},{4,0},{5,1},{6,2},{7,3},{8,4},{9,5},{1... | collective-permute-start | bytes 61448 | tf_op jit(solution)/shard_map/ppermute | solution.py:573
  26.3 1.8 %collective-permute-done.3.refs_1_ = bf16[40,256]{1,0:T(8,128)(2,1)S(1)} collective-permute-done((bf16[40,256]{1,0:T(8,128)(2,1)S(1)}, bf16[40,256]{1,0:T(8,128)(2,1)S(1)}, u32[]{:S(2)}, u32[]{:S(2)}) %collective-permute-start.3) | collective-permute-done | bytes 20512 | tf_op jit(solution)/shard_map/ppermute | solution.py:573
  28.1 1.9 %collective-permute-start.5 = (bf16[40,256]{1,0:T(8,128)(2,1)S(1)}, bf16[40,256]{1,0:T(8,128)(2,1)S(1)}, u32[]{:S(2)}, u32[]{:S(2)}) collective-permute-start(bf16[40,256]{1,0:T(8,128)(2,1)S(1)} %get-tuple-element.55.refs_0_), channel_id=1, source_target_pairs={{0,8},{1,9},{2,10},{3,11},{4,12},{5,13},{6,14},{7,15},{8,0},{9,1},... | collective-permute-start | bytes 61448 | tf_op jit(solution)/shard_map/ppermute | solution.py:573
  29.9 3.4 %collective-permute-done.5.refs_3_ = bf16[40,256]{1,0:T(8,128)(2,1)S(1)} collective-permute-done((bf16[40,256]{1,0:T(8,128)(2,1)S(1)}, bf16[40,256]{1,0:T(8,128)(2,1)S(1)}, u32[]{:S(2)}, u32[]{:S(2)}) %collective-permute-start.5) | collective-permute-done | bytes 20512 | tf_op jit(solution)/shard_map/ppermute | solution.py:573
  33.4 0.3 pick_near.1
  33.6 2.0 %collective-permute-start.14 = (bf16[768,512]{1,0:T(8,128)(2,1)S(1)}, bf16[768,512]{1,0:T(8,128)(2,1)S(1)}, u32[]{:S(2)}, u32[]{:S(2)}) collective-permute-start(bf16[768,512]{1,0:T(8,128)(2,1)S(1)} %get-tuple-element.66), channel_id=1, source_target_pairs={{0,1},{1,2},{2,3},{3,0},{4,5},{5,6},{6,7},{7,4},{8,9},{9,10},{10,1... | collective-permute-start | bytes 2359304 | tf_op jit(solution)/shard_map/ppermute | solution.py:576
  35.7 3.4 %copy-done.1 = bf16[1,1,16,128,2048]{4,3,2,1,0:T(8,128)(2,1)S(1)} copy-done((bf16[1,1,16,128,2048]{4,3,2,1,0:T(8,128)(2,1)S(1)}, bf16[1,1,16,128,2048]{4,3,2,1,0:T(8,128)(2,1)}, u32[]{:S(2)}) %copy-start.1) | copy-done | bytes 8388632
  39.0 0.2 local_attention.1.local
  39.3 1.3 %collective-permute-start.15 = (bf16[768,512]{1,0:T(8,128)(2,1)S(1)}, bf16[768,512]{1,0:T(8,128)(2,1)S(1)}, u32[]{:S(2)}, u32[]{:S(2)}) collective-permute-start(bf16[768,512]{1,0:T(8,128)(2,1)S(1)} %get-tuple-element.67), channel_id=1, source_target_pairs={{0,3},{1,0},{2,1},{3,2},{4,7},{5,4},{6,5},{7,6},{8,11},{9,8},{10,9... | collective-permute-start | bytes 2359304 | tf_op jit(solution)/shard_map/ppermute | solution.py:577
  40.6 0.0 collective-permute-done.8.refs_6_
  40.6 5.4 %collective-permute-done.11.refs_3_ = bf16[1040,512]{1,0:T(8,128)(2,1)S(1)} collective-permute-done((bf16[1040,512]{1,0:T(8,128)(2,1)S(1)}, bf16[1040,512]{1,0:T(8,128)(2,1)S(1)}, u32[]{:S(2)}, u32[]{:S(2)}) %collective-permute-start.11) | collective-permute-done | bytes 1064992 | tf_op jit(solution)/shard_map/ppermute | solution.py:575
  46.0 0.2 collective-permute-done.10.refs_7_
  46.2 0.1 fusion
  46.3 1.4 %collective-permute-start.12 = (bf16[2,512,256]{2,1,0:T(8,128)(2,1)S(1)}, bf16[2,512,256]{2,1,0:T(8,128)(2,1)S(1)}, u32[]{:S(2)}, u32[]{:S(2)}) collective-permute-start(bf16[2,512,256]{2,1,0:T(8,128)(2,1)S(1)} %get-tuple-element.101), channel_id=1, source_target_pairs={{0,32},{16,112},{32,64},{48,16},{64,96},{80,48},{96,0},{112,80},{1... | collective-permute-start | bytes 1572872 | tf_op jit(solution)/shard_map/ppermute | solution.py:586
  47.7 1.6 %collective-permute-start.13 = (bf16[2,512,256]{2,1,0:T(8,128)(2,1)S(1)}, bf16[2,512,256]{2,1,0:T(8,128)(2,1)S(1)}, u32[]{:S(2)}, u32[]{:S(2)}) collective-permute-start(bf16[2,512,256]{2,1,0:T(8,128)(2,1)S(1)} %get-tuple-element.100), channel_id=1, source_target_pairs={{0,32},{16,112},{32,64},{48,16},{64,96},{80,48},{96,0},{112,80},{1... | collective-permute-start | bytes 1572872 | tf_op jit(solution)/shard_map/ppermute | solution.py:586
  49.3 0.0 collective-permute-start.18
  49.3 13.0 %collective-permute-done.14.refs_1_ = bf16[768,512]{1,0:T(8,128)(2,1)S(1)} collective-permute-done((bf16[768,512]{1,0:T(8,128)(2,1)S(1)}, bf16[768,512]{1,0:T(8,128)(2,1)S(1)}, u32[]{:S(2)}, u32[]{:S(2)}) %collective-permute-start.14) | collective-permute-done | bytes 786464 | tf_op jit(solution)/shard_map/ppermute | solution.py:576
  62.3 0.0 collective-permute-start.19
  62.4 0.0 collective-permute-done.15.refs_2_
  62.4 0.0 collective-permute-done.12.refs_6_.refs_10_
  62.4 0.0 collective-permute-done.13.refs_7_.refs_11_
  62.4 0.6 collective-permute-start.16
  62.9 0.1 collective-permute-start.20
  63.0 1.2 product_far_l.1
  64.3 1.5 %collective-permute-done.16.refs_8_.refs_12_ = bf16[2,512,256]{2,1,0:T(8,128)(2,1)S(1)} collective-permute-done((bf16[2,512,256]{2,1,0:T(8,128)(2,1)S(1)}, bf16[2,512,256]{2,1,0:T(8,128)(2,1)S(1)}, u32[]{:S(2)}, u32[]{:S(2)}) %collective-permute-start.16) | collective-permute-done | bytes 524320 | tf_op jit(solution)/shard_map/ppermute | solution.py:590
  65.7 0.7 collective-permute-done.20.refs_9_.refs_13_
  66.5 1.2 product_far_r.1
  67.8 4.1 %collective-permute-start.21 = (bf16[256,1024]{1,0:T(8,128)(2,1)S(1)}, bf16[256,1024]{1,0:T(8,128)(2,1)S(1)}, u32[]{:S(2)}, u32[]{:S(2)}) collective-permute-start(bf16[256,1024]{1,0:T(8,128)(2,1)S(1)} %product_far_r.1), channel_id=1, source_target_pairs={{0,12},{1,13},{2,14},{3,15},{4,0},{5,1},{6,2},{7,3},{8,4},{9,5},{1... | collective-permute-start | bytes 1572872 | tf_op jit(solution)/shard_map/ppermute | solution.py:601
  71.9 0.5 collective-permute-start.6
  72.4 2.4 %collective-permute-start.22 = (bf16[80,512]{1,0:T(8,128)(2,1)S(1)}, bf16[80,512]{1,0:T(8,128)(2,1)S(1)}, u32[]{:S(2)}, u32[]{:S(2)}) collective-permute-start(bf16[80,512]{1,0:T(8,128)(2,1)S(1)} %get-tuple-element.76), channel_id=1, source_target_pairs={{0,2},{1,3},{2,0},{3,1},{4,6},{5,7},{6,4},{7,5},{8,10},{9,11},{10,... | collective-permute-start | bytes 245768 | tf_op jit(solution)/shard_map/ppermute | solution.py:603
  74.8 4.5 %product_near.1 = (bf16[256,1024]{1,0:T(8,128)(2,1)S(1)}, bf16[256,1024]{1,0:T(8,128)(2,1)S(1)}, bf16[256,1024]{1,0:T(8,128)(2,1)S(1)}, bf16[256,1024]{1,0:T(8,128)(2,1)S(1)}) custom-call(bf16[1024,512]{1,0:T(8,128)(2,1)S(1)} %get-tuple-element.81.refs_0_, bf16[768,512]{1,0:T(8,128)(2,1)S(1)} %collective-permute-done.14.refs_1_, ...), custom_call_target="tpu_custom_call" | custom-call | flops 1000 | bytes 1000 | tf_op jit(solution)/shard_map/product_near/pallas_call | solution.py:254
  79.3 0.1 collective-permute-start.24
  79.4 5.1 %collective-permute-done.22.refs_6_ = bf16[80,512]{1,0:T(8,128)(2,1)S(1)} collective-permute-done((bf16[80,512]{1,0:T(8,128)(2,1)S(1)}, bf16[80,512]{1,0:T(8,128)(2,1)S(1)}, u32[]{:S(2)}, u32[]{:S(2)}) %collective-permute-start.22) | collective-permute-done | bytes 81952 | tf_op jit(solution)/shard_map/ppermute | solution.py:603
  84.5 3.0 %collective-permute-start.25 = (bf16[256,1024]{1,0:T(8,128)(2,1)S(1)}, bf16[256,1024]{1,0:T(8,128)(2,1)S(1)}, u32[]{:S(2)}, u32[]{:S(2)}) collective-permute-start(bf16[256,1024]{1,0:T(8,128)(2,1)S(1)} %get-tuple-element.93), channel_id=1, source_target_pairs={{0,12},{1,13},{2,14},{3,15},{4,0},{5,1},{6,2},{7,3},{8,4},{9,5},{1... | collective-permute-start | bytes 1572872 | tf_op jit(solution)/shard_map/ppermute | solution.py:607
  87.5 0.4 collective-permute-done.17.from_down
  87.9 0.2 relay_sums.1
  88.1 0.1 collective-permute-start.23
  88.2 3.2 %collective-permute-start.26 = (bf16[256,1024]{1,0:T(8,128)(2,1)S(1)}, bf16[256,1024]{1,0:T(8,128)(2,1)S(1)}, u32[]{:S(2)}, u32[]{:S(2)}) collective-permute-start(bf16[256,1024]{1,0:T(8,128)(2,1)S(1)} %get-tuple-element.94), channel_id=1, source_target_pairs={{0,12},{1,13},{2,14},{3,15},{4,0},{5,1},{6,2},{7,3},{8,4},{9,5},{1... | collective-permute-start | bytes 1572872 | tf_op jit(solution)/shard_map/ppermute | solution.py:614
  91.4 1.5 %collective-permute-start.7 = (bf16[336,512]{1,0:T(8,128)(2,1)S(1)}, bf16[336,512]{1,0:T(8,128)(2,1)S(1)}, u32[]{:S(2)}, u32[]{:S(2)}) collective-permute-start(bf16[336,512]{1,0:T(8,128)(2,1)S(1)} %get-tuple-element.57), channel_id=1, source_target_pairs={{0,3},{1,0},{2,1},{3,2},{4,7},{5,4},{6,5},{7,6},{8,11},{9,8},{10,9... | collective-permute-start | bytes 1032200 | tf_op jit(solution)/shard_map/ppermute | solution.py:618
  93.6 5.1 %collective-permute-done.7.refs_5_.refs_2_ = bf16[336,512]{1,0:T(8,128)(2,1)S(1)} collective-permute-done((bf16[336,512]{1,0:T(8,128)(2,1)S(1)}, bf16[336,512]{1,0:T(8,128)(2,1)S(1)}, u32[]{:S(2)}, u32[]{:S(2)}) %collective-permute-start.7) | collective-permute-done | bytes 344096 | tf_op jit(solution)/shard_map/ppermute | solution.py:618
  98.7 0.8 unpack.1
  99.5 4.3 %pool_attention.1.pool = f32[16,72,128]{2,1,0:T(8,128)S(1)} custom-call(s32[16]{0:T(128)S(1)} %get-tuple-element.78.slots, s32[16]{0:T(128)S(1)} %get-tuple-element.79.alive, bf16[16,64,128]{2,1,0:T(8,128)(2,1)S(1)} %get-tuple-element.80.query, bf16[16,128,2048]{2,1,0:T(8,128)(2,1)S(1)} %bitcast.11, bf16[16,128,2048]{2,1,0:T(8,128)(2,1)S(1)} %bitcast.12, ...), custom_call_target="tpu_custom_call" | custom-call | flops 1000 | bytes 1000 | tf_op jit(solution)/shard_map/pool_attention/pallas_call | solution.py:344
  103.8 2.3 %product_own.1 = (f32[256,1024]{1,0:T(8,128)S(1)}, f32[256,1024]{1,0:T(8,128)S(1)}) custom-call(bf16[1024,512]{1,0:T(8,128)(2,1)S(1)} %get-tuple-element.81.refs_0_, bf16[336,512]{1,0:T(8,128)(2,1)S(1)} %collective-permute-done.6.refs_4_.refs_1_, bf16[336,512]{1,0:T(8,128)(2,1)S(1)} %collective-permute-done.7.refs_5_.refs_2_, ...), custom_call_target="tpu_custom_call" | custom-call | flops 1000 | bytes 1000 | tf_op jit(solution)/shard_map/product_own/pallas_call | solution.py:254
  106.2 3.0 %collective-permute-done.23.up_l = bf16[256,1024]{1,0:T(8,128)(2,1)S(1)} collective-permute-done((bf16[256,1024]{1,0:T(8,128)(2,1)S(1)}, bf16[256,1024]{1,0:T(8,128)(2,1)S(1)}, u32[]{:S(2)}, u32[]{:S(2)}) %collective-permute-start.23) | collective-permute-done | bytes 524320 | tf_op jit(solution)/shard_map/ppermute | solution.py:611
  109.2 2.9 %prefix_attention.1 = (bf16[1,256,2048]{2,1,0:T(8,128)(2,1)}, bf16[16,80,128]{2,1,0:T(8,128)(2,1)S(1)}) custom-call(s32[1]{0:T(128)S(6)} %copy.12.prompt_pages, f32[256,1024]{1,0:T(8,128)S(1)} %get-tuple-element.85.own_l, f32[256,1024]{1,0:T(8,128)S(1)} %get-tuple-element.86.own_r, bf16[256,1024]{1,0:T(8,128)(2,1)S(1)} %collective-permute-done.23.up_l, ...), custom_call_target="tpu_custom_call" | custom-call | flops 300000000 | bytes 6291456 | tf_op jit(solution)/shard_map/prefix_attention/pallas_call | solution.py:506
  112.1 13.8 %all_to_all.5.arrived = bf16[16,80,128]{2,1,0:T(8,128)(2,1)S(1)} all-to-all(bf16[16,80,128]{2,1,0:T(8,128)(2,1)S(1)} %get-tuple-element.98), channel_id=1, replica_groups=mesh['prompt'=8,'sample'=16] {'sample'}, dimensions={0} | all-to-all | bytes 655360 | tf_op jit(solution)/shard_map/all_to_all | solution.py:625
  125.9 1.0 combine.1
  (21 shorter events, 0.0 us)
Async XLA Ops:
  0.6 32.7 %copy-start = (bf16[1,4096,512]{2,1,0:T(8,128)(2,1)S(1)}, bf16[1,4096,512]{2,1,0:T(8,128)(2,1)}, u32[]{:S(2)}) copy-start(bf16[1,4096,512]{2,1,0:T(8,128)(2,1)} %param.10) | copy-start | bytes 12582916
  0.6 8.1 %copy-start.4 = (s32[1,1,16]{2,1,0:T(1,128)S(1)}, s32[1,1,16]{2,1,0:T(1,128)}, u32[]{:S(2)}) copy-start(s32[1,1,16]{2,1,0:T(1,128)} %where.1) | copy-start | bytes 196
  0.6 9.4 %collective-permute-start = (bf16[512,256]{1,0:T(8,128)(2,1)}, bf16[512,256]{1,0:T(8,128)(2,1)S(1)}, u32[]{:S(2)}, u32[]{:S(2)}) collective-permute-start(bf16[512,256]{1,0:T(8,128)(2,1)} %param.11), channel_id=1, source_target_pairs={{0,1},{1,2},{2,3},{3,0},{4,5},{5,6},{6,7},{7,4},{8,9},{9,10},{10,1... | collective-permute-start | bytes 786440 | tf_op jit(solution)/shard_map/ppermute | solution.py:565
  2.3 9.4 %collective-permute-start.1 = (bf16[512,256]{1,0:T(8,128)(2,1)}, bf16[512,256]{1,0:T(8,128)(2,1)S(1)}, u32[]{:S(2)}, u32[]{:S(2)}) collective-permute-start(bf16[512,256]{1,0:T(8,128)(2,1)} %param.11), channel_id=1, source_target_pairs={{0,3},{1,0},{2,1},{3,2},{4,7},{5,4},{6,5},{7,6},{8,11},{9,8},{10,9... | collective-permute-start | bytes 786440 | tf_op jit(solution)/shard_map/ppermute | solution.py:566
  4.0 12.9 %collective-permute-start.2 = (bf16[512,256]{1,0:T(8,128)(2,1)}, bf16[512,256]{1,0:T(8,128)(2,1)S(1)}, u32[]{:S(2)}, u32[]{:S(2)}) collective-permute-start(bf16[512,256]{1,0:T(8,128)(2,1)} %param.11), channel_id=1, source_target_pairs={{0,2},{1,3},{2,0},{3,1},{4,6},{5,7},{6,4},{7,5},{8,10},{9,11},{10,... | collective-permute-start | bytes 786440 | tf_op jit(solution)/shard_map/ppermute | solution.py:564
  8.7 0.8 copy-start.2
  9.5 26.2 %copy-start.3 = (bf16[1,1,2048]{2,1,0:T(2,128)(2,1)S(1)}, bf16[1,1,2048]{2,1,0:T(2,128)(2,1)}, u32[]{:S(2)}) copy-start(bf16[1,1,2048]{2,1,0:T(2,128)(2,1)} %param.13) | copy-start | bytes 12292
  18.0 2.7 %collective-permute-start.9 = (bf16[4,512,256]{2,1,0:T(8,128)(2,1)S(1)}, bf16[4,512,256]{2,1,0:T(8,128)(2,1)S(1)}, u32[]{:S(2)}, u32[]{:S(2)}) collective-permute-start(bf16[4,512,256]{2,1,0:T(8,128)(2,1)S(1)} %pad_maximum_fusion.refs_4_), channel_id=1, source_target_pairs={{0,16},{16,0},{32,48},{48,32},{64,80},{80,64},{96,112},{112,96},{1... | collective-permute-start | bytes 3145736 | tf_op jit(solution)/shard_map/ppermute | solution.py:581
  18.0 27.9 %collective-permute-start.11 = (bf16[1040,512]{1,0:T(8,128)(2,1)S(1)}, bf16[1040,512]{1,0:T(8,128)(2,1)S(1)}, u32[]{:S(2)}, u32[]{:S(2)}) collective-permute-start(bf16[1040,512]{1,0:T(8,128)(2,1)S(1)} %get-tuple-element.62), channel_id=1, source_target_pairs={{0,2},{1,3},{2,0},{3,1},{4,6},{5,7},{6,4},{7,5},{8,10},{9,11},{10,... | collective-permute-start | bytes 3194888 | tf_op jit(solution)/shard_map/ppermute | solution.py:575
  19.0 21.7 %collective-permute-start.8 = (bf16[4,512,256]{2,1,0:T(8,128)(2,1)S(1)}, bf16[4,512,256]{2,1,0:T(8,128)(2,1)S(1)}, u32[]{:S(2)}, u32[]{:S(2)}) collective-permute-start(bf16[4,512,256]{2,1,0:T(8,128)(2,1)S(1)} %pad_maximum_fusion.refs_4_), channel_id=1, source_target_pairs={{0,32},{16,112},{32,64},{48,16},{64,96},{80,48},{96,0},{112,80},{1... | collective-permute-start | bytes 3145736 | tf_op jit(solution)/shard_map/ppermute | solution.py:580
  20.7 25.5 %collective-permute-start.10 = (bf16[4,512,256]{2,1,0:T(8,128)(2,1)S(1)}, bf16[4,512,256]{2,1,0:T(8,128)(2,1)S(1)}, u32[]{:S(2)}, u32[]{:S(2)}) collective-permute-start(bf16[4,512,256]{2,1,0:T(8,128)(2,1)S(1)} %collective-permute-done.9.refs_5_), channel_id=1, source_target_pairs={{0,32},{16,112},{32,64},{48,16},{64,96},{80,48},{96,0},{112,80},{1... | collective-permute-start | bytes 3145736 | tf_op jit(solution)/shard_map/ppermute | solution.py:582
  22.3 5.8 %collective-permute-start.3 = (bf16[40,256]{1,0:T(8,128)(2,1)S(1)}, bf16[40,256]{1,0:T(8,128)(2,1)S(1)}, u32[]{:S(2)}, u32[]{:S(2)}) collective-permute-start(bf16[40,256]{1,0:T(8,128)(2,1)S(1)} %get-tuple-element.55.refs_0_), channel_id=1, source_target_pairs={{0,4},{1,5},{2,6},{3,7},{4,8},{5,9},{6,10},{7,11},{8,12},{9,13},{1... | collective-permute-start | bytes 61448 | tf_op jit(solution)/shard_map/ppermute | solution.py:573
  24.2 5.7 %collective-permute-start.4 = (bf16[40,256]{1,0:T(8,128)(2,1)S(1)}, bf16[40,256]{1,0:T(8,128)(2,1)S(1)}, u32[]{:S(2)}, u32[]{:S(2)}) collective-permute-start(bf16[40,256]{1,0:T(8,128)(2,1)S(1)} %get-tuple-element.55.refs_0_), channel_id=1, source_target_pairs={{0,12},{1,13},{2,14},{3,15},{4,0},{5,1},{6,2},{7,3},{8,4},{9,5},{1... | collective-permute-start | bytes 61448 | tf_op jit(solution)/shard_map/ppermute | solution.py:573
  28.1 5.3 %collective-permute-start.5 = (bf16[40,256]{1,0:T(8,128)(2,1)S(1)}, bf16[40,256]{1,0:T(8,128)(2,1)S(1)}, u32[]{:S(2)}, u32[]{:S(2)}) collective-permute-start(bf16[40,256]{1,0:T(8,128)(2,1)S(1)} %get-tuple-element.55.refs_0_), channel_id=1, source_target_pairs={{0,8},{1,9},{2,10},{3,11},{4,12},{5,13},{6,14},{7,15},{8,0},{9,1},... | collective-permute-start | bytes 61448 | tf_op jit(solution)/shard_map/ppermute | solution.py:573
  33.6 28.7 %collective-permute-start.14 = (bf16[768,512]{1,0:T(8,128)(2,1)S(1)}, bf16[768,512]{1,0:T(8,128)(2,1)S(1)}, u32[]{:S(2)}, u32[]{:S(2)}) collective-permute-start(bf16[768,512]{1,0:T(8,128)(2,1)S(1)} %get-tuple-element.66), channel_id=1, source_target_pairs={{0,1},{1,2},{2,3},{3,0},{4,5},{5,6},{6,7},{7,4},{8,9},{9,10},{10,1... | collective-permute-start | bytes 2359304 | tf_op jit(solution)/shard_map/ppermute | solution.py:576
  35.7 3.4 %copy-start.1 = (bf16[1,1,16,128,2048]{4,3,2,1,0:T(8,128)(2,1)S(1)}, bf16[1,1,16,128,2048]{4,3,2,1,0:T(8,128)(2,1)}, u32[]{:S(2)}) copy-start(bf16[1,1,16,128,2048]{4,3,2,1,0:T(8,128)(2,1)} %param.14) | copy-start | bytes 25165828
  39.3 23.1 %collective-permute-start.15 = (bf16[768,512]{1,0:T(8,128)(2,1)S(1)}, bf16[768,512]{1,0:T(8,128)(2,1)S(1)}, u32[]{:S(2)}, u32[]{:S(2)}) collective-permute-start(bf16[768,512]{1,0:T(8,128)(2,1)S(1)} %get-tuple-element.67), channel_id=1, source_target_pairs={{0,3},{1,0},{2,1},{3,2},{4,7},{5,4},{6,5},{7,6},{8,11},{9,8},{10,9... | collective-permute-start | bytes 2359304 | tf_op jit(solution)/shard_map/ppermute | solution.py:577
  46.3 16.1 %collective-permute-start.12 = (bf16[2,512,256]{2,1,0:T(8,128)(2,1)S(1)}, bf16[2,512,256]{2,1,0:T(8,128)(2,1)S(1)}, u32[]{:S(2)}, u32[]{:S(2)}) collective-permute-start(bf16[2,512,256]{2,1,0:T(8,128)(2,1)S(1)} %get-tuple-element.101), channel_id=1, source_target_pairs={{0,32},{16,112},{32,64},{48,16},{64,96},{80,48},{96,0},{112,80},{1... | collective-permute-start | bytes 1572872 | tf_op jit(solution)/shard_map/ppermute | solution.py:586
  47.7 14.6 %collective-permute-start.13 = (bf16[2,512,256]{2,1,0:T(8,128)(2,1)S(1)}, bf16[2,512,256]{2,1,0:T(8,128)(2,1)S(1)}, u32[]{:S(2)}, u32[]{:S(2)}) collective-permute-start(bf16[2,512,256]{2,1,0:T(8,128)(2,1)S(1)} %get-tuple-element.100), channel_id=1, source_target_pairs={{0,32},{16,112},{32,64},{48,16},{64,96},{80,48},{96,0},{112,80},{1... | collective-permute-start | bytes 1572872 | tf_op jit(solution)/shard_map/ppermute | solution.py:586
  49.3 17.2 %collective-permute-start.18 = (bf16[4,512,256]{2,1,0:T(8,128)(2,1)S(1)}, bf16[4,512,256]{2,1,0:T(8,128)(2,1)S(1)}, u32[]{:S(2)}, u32[]{:S(2)}) collective-permute-start(bf16[4,512,256]{2,1,0:T(8,128)(2,1)S(1)} %collective-permute-done.8.refs_6_), channel_id=1, source_target_pairs={{0,16},{16,0},{32,48},{48,32},{64,80},{80,64},{96,112},{112,96},{1... | collective-permute-start | bytes 3145736 | tf_op jit(solution)/shard_map/ppermute | solution.py:587
  62.3 4.2 %collective-permute-start.19 = (bf16[4,512,256]{2,1,0:T(8,128)(2,1)S(1)}, bf16[4,512,256]{2,1,0:T(8,128)(2,1)S(1)}, u32[]{:S(2)}, u32[]{:S(2)}) collective-permute-start(bf16[4,512,256]{2,1,0:T(8,128)(2,1)S(1)} %collective-permute-done.10.refs_7_), channel_id=1, source_target_pairs={{0,16},{16,0},{32,48},{48,32},{64,80},{80,64},{96,112},{112,96},{1... | collective-permute-start | bytes 3145736 | tf_op jit(solution)/shard_map/ppermute | solution.py:588
  62.4 3.4 %collective-permute-start.16 = (bf16[2,512,256]{2,1,0:T(8,128)(2,1)S(1)}, bf16[2,512,256]{2,1,0:T(8,128)(2,1)S(1)}, u32[]{:S(2)}, u32[]{:S(2)}) collective-permute-start(bf16[2,512,256]{2,1,0:T(8,128)(2,1)S(1)} %collective-permute-done.12.refs_6_.refs_10_), channel_id=1, source_target_pairs={{0,16},{16,0},{32,48},{48,32},{64,80},{80,64},{96,112},{112,96},{1... | collective-permute-start | bytes 1572872 | tf_op jit(solution)/shard_map/ppermute | solution.py:590
  62.9 3.6 %collective-permute-start.20 = (bf16[2,512,256]{2,1,0:T(8,128)(2,1)S(1)}, bf16[2,512,256]{2,1,0:T(8,128)(2,1)S(1)}, u32[]{:S(2)}, u32[]{:S(2)}) collective-permute-start(bf16[2,512,256]{2,1,0:T(8,128)(2,1)S(1)} %collective-permute-done.13.refs_7_.refs_11_), channel_id=1, source_target_pairs={{0,16},{16,0},{32,48},{48,32},{64,80},{80,64},{96,112},{112,96},{1... | collective-permute-start | bytes 1572872 | tf_op jit(solution)/shard_map/ppermute | solution.py:590
  66.5 33.0 %slice-start = ((s8[8388608]{0:T(1024)(128)(4,1)}), s8[4194304]{0:T(1024)(128)(4,1)S(1)}, s32[]{:S(2)}) async-start(s8[8388608]{0:T(1024)(128)(4,1)} %bitcast.9), calls=%async_computation.1 | async-start | bytes 8388608
  67.8 19.7 %collective-permute-start.21 = (bf16[256,1024]{1,0:T(8,128)(2,1)S(1)}, bf16[256,1024]{1,0:T(8,128)(2,1)S(1)}, u32[]{:S(2)}, u32[]{:S(2)}) collective-permute-start(bf16[256,1024]{1,0:T(8,128)(2,1)S(1)} %product_far_r.1), channel_id=1, source_target_pairs={{0,12},{1,13},{2,14},{3,15},{4,0},{5,1},{6,2},{7,3},{8,4},{9,5},{1... | collective-permute-start | bytes 1572872 | tf_op jit(solution)/shard_map/ppermute | solution.py:601
  71.9 16.0 %collective-permute-start.17 = (bf16[256,1024]{1,0:T(8,128)(2,1)S(1)}, bf16[256,1024]{1,0:T(8,128)(2,1)S(1)}, u32[]{:S(2)}, u32[]{:S(2)}) collective-permute-start(bf16[256,1024]{1,0:T(8,128)(2,1)S(1)} %product_far_l.1), channel_id=1, source_target_pairs={{0,4},{1,5},{2,6},{3,7},{4,8},{5,9},{6,10},{7,11},{8,12},{9,13},{1... | collective-permute-start | bytes 1572872 | tf_op jit(solution)/shard_map/ppermute | solution.py:600
  71.9 19.6 %collective-permute-start.6 = (bf16[336,512]{1,0:T(8,128)(2,1)S(1)}, bf16[336,512]{1,0:T(8,128)(2,1)S(1)}, u32[]{:S(2)}, u32[]{:S(2)}) collective-permute-start(bf16[336,512]{1,0:T(8,128)(2,1)S(1)} %get-tuple-element.56), channel_id=1, source_target_pairs={{0,1},{1,2},{2,3},{3,0},{4,5},{5,6},{6,7},{7,4},{8,9},{9,10},{10,1... | collective-permute-start | bytes 1032200 | tf_op jit(solution)/shard_map/ppermute | solution.py:617
  72.4 27.1 %slice-start.1 = ((s8[8388608]{0:T(1024)(128)(4,1)}), s8[4194304]{0:T(1024)(128)(4,1)S(1)}, s32[]{:S(2)}) async-start(s8[8388608]{0:T(1024)(128)(4,1)} %bitcast.9), calls=%async_computation.2 | async-start | bytes 8388608
  72.4 12.1 %collective-permute-start.22 = (bf16[80,512]{1,0:T(8,128)(2,1)S(1)}, bf16[80,512]{1,0:T(8,128)(2,1)S(1)}, u32[]{:S(2)}, u32[]{:S(2)}) collective-permute-start(bf16[80,512]{1,0:T(8,128)(2,1)S(1)} %get-tuple-element.76), channel_id=1, source_target_pairs={{0,2},{1,3},{2,0},{3,1},{4,6},{5,7},{6,4},{7,5},{8,10},{9,11},{10,... | collective-permute-start | bytes 245768 | tf_op jit(solution)/shard_map/ppermute | solution.py:603
  79.3 26.8 %collective-permute-start.24 = (bf16[256,1024]{1,0:T(8,128)(2,1)S(1)}, bf16[256,1024]{1,0:T(8,128)(2,1)S(1)}, u32[]{:S(2)}, u32[]{:S(2)}) collective-permute-start(bf16[256,1024]{1,0:T(8,128)(2,1)S(1)} %get-tuple-element.92), channel_id=1, source_target_pairs={{0,4},{1,5},{2,6},{3,7},{4,8},{5,9},{6,10},{7,11},{8,12},{9,13},{1... | collective-permute-start | bytes 1572872 | tf_op jit(solution)/shard_map/ppermute | solution.py:607
  84.5 21.7 %collective-permute-start.25 = (bf16[256,1024]{1,0:T(8,128)(2,1)S(1)}, bf16[256,1024]{1,0:T(8,128)(2,1)S(1)}, u32[]{:S(2)}, u32[]{:S(2)}) collective-permute-start(bf16[256,1024]{1,0:T(8,128)(2,1)S(1)} %get-tuple-element.93), channel_id=1, source_target_pairs={{0,12},{1,13},{2,14},{3,15},{4,0},{5,1},{6,2},{7,3},{8,4},{9,5},{1... | collective-permute-start | bytes 1572872 | tf_op jit(solution)/shard_map/ppermute | solution.py:607
  88.1 21.1 %collective-permute-start.23 = (bf16[256,1024]{1,0:T(8,128)(2,1)S(1)}, bf16[256,1024]{1,0:T(8,128)(2,1)S(1)}, u32[]{:S(2)}, u32[]{:S(2)}) collective-permute-start(bf16[256,1024]{1,0:T(8,128)(2,1)S(1)} %get-tuple-element.91), channel_id=1, source_target_pairs={{0,4},{1,5},{2,6},{3,7},{4,8},{5,9},{6,10},{7,11},{8,12},{9,13},{1... | collective-permute-start | bytes 1572872 | tf_op jit(solution)/shard_map/ppermute | solution.py:611
  88.2 21.0 %collective-permute-start.26 = (bf16[256,1024]{1,0:T(8,128)(2,1)S(1)}, bf16[256,1024]{1,0:T(8,128)(2,1)S(1)}, u32[]{:S(2)}, u32[]{:S(2)}) collective-permute-start(bf16[256,1024]{1,0:T(8,128)(2,1)S(1)} %get-tuple-element.94), channel_id=1, source_target_pairs={{0,12},{1,13},{2,14},{3,15},{4,0},{5,1},{6,2},{7,3},{8,4},{9,5},{1... | collective-permute-start | bytes 1572872 | tf_op jit(solution)/shard_map/ppermute | solution.py:614
  91.4 7.3 %collective-permute-start.7 = (bf16[336,512]{1,0:T(8,128)(2,1)S(1)}, bf16[336,512]{1,0:T(8,128)(2,1)S(1)}, u32[]{:S(2)}, u32[]{:S(2)}) collective-permute-start(bf16[336,512]{1,0:T(8,128)(2,1)S(1)} %get-tuple-element.57), channel_id=1, source_target_pairs={{0,3},{1,0},{2,1},{3,2},{4,7},{5,4},{6,5},{7,6},{8,11},{9,8},{10,9... | collective-permute-start | bytes 1032200 | tf_op jit(solution)/shard_map/ppermute | solution.py:618

commit v12 on v11

--- a/solution.py
+++ b/solution.py
@@ -601,11 +601,13 @@
     from_up = lax.ppermute(far_r, "sample", Z_DOWN)
     far_blocks, rows_right = tie((far_blocks, rows_right))
     far_blocks = lax.ppermute(far_blocks, "sample", X_FAR)
+    others[1], last_right, last_left, far_blocks = tie(
+        (others[1], last_right, last_left, far_blocks)
+    )
     up_l, up_r, down_l, down_r = product(
         others, pieces, ((1,) * 4, (2,) * 4), BF16, "product_near"
     )
     up_r, down_l = lax.ppermute(up_r, "sample", Z_UP), lax.ppermute(down_l, "sample", Z_DOWN)
-    from_down, from_up, far_blocks = tie((from_down, from_up, far_blocks))
     up_l, down_r = relay(up_l, down_r, from_down, from_up)
     sums = [
         lax.ppermute(up_l, "sample", Z_UP),

time: 127 us -> 127 us (level)
  starting transfers between devices: 37.2 us -> 34.2 us
  waiting for transfers between devices: 46.6 us -> 49.6 us
    ppermute x3, starting transfers between devices: 5.9 us -> 4.22 us  [per_device(): lax.ppermute(block, 'sample', to)]
    ppermute x3, waiting for transfers between devices: 5.18 us -> 6.57 us  [per_device(): lax.ppermute(block, 'sample', to)]
  transfers between devices with their start and end apart: 27 -> 27, of which waited for: 14 -> 15; matrix products, arithmetic and copies ran while one was open for 0% -> 0% of each run, Pallas kernels for 13% -> 13%
where the time goes in v12:
time: 127 us
  waiting for transfers between devices  49.6 us (39%)
  starting transfers between devices  34.2 us (27%)
  Pallas kernels  21.1 us (17%)
  blocking collectives  13.8 us (11%)
  local copies, waits for them, and re-layouts  4.22 us (3%)
  between operations  2.8 us (2%)
    all_to_all x1, blocking collectives, per_device(): lax.all_to_all(packed, 'sample', split_axis=0, concat_axis=0, tiled=True)  13.8 us
    ppermute x1, waiting for transfers between devices, per_device(): rows_right = lax.ppermute(to_right, 'sample', X_RIGHT)  13 us
    pallas_call x2, Pallas kernels, product(): pl.pallas_call(functools.partial(product_kernel, blocks), out_shape=outs,...  6.81 us
    ppermute x3, waiting for transfers between devices, per_device(): lax.ppermute(block, 'sample', to)  6.57 us
    ppermute x1, waiting for transfers between devices, per_device(): rows_far = lax.ppermute(to_far, 'sample', X_FAR)  5.65 us
    ppermute x1, waiting for transfers between devices, per_device(): last_left = lax.ppermute(last_left, 'sample', X_LEFT)  5.55 us
    ppermute x1, waiting for transfers between devices, per_device(): weight_far = lax.ppermute(kv_weight, 'sample', X_FAR)  5.14 us
    ppermute x1, waiting for transfers between devices, per_device(): far_blocks = lax.ppermute(far_blocks, 'sample', X_FAR)  4.72 us
  transfers between devices with their start and end apart: 27, of which 15 were waited for; matrix products, arithmetic and copies ran while one was open for 0% of the time, Pallas kernels for 13%

profile of v12, /device:TPU:0, one launch (start us, length us, event | category | flops | bytes accessed | tf_op | source)
XLA Modules:
  0.0 126.9 jit_solution(4905005946207144681)
XLA Ops:
  0.6 1.6 %collective-permute-start = (bf16[512,256]{1,0:T(8,128)(2,1)}, bf16[512,256]{1,0:T(8,128)(2,1)S(1)}, u32[]{:S(2)}, u32[]{:S(2)}) collective-permute-start(bf16[512,256]{1,0:T(8,128)(2,1)} %param.11), channel_id=1, source_target_pairs={{0,1},{1,2},{2,3},{3,0},{4,5},{5,6},{6,7},{7,4},{8,9},{9,10},{10,1... | collective-permute-start | bytes 786440 | tf_op jit(solution)/shard_map/ppermute | solution.py:565
  2.3 1.7 %collective-permute-start.1 = (bf16[512,256]{1,0:T(8,128)(2,1)}, bf16[512,256]{1,0:T(8,128)(2,1)S(1)}, u32[]{:S(2)}, u32[]{:S(2)}) collective-permute-start(bf16[512,256]{1,0:T(8,128)(2,1)} %param.11), channel_id=1, source_target_pairs={{0,3},{1,0},{2,1},{3,2},{4,7},{5,4},{6,5},{7,6},{8,11},{9,8},{10,9... | collective-permute-start | bytes 786440 | tf_op jit(solution)/shard_map/ppermute | solution.py:566
  4.0 1.9 %collective-permute-start.2 = (bf16[512,256]{1,0:T(8,128)(2,1)}, bf16[512,256]{1,0:T(8,128)(2,1)S(1)}, u32[]{:S(2)}, u32[]{:S(2)}) collective-permute-start(bf16[512,256]{1,0:T(8,128)(2,1)} %param.11), channel_id=1, source_target_pairs={{0,2},{1,3},{2,0},{3,1},{4,6},{5,7},{6,4},{7,5},{8,10},{9,11},{10,... | collective-permute-start | bytes 786440 | tf_op jit(solution)/shard_map/ppermute | solution.py:564
  5.9 1.6 %pick_far.1 = (bf16[1024,512]{1,0:T(8,128)(2,1)S(1)}, bf16[1040,512]{1,0:T(8,128)(2,1)S(1)}) custom-call(bf16[4,4,256,512]{3,2,1,0:T(8,128)(2,1)} %bitcast.15), custom_call_target="tpu_custom_call" | custom-call | flops 1000 | bytes 1000 | tf_op jit(solution)/shard_map/pick_far/pallas_call | solution.py:183
  8.7 0.0 copy-start.2
  8.7 0.7 copy-done.2
  9.5 0.6 prepare.1
  10.1 1.6 %collective-permute-done.1 = bf16[512,256]{1,0:T(8,128)(2,1)S(1)} collective-permute-done((bf16[512,256]{1,0:T(8,128)(2,1)}, bf16[512,256]{1,0:T(8,128)(2,1)S(1)}, u32[]{:S(2)}, u32[]{:S(2)}) %collective-permute-start.1) | collective-permute-done | bytes 262176 | tf_op jit(solution)/shard_map/ppermute | solution.py:566
  11.7 5.1 %collective-permute-done.2 = bf16[512,256]{1,0:T(8,128)(2,1)S(1)} collective-permute-done((bf16[512,256]{1,0:T(8,128)(2,1)}, bf16[512,256]{1,0:T(8,128)(2,1)S(1)}, u32[]{:S(2)}, u32[]{:S(2)}) %collective-permute-start.2) | collective-permute-done | bytes 262176 | tf_op jit(solution)/shard_map/ppermute | solution.py:564
  16.9 1.1 pad_maximum_fusion.refs_4_
  18.0 0.1 collective-permute-start.4
  18.0 0.9 collective-permute-start.6
  19.0 1.6 %collective-permute-start.3 = (bf16[4,512,256]{2,1,0:T(8,128)(2,1)S(1)}, bf16[4,512,256]{2,1,0:T(8,128)(2,1)S(1)}, u32[]{:S(2)}, u32[]{:S(2)}) collective-permute-start(bf16[4,512,256]{2,1,0:T(8,128)(2,1)S(1)} %pad_maximum_fusion.refs_4_), channel_id=1, source_target_pairs={{0,32},{16,112},{32,64},{48,16},{64,96},{80,48},{96,0},{112,80},{1... | collective-permute-start | bytes 3145736 | tf_op jit(solution)/shard_map/ppermute | solution.py:580
  20.5 0.2 collective-permute-done.4.refs_5_
  20.7 1.6 %collective-permute-start.5 = (bf16[4,512,256]{2,1,0:T(8,128)(2,1)S(1)}, bf16[4,512,256]{2,1,0:T(8,128)(2,1)S(1)}, u32[]{:S(2)}, u32[]{:S(2)}) collective-permute-start(bf16[4,512,256]{2,1,0:T(8,128)(2,1)S(1)} %collective-permute-done.4.refs_5_), channel_id=1, source_target_pairs={{0,32},{16,112},{32,64},{48,16},{64,96},{80,48},{96,0},{112,80},{1... | collective-permute-start | bytes 3145736 | tf_op jit(solution)/shard_map/ppermute | solution.py:582
  22.3 4.0 %collective-permute-start.10 = (bf16[40,256]{1,0:T(8,128)(2,1)S(1)}, bf16[40,256]{1,0:T(8,128)(2,1)S(1)}, u32[]{:S(2)}, u32[]{:S(2)}) collective-permute-start(bf16[40,256]{1,0:T(8,128)(2,1)S(1)} %get-tuple-element.63.refs_0_), channel_id=1, source_target_pairs={{0,12},{1,13},{2,14},{3,15},{4,0},{5,1},{6,2},{7,3},{8,4},{9,5},{1... | collective-permute-start | bytes 61448 | tf_op jit(solution)/shard_map/ppermute | solution.py:573
  26.3 1.5 %collective-permute-done.10.refs_2_ = bf16[40,256]{1,0:T(8,128)(2,1)S(1)} collective-permute-done((bf16[40,256]{1,0:T(8,128)(2,1)S(1)}, bf16[40,256]{1,0:T(8,128)(2,1)S(1)}, u32[]{:S(2)}, u32[]{:S(2)}) %collective-permute-start.10) | collective-permute-done | bytes 20512 | tf_op jit(solution)/shard_map/ppermute | solution.py:573
  27.8 0.2 collective-permute-start.9
  28.0 3.8 %collective-permute-done.11.refs_3_ = bf16[40,256]{1,0:T(8,128)(2,1)S(1)} collective-permute-done((bf16[40,256]{1,0:T(8,128)(2,1)S(1)}, bf16[40,256]{1,0:T(8,128)(2,1)S(1)}, u32[]{:S(2)}, u32[]{:S(2)}) %collective-permute-start.11) | collective-permute-done | bytes 20512 | tf_op jit(solution)/shard_map/ppermute | solution.py:573
  31.8 1.3 %collective-permute-done.9.refs_1_ = bf16[40,256]{1,0:T(8,128)(2,1)S(1)} collective-permute-done((bf16[40,256]{1,0:T(8,128)(2,1)S(1)}, bf16[40,256]{1,0:T(8,128)(2,1)S(1)}, u32[]{:S(2)}, u32[]{:S(2)}) %collective-permute-start.9) | collective-permute-done | bytes 20512 | tf_op jit(solution)/shard_map/ppermute | solution.py:573
  33.1 0.3 pick_near.1
  33.3 2.1 %collective-permute-start.12 = (bf16[768,512]{1,0:T(8,128)(2,1)S(1)}, bf16[768,512]{1,0:T(8,128)(2,1)S(1)}, u32[]{:S(2)}, u32[]{:S(2)}) collective-permute-start(bf16[768,512]{1,0:T(8,128)(2,1)S(1)} %get-tuple-element.64), channel_id=1, source_target_pairs={{0,1},{1,2},{2,3},{3,0},{4,5},{5,6},{6,7},{7,4},{8,9},{9,10},{10,1... | collective-permute-start | bytes 2359304 | tf_op jit(solution)/shard_map/ppermute | solution.py:576
  35.5 3.4 %copy-done.1 = bf16[1,1,16,128,2048]{4,3,2,1,0:T(8,128)(2,1)S(1)} copy-done((bf16[1,1,16,128,2048]{4,3,2,1,0:T(8,128)(2,1)S(1)}, bf16[1,1,16,128,2048]{4,3,2,1,0:T(8,128)(2,1)}, u32[]{:S(2)}) %copy-start.1) | copy-done | bytes 8388632
  38.9 0.2 local_attention.1.local
  39.1 1.2 collective-permute-start.13
  40.3 5.7 %collective-permute-done.6.refs_3_ = bf16[1040,512]{1,0:T(8,128)(2,1)S(1)} collective-permute-done((bf16[1040,512]{1,0:T(8,128)(2,1)S(1)}, bf16[1040,512]{1,0:T(8,128)(2,1)S(1)}, u32[]{:S(2)}, u32[]{:S(2)}) %collective-permute-start.6) | collective-permute-done | bytes 1064992 | tf_op jit(solution)/shard_map/ppermute | solution.py:575
  46.0 0.2 collective-permute-done.5.refs_7_
  46.2 0.1 fusion
  46.3 1.4 %collective-permute-start.7 = (bf16[2,512,256]{2,1,0:T(8,128)(2,1)S(1)}, bf16[2,512,256]{2,1,0:T(8,128)(2,1)S(1)}, u32[]{:S(2)}, u32[]{:S(2)}) collective-permute-start(bf16[2,512,256]{2,1,0:T(8,128)(2,1)S(1)} %get-tuple-element.103), channel_id=1, source_target_pairs={{0,32},{16,112},{32,64},{48,16},{64,96},{80,48},{96,0},{112,80},{1... | collective-permute-start | bytes 1572872 | tf_op jit(solution)/shard_map/ppermute | solution.py:586
  47.7 1.6 %collective-permute-start.8 = (bf16[2,512,256]{2,1,0:T(8,128)(2,1)S(1)}, bf16[2,512,256]{2,1,0:T(8,128)(2,1)S(1)}, u32[]{:S(2)}, u32[]{:S(2)}) collective-permute-start(bf16[2,512,256]{2,1,0:T(8,128)(2,1)S(1)} %get-tuple-element.102), channel_id=1, source_target_pairs={{0,32},{16,112},{32,64},{48,16},{64,96},{80,48},{96,0},{112,80},{1... | collective-permute-start | bytes 1572872 | tf_op jit(solution)/shard_map/ppermute | solution.py:586
  49.3 13.0 %collective-permute-done.12.refs_1_ = bf16[768,512]{1,0:T(8,128)(2,1)S(1)} collective-permute-done((bf16[768,512]{1,0:T(8,128)(2,1)S(1)}, bf16[768,512]{1,0:T(8,128)(2,1)S(1)}, u32[]{:S(2)}, u32[]{:S(2)}) %collective-permute-start.12) | collective-permute-done | bytes 786464 | tf_op jit(solution)/shard_map/ppermute | solution.py:576
  62.3 0.0 collective-permute-start.18
  62.4 0.0 collective-permute-done.13.refs_2_
  62.4 0.6 collective-permute-start.19
  62.9 0.1 collective-permute-start.20
  63.0 1.2 product_far_l.1
  64.3 1.5 %collective-permute-done.19.refs_12_.refs_8_ = bf16[2,512,256]{2,1,0:T(8,128)(2,1)S(1)} collective-permute-done((bf16[2,512,256]{2,1,0:T(8,128)(2,1)S(1)}, bf16[2,512,256]{2,1,0:T(8,128)(2,1)S(1)}, u32[]{:S(2)}, u32[]{:S(2)}) %collective-permute-start.19) | collective-permute-done | bytes 524320 | tf_op jit(solution)/shard_map/ppermute | solution.py:590
  65.7 0.7 collective-permute-done.20.refs_13_.refs_9_
  66.5 0.0 collective-permute-done.17.refs_8_.refs_4_
  66.5 0.0 collective-permute-done.18.refs_9_.refs_5_
  66.5 1.2 product_far_r.1
  67.8 4.1 %collective-permute-start.22 = (bf16[256,1024]{1,0:T(8,128)(2,1)S(1)}, bf16[256,1024]{1,0:T(8,128)(2,1)S(1)}, u32[]{:S(2)}, u32[]{:S(2)}) collective-permute-start(bf16[256,1024]{1,0:T(8,128)(2,1)S(1)} %product_far_r.1), channel_id=1, source_target_pairs={{0,12},{1,13},{2,14},{3,15},{4,0},{5,1},{6,2},{7,3},{8,4},{9,5},{1... | collective-permute-start | bytes 1572872 | tf_op jit(solution)/shard_map/ppermute | solution.py:601
  71.9 1.2 collective-permute-start.14
  73.1 4.7 %collective-permute-done.14.refs_6_ = bf16[80,512]{1,0:T(8,128)(2,1)S(1)} collective-permute-done((bf16[80,512]{1,0:T(8,128)(2,1)S(1)}, bf16[80,512]{1,0:T(8,128)(2,1)S(1)}, u32[]{:S(2)}, u32[]{:S(2)}) %collective-permute-start.14) | collective-permute-done | bytes 81952 | tf_op jit(solution)/shard_map/ppermute | solution.py:603
  77.8 0.5 collective-permute-start.15
  78.3 4.5 %product_near.1 = (bf16[256,1024]{1,0:T(8,128)(2,1)S(1)}, bf16[256,1024]{1,0:T(8,128)(2,1)S(1)}, bf16[256,1024]{1,0:T(8,128)(2,1)S(1)}, bf16[256,1024]{1,0:T(8,128)(2,1)S(1)}) custom-call(bf16[1024,512]{1,0:T(8,128)(2,1)S(1)} %get-tuple-element.78.refs_0_, bf16[768,512]{1,0:T(8,128)(2,1)S(1)} %collective-permute-done.12.refs_1_, ...), custom_call_target="tpu_custom_call" | custom-call | flops 1000 | bytes 1000 | tf_op jit(solution)/shard_map/product_near/pallas_call | solution.py:254
  82.8 0.1 collective-permute-start.24
  82.9 3.3 %collective-permute-start.25 = (bf16[256,1024]{1,0:T(8,128)(2,1)S(1)}, bf16[256,1024]{1,0:T(8,128)(2,1)S(1)}, u32[]{:S(2)}, u32[]{:S(2)}) collective-permute-start(bf16[256,1024]{1,0:T(8,128)(2,1)S(1)} %get-tuple-element.95), channel_id=1, source_target_pairs={{0,12},{1,13},{2,14},{3,15},{4,0},{5,1},{6,2},{7,3},{8,4},{9,5},{1... | collective-permute-start | bytes 1572872 | tf_op jit(solution)/shard_map/ppermute | solution.py:610
  86.2 0.0 collective-permute-done.22.from_up
  86.2 1.7 %collective-permute-done.21.from_down = bf16[256,1024]{1,0:T(8,128)(2,1)S(1)} collective-permute-done((bf16[256,1024]{1,0:T(8,128)(2,1)S(1)}, bf16[256,1024]{1,0:T(8,128)(2,1)S(1)}, u32[]{:S(2)}, u32[]{:S(2)}) %collective-permute-start.21) | collective-permute-done | bytes 524320 | tf_op jit(solution)/shard_map/ppermute | solution.py:600
  87.9 0.2 relay_sums.1
  88.1 0.1 collective-permute-start.23
  88.2 3.2 %collective-permute-start.26 = (bf16[256,1024]{1,0:T(8,128)(2,1)S(1)}, bf16[256,1024]{1,0:T(8,128)(2,1)S(1)}, u32[]{:S(2)}, u32[]{:S(2)}) collective-permute-start(bf16[256,1024]{1,0:T(8,128)(2,1)S(1)} %get-tuple-element.96), channel_id=1, source_target_pairs={{0,12},{1,13},{2,14},{3,15},{4,0},{5,1},{6,2},{7,3},{8,4},{9,5},{1... | collective-permute-start | bytes 1572872 | tf_op jit(solution)/shard_map/ppermute | solution.py:616
  91.4 0.0 collective-permute-done.15.refs_4_.refs_1_
  91.4 1.1 collective-permute-start.16
  93.1 5.6 %collective-permute-done.16.refs_5_.refs_2_ = bf16[336,512]{1,0:T(8,128)(2,1)S(1)} collective-permute-done((bf16[336,512]{1,0:T(8,128)(2,1)S(1)}, bf16[336,512]{1,0:T(8,128)(2,1)S(1)}, u32[]{:S(2)}, u32[]{:S(2)}) %collective-permute-start.16) | collective-permute-done | bytes 344096 | tf_op jit(solution)/shard_map/ppermute | solution.py:620
  98.7 0.8 unpack.1
  99.5 4.3 %pool_attention.1.pool = f32[16,72,128]{2,1,0:T(8,128)S(1)} custom-call(s32[16]{0:T(128)S(1)} %get-tuple-element.75.slots, s32[16]{0:T(128)S(1)} %get-tuple-element.76.alive, bf16[16,64,128]{2,1,0:T(8,128)(2,1)S(1)} %get-tuple-element.77.query, bf16[16,128,2048]{2,1,0:T(8,128)(2,1)S(1)} %bitcast.11, bf16[16,128,2048]{2,1,0:T(8,128)(2,1)S(1)} %bitcast.12, ...), custom_call_target="tpu_custom_call" | custom-call | flops 1000 | bytes 1000 | tf_op jit(solution)/shard_map/pool_attention/pallas_call | solution.py:344
  103.8 2.3 %product_own.1 = (f32[256,1024]{1,0:T(8,128)S(1)}, f32[256,1024]{1,0:T(8,128)S(1)}) custom-call(bf16[1024,512]{1,0:T(8,128)(2,1)S(1)} %get-tuple-element.78.refs_0_, bf16[336,512]{1,0:T(8,128)(2,1)S(1)} %collective-permute-done.15.refs_4_.refs_1_, bf16[336,512]{1,0:T(8,128)(2,1)S(1)} %collective-permute-done.16.refs_5_.refs_2_, ...), custom_call_target="tpu_custom_call" | custom-call | flops 1000 | bytes 1000 | tf_op jit(solution)/shard_map/product_own/pallas_call | solution.py:254
  106.2 0.0 collective-permute-done.25.down_l
  106.2 3.0 %collective-permute-done.23.up_l = bf16[256,1024]{1,0:T(8,128)(2,1)S(1)} collective-permute-done((bf16[256,1024]{1,0:T(8,128)(2,1)S(1)}, bf16[256,1024]{1,0:T(8,128)(2,1)S(1)}, u32[]{:S(2)}, u32[]{:S(2)}) %collective-permute-start.23) | collective-permute-done | bytes 524320 | tf_op jit(solution)/shard_map/ppermute | solution.py:613
  109.2 2.9 %prefix_attention.1 = (bf16[1,256,2048]{2,1,0:T(8,128)(2,1)}, bf16[16,80,128]{2,1,0:T(8,128)(2,1)S(1)}) custom-call(s32[1]{0:T(128)S(6)} %copy.12.prompt_pages, f32[256,1024]{1,0:T(8,128)S(1)} %get-tuple-element.87.own_l, f32[256,1024]{1,0:T(8,128)S(1)} %get-tuple-element.88.own_r, bf16[256,1024]{1,0:T(8,128)(2,1)S(1)} %collective-permute-done.23.up_l, ...), custom_call_target="tpu_custom_call" | custom-call | flops 300000000 | bytes 6291456 | tf_op jit(solution)/shard_map/prefix_attention/pallas_call | solution.py:506
  112.1 13.8 %all_to_all.5.arrived = bf16[16,80,128]{2,1,0:T(8,128)(2,1)S(1)} all-to-all(bf16[16,80,128]{2,1,0:T(8,128)(2,1)S(1)} %get-tuple-element.100), channel_id=1, replica_groups=mesh['prompt'=8,'sample'=16] {'sample'}, dimensions={0} | all-to-all | bytes 655360 | tf_op jit(solution)/shard_map/all_to_all | solution.py:627
  125.9 1.0 combine.1
  (21 shorter events, 0.0 us)
Async XLA Ops:
  0.6 32.4 %copy-start = (bf16[1,4096,512]{2,1,0:T(8,128)(2,1)S(1)}, bf16[1,4096,512]{2,1,0:T(8,128)(2,1)}, u32[]{:S(2)}) copy-start(bf16[1,4096,512]{2,1,0:T(8,128)(2,1)} %param.10) | copy-start | bytes 12582916
  0.6 8.1 %copy-start.4 = (s32[1,1,16]{2,1,0:T(1,128)S(1)}, s32[1,1,16]{2,1,0:T(1,128)}, u32[]{:S(2)}) copy-start(s32[1,1,16]{2,1,0:T(1,128)} %where.1) | copy-start | bytes 196
  0.6 9.4 %collective-permute-start = (bf16[512,256]{1,0:T(8,128)(2,1)}, bf16[512,256]{1,0:T(8,128)(2,1)S(1)}, u32[]{:S(2)}, u32[]{:S(2)}) collective-permute-start(bf16[512,256]{1,0:T(8,128)(2,1)} %param.11), channel_id=1, source_target_pairs={{0,1},{1,2},{2,3},{3,0},{4,5},{5,6},{6,7},{7,4},{8,9},{9,10},{10,1... | collective-permute-start | bytes 786440 | tf_op jit(solution)/shard_map/ppermute | solution.py:565
  2.3 9.4 %collective-permute-start.1 = (bf16[512,256]{1,0:T(8,128)(2,1)}, bf16[512,256]{1,0:T(8,128)(2,1)S(1)}, u32[]{:S(2)}, u32[]{:S(2)}) collective-permute-start(bf16[512,256]{1,0:T(8,128)(2,1)} %param.11), channel_id=1, source_target_pairs={{0,3},{1,0},{2,1},{3,2},{4,7},{5,4},{6,5},{7,6},{8,11},{9,8},{10,9... | collective-permute-start | bytes 786440 | tf_op jit(solution)/shard_map/ppermute | solution.py:566
  4.0 12.9 %collective-permute-start.2 = (bf16[512,256]{1,0:T(8,128)(2,1)}, bf16[512,256]{1,0:T(8,128)(2,1)S(1)}, u32[]{:S(2)}, u32[]{:S(2)}) collective-permute-start(bf16[512,256]{1,0:T(8,128)(2,1)} %param.11), channel_id=1, source_target_pairs={{0,2},{1,3},{2,0},{3,1},{4,6},{5,7},{6,4},{7,5},{8,10},{9,11},{10,... | collective-permute-start | bytes 786440 | tf_op jit(solution)/shard_map/ppermute | solution.py:564
  8.7 0.8 copy-start.2
  9.5 26.0 %copy-start.3 = (bf16[1,1,2048]{2,1,0:T(2,128)(2,1)S(1)}, bf16[1,1,2048]{2,1,0:T(2,128)(2,1)}, u32[]{:S(2)}) copy-start(bf16[1,1,2048]{2,1,0:T(2,128)(2,1)} %param.13) | copy-start | bytes 12292
  18.0 2.7 %collective-permute-start.4 = (bf16[4,512,256]{2,1,0:T(8,128)(2,1)S(1)}, bf16[4,512,256]{2,1,0:T(8,128)(2,1)S(1)}, u32[]{:S(2)}, u32[]{:S(2)}) collective-permute-start(bf16[4,512,256]{2,1,0:T(8,128)(2,1)S(1)} %pad_maximum_fusion.refs_4_), channel_id=1, source_target_pairs={{0,16},{16,0},{32,48},{48,32},{64,80},{80,64},{96,112},{112,96},{1... | collective-permute-start | bytes 3145736 | tf_op jit(solution)/shard_map/ppermute | solution.py:581
  18.0 27.9 %collective-permute-start.6 = (bf16[1040,512]{1,0:T(8,128)(2,1)S(1)}, bf16[1040,512]{1,0:T(8,128)(2,1)S(1)}, u32[]{:S(2)}, u32[]{:S(2)}) collective-permute-start(bf16[1040,512]{1,0:T(8,128)(2,1)S(1)} %get-tuple-element.60), channel_id=1, source_target_pairs={{0,2},{1,3},{2,0},{3,1},{4,6},{5,7},{6,4},{7,5},{8,10},{9,11},{10,... | collective-permute-start | bytes 3194888 | tf_op jit(solution)/shard_map/ppermute | solution.py:575
  19.0 21.4 %collective-permute-start.3 = (bf16[4,512,256]{2,1,0:T(8,128)(2,1)S(1)}, bf16[4,512,256]{2,1,0:T(8,128)(2,1)S(1)}, u32[]{:S(2)}, u32[]{:S(2)}) collective-permute-start(bf16[4,512,256]{2,1,0:T(8,128)(2,1)S(1)} %pad_maximum_fusion.refs_4_), channel_id=1, source_target_pairs={{0,32},{16,112},{32,64},{48,16},{64,96},{80,48},{96,0},{112,80},{1... | collective-permute-start | bytes 3145736 | tf_op jit(solution)/shard_map/ppermute | solution.py:580
  20.7 25.5 %collective-permute-start.5 = (bf16[4,512,256]{2,1,0:T(8,128)(2,1)S(1)}, bf16[4,512,256]{2,1,0:T(8,128)(2,1)S(1)}, u32[]{:S(2)}, u32[]{:S(2)}) collective-permute-start(bf16[4,512,256]{2,1,0:T(8,128)(2,1)S(1)} %collective-permute-done.4.refs_5_), channel_id=1, source_target_pairs={{0,32},{16,112},{32,64},{48,16},{64,96},{80,48},{96,0},{112,80},{1... | collective-permute-start | bytes 3145736 | tf_op jit(solution)/shard_map/ppermute | solution.py:582
  22.3 5.5 %collective-permute-start.10 = (bf16[40,256]{1,0:T(8,128)(2,1)S(1)}, bf16[40,256]{1,0:T(8,128)(2,1)S(1)}, u32[]{:S(2)}, u32[]{:S(2)}) collective-permute-start(bf16[40,256]{1,0:T(8,128)(2,1)S(1)} %get-tuple-element.63.refs_0_), channel_id=1, source_target_pairs={{0,12},{1,13},{2,14},{3,15},{4,0},{5,1},{6,2},{7,3},{8,4},{9,5},{1... | collective-permute-start | bytes 61448 | tf_op jit(solution)/shard_map/ppermute | solution.py:573
  26.3 5.5 %collective-permute-start.11 = (bf16[40,256]{1,0:T(8,128)(2,1)S(1)}, bf16[40,256]{1,0:T(8,128)(2,1)S(1)}, u32[]{:S(2)}, u32[]{:S(2)}) collective-permute-start(bf16[40,256]{1,0:T(8,128)(2,1)S(1)} %get-tuple-element.63.refs_0_), channel_id=1, source_target_pairs={{0,8},{1,9},{2,10},{3,11},{4,12},{5,13},{6,14},{7,15},{8,0},{9,1},... | collective-permute-start | bytes 61448 | tf_op jit(solution)/shard_map/ppermute | solution.py:573
  27.8 5.3 %collective-permute-start.9 = (bf16[40,256]{1,0:T(8,128)(2,1)S(1)}, bf16[40,256]{1,0:T(8,128)(2,1)S(1)}, u32[]{:S(2)}, u32[]{:S(2)}) collective-permute-start(bf16[40,256]{1,0:T(8,128)(2,1)S(1)} %get-tuple-element.63.refs_0_), channel_id=1, source_target_pairs={{0,4},{1,5},{2,6},{3,7},{4,8},{5,9},{6,10},{7,11},{8,12},{9,13},{1... | collective-permute-start | bytes 61448 | tf_op jit(solution)/shard_map/ppermute | solution.py:573
  33.3 29.0 %collective-permute-start.12 = (bf16[768,512]{1,0:T(8,128)(2,1)S(1)}, bf16[768,512]{1,0:T(8,128)(2,1)S(1)}, u32[]{:S(2)}, u32[]{:S(2)}) collective-permute-start(bf16[768,512]{1,0:T(8,128)(2,1)S(1)} %get-tuple-element.64), channel_id=1, source_target_pairs={{0,1},{1,2},{2,3},{3,0},{4,5},{5,6},{6,7},{7,4},{8,9},{9,10},{10,1... | collective-permute-start | bytes 2359304 | tf_op jit(solution)/shard_map/ppermute | solution.py:576
  35.5 3.4 %copy-start.1 = (bf16[1,1,16,128,2048]{4,3,2,1,0:T(8,128)(2,1)S(1)}, bf16[1,1,16,128,2048]{4,3,2,1,0:T(8,128)(2,1)}, u32[]{:S(2)}) copy-start(bf16[1,1,16,128,2048]{4,3,2,1,0:T(8,128)(2,1)} %param.14) | copy-start | bytes 25165828
  39.1 23.3 %collective-permute-start.13 = (bf16[768,512]{1,0:T(8,128)(2,1)S(1)}, bf16[768,512]{1,0:T(8,128)(2,1)S(1)}, u32[]{:S(2)}, u32[]{:S(2)}) collective-permute-start(bf16[768,512]{1,0:T(8,128)(2,1)S(1)} %get-tuple-element.65), channel_id=1, source_target_pairs={{0,3},{1,0},{2,1},{3,2},{4,7},{5,4},{6,5},{7,6},{8,11},{9,8},{10,9... | collective-permute-start | bytes 2359304 | tf_op jit(solution)/shard_map/ppermute | solution.py:577
  46.3 16.1 %collective-permute-start.7 = (bf16[2,512,256]{2,1,0:T(8,128)(2,1)S(1)}, bf16[2,512,256]{2,1,0:T(8,128)(2,1)S(1)}, u32[]{:S(2)}, u32[]{:S(2)}) collective-permute-start(bf16[2,512,256]{2,1,0:T(8,128)(2,1)S(1)} %get-tuple-element.103), channel_id=1, source_target_pairs={{0,32},{16,112},{32,64},{48,16},{64,96},{80,48},{96,0},{112,80},{1... | collective-permute-start | bytes 1572872 | tf_op jit(solution)/shard_map/ppermute | solution.py:586
  47.7 14.6 %collective-permute-start.8 = (bf16[2,512,256]{2,1,0:T(8,128)(2,1)S(1)}, bf16[2,512,256]{2,1,0:T(8,128)(2,1)S(1)}, u32[]{:S(2)}, u32[]{:S(2)}) collective-permute-start(bf16[2,512,256]{2,1,0:T(8,128)(2,1)S(1)} %get-tuple-element.102), channel_id=1, source_target_pairs={{0,32},{16,112},{32,64},{48,16},{64,96},{80,48},{96,0},{112,80},{1... | collective-permute-start | bytes 1572872 | tf_op jit(solution)/shard_map/ppermute | solution.py:586
  49.3 17.2 %collective-permute-start.17 = (bf16[4,512,256]{2,1,0:T(8,128)(2,1)S(1)}, bf16[4,512,256]{2,1,0:T(8,128)(2,1)S(1)}, u32[]{:S(2)}, u32[]{:S(2)}) collective-permute-start(bf16[4,512,256]{2,1,0:T(8,128)(2,1)S(1)} %collective-permute-done.3.refs_6_), channel_id=1, source_target_pairs={{0,16},{16,0},{32,48},{48,32},{64,80},{80,64},{96,112},{112,96},{1... | collective-permute-start | bytes 3145736 | tf_op jit(solution)/shard_map/ppermute | solution.py:587
  62.3 4.2 %collective-permute-start.18 = (bf16[4,512,256]{2,1,0:T(8,128)(2,1)S(1)}, bf16[4,512,256]{2,1,0:T(8,128)(2,1)S(1)}, u32[]{:S(2)}, u32[]{:S(2)}) collective-permute-start(bf16[4,512,256]{2,1,0:T(8,128)(2,1)S(1)} %collective-permute-done.5.refs_7_), channel_id=1, source_target_pairs={{0,16},{16,0},{32,48},{48,32},{64,80},{80,64},{96,112},{112,96},{1... | collective-permute-start | bytes 3145736 | tf_op jit(solution)/shard_map/ppermute | solution.py:588
  62.4 3.4 %collective-permute-start.19 = (bf16[2,512,256]{2,1,0:T(8,128)(2,1)S(1)}, bf16[2,512,256]{2,1,0:T(8,128)(2,1)S(1)}, u32[]{:S(2)}, u32[]{:S(2)}) collective-permute-start(bf16[2,512,256]{2,1,0:T(8,128)(2,1)S(1)} %collective-permute-done.7.refs_10_.refs_6_), channel_id=1, source_target_pairs={{0,16},{16,0},{32,48},{48,32},{64,80},{80,64},{96,112},{112,96},{1... | collective-permute-start | bytes 1572872 | tf_op jit(solution)/shard_map/ppermute | solution.py:590
  62.9 3.6 %collective-permute-start.20 = (bf16[2,512,256]{2,1,0:T(8,128)(2,1)S(1)}, bf16[2,512,256]{2,1,0:T(8,128)(2,1)S(1)}, u32[]{:S(2)}, u32[]{:S(2)}) collective-permute-start(bf16[2,512,256]{2,1,0:T(8,128)(2,1)S(1)} %collective-permute-done.8.refs_11_.refs_7_), channel_id=1, source_target_pairs={{0,16},{16,0},{32,48},{48,32},{64,80},{80,64},{96,112},{112,96},{1... | collective-permute-start | bytes 1572872 | tf_op jit(solution)/shard_map/ppermute | solution.py:590
  66.5 33.0 %slice-start = ((s8[8388608]{0:T(1024)(128)(4,1)}), s8[4194304]{0:T(1024)(128)(4,1)S(1)}, s32[]{:S(2)}) async-start(s8[8388608]{0:T(1024)(128)(4,1)} %bitcast.9), calls=%async_computation.1 | async-start | bytes 8388608
  67.8 18.5 %collective-permute-start.22 = (bf16[256,1024]{1,0:T(8,128)(2,1)S(1)}, bf16[256,1024]{1,0:T(8,128)(2,1)S(1)}, u32[]{:S(2)}, u32[]{:S(2)}) collective-permute-start(bf16[256,1024]{1,0:T(8,128)(2,1)S(1)} %product_far_r.1), channel_id=1, source_target_pairs={{0,12},{1,13},{2,14},{3,15},{4,0},{5,1},{6,2},{7,3},{8,4},{9,5},{1... | collective-permute-start | bytes 1572872 | tf_op jit(solution)/shard_map/ppermute | solution.py:601
  71.9 16.0 %collective-permute-start.21 = (bf16[256,1024]{1,0:T(8,128)(2,1)S(1)}, bf16[256,1024]{1,0:T(8,128)(2,1)S(1)}, u32[]{:S(2)}, u32[]{:S(2)}) collective-permute-start(bf16[256,1024]{1,0:T(8,128)(2,1)S(1)} %product_far_l.1), channel_id=1, source_target_pairs={{0,4},{1,5},{2,6},{3,7},{4,8},{5,9},{6,10},{7,11},{8,12},{9,13},{1... | collective-permute-start | bytes 1572872 | tf_op jit(solution)/shard_map/ppermute | solution.py:600
  71.9 5.9 %collective-permute-start.14 = (bf16[80,512]{1,0:T(8,128)(2,1)S(1)}, bf16[80,512]{1,0:T(8,128)(2,1)S(1)}, u32[]{:S(2)}, u32[]{:S(2)}) collective-permute-start(bf16[80,512]{1,0:T(8,128)(2,1)S(1)} %get-tuple-element.70), channel_id=1, source_target_pairs={{0,2},{1,3},{2,0},{3,1},{4,6},{5,7},{6,4},{7,5},{8,10},{9,11},{10,... | collective-permute-start | bytes 245768 | tf_op jit(solution)/shard_map/ppermute | solution.py:603
  77.8 21.7 %slice-start.1 = ((s8[8388608]{0:T(1024)(128)(4,1)}), s8[4194304]{0:T(1024)(128)(4,1)S(1)}, s32[]{:S(2)}) async-start(s8[8388608]{0:T(1024)(128)(4,1)} %bitcast.9), calls=%async_computation.2 | async-start | bytes 8388608
  77.8 13.6 %collective-permute-start.15 = (bf16[336,512]{1,0:T(8,128)(2,1)S(1)}, bf16[336,512]{1,0:T(8,128)(2,1)S(1)}, u32[]{:S(2)}, u32[]{:S(2)}) collective-permute-start(bf16[336,512]{1,0:T(8,128)(2,1)S(1)} %get-tuple-element.71), channel_id=1, source_target_pairs={{0,1},{1,2},{2,3},{3,0},{4,5},{5,6},{6,7},{7,4},{8,9},{9,10},{10,1... | collective-permute-start | bytes 1032200 | tf_op jit(solution)/shard_map/ppermute | solution.py:619
  82.8 23.3 %collective-permute-start.24 = (bf16[256,1024]{1,0:T(8,128)(2,1)S(1)}, bf16[256,1024]{1,0:T(8,128)(2,1)S(1)}, u32[]{:S(2)}, u32[]{:S(2)}) collective-permute-start(bf16[256,1024]{1,0:T(8,128)(2,1)S(1)} %get-tuple-element.94), channel_id=1, source_target_pairs={{0,4},{1,5},{2,6},{3,7},{4,8},{5,9},{6,10},{7,11},{8,12},{9,13},{1... | collective-permute-start | bytes 1572872 | tf_op jit(solution)/shard_map/ppermute | solution.py:610
  82.9 23.3 %collective-permute-start.25 = (bf16[256,1024]{1,0:T(8,128)(2,1)S(1)}, bf16[256,1024]{1,0:T(8,128)(2,1)S(1)}, u32[]{:S(2)}, u32[]{:S(2)}) collective-permute-start(bf16[256,1024]{1,0:T(8,128)(2,1)S(1)} %get-tuple-element.95), channel_id=1, source_target_pairs={{0,12},{1,13},{2,14},{3,15},{4,0},{5,1},{6,2},{7,3},{8,4},{9,5},{1... | collective-permute-start | bytes 1572872 | tf_op jit(solution)/shard_map/ppermute | solution.py:610
  88.1 21.1 %collective-permute-start.23 = (bf16[256,1024]{1,0:T(8,128)(2,1)S(1)}, bf16[256,1024]{1,0:T(8,128)(2,1)S(1)}, u32[]{:S(2)}, u32[]{:S(2)}) collective-permute-start(bf16[256,1024]{1,0:T(8,128)(2,1)S(1)} %get-tuple-element.93), channel_id=1, source_target_pairs={{0,4},{1,5},{2,6},{3,7},{4,8},{5,9},{6,10},{7,11},{8,12},{9,13},{1... | collective-permute-start | bytes 1572872 | tf_op jit(solution)/shard_map/ppermute | solution.py:613
  88.2 21.0 %collective-permute-start.26 = (bf16[256,1024]{1,0:T(8,128)(2,1)S(1)}, bf16[256,1024]{1,0:T(8,128)(2,1)S(1)}, u32[]{:S(2)}, u32[]{:S(2)}) collective-permute-start(bf16[256,1024]{1,0:T(8,128)(2,1)S(1)} %get-tuple-element.96), channel_id=1, source_target_pairs={{0,12},{1,13},{2,14},{3,15},{4,0},{5,1},{6,2},{7,3},{8,4},{9,5},{1... | collective-permute-start | bytes 1572872 | tf_op jit(solution)/shard_map/ppermute | solution.py:616
  91.4 7.3 %collective-permute-start.16 = (bf16[336,512]{1,0:T(8,128)(2,1)S(1)}, bf16[336,512]{1,0:T(8,128)(2,1)S(1)}, u32[]{:S(2)}, u32[]{:S(2)}) collective-permute-start(bf16[336,512]{1,0:T(8,128)(2,1)S(1)} %get-tuple-element.72), channel_id=1, source_target_pairs={{0,3},{1,0},{2,1},{3,2},{4,7},{5,4},{6,5},{7,6},{8,11},{9,8},{10,9... | collective-permute-start | bytes 1032200 | tf_op jit(solution)/shard_map/ppermute | solution.py:620

commit v13 on v9

--- a/solution.py
+++ b/solution.py
@@ -257,27 +257,26 @@
     )(*states, *pieces)
 
 
-def product_far_kernel(*refs):
-    states, pieces, outs = refs[:4], refs[4:14], refs[14:]
-    for j in range(8):
+def product_far_kernel(first, *refs):
+    states, pieces, out = refs[:4], refs[4:-1], refs[-1]
+    for j in range(4):
         total = jnp.zeros((ROWS, COLUMNS), F32)
         for d in range(4):
-            total += jnp.dot(
-                states[d][:ROWS], weight_of(pieces, j, d), preferred_element_type=F32
-            )
-        outs[j // 4][:, (j % 4) * COLUMNS : (j % 4 + 1) * COLUMNS] = total.astype(BF16)
-
-
-def product_far(states, pieces):
+            part = pieces[j][d] if first + j < 6 else weight_of((None,) * 4 + pieces, first + j, d)
+            total += jnp.dot(states[d][:ROWS], part, preferred_element_type=F32)
+        out[:, j * COLUMNS : (j + 1) * COLUMNS] = total.astype(BF16)
+
+
+def product_far(states, pieces, first, name):
     vmem = pl.BlockSpec(memory_space=pltpu.VMEM)
     return pl.pallas_call(
-        product_far_kernel,
-        out_shape=[jax.ShapeDtypeStruct((ROWS, KVW // 2), BF16)] * 2,
-        in_specs=[vmem] * 14,
-        out_specs=[vmem] * 2,
+        functools.partial(product_far_kernel, first),
+        out_shape=jax.ShapeDtypeStruct((ROWS, KVW // 2), BF16),
+        in_specs=[vmem] * (4 + len(pieces)),
+        out_specs=vmem,
         compiler_params=params(20),
         cost_estimate=cost(1000, 1000),
-        name="product_far",
+        name=name,
     )(*states, *pieces)
 
 
@@ -488,10 +487,9 @@
     first = logs.astype(BF16).astype(F32)
     second = (logs - first).astype(BF16).astype(F32)
     third = logs - first - second
-    terms = jnp.zeros((SAMPLES * HEADS, HEAD_SIZE), F32)
-    for g in range(GROUPS):
-        for t, term in enumerate((first, second, third)):
-            terms = put_lane(terms, t * GROUPS + g, term[:, g : g + 1])
+    lane = lax.broadcasted_iota(jnp.int32, logs.shape, 1)
+    later = jnp.where(lane < 2 * GROUPS, pltpu.roll(second, GROUPS, 1), pltpu.roll(third, 2 * GROUPS, 1))
+    terms = jnp.where(lane < GROUPS, first, jnp.where(lane < 3 * GROUPS, later, 0.0))
     padding = jnp.zeros((SENT - QUERY_HEADS - HEADS, HEAD_SIZE), F32)
     for r, source in enumerate(sources):
         rows = jnp.concatenate([terms[r * HEADS : (r + 1) * HEADS], padding])
@@ -590,7 +588,10 @@
     ]
     others = [own_states, rows_right, rows_left, rows_far]
 
-    far_l, far_r = product_far(others, pieces)
+    far_l = product_far(others, pieces[:4], 0, "product_far_l")
+    far_other[0], far_l = tie((far_other[0], far_l))
+    pieces[8] = far_other[0]
+    far_r = product_far(others, pieces[4:], 4, "product_far_r")
     from_down = lax.ppermute(far_l, "sample", Z_UP)
     from_up = lax.ppermute(far_r, "sample", Z_DOWN)
     last_far, rows_right = tie((last_far, rows_right))

time: 127 us -> 126 us (level)
  Pallas kernels: 24.6 us -> 21.1 us
  starting transfers between devices: 32.8 us -> 34.4 us
  waiting for transfers between devices: 47 us -> 48.6 us
    pallas_call x1, Pallas kernels: 2.91 us -> 0.24 us  [local_attention(): pl.pallas_call(local_kernel, out_shape=jax.ShapeDtypeStruct((PACK, HEAD_S...]
    ppermute x1, waiting for transfers between devices: 7.08 us -> 9.07 us  [per_device(): lax.ppermute(up_l, 'sample', Z_UP)]
    ppermute x1, starting transfers between devices: 1.99 us -> 0.01 us  [per_device(): from_down = lax.ppermute(far_l, 'sample', Z_UP)]
    ppermute x1, starting transfers between devices: 2.2 us -> 4.11 us  [per_device(): from_up = lax.ppermute(far_r, 'sample', Z_DOWN)]
    ppermute x1, waiting for transfers between devices: 0.01 us -> 1.84 us  [per_device(): rows_far = lax.ppermute(to_far, 'sample', X_FAR)]
    ppermute x1, starting transfers between devices: 1.99 us -> 3.28 us  [per_device(): lax.ppermute(down_l, 'sample', Z_DOWN)]
  transfers between devices with their start and end apart: 27 -> 27, of which waited for: 13 -> 14; matrix products, arithmetic and copies ran while one was open for 0% -> 0% of each run, Pallas kernels for 14% -> 13%
where the time goes in v13:
time: 126 us
  waiting for transfers between devices  48.6 us (39%)
  starting transfers between devices  34.4 us (27%)
  Pallas kernels  21.1 us (17%)
  blocking collectives  12.4 us (10%)
  local copies, waits for them, and re-layouts  5.57 us (4%)
  between operations  2.79 us (2%)
    ppermute x1, waiting for transfers between devices, per_device(): rows_right = lax.ppermute(to_right, 'sample', X_RIGHT)  14.9 us
    all_to_all x1, blocking collectives, per_device(): lax.all_to_all(packed, 'sample', split_axis=0, concat_axis=0, tiled=True)  12.4 us
    ppermute x1, waiting for transfers between devices, per_device(): lax.ppermute(up_l, 'sample', Z_UP)  9.07 us
    pallas_call x2, Pallas kernels, product(): pl.pallas_call(functools.partial(product_kernel, blocks), out_shape=outs,...  6.81 us
    ppermute x1, waiting for transfers between devices, per_device(): last_far = lax.ppermute(last_far, 'sample', X_FAR)  6.57 us
    ppermute x3, starting transfers between devices, per_device(): lax.ppermute(block, 'sample', to)  6.07 us
    unnamed x14, local copies, waits for them, and re-layouts  5.5 us
    ppermute x1, waiting for transfers between devices, per_device(): weight_far = lax.ppermute(kv_weight, 'sample', X_FAR)  5.14 us
  transfers between devices with their start and end apart: 27, of which 14 were waited for; matrix products, arithmetic and copies ran while one was open for 0% of the time, Pallas kernels for 13%

profile of v13, /device:TPU:0, one launch (start us, length us, event | category | flops | bytes accessed | tf_op | source)
XLA Modules:
  0.0 125.9 jit_solution(11357728453265992267)
XLA Ops:
  0.6 1.6 %collective-permute-start = (bf16[512,256]{1,0:T(8,128)(2,1)}, bf16[512,256]{1,0:T(8,128)(2,1)S(1)}, u32[]{:S(2)}, u32[]{:S(2)}) collective-permute-start(bf16[512,256]{1,0:T(8,128)(2,1)} %param.11), channel_id=1, source_target_pairs={{0,1},{1,2},{2,3},{3,0},{4,5},{5,6},{6,7},{7,4},{8,9},{9,10},{10,1... | collective-permute-start | bytes 786440 | tf_op jit(solution)/shard_map/ppermute | solution.py:560
  2.3 1.7 %collective-permute-start.1 = (bf16[512,256]{1,0:T(8,128)(2,1)}, bf16[512,256]{1,0:T(8,128)(2,1)S(1)}, u32[]{:S(2)}, u32[]{:S(2)}) collective-permute-start(bf16[512,256]{1,0:T(8,128)(2,1)} %param.11), channel_id=1, source_target_pairs={{0,3},{1,0},{2,1},{3,2},{4,7},{5,4},{6,5},{7,6},{8,11},{9,8},{10,9... | collective-permute-start | bytes 786440 | tf_op jit(solution)/shard_map/ppermute | solution.py:561
  3.9 1.9 %collective-permute-start.2 = (bf16[512,256]{1,0:T(8,128)(2,1)}, bf16[512,256]{1,0:T(8,128)(2,1)S(1)}, u32[]{:S(2)}, u32[]{:S(2)}) collective-permute-start(bf16[512,256]{1,0:T(8,128)(2,1)} %param.11), channel_id=1, source_target_pairs={{0,2},{1,3},{2,0},{3,1},{4,6},{5,7},{6,4},{7,5},{8,10},{9,11},{10,... | collective-permute-start | bytes 786440 | tf_op jit(solution)/shard_map/ppermute | solution.py:559
  5.8 1.5 %pick_far.1 = (bf16[1024,512]{1,0:T(8,128)(2,1)S(1)}, bf16[768,512]{1,0:T(8,128)(2,1)S(1)}) custom-call(bf16[4,4,256,512]{3,2,1,0:T(8,128)(2,1)} %bitcast.15), custom_call_target="tpu_custom_call" | custom-call | flops 1000 | bytes 1000 | tf_op jit(solution)/shard_map/pick_far/pallas_call | solution.py:178
  8.6 0.0 copy-start.2
  8.6 0.7 copy-done.2
  9.4 0.7 copy-done.4
  10.0 0.6 prepare.1
  10.6 1.1 collective-permute-done.1
  11.7 5.1 %collective-permute-done.2 = bf16[512,256]{1,0:T(8,128)(2,1)S(1)} collective-permute-done((bf16[512,256]{1,0:T(8,128)(2,1)}, bf16[512,256]{1,0:T(8,128)(2,1)S(1)}, u32[]{:S(2)}, u32[]{:S(2)}) %collective-permute-start.2) | collective-permute-done | bytes 262176 | tf_op jit(solution)/shard_map/ppermute | solution.py:559
  16.9 1.1 pad_maximum_fusion.refs_4_
  17.9 0.1 collective-permute-start.9
  18.0 1.6 %collective-permute-start.8 = (bf16[4,512,256]{2,1,0:T(8,128)(2,1)S(1)}, bf16[4,512,256]{2,1,0:T(8,128)(2,1)S(1)}, u32[]{:S(2)}, u32[]{:S(2)}) collective-permute-start(bf16[4,512,256]{2,1,0:T(8,128)(2,1)S(1)} %pad_maximum_fusion.refs_4_), channel_id=1, source_target_pairs={{0,32},{16,112},{32,64},{48,16},{64,96},{80,48},{96,0},{112,80},{1... | collective-permute-start | bytes 3145736 | tf_op jit(solution)/shard_map/ppermute | solution.py:575
  19.7 1.0 collective-permute-done.9.refs_5_
  20.7 1.6 %collective-permute-start.10 = (bf16[4,512,256]{2,1,0:T(8,128)(2,1)S(1)}, bf16[4,512,256]{2,1,0:T(8,128)(2,1)S(1)}, u32[]{:S(2)}, u32[]{:S(2)}) collective-permute-start(bf16[4,512,256]{2,1,0:T(8,128)(2,1)S(1)} %collective-permute-done.9.refs_5_), channel_id=1, source_target_pairs={{0,32},{16,112},{32,64},{48,16},{64,96},{80,48},{96,0},{112,80},{1... | collective-permute-start | bytes 3145736 | tf_op jit(solution)/shard_map/ppermute | solution.py:577
  22.3 0.8 collective-permute-start.11
  23.1 1.9 %collective-permute-start.3 = (bf16[40,256]{1,0:T(8,128)(2,1)S(1)}, bf16[40,256]{1,0:T(8,128)(2,1)S(1)}, u32[]{:S(2)}, u32[]{:S(2)}) collective-permute-start(bf16[40,256]{1,0:T(8,128)(2,1)S(1)} %get-tuple-element.59.refs_0_), channel_id=1, source_target_pairs={{0,4},{1,5},{2,6},{3,7},{4,8},{5,9},{6,10},{7,11},{8,12},{9,13},{1... | collective-permute-start | bytes 61448 | tf_op jit(solution)/shard_map/ppermute | solution.py:568
  25.0 2.1 %collective-permute-start.4 = (bf16[40,256]{1,0:T(8,128)(2,1)S(1)}, bf16[40,256]{1,0:T(8,128)(2,1)S(1)}, u32[]{:S(2)}, u32[]{:S(2)}) collective-permute-start(bf16[40,256]{1,0:T(8,128)(2,1)S(1)} %get-tuple-element.59.refs_0_), channel_id=1, source_target_pairs={{0,12},{1,13},{2,14},{3,15},{4,0},{5,1},{6,2},{7,3},{8,4},{9,5},{1... | collective-permute-start | bytes 61448 | tf_op jit(solution)/shard_map/ppermute | solution.py:568
  27.1 1.8 %collective-permute-done.3.refs_1_ = bf16[40,256]{1,0:T(8,128)(2,1)S(1)} collective-permute-done((bf16[40,256]{1,0:T(8,128)(2,1)S(1)}, bf16[40,256]{1,0:T(8,128)(2,1)S(1)}, u32[]{:S(2)}, u32[]{:S(2)}) %collective-permute-start.3) | collective-permute-done | bytes 20512 | tf_op jit(solution)/shard_map/ppermute | solution.py:568
  28.9 2.0 %collective-permute-start.5 = (bf16[40,256]{1,0:T(8,128)(2,1)S(1)}, bf16[40,256]{1,0:T(8,128)(2,1)S(1)}, u32[]{:S(2)}, u32[]{:S(2)}) collective-permute-start(bf16[40,256]{1,0:T(8,128)(2,1)S(1)} %get-tuple-element.59.refs_0_), channel_id=1, source_target_pairs={{0,8},{1,9},{2,10},{3,11},{4,12},{5,13},{6,14},{7,15},{8,0},{9,1},... | collective-permute-start | bytes 61448 | tf_op jit(solution)/shard_map/ppermute | solution.py:568
  30.9 3.2 %collective-permute-done.5.refs_3_ = bf16[40,256]{1,0:T(8,128)(2,1)S(1)} collective-permute-done((bf16[40,256]{1,0:T(8,128)(2,1)S(1)}, bf16[40,256]{1,0:T(8,128)(2,1)S(1)}, u32[]{:S(2)}, u32[]{:S(2)}) %collective-permute-start.5) | collective-permute-done | bytes 20512 | tf_op jit(solution)/shard_map/ppermute | solution.py:568
  34.2 0.3 pick_near.1
  34.5 2.1 %collective-permute-start.14 = (bf16[848,512]{1,0:T(8,128)(2,1)S(1)}, bf16[848,512]{1,0:T(8,128)(2,1)S(1)}, u32[]{:S(2)}, u32[]{:S(2)}) collective-permute-start(bf16[848,512]{1,0:T(8,128)(2,1)S(1)} %get-tuple-element.69), channel_id=1, source_target_pairs={{0,1},{1,2},{2,3},{3,0},{4,5},{5,6},{6,7},{7,4},{8,9},{9,10},{10,1... | collective-permute-start | bytes 2605064 | tf_op jit(solution)/shard_map/ppermute | solution.py:571
  36.5 1.2 collective-permute-start.15
  37.8 3.4 %copy-done.1 = bf16[1,1,16,128,2048]{4,3,2,1,0:T(8,128)(2,1)S(1)} copy-done((bf16[1,1,16,128,2048]{4,3,2,1,0:T(8,128)(2,1)S(1)}, bf16[1,1,16,128,2048]{4,3,2,1,0:T(8,128)(2,1)}, u32[]{:S(2)}) %copy-start.1) | copy-done | bytes 8388632
  41.2 0.7 copy-done.3
  41.9 0.2 local_attention.1.local
  42.1 1.8 %collective-permute-done.11.refs_3_ = bf16[768,512]{1,0:T(8,128)(2,1)S(1)} collective-permute-done((bf16[768,512]{1,0:T(8,128)(2,1)S(1)}, bf16[768,512]{1,0:T(8,128)(2,1)S(1)}, u32[]{:S(2)}, u32[]{:S(2)}) %collective-permute-start.11) | collective-permute-done | bytes 786464 | tf_op jit(solution)/shard_map/ppermute | solution.py:570
  44.0 0.0 collective-permute-done.8.refs_6_
  44.0 1.4 %collective-permute-done.10.refs_7_ = bf16[4,512,256]{2,1,0:T(8,128)(2,1)S(1)} collective-permute-done((bf16[4,512,256]{2,1,0:T(8,128)(2,1)S(1)}, bf16[4,512,256]{2,1,0:T(8,128)(2,1)S(1)}, u32[]{:S(2)}, u32[]{:S(2)}) %collective-permute-start.10) | collective-permute-done | bytes 1048608 | tf_op jit(solution)/shard_map/ppermute | solution.py:577
  45.4 0.1 fusion
  45.4 0.6 collective-permute-start.12
  46.0 1.4 %collective-permute-start.13 = (bf16[2,512,256]{2,1,0:T(8,128)(2,1)S(1)}, bf16[2,512,256]{2,1,0:T(8,128)(2,1)S(1)}, u32[]{:S(2)}, u32[]{:S(2)}) collective-permute-start(bf16[2,512,256]{2,1,0:T(8,128)(2,1)S(1)} %get-tuple-element.108), channel_id=1, source_target_pairs={{0,32},{16,112},{32,64},{48,16},{64,96},{80,48},{96,0},{112,80},{1... | collective-permute-start | bytes 1572872 | tf_op jit(solution)/shard_map/ppermute | solution.py:581
  47.4 0.4 collective-permute-start.18
  47.9 14.9 %collective-permute-done.14.refs_1_.refs_4_ = bf16[848,512]{1,0:T(8,128)(2,1)S(1)} collective-permute-done((bf16[848,512]{1,0:T(8,128)(2,1)S(1)}, bf16[848,512]{1,0:T(8,128)(2,1)S(1)}, u32[]{:S(2)}, u32[]{:S(2)}) %collective-permute-start.14) | collective-permute-done | bytes 868384 | tf_op jit(solution)/shard_map/ppermute | solution.py:571
  62.8 0.0 collective-permute-start.19
  62.8 0.0 collective-permute-done.15.refs_2_.refs_5_
  62.8 0.6 collective-permute-start.16
  63.4 0.1 collective-permute-start.20
  63.5 1.2 product_far_l.1
  64.7 1.5 %collective-permute-done.16.refs_8_.refs_12_ = bf16[2,512,256]{2,1,0:T(8,128)(2,1)S(1)} collective-permute-done((bf16[2,512,256]{2,1,0:T(8,128)(2,1)S(1)}, bf16[2,512,256]{2,1,0:T(8,128)(2,1)S(1)}, u32[]{:S(2)}, u32[]{:S(2)}) %collective-permute-start.16) | collective-permute-done | bytes 524320 | tf_op jit(solution)/shard_map/ppermute | solution.py:585
  66.2 0.7 collective-permute-done.20.refs_9_.refs_13_
  67.0 1.2 product_far_r.1
  68.2 0.0 slice-start
  68.2 4.1 %collective-permute-start.21 = (bf16[256,1024]{1,0:T(8,128)(2,1)S(1)}, bf16[256,1024]{1,0:T(8,128)(2,1)S(1)}, u32[]{:S(2)}, u32[]{:S(2)}) collective-permute-start(bf16[256,1024]{1,0:T(8,128)(2,1)S(1)} %product_far_r.1), channel_id=1, source_target_pairs={{0,12},{1,13},{2,14},{3,15},{4,0},{5,1},{6,2},{7,3},{8,4},{9,5},{1... | collective-permute-start | bytes 1572872 | tf_op jit(solution)/shard_map/ppermute | solution.py:596
  72.3 0.8 collective-permute-start.22
  73.2 0.5 collective-permute-start.6
  73.7 4.5 %product_near.1 = (bf16[256,1024]{1,0:T(8,128)(2,1)S(1)}, bf16[256,1024]{1,0:T(8,128)(2,1)S(1)}, bf16[256,1024]{1,0:T(8,128)(2,1)S(1)}, bf16[256,1024]{1,0:T(8,128)(2,1)S(1)}) custom-call(bf16[1024,512]{1,0:T(8,128)(2,1)S(1)} %get-tuple-element.94.refs_0_, bf16[848,512]{1,0:T(8,128)(2,1)S(1)} %collective-permute-done.14.refs_1_.refs_4_, ...), custom_call_target="tpu_custom_call" | custom-call | flops 1000 | bytes 1000 | tf_op jit(solution)/shard_map/product_near/pallas_call | solution.py:249
  78.2 0.1 collective-permute-start.24
  78.3 6.6 %collective-permute-done.22.refs_6_.refs_3_ = bf16[336,512]{1,0:T(8,128)(2,1)S(1)} collective-permute-done((bf16[336,512]{1,0:T(8,128)(2,1)S(1)}, bf16[336,512]{1,0:T(8,128)(2,1)S(1)}, u32[]{:S(2)}, u32[]{:S(2)}) %collective-permute-start.22) | collective-permute-done | bytes 344096 | tf_op jit(solution)/shard_map/ppermute | solution.py:598
  84.8 3.3 %collective-permute-start.25 = (bf16[256,1024]{1,0:T(8,128)(2,1)S(1)}, bf16[256,1024]{1,0:T(8,128)(2,1)S(1)}, u32[]{:S(2)}, u32[]{:S(2)}) collective-permute-start(bf16[256,1024]{1,0:T(8,128)(2,1)S(1)} %get-tuple-element.101), channel_id=1, source_target_pairs={{0,12},{1,13},{2,14},{3,15},{4,0},{5,1},{6,2},{7,3},{8,4},{9,5},{1... | collective-permute-start | bytes 1572872 | tf_op jit(solution)/shard_map/ppermute | solution.py:602
  88.1 0.2 collective-permute-done.17.from_down
  88.4 0.2 relay_sums.1
  88.6 0.1 collective-permute-start.23
  88.7 3.2 %collective-permute-start.26 = (bf16[256,1024]{1,0:T(8,128)(2,1)S(1)}, bf16[256,1024]{1,0:T(8,128)(2,1)S(1)}, u32[]{:S(2)}, u32[]{:S(2)}) collective-permute-start(bf16[256,1024]{1,0:T(8,128)(2,1)S(1)} %get-tuple-element.102), channel_id=1, source_target_pairs={{0,12},{1,13},{2,14},{3,15},{4,0},{5,1},{6,2},{7,3},{8,4},{9,5},{1... | collective-permute-start | bytes 1572872 | tf_op jit(solution)/shard_map/ppermute | solution.py:609
  91.9 0.5 collective-permute-start.7
  93.0 0.8 unpack.1
  93.9 4.3 %pool_attention.1.pool = f32[16,72,128]{2,1,0:T(8,128)S(1)} custom-call(s32[16]{0:T(128)S(1)} %get-tuple-element.91.slots, s32[16]{0:T(128)S(1)} %get-tuple-element.92.alive, bf16[16,64,128]{2,1,0:T(8,128)(2,1)S(1)} %get-tuple-element.93.query, bf16[16,128,2048]{2,1,0:T(8,128)(2,1)S(1)} %bitcast.11, bf16[16,128,2048]{2,1,0:T(8,128)(2,1)S(1)} %bitcast.12, ...), custom_call_target="tpu_custom_call" | custom-call | flops 1000 | bytes 1000 | tf_op jit(solution)/shard_map/pool_attention/pallas_call | solution.py:339
  98.2 0.1 collective-permute-done.7.refs_2_
  98.3 2.3 %product_own.1 = (f32[256,1024]{1,0:T(8,128)S(1)}, f32[256,1024]{1,0:T(8,128)S(1)}) custom-call(bf16[1024,512]{1,0:T(8,128)(2,1)S(1)} %get-tuple-element.94.refs_0_, bf16[256,512]{1,0:T(8,128)(2,1)S(1)} %collective-permute-done.6.refs_1_, bf16[256,512]{1,0:T(8,128)(2,1)S(1)} %collective-permute-done.7.refs_2_, ...), custom_call_target="tpu_custom_call" | custom-call | flops 1000 | bytes 1000 | tf_op jit(solution)/shard_map/product_own/pallas_call | solution.py:249
  100.6 9.1 %collective-permute-done.23.up_l = bf16[256,1024]{1,0:T(8,128)(2,1)S(1)} collective-permute-done((bf16[256,1024]{1,0:T(8,128)(2,1)S(1)}, bf16[256,1024]{1,0:T(8,128)(2,1)S(1)}, u32[]{:S(2)}, u32[]{:S(2)}) %collective-permute-start.23) | collective-permute-done | bytes 524320 | tf_op jit(solution)/shard_map/ppermute | solution.py:606
  109.7 2.9 %prefix_attention.1 = (bf16[1,256,2048]{2,1,0:T(8,128)(2,1)}, bf16[16,80,128]{2,1,0:T(8,128)(2,1)S(1)}) custom-call(s32[1]{0:T(128)S(6)} %copy.12.prompt_pages, f32[256,1024]{1,0:T(8,128)S(1)} %get-tuple-element.98.own_l, f32[256,1024]{1,0:T(8,128)S(1)} %get-tuple-element.99.own_r, bf16[256,1024]{1,0:T(8,128)(2,1)S(1)} %collective-permute-done.23.up_l, ...), custom_call_target="tpu_custom_call" | custom-call | flops 300000000 | bytes 6291456 | tf_op jit(solution)/shard_map/prefix_attention/pallas_call | solution.py:501
  112.6 12.4 %all_to_all.5.arrived = bf16[16,80,128]{2,1,0:T(8,128)(2,1)S(1)} all-to-all(bf16[16,80,128]{2,1,0:T(8,128)(2,1)S(1)} %get-tuple-element.106), channel_id=1, replica_groups=mesh['prompt'=8,'sample'=16] {'sample'}, dimensions={0} | all-to-all | bytes 655360 | tf_op jit(solution)/shard_map/all_to_all | solution.py:621
  125.0 1.0 combine.1
  (21 shorter events, 0.0 us)
Async XLA Ops:
  0.6 33.5 %copy-start = (bf16[1,4096,512]{2,1,0:T(8,128)(2,1)S(1)}, bf16[1,4096,512]{2,1,0:T(8,128)(2,1)}, u32[]{:S(2)}) copy-start(bf16[1,4096,512]{2,1,0:T(8,128)(2,1)} %param.10) | copy-start | bytes 12582916
  0.6 10.0 %collective-permute-start = (bf16[512,256]{1,0:T(8,128)(2,1)}, bf16[512,256]{1,0:T(8,128)(2,1)S(1)}, u32[]{:S(2)}, u32[]{:S(2)}) collective-permute-start(bf16[512,256]{1,0:T(8,128)(2,1)} %param.11), channel_id=1, source_target_pairs={{0,1},{1,2},{2,3},{3,0},{4,5},{5,6},{6,7},{7,4},{8,9},{9,10},{10,1... | collective-permute-start | bytes 786440 | tf_op jit(solution)/shard_map/ppermute | solution.py:560
  2.3 9.4 %collective-permute-start.1 = (bf16[512,256]{1,0:T(8,128)(2,1)}, bf16[512,256]{1,0:T(8,128)(2,1)S(1)}, u32[]{:S(2)}, u32[]{:S(2)}) collective-permute-start(bf16[512,256]{1,0:T(8,128)(2,1)} %param.11), channel_id=1, source_target_pairs={{0,3},{1,0},{2,1},{3,2},{4,7},{5,4},{6,5},{7,6},{8,11},{9,8},{10,9... | collective-permute-start | bytes 786440 | tf_op jit(solution)/shard_map/ppermute | solution.py:561
  3.9 12.9 %collective-permute-start.2 = (bf16[512,256]{1,0:T(8,128)(2,1)}, bf16[512,256]{1,0:T(8,128)(2,1)S(1)}, u32[]{:S(2)}, u32[]{:S(2)}) collective-permute-start(bf16[512,256]{1,0:T(8,128)(2,1)} %param.11), channel_id=1, source_target_pairs={{0,2},{1,3},{2,0},{3,1},{4,6},{5,7},{6,4},{7,5},{8,10},{9,11},{10,... | collective-permute-start | bytes 786440 | tf_op jit(solution)/shard_map/ppermute | solution.py:559
  8.6 0.8 copy-start.2
  9.4 0.7 copy-start.4
  17.9 2.7 %collective-permute-start.9 = (bf16[4,512,256]{2,1,0:T(8,128)(2,1)S(1)}, bf16[4,512,256]{2,1,0:T(8,128)(2,1)S(1)}, u32[]{:S(2)}, u32[]{:S(2)}) collective-permute-start(bf16[4,512,256]{2,1,0:T(8,128)(2,1)S(1)} %pad_maximum_fusion.refs_4_), channel_id=1, source_target_pairs={{0,16},{16,0},{32,48},{48,32},{64,80},{80,64},{96,112},{112,96},{1... | collective-permute-start | bytes 3145736 | tf_op jit(solution)/shard_map/ppermute | solution.py:576
  18.0 25.9 %collective-permute-start.8 = (bf16[4,512,256]{2,1,0:T(8,128)(2,1)S(1)}, bf16[4,512,256]{2,1,0:T(8,128)(2,1)S(1)}, u32[]{:S(2)}, u32[]{:S(2)}) collective-permute-start(bf16[4,512,256]{2,1,0:T(8,128)(2,1)S(1)} %pad_maximum_fusion.refs_4_), channel_id=1, source_target_pairs={{0,32},{16,112},{32,64},{48,16},{64,96},{80,48},{96,0},{112,80},{1... | collective-permute-start | bytes 3145736 | tf_op jit(solution)/shard_map/ppermute | solution.py:575
  20.7 24.7 %collective-permute-start.10 = (bf16[4,512,256]{2,1,0:T(8,128)(2,1)S(1)}, bf16[4,512,256]{2,1,0:T(8,128)(2,1)S(1)}, u32[]{:S(2)}, u32[]{:S(2)}) collective-permute-start(bf16[4,512,256]{2,1,0:T(8,128)(2,1)S(1)} %collective-permute-done.9.refs_5_), channel_id=1, source_target_pairs={{0,32},{16,112},{32,64},{48,16},{64,96},{80,48},{96,0},{112,80},{1... | collective-permute-start | bytes 3145736 | tf_op jit(solution)/shard_map/ppermute | solution.py:577
  22.3 21.7 %collective-permute-start.11 = (bf16[768,512]{1,0:T(8,128)(2,1)S(1)}, bf16[768,512]{1,0:T(8,128)(2,1)S(1)}, u32[]{:S(2)}, u32[]{:S(2)}) collective-permute-start(bf16[768,512]{1,0:T(8,128)(2,1)S(1)} %get-tuple-element.66), channel_id=1, source_target_pairs={{0,2},{1,3},{2,0},{3,1},{4,6},{5,7},{6,4},{7,5},{8,10},{9,11},{10,... | collective-permute-start | bytes 2359304 | tf_op jit(solution)/shard_map/ppermute | solution.py:570
  23.1 5.8 %collective-permute-start.3 = (bf16[40,256]{1,0:T(8,128)(2,1)S(1)}, bf16[40,256]{1,0:T(8,128)(2,1)S(1)}, u32[]{:S(2)}, u32[]{:S(2)}) collective-permute-start(bf16[40,256]{1,0:T(8,128)(2,1)S(1)} %get-tuple-element.59.refs_0_), channel_id=1, source_target_pairs={{0,4},{1,5},{2,6},{3,7},{4,8},{5,9},{6,10},{7,11},{8,12},{9,13},{1... | collective-permute-start | bytes 61448 | tf_op jit(solution)/shard_map/ppermute | solution.py:568
  25.0 5.9 %collective-permute-start.4 = (bf16[40,256]{1,0:T(8,128)(2,1)S(1)}, bf16[40,256]{1,0:T(8,128)(2,1)S(1)}, u32[]{:S(2)}, u32[]{:S(2)}) collective-permute-start(bf16[40,256]{1,0:T(8,128)(2,1)S(1)} %get-tuple-element.59.refs_0_), channel_id=1, source_target_pairs={{0,12},{1,13},{2,14},{3,15},{4,0},{5,1},{6,2},{7,3},{8,4},{9,5},{1... | collective-permute-start | bytes 61448 | tf_op jit(solution)/shard_map/ppermute | solution.py:568
  28.9 5.3 %collective-permute-start.5 = (bf16[40,256]{1,0:T(8,128)(2,1)S(1)}, bf16[40,256]{1,0:T(8,128)(2,1)S(1)}, u32[]{:S(2)}, u32[]{:S(2)}) collective-permute-start(bf16[40,256]{1,0:T(8,128)(2,1)S(1)} %get-tuple-element.59.refs_0_), channel_id=1, source_target_pairs={{0,8},{1,9},{2,10},{3,11},{4,12},{5,13},{6,14},{7,15},{8,0},{9,1},... | collective-permute-start | bytes 61448 | tf_op jit(solution)/shard_map/ppermute | solution.py:568
  34.5 28.3 %collective-permute-start.14 = (bf16[848,512]{1,0:T(8,128)(2,1)S(1)}, bf16[848,512]{1,0:T(8,128)(2,1)S(1)}, u32[]{:S(2)}, u32[]{:S(2)}) collective-permute-start(bf16[848,512]{1,0:T(8,128)(2,1)S(1)} %get-tuple-element.69), channel_id=1, source_target_pairs={{0,1},{1,2},{2,3},{3,0},{4,5},{5,6},{6,7},{7,4},{8,9},{9,10},{10,1... | collective-permute-start | bytes 2605064 | tf_op jit(solution)/shard_map/ppermute | solution.py:571
  36.5 26.3 %collective-permute-start.15 = (bf16[848,512]{1,0:T(8,128)(2,1)S(1)}, bf16[848,512]{1,0:T(8,128)(2,1)S(1)}, u32[]{:S(2)}, u32[]{:S(2)}) collective-permute-start(bf16[848,512]{1,0:T(8,128)(2,1)S(1)} %get-tuple-element.70), channel_id=1, source_target_pairs={{0,3},{1,0},{2,1},{3,2},{4,7},{5,4},{6,5},{7,6},{8,11},{9,8},{10,9... | collective-permute-start | bytes 2605064 | tf_op jit(solution)/shard_map/ppermute | solution.py:572
  37.8 3.4 %copy-start.1 = (bf16[1,1,16,128,2048]{4,3,2,1,0:T(8,128)(2,1)S(1)}, bf16[1,1,16,128,2048]{4,3,2,1,0:T(8,128)(2,1)}, u32[]{:S(2)}) copy-start(bf16[1,1,16,128,2048]{4,3,2,1,0:T(8,128)(2,1)} %param.14) | copy-start | bytes 25165828
  41.2 0.7 copy-start.3
  45.4 17.4 %collective-permute-start.12 = (bf16[2,512,256]{2,1,0:T(8,128)(2,1)S(1)}, bf16[2,512,256]{2,1,0:T(8,128)(2,1)S(1)}, u32[]{:S(2)}, u32[]{:S(2)}) collective-permute-start(bf16[2,512,256]{2,1,0:T(8,128)(2,1)S(1)} %get-tuple-element.109), channel_id=1, source_target_pairs={{0,32},{16,112},{32,64},{48,16},{64,96},{80,48},{96,0},{112,80},{1... | collective-permute-start | bytes 1572872 | tf_op jit(solution)/shard_map/ppermute | solution.py:581
  46.0 16.8 %collective-permute-start.13 = (bf16[2,512,256]{2,1,0:T(8,128)(2,1)S(1)}, bf16[2,512,256]{2,1,0:T(8,128)(2,1)S(1)}, u32[]{:S(2)}, u32[]{:S(2)}) collective-permute-start(bf16[2,512,256]{2,1,0:T(8,128)(2,1)S(1)} %get-tuple-element.108), channel_id=1, source_target_pairs={{0,32},{16,112},{32,64},{48,16},{64,96},{80,48},{96,0},{112,80},{1... | collective-permute-start | bytes 1572872 | tf_op jit(solution)/shard_map/ppermute | solution.py:581
  47.4 19.5 %collective-permute-start.18 = (bf16[4,512,256]{2,1,0:T(8,128)(2,1)S(1)}, bf16[4,512,256]{2,1,0:T(8,128)(2,1)S(1)}, u32[]{:S(2)}, u32[]{:S(2)}) collective-permute-start(bf16[4,512,256]{2,1,0:T(8,128)(2,1)S(1)} %collective-permute-done.8.refs_6_), channel_id=1, source_target_pairs={{0,16},{16,0},{32,48},{48,32},{64,80},{80,64},{96,112},{112,96},{1... | collective-permute-start | bytes 3145736 | tf_op jit(solution)/shard_map/ppermute | solution.py:582
  62.8 4.2 %collective-permute-start.19 = (bf16[4,512,256]{2,1,0:T(8,128)(2,1)S(1)}, bf16[4,512,256]{2,1,0:T(8,128)(2,1)S(1)}, u32[]{:S(2)}, u32[]{:S(2)}) collective-permute-start(bf16[4,512,256]{2,1,0:T(8,128)(2,1)S(1)} %collective-permute-done.10.refs_7_), channel_id=1, source_target_pairs={{0,16},{16,0},{32,48},{48,32},{64,80},{80,64},{96,112},{112,96},{1... | collective-permute-start | bytes 3145736 | tf_op jit(solution)/shard_map/ppermute | solution.py:583
  62.8 3.4 %collective-permute-start.16 = (bf16[2,512,256]{2,1,0:T(8,128)(2,1)S(1)}, bf16[2,512,256]{2,1,0:T(8,128)(2,1)S(1)}, u32[]{:S(2)}, u32[]{:S(2)}) collective-permute-start(bf16[2,512,256]{2,1,0:T(8,128)(2,1)S(1)} %collective-permute-done.12.refs_6_.refs_10_), channel_id=1, source_target_pairs={{0,16},{16,0},{32,48},{48,32},{64,80},{80,64},{96,112},{112,96},{1... | collective-permute-start | bytes 1572872 | tf_op jit(solution)/shard_map/ppermute | solution.py:585
  63.4 3.6 %collective-permute-start.20 = (bf16[2,512,256]{2,1,0:T(8,128)(2,1)S(1)}, bf16[2,512,256]{2,1,0:T(8,128)(2,1)S(1)}, u32[]{:S(2)}, u32[]{:S(2)}) collective-permute-start(bf16[2,512,256]{2,1,0:T(8,128)(2,1)S(1)} %collective-permute-done.13.refs_7_.refs_11_), channel_id=1, source_target_pairs={{0,16},{16,0},{32,48},{48,32},{64,80},{80,64},{96,112},{112,96},{1... | collective-permute-start | bytes 1572872 | tf_op jit(solution)/shard_map/ppermute | solution.py:585
  68.2 25.6 %slice-start = ((s8[8388608]{0:T(1024)(128)(4,1)}), s8[4194304]{0:T(1024)(128)(4,1)S(1)}, s32[]{:S(2)}) async-start(s8[8388608]{0:T(1024)(128)(4,1)} %bitcast.9), calls=%async_computation.1 | async-start | bytes 8388608
  68.2 19.9 %collective-permute-start.21 = (bf16[256,1024]{1,0:T(8,128)(2,1)S(1)}, bf16[256,1024]{1,0:T(8,128)(2,1)S(1)}, u32[]{:S(2)}, u32[]{:S(2)}) collective-permute-start(bf16[256,1024]{1,0:T(8,128)(2,1)S(1)} %product_far_r.1), channel_id=1, source_target_pairs={{0,12},{1,13},{2,14},{3,15},{4,0},{5,1},{6,2},{7,3},{8,4},{9,5},{1... | collective-permute-start | bytes 1572872 | tf_op jit(solution)/shard_map/ppermute | solution.py:596
  72.3 16.0 %collective-permute-start.17 = (bf16[256,1024]{1,0:T(8,128)(2,1)S(1)}, bf16[256,1024]{1,0:T(8,128)(2,1)S(1)}, u32[]{:S(2)}, u32[]{:S(2)}) collective-permute-start(bf16[256,1024]{1,0:T(8,128)(2,1)S(1)} %product_far_l.1), channel_id=1, source_target_pairs={{0,4},{1,5},{2,6},{3,7},{4,8},{5,9},{6,10},{7,11},{8,12},{9,13},{1... | collective-permute-start | bytes 1572872 | tf_op jit(solution)/shard_map/ppermute | solution.py:595
  72.3 12.5 %collective-permute-start.22 = (bf16[336,512]{1,0:T(8,128)(2,1)S(1)}, bf16[336,512]{1,0:T(8,128)(2,1)S(1)}, u32[]{:S(2)}, u32[]{:S(2)}) collective-permute-start(bf16[336,512]{1,0:T(8,128)(2,1)S(1)} %get-tuple-element.80), channel_id=1, source_target_pairs={{0,2},{1,3},{2,0},{3,1},{4,6},{5,7},{6,4},{7,5},{8,10},{9,11},{10,... | collective-permute-start | bytes 1032200 | tf_op jit(solution)/shard_map/ppermute | solution.py:598
  73.2 20.7 %slice-start.1 = ((s8[8388608]{0:T(1024)(128)(4,1)}), s8[4194304]{0:T(1024)(128)(4,1)S(1)}, s32[]{:S(2)}) async-start(s8[8388608]{0:T(1024)(128)(4,1)} %bitcast.9), calls=%async_computation.2 | async-start | bytes 8388608
  73.2 18.7 %collective-permute-start.6 = (bf16[256,512]{1,0:T(8,128)(2,1)S(1)}, bf16[256,512]{1,0:T(8,128)(2,1)S(1)}, u32[]{:S(2)}, u32[]{:S(2)}) collective-permute-start(bf16[256,512]{1,0:T(8,128)(2,1)S(1)} %get-tuple-element.60), channel_id=1, source_target_pairs={{0,1},{1,2},{2,3},{3,0},{4,5},{5,6},{6,7},{7,4},{8,9},{9,10},{10,1... | collective-permute-start | bytes 786440 | tf_op jit(solution)/shard_map/ppermute | solution.py:615
  78.2 22.4 %collective-permute-start.24 = (bf16[256,1024]{1,0:T(8,128)(2,1)S(1)}, bf16[256,1024]{1,0:T(8,128)(2,1)S(1)}, u32[]{:S(2)}, u32[]{:S(2)}) collective-permute-start(bf16[256,1024]{1,0:T(8,128)(2,1)S(1)} %get-tuple-element.100), channel_id=1, source_target_pairs={{0,4},{1,5},{2,6},{3,7},{4,8},{5,9},{6,10},{7,11},{8,12},{9,13},{1... | collective-permute-start | bytes 1572872 | tf_op jit(solution)/shard_map/ppermute | solution.py:602
  84.8 15.8 %collective-permute-start.25 = (bf16[256,1024]{1,0:T(8,128)(2,1)S(1)}, bf16[256,1024]{1,0:T(8,128)(2,1)S(1)}, u32[]{:S(2)}, u32[]{:S(2)}) collective-permute-start(bf16[256,1024]{1,0:T(8,128)(2,1)S(1)} %get-tuple-element.101), channel_id=1, source_target_pairs={{0,12},{1,13},{2,14},{3,15},{4,0},{5,1},{6,2},{7,3},{8,4},{9,5},{1... | collective-permute-start | bytes 1572872 | tf_op jit(solution)/shard_map/ppermute | solution.py:602
  88.6 21.1 %collective-permute-start.23 = (bf16[256,1024]{1,0:T(8,128)(2,1)S(1)}, bf16[256,1024]{1,0:T(8,128)(2,1)S(1)}, u32[]{:S(2)}, u32[]{:S(2)}) collective-permute-start(bf16[256,1024]{1,0:T(8,128)(2,1)S(1)} %get-tuple-element.87), channel_id=1, source_target_pairs={{0,4},{1,5},{2,6},{3,7},{4,8},{5,9},{6,10},{7,11},{8,12},{9,13},{1... | collective-permute-start | bytes 1572872 | tf_op jit(solution)/shard_map/ppermute | solution.py:606
  88.7 21.0 %collective-permute-start.26 = (bf16[256,1024]{1,0:T(8,128)(2,1)S(1)}, bf16[256,1024]{1,0:T(8,128)(2,1)S(1)}, u32[]{:S(2)}, u32[]{:S(2)}) collective-permute-start(bf16[256,1024]{1,0:T(8,128)(2,1)S(1)} %get-tuple-element.102), channel_id=1, source_target_pairs={{0,12},{1,13},{2,14},{3,15},{4,0},{5,1},{6,2},{7,3},{8,4},{9,5},{1... | collective-permute-start | bytes 1572872 | tf_op jit(solution)/shard_map/ppermute | solution.py:609
  91.9 6.4 %collective-permute-start.7 = (bf16[256,512]{1,0:T(8,128)(2,1)S(1)}, bf16[256,512]{1,0:T(8,128)(2,1)S(1)}, u32[]{:S(2)}, u32[]{:S(2)}) collective-permute-start(bf16[256,512]{1,0:T(8,128)(2,1)S(1)} %get-tuple-element.61), channel_id=1, source_target_pairs={{0,3},{1,0},{2,1},{3,2},{4,7},{5,4},{6,5},{7,6},{8,11},{9,8},{10,9... | collective-permute-start | bytes 786440 | tf_op jit(solution)/shard_map/ppermute | solution.py:616
